TPU v7x, 32 devices: a whole 2x2x4 slice. The times are simulated.
32 devices in a mesh: facet: 16 (over z, x, core), band: 2 (over y).
Axes of the slice: x: 2, y: 2, z: 4, core: 2. Of those that a mesh axis runs over, the one named last changes fastest.
Arguments:
- facet_strips: float32 [2, 16, 2, 8, 4096], P('band', 'facet'), may hold values from -6 to 6
- subgrid_offsets: int32 [2, 16], replicated, may hold values from 0 to 4095
- sample_cells: int32 [2, 2, 16, 2, 512], P('band', None, 'facet'), may hold values from 0 to 511, as said below
- sample_values: float32 [2, 2, 16, 2, 512], P('band', None, 'facet'), may hold values from -6 to 6
- sample_weights: float32 [2, 2, 16, 512], P('band', None, 'facet'), may hold values from 0.1 to 1
- sample_flags: int32 [2, 2, 16, 512], P('band', None, 'facet'), may hold values 0 or 1
Outputs:
- residual_strips: float32 [16, 8, 2, 4096], P('facet', 'band')
Inputs may be any that keep to these rules, and one draw needn't show every extreme that they name: `sample_cells`: slot 0 holds a row of 0 to (16 // 8) * 8 - 1, slot 1 a column of 0 to 512 - 1; every subgrid of every sub-band and front has a sample at its last row and last column.
All inputs are finite; a program needn't handle non-finite values. No bound on the sum of `sample_flags` on one device may be relied on, other than what follows from the above.
Results may differ from a plain program's by a relative error of at most 0.006.
Values may be sent and summed in bfloat16 or wider, within the bound.
No kernel may reach another device: no remote copies, remote signals or barrier semaphores. Data moves between devices by JAX's collectives and lax.ppermute only.
A program may use at most 64 MiB of HBM per device.

v0:
```python
import functools
import math

import jax
import jax.numpy as jnp
import ml_dtypes
import numpy as np
from jax import lax
from jax.experimental import pallas as pl
from jax.experimental.pallas import tpu as pltpu
from jax.sharding import PartitionSpec as P

CONTRIB = 64
FACET_ROWS = 8
LANES = 128
HALF = LANES // 2
VMEM_LIMIT = 48 * 1024 * 1024
F32 = jnp.float32
BF16 = jnp.bfloat16


def phases(rows, cols, length, rotation):
    product = np.outer(rows, cols) % length
    return np.exp(rotation * 2j * np.pi * product / length)


def from_left(matrix):
    return np.block([[matrix.real, -matrix.imag], [matrix.imag, matrix.real]])


def from_right(matrix):
    return np.block([[matrix.real, matrix.imag], [-matrix.imag, matrix.real]])


def high_low(table):
    high = table.astype(ml_dtypes.bfloat16)
    low = (table - high.astype(np.float64)).astype(ml_dtypes.bfloat16)
    return np.stack([high, low])


def side_by_side(values):
    straight = np.concatenate([values.real, values.real], axis=-1)
    crossed = np.concatenate([-values.imag, values.imag], axis=-1)
    return np.stack([straight, crossed]).astype(np.float32)


def tables(length):
    blocks = length // CONTRIB
    short = np.arange(CONTRIB)
    outer = np.concatenate([np.arange(0, blocks, 2), np.arange(1, blocks, 2)])
    window = 1.0 + 0.5 * np.cos(np.arange(length) * (2.0 * math.pi / length))
    turn = np.tile(phases(short, short, length, -1), (1, 2))
    pair = np.eye(2)
    subgrid_len = FACET_ROWS * CONTRIB
    return dict(
        window=(window * length**-0.5).reshape(length // LANES, LANES).astype(np.float32),
        turn=np.stack([turn.real, turn.imag]).astype(np.float32),
        shift=side_by_side(phases(short, short, CONTRIB, -1)),
        outer_minus=high_low(from_left(phases(short, outer, blocks, -1))),
        inner_minus=high_low(from_right(np.kron(pair, phases(short, short, CONTRIB, -1)))),
        piece=high_low(from_right(phases(short, short, CONTRIB, 1)) * CONTRIB**-0.5),
        inner_plus=high_low(from_right(np.kron(pair, phases(short, short, CONTRIB, 1)))),
        outer_plus=high_low(from_left(phases(outer, short, blocks, 1))),
        partial=high_low(from_right(phases(short, short, CONTRIB, -1)).T * CONTRIB**-0.5),
        grid_turn=side_by_side(phases(np.arange(FACET_ROWS), short, subgrid_len, -1)),
        model=high_low(from_right(phases(short, short, CONTRIB, -1)).T * subgrid_len**-0.5),
        back=high_low(from_right(phases(short, short, CONTRIB, 1)) * subgrid_len**-0.5),
    )


def split(values):
    high = values.astype(BF16)
    return high, (values - high.astype(F32)).astype(BF16)


def dot(left, right, dims=((1,), (0,))):
    return lax.dot_general(left, right, (dims, ((), ())), preferred_element_type=F32)


def times_table(values, table, dims=((1,), (0,))):
    high, low = split(values)
    return dot(high, table[0], dims) + dot(low, table[0], dims) + dot(high, table[1], dims)


def table_times(table, values, dims=((1,), (0,))):
    high, low = split(values)
    return dot(table[0], high, dims) + dot(table[0], low, dims) + dot(table[1], high, dims)


def iota(shape, dimension):
    return lax.broadcasted_iota(jnp.int32, shape, dimension)


def swap_halves(values):
    return pltpu.roll(values, HALF, 1)


def offsets_on_lanes(offsets_ref, columns):
    fronts, owners = offsets_ref.shape
    lane = iota((1, fronts * owners * columns), 1)
    spread = jnp.zeros_like(lane)
    for place in range(fronts * owners):
        begin = place * columns
        here = (lane >= begin) & (lane < begin + columns)
        spread = jnp.where(here, offsets_ref[place % fronts, place // fronts], spread)
    return lane, spread


def place_shifts(offsets_ref, shift_ref, straight_ref, crossed_ref, columns):
    fronts, owners = offsets_ref.shape
    for place in range(fronts * owners):
        residue = offsets_ref[place % fronts, place // fronts] % CONTRIB
        rows = pl.ds(place * columns, columns)
        straight_ref[rows, :] = jnp.broadcast_to(
            shift_ref[0, pl.ds(residue, 1), :], (columns, LANES)
        )
        crossed_ref[rows, :] = jnp.broadcast_to(
            shift_ref[1, pl.ds(residue, 1), :], (columns, LANES)
        )


def one_hot(shape, targets):
    return jnp.where(iota(shape, 0) == targets, 1.0, 0.0).astype(BF16)


def turned_eighths(values, rotation):
    sign = jnp.where(iota(values[0].shape, 1) < HALF, -rotation, rotation).astype(F32)

    def quarter_turn(value):
        return swap_halves(value) * sign

    def four(a, b, c, d):
        even_sum, even_diff = a + c, a - c
        odd_sum, odd_diff = b + d, quarter_turn(b - d)
        return even_sum + odd_sum, even_diff + odd_diff, even_sum - odd_sum, even_diff - odd_diff

    even = four(*values[0::2])
    odd = four(*values[1::2])
    root = math.sqrt(0.5)
    turned = (
        odd[0],
        (odd[1] + quarter_turn(odd[1])) * root,
        quarter_turn(odd[2]),
        (quarter_turn(odd[3]) - odd[3]) * root,
    )
    return [e + o for e, o in zip(even, turned)] + [e - o for e, o in zip(even, turned)]


def predict_kernel(
    offsets_ref, strips_ref, window_ref, turn_ref, shift_ref, outer_ref, inner_ref, piece_ref,
    out_ref, real_ref, imag_ref, straight_ref, crossed_ref,
):
    columns, length = strips_ref.shape[1:]
    groups = length // LANES
    pairs = columns // 2
    place_shifts(offsets_ref, shift_ref, straight_ref, crossed_ref, columns)
    window = window_ref[...]
    low_half = iota((groups, LANES), 1) < HALF
    sections = []
    for part, held in enumerate((real_ref, imag_ref)):
        for group in range(groups):
            held[group * columns : (group + 1) * columns, :] = strips_ref[
                part, :, group * LANES : (group + 1) * LANES
            ]
        even, odd = [], []
        for pair in range(pairs):
            first = held[pl.ds(2 * pair, groups, stride=columns), :] * window
            second = held[pl.ds(2 * pair + 1, groups, stride=columns), :] * window
            even.append(jnp.where(low_half, first, swap_halves(second)))
            odd.append(jnp.where(low_half, swap_halves(first), second))
        sections += [jnp.concatenate(even, axis=1), jnp.concatenate(odd, axis=1)]
    section = table_times(outer_ref, jnp.concatenate(sections, axis=0))
    turned = []
    for pair in range(pairs):
        lanes = slice(pair * LANES, (pair + 1) * LANES)
        real, imag = section[:CONTRIB, lanes], section[CONTRIB:, lanes]
        turned.append(
            jnp.concatenate(
                [
                    real * turn_ref[0] - imag * turn_ref[1],
                    real * turn_ref[1] + imag * turn_ref[0],
                ],
                axis=1,
            )
        )
    inner = times_table(jnp.concatenate(turned, axis=0), inner_ref)
    spectrum = jnp.concatenate(
        [
            jnp.concatenate(
                [
                    inner[pair * CONTRIB : (pair + 1) * CONTRIB, part * LANES : (part + 1) * LANES]
                    for pair in range(pairs)
                ],
                axis=1,
            )
            for part in range(2)
        ],
        axis=0,
    )
    blocks = length // CONTRIB
    lane, spread = offsets_on_lanes(offsets_ref, columns)
    first_block, residue = spread // CONTRIB, spread % CONTRIB
    base = lane % columns * blocks
    width = lane.shape[1]
    shape = (columns * blocks, width)
    high, low = split(spectrum)
    pick = one_hot(shape, base + first_block)
    inside = dot(high, pick) + dot(low, pick)
    pick = one_hot(shape, base + (first_block + 1) % blocks)
    beyond = dot(high, pick) + dot(low, pick)
    kappa = iota((2 * CONTRIB, width), 0) % CONTRIB
    cutout = jnp.where(kappa >= residue, inside, beyond)
    piece = times_table(cutout.T, piece_ref)
    out_ref[...] = (piece * straight_ref[...] + swap_halves(piece) * crossed_ref[...]).astype(BF16)


def subgrid_kernel(
    pieces_ref, cells_ref, values_ref, weights_ref, flags_ref, turn_ref, model_ref, back_ref,
    out_ref, held_ref, *, columns, bands,
):
    fronts, _, samples = cells_ref.shape
    facets = pieces_ref.shape[0] // (fronts * columns)
    groups = facets // FACET_ROWS
    rows = groups * columns
    depth = FACET_ROWS * rows
    share = columns // bands
    pieces = pieces_ref[...].astype(F32)

    def block(facet, front):
        begin = (facet * fronts + front) * columns
        return pieces[begin : begin + columns, :]

    sky = [
        jnp.concatenate(
            [block(j * FACET_ROWS + i, t) for t in range(fronts) for j in range(groups)], axis=0
        )
        for i in range(FACET_ROWS)
    ]
    sky = turned_eighths(sky, -1.0)
    sky = [
        value * turn_ref[0, i : i + 1, :] + swap_halves(value) * turn_ref[1, i : i + 1, :]
        for i, value in enumerate(sky)
    ]
    stacked = jnp.concatenate(
        [value[t * rows : (t + 1) * rows, :] for t in range(fronts) for value in sky], axis=0
    )
    model = table_times(model_ref, stacked, ((1,), (1,)))
    grids = []
    for t in range(fronts):
        row, col = cells_ref[t, 0:1, :], cells_ref[t, 1:2, :]
        pick = one_hot((depth, samples), col % FACET_ROWS * rows + row)
        high, low = split(model[:, t * depth : (t + 1) * depth])
        line = dot(high, pick) + dot(low, pick)
        mask = iota((HALF, samples), 0) == col // FACET_ROWS
        factor = weights_ref[t] * flags_ref[t].astype(F32)
        highs, lows = [], []
        for part in range(2):
            predicted = jnp.sum(
                jnp.where(mask, line[part * HALF : (part + 1) * HALF, :], 0.0),
                axis=0,
                keepdims=True,
            )
            residual = factor * (values_ref[t, part : part + 1, :] - predicted)
            high = residual.astype(BF16).astype(F32)
            highs.append(jnp.where(mask, high, 0.0).astype(BF16))
            lows.append(jnp.where(mask, residual - high, 0.0).astype(BF16))
        grids.append(
            dot(pick, jnp.concatenate(highs, axis=0), ((1,), (1,)))
            + dot(pick, jnp.concatenate(lows, axis=0), ((1,), (1,)))
        )
    back = times_table(jnp.concatenate(grids, axis=0), back_ref)
    lines = []
    for i in range(FACET_ROWS):
        value = jnp.concatenate(
            [
                back[t * depth + i * rows : t * depth + (i + 1) * rows, :]
                for t in range(fronts)
            ],
            axis=0,
        )
        lines.append(
            value * turn_ref[0, i : i + 1, :] - swap_halves(value) * turn_ref[1, i : i + 1, :]
        )
    lines = turned_eighths(lines, 1.0)
    for i in range(FACET_ROWS):
        for t in range(fronts):
            for j in range(groups):
                for b in range(bands):
                    source = (t * groups + j) * columns + b * share
                    target = ((b * facets + j * FACET_ROWS + i) * fronts + t) * share
                    held_ref[target : target + share, :] = lines[i][source : source + share, :]
    out_ref[...] = held_ref[...].astype(BF16)


def return_kernel(
    offsets_ref, pieces_ref, window_ref, turn_ref, shift_ref, partial_ref, inner_ref, outer_ref,
    out_ref, straight_ref, crossed_ref, *line_refs, bands,
):
    columns, _, length = out_ref.shape
    blocks = length // CONTRIB
    groups = length // LANES
    pairs = (columns + 1) // 2
    place_shifts(offsets_ref, shift_ref, straight_ref, crossed_ref, columns)
    width = pieces_ref.shape[0] // bands
    summed = pieces_ref[0:width, :].astype(F32)
    for b in range(1, bands):
        summed += pieces_ref[b * width : (b + 1) * width, :].astype(F32)
    summed = summed * straight_ref[...] - swap_halves(summed) * crossed_ref[...]
    residues = table_times(partial_ref, summed, ((1,), (1,)))
    lane, spread = offsets_on_lanes(offsets_ref, columns)
    first_block, residue = spread // CONTRIB, spread % CONTRIB
    base = lane % columns * blocks
    kappa = iota((2 * CONTRIB, width), 0) % CONTRIB
    inside = kappa >= residue
    both = jnp.concatenate(
        [jnp.where(inside, residues, 0.0), jnp.where(inside, 0.0, residues)], axis=1
    )
    targets = jnp.concatenate(
        [base + first_block, base + (first_block + 1) % blocks], axis=1
    )
    put = one_hot((2 * pairs * blocks, 2 * width), targets)
    high, low = split(both)
    spectrum = dot(high, put, ((1,), (1,))) + dot(low, put, ((1,), (1,)))
    inner = times_table(
        jnp.concatenate(
            [
                jnp.concatenate(
                    [
                        spectrum[:CONTRIB, pair * LANES : (pair + 1) * LANES],
                        spectrum[CONTRIB:, pair * LANES : (pair + 1) * LANES],
                    ],
                    axis=1,
                )
                for pair in range(pairs)
            ],
            axis=0,
        ),
        inner_ref,
    )
    reals, imags = [], []
    for pair in range(pairs):
        rows = slice(pair * CONTRIB, (pair + 1) * CONTRIB)
        real, imag = inner[rows, :LANES], inner[rows, LANES:]
        reals.append(real * turn_ref[0] + imag * turn_ref[1])
        imags.append(imag * turn_ref[0] - real * turn_ref[1])
    lines = table_times(
        outer_ref,
        jnp.concatenate(
            [jnp.concatenate(reals, axis=1), jnp.concatenate(imags, axis=1)], axis=0
        ),
    )
    window = window_ref[...]
    low_half = iota((groups, LANES), 1) < HALF
    for part in range(2):
        for pair in range(pairs):
            lanes = slice(pair * LANES, (pair + 1) * LANES)
            begin = part * blocks
            even = lines[begin : begin + groups, lanes]
            odd = lines[begin + groups : begin + blocks, lanes]
            line_refs[2 * pair][pl.ds(part, groups, stride=2), :] = (
                jnp.where(low_half, even, swap_halves(odd)) * window
            )
            if 2 * pair + 1 < columns:
                line_refs[2 * pair + 1][pl.ds(part, groups, stride=2), :] = (
                    jnp.where(low_half, swap_halves(even), odd) * window
                )
    for column in range(columns):
        for group in range(groups):
            out_ref[column, :, group * LANES : (group + 1) * LANES] = line_refs[column][
                2 * group : 2 * group + 2, :
            ]


def kernel_call(kernel, name, out_shape, in_smem, scratch, *operands):
    smem = pl.BlockSpec(memory_space=pltpu.SMEM)
    vmem = pl.BlockSpec(memory_space=pltpu.VMEM)
    specs = [smem if index < in_smem else vmem for index in range(len(operands))]
    return pl.pallas_call(
        kernel,
        out_shape=out_shape,
        in_specs=specs,
        out_specs=vmem,
        scratch_shapes=[pltpu.VMEM(shape, F32) for shape in scratch],
        compiler_params=pltpu.CompilerParams(vmem_limit_bytes=VMEM_LIMIT),
        name=name,
    )(*operands)


def local(facets, bands, strips, offsets, cells, values, weights, flags):
    columns, length = strips.shape[-2:]
    fronts = offsets.shape[0]
    share = columns // bands
    made = {key: jnp.asarray(value) for key, value in tables(length).items()}
    rows = facets * fronts * columns
    held = length // LANES * columns
    pieces = kernel_call(
        predict_kernel, "predict", jax.ShapeDtypeStruct((rows, LANES), BF16), 1,
        [(held, LANES)] * 2 + [(rows, LANES)] * 2,
        offsets, strips[0, 0], made["window"], made["turn"], made["shift"],
        made["outer_minus"], made["inner_minus"], made["piece"],
    )
    arrived = lax.all_to_all(pieces, "facet", split_axis=0, concat_axis=0, tiled=True)
    returned = kernel_call(
        functools.partial(subgrid_kernel, columns=columns, bands=bands), "subgrid",
        jax.ShapeDtypeStruct((rows, LANES), BF16), 0, [(rows, LANES)],
        arrived, cells[0, :, 0], values[0, :, 0], weights[0], flags[0],
        made["grid_turn"], made["model"], made["back"],
    )
    delivered = lax.all_to_all(
        returned, ("band", "facet"), split_axis=0, concat_axis=0, tiled=True
    )
    width = facets * fronts * share
    lines = kernel_call(
        functools.partial(return_kernel, bands=bands), "lines",
        jax.ShapeDtypeStruct((share, 2, length), F32), 1,
        [(width, LANES)] * 2 + [(2 * length // LANES, LANES)] * share,
        offsets, delivered, made["window"], made["turn"], made["shift"],
        made["partial"], made["inner_plus"], made["outer_plus"],
    )
    return lines[None]


def solution(mesh):
    placed = (
        P("band", "facet", None, None, None),
        P(),
        P("band", None, "facet", None, None),
        P("band", None, "facet", None, None),
        P("band", None, "facet", None),
        P("band", None, "facet", None),
    )
    return jax.shard_map(
        functools.partial(local, mesh.shape["facet"], mesh.shape["band"]),
        mesh=mesh,
        in_specs=placed,
        out_specs=P("facet", "band", None, None),
        check_vma=False,
    )
```

profile of v0, /device:TPU:0, one launch (start us, length us, event | category | flops | bytes accessed | tf_op | source)
XLA Modules:
  0.0 35.3 jit_solution(5760677000510129708)
XLA Ops:
  0.0 0.0 copy-start.8
  0.0 0.0 copy-start.18
  0.0 0.7 %copy-done.8 = f32[32,128]{1,0:T(8,128)S(1)} copy-done((f32[32,128]{1,0:T(8,128)S(1)}, f32[32,128]{1,0:T(8,128)}, u32[]{:S(2)}) %copy-start.8) | copy-done | bytes 16408
  0.7 0.0 copy-done.18
  0.7 0.0 copy-start.1
  0.7 0.9 %copy-done.1 = f32[1,1,2,8,4096]{4,3,2,1,0:T(8,128)S(1)} copy-done((f32[1,1,2,8,4096]{4,3,2,1,0:T(8,128)S(1)}, f32[1,1,2,8,4096]{4,3,2,1,0:T(8,128)}, u32[]{:S(2)}) %copy-start.1) | copy-done | bytes 262168
  1.7 0.0 copy-start.2
  1.7 0.9 %copy-done.2 = bf16[2,256,256]{2,1,0:T(8,128)(2,1)S(1)} copy-done((bf16[2,256,256]{2,1,0:T(8,128)(2,1)S(1)}, bf16[2,256,256]{2,1,0:T(8,128)(2,1)}, u32[]{:S(2)}) %copy-start.2) | copy-done | bytes 262168
  2.6 0.0 copy-start.3
  2.6 0.8 %copy-done.3 = f32[2,64,128]{2,1,0:T(8,128)S(1)} copy-done((f32[2,64,128]{2,1,0:T(8,128)S(1)}, f32[2,64,128]{2,1,0:T(8,128)}, u32[]{:S(2)}) %copy-start.3) | copy-done | bytes 65560
  3.5 0.0 copy-start.4
  3.5 0.8 %copy-done.4 = f32[2,64,128]{2,1,0:T(8,128)S(1)} copy-done((f32[2,64,128]{2,1,0:T(8,128)S(1)}, f32[2,64,128]{2,1,0:T(8,128)}, u32[]{:S(2)}) %copy-start.4) | copy-done | bytes 65560
  4.3 0.0 copy-start.11
  4.3 0.8 %copy-done.11 = bf16[2,128,128]{2,1,0:T(8,128)(2,1)S(1)} copy-done((bf16[2,128,128]{2,1,0:T(8,128)(2,1)S(1)}, bf16[2,128,128]{2,1,0:T(8,128)(2,1)}, u32[]{:S(2)}) %copy-start.11) | copy-done | bytes 65560
  5.1 0.0 copy-start.12
  5.1 0.8 %copy-done.12 = bf16[2,128,128]{2,1,0:T(8,128)(2,1)S(1)} copy-done((bf16[2,128,128]{2,1,0:T(8,128)(2,1)S(1)}, bf16[2,128,128]{2,1,0:T(8,128)(2,1)}, u32[]{:S(2)}) %copy-start.12) | copy-done | bytes 65560
  6.0 0.0 copy-start.9
  6.0 0.0 copy-start.10
  6.0 1.9 %predict.1 = bf16[256,128]{1,0:T(8,128)(2,1)S(1)} custom-call(s32[2,16]{1,0:T(2,128)S(1)} %copy-done.18, f32[2,8,4096]{2,1,0:T(8,128)S(1)} %bitcast.13, f32[32,128]{1,0:T(8,128)S(1)} %copy-done.8, f32[2,64,128]{2,1,0:T(8,128)S(1)} %copy-done.4, f32[2,64,128]{2,1,0:T(8,128)S(1)} %copy-done.3, bf16[2,128,128]{2,1,0:T(8,128)(2,1)S(1)} %copy-done.12, ...), custom_call_target="tpu_custom_call" | custom-call | tf_op jit(solution)/shard_map/predict/pallas_call | solution.py:378
  7.9 0.0 copy-start.13
  7.9 0.0 copy-start.14
  7.9 0.0 copy-start.15
  7.9 0.0 copy-start.16
  7.9 0.0 copy-start.17
  8.0 0.0 copy-start
  8.0 14.2 %all_to_all.22 = bf16[16,16,128]{2,1,0:T(8,128)(2,1)S(1)} all-to-all(bf16[16,16,128]{2,1,0:T(8,128)(2,1)S(1)} %bitcast.14), channel_id=1, replica_groups=mesh['facet'=16,'band'=2] {'facet'}, dimensions={0} | all-to-all | bytes 131072 | tf_op jit(solution)/shard_map/all_to_all | solution.py:402
  22.2 0.0 copy-done.9
  22.2 0.0 copy-done.10
  22.2 0.0 copy-done.13
  22.2 0.0 copy-done.14
  22.2 0.0 copy-done.15
  22.2 0.0 copy-done.16
  22.2 0.0 copy-done.17
  22.2 0.0 copy-start.7
  22.2 1.5 %subgrid.1 = bf16[256,128]{1,0:T(8,128)(2,1)S(1)} custom-call(bf16[256,128]{1,0:T(8,128)(2,1)S(1)} %bitcast.11, s32[2,2,512]{2,1,0:T(2,128)S(1)} %bitcast.15, f32[2,2,512]{2,1,0:T(2,128)S(1)} %bitcast.16, f32[2,1,512]{2,1,0:T(1,128)S(1)} %bitcast.17, s32[2,1,512]{2,1,0:T(1,128)S(1)} %bitcast.18, f32[2,8,128]{2,1,0:T(8,128)S(1)} %copy-done.15, ...), custom_call_target="tpu_custom_call" | custom-call | tf_op jit(solution)/shard_map/subgrid/pallas_call | solution.py:378
  23.8 0.0 copy-start.5
  23.8 0.0 copy-start.6
  23.8 9.2 %all_to_all.23 = bf16[32,8,128]{2,1,0:T(8,128)(2,1)S(1)} all-to-all(bf16[32,8,128]{2,1,0:T(8,128)(2,1)S(1)} %bitcast.12), channel_id=1, replica_groups=mesh['facet'=16,'band'=2] {'band','facet'}, dimensions={0} | all-to-all | bytes 131072 | tf_op jit(solution)/shard_map/all_to_all | solution.py:409
  33.0 0.0 copy-done
  33.0 0.0 copy-done.7
  33.0 0.0 copy-done.5
  33.0 0.0 copy-done.6
  33.0 2.3 %lines.1 = f32[4,2,4096]{2,1,0:T(2,128)} custom-call(s32[2,16]{1,0:T(2,128)S(1)} %copy-done.18, bf16[256,128]{1,0:T(8,128)(2,1)S(1)} %bitcast.10, f32[32,128]{1,0:T(8,128)S(1)} %copy-done.8, f32[2,64,128]{2,1,0:T(8,128)S(1)} %copy-done.5, f32[2,64,128]{2,1,0:T(8,128)S(1)} %copy-done.3, bf16[2,128,128]{2,1,0:T(8,128)(2,1)S(1)} %copy-done.6, ...), custom_call_target="tpu_custom_call" | custom-call | tf_op jit(solution)/shard_map/lines/pallas_call | solution.py:378
Async XLA Ops:
  0.0 0.7 %copy-start.8 = (f32[32,128]{1,0:T(8,128)S(1)}, f32[32,128]{1,0:T(8,128)}, u32[]{:S(2)}) copy-start(f32[32,128]{1,0:T(8,128)} %constant.24.clone.window_ref) | copy-start | bytes 49156
  0.0 0.7 %copy-start.18 = (s32[2,16]{1,0:T(2,128)S(1)}, s32[2,16]{1,0:T(2,128)}, u32[]{:S(2)}) copy-start(s32[2,16]{1,0:T(2,128)} %offsets_ref.3) | copy-start | bytes 388
  0.7 1.0 %copy-start.1 = (f32[1,1,2,8,4096]{4,3,2,1,0:T(8,128)S(1)}, f32[1,1,2,8,4096]{4,3,2,1,0:T(8,128)}, u32[]{:S(2)}) copy-start(f32[1,1,2,8,4096]{4,3,2,1,0:T(8,128)} %param.18) | copy-start | bytes 786436
  1.7 0.9 %copy-start.2 = (bf16[2,256,256]{2,1,0:T(8,128)(2,1)S(1)}, bf16[2,256,256]{2,1,0:T(8,128)(2,1)}, u32[]{:S(2)}) copy-start(bf16[2,256,256]{2,1,0:T(8,128)(2,1)} %constant.28.clone.inner_ref) | copy-start | bytes 786436
  2.6 0.8 %copy-start.3 = (f32[2,64,128]{2,1,0:T(8,128)S(1)}, f32[2,64,128]{2,1,0:T(8,128)}, u32[]{:S(2)}) copy-start(f32[2,64,128]{2,1,0:T(8,128)} %constant.26.clone.shift_ref) | copy-start | bytes 196612
  3.5 0.8 %copy-start.4 = (f32[2,64,128]{2,1,0:T(8,128)S(1)}, f32[2,64,128]{2,1,0:T(8,128)}, u32[]{:S(2)}) copy-start(f32[2,64,128]{2,1,0:T(8,128)} %constant.25.clone.turn_ref) | copy-start | bytes 196612
  4.3 0.8 %copy-start.11 = (bf16[2,128,128]{2,1,0:T(8,128)(2,1)S(1)}, bf16[2,128,128]{2,1,0:T(8,128)(2,1)}, u32[]{:S(2)}) copy-start(bf16[2,128,128]{2,1,0:T(8,128)(2,1)} %constant.29.clone.piece_ref) | copy-start | bytes 196612
  5.1 0.8 %copy-start.12 = (bf16[2,128,128]{2,1,0:T(8,128)(2,1)S(1)}, bf16[2,128,128]{2,1,0:T(8,128)(2,1)}, u32[]{:S(2)}) copy-start(bf16[2,128,128]{2,1,0:T(8,128)(2,1)} %constant.27.clone.outer_ref) | copy-start | bytes 196612
  6.0 16.2 %copy-start.9 = (bf16[2,128,128]{2,1,0:T(8,128)(2,1)S(1)}, bf16[2,128,128]{2,1,0:T(8,128)(2,1)}, u32[]{:S(2)}) copy-start(bf16[2,128,128]{2,1,0:T(8,128)(2,1)} %constant.35.clone.back_ref) | copy-start | bytes 196612
  6.0 16.2 %copy-start.10 = (bf16[2,128,128]{2,1,0:T(8,128)(2,1)S(1)}, bf16[2,128,128]{2,1,0:T(8,128)(2,1)}, u32[]{:S(2)}) copy-start(bf16[2,128,128]{2,1,0:T(8,128)(2,1)} %constant.34.clone.model_ref) | copy-start | bytes 196612
  7.9 14.3 %copy-start.13 = (s32[1,2,1,2,512]{4,3,2,1,0:T(2,128)S(1)}, s32[1,2,1,2,512]{4,3,2,1,0:T(2,128)}, u32[]{:S(2)}) copy-start(s32[1,2,1,2,512]{4,3,2,1,0:T(2,128)} %param.20) | copy-start | bytes 24580
  7.9 14.3 %copy-start.14 = (f32[1,2,1,2,512]{4,3,2,1,0:T(2,128)S(1)}, f32[1,2,1,2,512]{4,3,2,1,0:T(2,128)}, u32[]{:S(2)}) copy-start(f32[1,2,1,2,512]{4,3,2,1,0:T(2,128)} %param.21) | copy-start | bytes 24580
  7.9 14.3 %copy-start.15 = (f32[2,8,128]{2,1,0:T(8,128)S(1)}, f32[2,8,128]{2,1,0:T(8,128)}, u32[]{:S(2)}) copy-start(f32[2,8,128]{2,1,0:T(8,128)} %constant.33.clone.turn_ref) | copy-start | bytes 24580
  7.9 14.3 %copy-start.16 = (f32[1,2,1,512]{3,2,1,0:T(1,128)S(1)}, f32[1,2,1,512]{3,2,1,0:T(1,128)}, u32[]{:S(2)}) copy-start(f32[1,2,1,512]{3,2,1,0:T(1,128)} %param.22) | copy-start | bytes 12292
  7.9 14.3 %copy-start.17 = (s32[1,2,1,512]{3,2,1,0:T(1,128)S(1)}, s32[1,2,1,512]{3,2,1,0:T(1,128)}, u32[]{:S(2)}) copy-start(s32[1,2,1,512]{3,2,1,0:T(1,128)} %param.23) | copy-start | bytes 12292
  8.0 25.1 %copy-start = (bf16[2,256,256]{2,1,0:T(8,128)(2,1)S(1)}, bf16[2,256,256]{2,1,0:T(8,128)(2,1)}, u32[]{:S(2)}) copy-start(bf16[2,256,256]{2,1,0:T(8,128)(2,1)} %constant.30.clone.inner_ref) | copy-start | bytes 786436
  22.2 10.8 %copy-start.7 = (bf16[2,128,128]{2,1,0:T(8,128)(2,1)S(1)}, bf16[2,128,128]{2,1,0:T(8,128)(2,1)}, u32[]{:S(2)}) copy-start(bf16[2,128,128]{2,1,0:T(8,128)(2,1)} %constant.31.clone.outer_ref) | copy-start | bytes 196612
  23.8 9.3 %copy-start.5 = (f32[2,64,128]{2,1,0:T(8,128)S(1)}, f32[2,64,128]{2,1,0:T(8,128)}, u32[]{:S(2)}) copy-start(f32[2,64,128]{2,1,0:T(8,128)} %constant.25.clone.turn_ref) | copy-start | bytes 196612
  23.8 9.3 %copy-start.6 = (bf16[2,128,128]{2,1,0:T(8,128)(2,1)S(1)}, bf16[2,128,128]{2,1,0:T(8,128)(2,1)}, u32[]{:S(2)}) copy-start(bf16[2,128,128]{2,1,0:T(8,128)(2,1)} %constant.32.clone.partial_ref) | copy-start | bytes 196612
where the time goes:
time: 35.8 us; the launch traced here: 35.3 us
  blocking collectives  23.4 us (65%)
  local copies, waits for them, and re-layouts  6.04 us (17%)
  Pallas kernels  5.7 us (16%)
    all_to_all x1, blocking collectives, local(): lax.all_to_all(pieces, 'facet', split_axis=0, concat_axis=0, tiled=True)  14.2 us
    all_to_all x1, blocking collectives, local(): lax.all_to_all(returned, ('band', 'facet'), split_axis=0, concat_axis=0,...  9.24 us
    unnamed x38, local copies, waits for them, and re-layouts  6.04 us
    pallas_call x3, Pallas kernels, kernel_call(): pl.pallas_call(kernel, out_shape=out_shape, in_specs=specs, out_specs=vme...  5.7 us

commit v1 on v0

--- a/solution.py
+++ b/solution.py
@@ -146,14 +146,23 @@
     return [e + o for e, o in zip(even, turned)] + [e - o for e, o in zip(even, turned)]
 
 
-def predict_kernel(
-    offsets_ref, strips_ref, window_ref, turn_ref, shift_ref, outer_ref, inner_ref, piece_ref,
-    out_ref, real_ref, imag_ref, straight_ref, crossed_ref,
-):
+def predict_kernel(*refs):
+    count = 8
+    copies = [
+        pltpu.make_async_copy(refs[i], refs[count + 1 + i], refs[-1].at[i]) for i in range(count)
+    ]
+    for copy in copies:
+        copy.start()
+    out_ref = refs[count]
+    strips_ref, window_ref, outer_ref, turn_ref, inner_ref, offsets_ref, shift_ref, piece_ref = (
+        refs[count + 1 : 2 * count + 1]
+    )
+    real_ref, imag_ref, straight_ref, crossed_ref = refs[2 * count + 1 : -1]
     columns, length = strips_ref.shape[1:]
     groups = length // LANES
     pairs = columns // 2
-    place_shifts(offsets_ref, shift_ref, straight_ref, crossed_ref, columns)
+    copies[0].wait()
+    copies[1].wait()
     window = window_ref[...]
     low_half = iota((groups, LANES), 1) < HALF
     sections = []
@@ -169,6 +178,9 @@
             even.append(jnp.where(low_half, first, swap_halves(second)))
             odd.append(jnp.where(low_half, swap_halves(first), second))
         sections += [jnp.concatenate(even, axis=1), jnp.concatenate(odd, axis=1)]
+    for copy in copies[2:]:
+        copy.wait()
+    place_shifts(offsets_ref, shift_ref, straight_ref, crossed_ref, columns)
     section = table_times(outer_ref, jnp.concatenate(sections, axis=0))
     turned = []
     for pair in range(pairs):
@@ -371,19 +383,20 @@
             ]
 
 
-def kernel_call(kernel, name, out_shape, in_smem, scratch, *operands):
-    smem = pl.BlockSpec(memory_space=pltpu.SMEM)
-    vmem = pl.BlockSpec(memory_space=pltpu.VMEM)
-    specs = [smem if index < in_smem else vmem for index in range(len(operands))]
+def kernel_call(kernel, name, out_shape, spaces, scratch, *operands):
     return pl.pallas_call(
         kernel,
         out_shape=out_shape,
-        in_specs=specs,
-        out_specs=vmem,
-        scratch_shapes=[pltpu.VMEM(shape, F32) for shape in scratch],
+        in_specs=[pl.BlockSpec(memory_space=space) for space in spaces],
+        out_specs=pl.BlockSpec(memory_space=pltpu.VMEM),
+        scratch_shapes=scratch,
         compiler_params=pltpu.CompilerParams(vmem_limit_bytes=VMEM_LIMIT),
         name=name,
     )(*operands)
+
+
+def wide(rows):
+    return pltpu.VMEM((rows, LANES), F32)
 
 
 def local(facets, bands, strips, offsets, cells, values, weights, flags):
@@ -393,16 +406,28 @@
     made = {key: jnp.asarray(value) for key, value in tables(length).items()}
     rows = facets * fronts * columns
     held = length // LANES * columns
+    fetched = [
+        strips[0, 0], made["window"], made["outer_minus"], made["turn"], made["inner_minus"],
+        offsets, made["shift"], made["piece"],
+    ]
+    is_scalar = [array is offsets for array in fetched]
+    fetched = [pltpu.with_memory_space_constraint(array, pltpu.HBM) for array in fetched]
     pieces = kernel_call(
-        predict_kernel, "predict", jax.ShapeDtypeStruct((rows, LANES), BF16), 1,
-        [(held, LANES)] * 2 + [(rows, LANES)] * 2,
-        offsets, strips[0, 0], made["window"], made["turn"], made["shift"],
-        made["outer_minus"], made["inner_minus"], made["piece"],
+        predict_kernel, "predict", jax.ShapeDtypeStruct((rows, LANES), BF16),
+        [pltpu.HBM] * len(fetched),
+        [
+            (pltpu.SMEM if scalar else pltpu.VMEM)(array.shape, array.dtype)
+            for array, scalar in zip(fetched, is_scalar)
+        ]
+        + [wide(held)] * 2
+        + [wide(rows)] * 2
+        + [pltpu.SemaphoreType.DMA((len(fetched),))],
+        *fetched,
     )
     arrived = lax.all_to_all(pieces, "facet", split_axis=0, concat_axis=0, tiled=True)
     returned = kernel_call(
         functools.partial(subgrid_kernel, columns=columns, bands=bands), "subgrid",
-        jax.ShapeDtypeStruct((rows, LANES), BF16), 0, [(rows, LANES)],
+        jax.ShapeDtypeStruct((rows, LANES), BF16), [pltpu.VMEM] * 8, [wide(rows)],
         arrived, cells[0, :, 0], values[0, :, 0], weights[0], flags[0],
         made["grid_turn"], made["model"], made["back"],
     )
@@ -412,8 +437,8 @@
     width = facets * fronts * share
     lines = kernel_call(
         functools.partial(return_kernel, bands=bands), "lines",
-        jax.ShapeDtypeStruct((share, 2, length), F32), 1,
-        [(width, LANES)] * 2 + [(2 * length // LANES, LANES)] * share,
+        jax.ShapeDtypeStruct((share, 2, length), F32), [pltpu.SMEM] + [pltpu.VMEM] * 7,
+        [wide(width)] * 2 + [wide(2 * length // LANES)] * share,
         offsets, delivered, made["window"], made["turn"], made["shift"],
         made["partial"], made["inner_plus"], made["outer_plus"],
     )

time: 35.8 us -> 30.8 us (0.86)
  local copies, waits for them, and re-layouts: 6.04 us -> 0.72 us
  Pallas kernels: 5.7 us -> 6.27 us
    unnamed x38 -> x28, local copies, waits for them, and re-layouts: 6.04 us -> 0.72 us
    pallas_call x3, Pallas kernels: 5.7 us -> 6.27 us  [kernel_call(): pl.pallas_call(kernel, out_shape=out_shape, in_specs=[pl.BlockSpec(memory...]
where the time goes in v1:
time: 30.8 us; the launch traced here: 30.6 us
  blocking collectives  23.4 us (76%)
  Pallas kernels  6.27 us (20%)
  local copies, waits for them, and re-layouts  0.72 us (2%)
    all_to_all x1, blocking collectives, local(): lax.all_to_all(pieces, 'facet', split_axis=0, concat_axis=0, tiled=True)  14.2 us
    all_to_all x1, blocking collectives, local(): lax.all_to_all(returned, ('band', 'facet'), split_axis=0, concat_axis=0,...  9.24 us
    pallas_call x3, Pallas kernels, kernel_call(): pl.pallas_call(kernel, out_shape=out_shape, in_specs=[pl.BlockSpec(memory...  6.27 us
    unnamed x28, local copies, waits for them, and re-layouts  0.72 us

profile of v1, /device:TPU:0, one launch (start us, length us, event | category | flops | bytes accessed | tf_op | source)
XLA Modules:
  0.0 30.6 jit_solution(4727174329206717130)
XLA Ops:
  0.0 0.0 copy-start.6
  0.0 0.0 copy-start.7
  0.0 0.0 copy-start.12
  0.0 2.5 %predict.1 = bf16[256,128]{1,0:T(8,128)(2,1)S(1)} custom-call(f32[2,8,4096]{2,1,0:T(8,128)} %bitcast.18, f32[32,128]{1,0:T(8,128)} %constant.24.clone.refs_1_.window_ref, bf16[2,128,128]{2,1,0:T(8,128)(2,1)} %constant.27.clone.refs_2_, f32[2,64,128]{2,1,0:T(8,128)} %constant.25.clone.refs_3_.turn_ref, bf16[2,256,256]{2,1,0:T(8,128)(2,1)} %constant.28.clone.refs_4_, ...), custom_call_target="tpu_custom_call" | custom-call | tf_op jit(solution)/shard_map/predict/pallas_call | solution.py:387
  2.5 0.0 copy-start.8
  2.5 0.0 copy-start.9
  2.5 0.0 copy-start.10
  2.5 0.0 copy-start.11
  2.5 0.0 copy-start
  2.6 14.2 %all_to_all.22 = bf16[16,16,128]{2,1,0:T(8,128)(2,1)S(1)} all-to-all(bf16[16,16,128]{2,1,0:T(8,128)(2,1)S(1)} %bitcast.13), channel_id=1, replica_groups=mesh['facet'=16,'band'=2] {'facet'}, dimensions={0} | all-to-all | bytes 131072 | tf_op jit(solution)/shard_map/all_to_all | solution.py:427
  16.7 0.0 copy-done.6
  16.8 0.0 copy-done.7
  16.8 0.0 copy-done.12
  16.8 0.0 copy-done.8
  16.8 0.0 copy-done.9
  16.8 0.0 copy-done.10
  16.8 0.0 copy-done.11
  16.8 0.0 copy-start.3
  16.8 0.0 copy-start.4
  16.8 0.0 copy-start.5
  16.8 1.5 %subgrid.1 = bf16[256,128]{1,0:T(8,128)(2,1)S(1)} custom-call(bf16[256,128]{1,0:T(8,128)(2,1)S(1)} %bitcast.11, s32[2,2,512]{2,1,0:T(2,128)S(1)} %bitcast.14, f32[2,2,512]{2,1,0:T(2,128)S(1)} %bitcast.15, f32[2,1,512]{2,1,0:T(1,128)S(1)} %bitcast.16, s32[2,1,512]{2,1,0:T(1,128)S(1)} %bitcast.17, f32[2,8,128]{2,1,0:T(8,128)S(1)} %copy-done.10, ...), custom_call_target="tpu_custom_call" | custom-call | tf_op jit(solution)/shard_map/subgrid/pallas_call | solution.py:387
  18.4 0.0 copy-start.1
  18.4 0.0 copy-start.2
  18.4 9.2 %all_to_all.23 = bf16[32,8,128]{2,1,0:T(8,128)(2,1)S(1)} all-to-all(bf16[32,8,128]{2,1,0:T(8,128)(2,1)S(1)} %bitcast.12), channel_id=1, replica_groups=mesh['facet'=16,'band'=2] {'band','facet'}, dimensions={0} | all-to-all | bytes 131072 | tf_op jit(solution)/shard_map/all_to_all | solution.py:434
  27.6 0.0 copy-start.13
  27.6 0.0 copy-done
  27.6 0.0 copy-done.3
  27.6 0.0 copy-done.4
  27.6 0.0 copy-done.5
  27.7 0.0 copy-done.1
  27.7 0.0 copy-done.2
  27.7 0.6 %copy-done.13 = s32[2,16]{1,0:T(2,128)S(1)} copy-done((s32[2,16]{1,0:T(2,128)S(1)}, s32[2,16]{1,0:T(2,128)}, u32[]{:S(2)}) %copy-start.13) | copy-done | bytes 152
  28.3 2.3 %lines.1 = f32[4,2,4096]{2,1,0:T(2,128)} custom-call(s32[2,16]{1,0:T(2,128)S(1)} %copy-done.13, bf16[256,128]{1,0:T(8,128)(2,1)S(1)} %bitcast.10, f32[32,128]{1,0:T(8,128)S(1)} %copy-done.5, f32[2,64,128]{2,1,0:T(8,128)S(1)} %copy-done.2, f32[2,64,128]{2,1,0:T(8,128)S(1)} %copy-done.1, bf16[2,128,128]{2,1,0:T(8,128)(2,1)S(1)} %copy-done.3, ...), custom_call_target="tpu_custom_call" | custom-call | tf_op jit(solution)/shard_map/lines/pallas_call | solution.py:387
Async XLA Ops:
  0.0 16.8 %copy-start.6 = (bf16[2,128,128]{2,1,0:T(8,128)(2,1)S(1)}, bf16[2,128,128]{2,1,0:T(8,128)(2,1)}, u32[]{:S(2)}) copy-start(bf16[2,128,128]{2,1,0:T(8,128)(2,1)} %constant.35.clone.back_ref) | copy-start | bytes 196612
  0.0 16.8 %copy-start.7 = (bf16[2,128,128]{2,1,0:T(8,128)(2,1)S(1)}, bf16[2,128,128]{2,1,0:T(8,128)(2,1)}, u32[]{:S(2)}) copy-start(bf16[2,128,128]{2,1,0:T(8,128)(2,1)} %constant.34.clone.model_ref) | copy-start | bytes 196612
  0.0 16.8 %copy-start.12 = (s32[1,2,1,512]{3,2,1,0:T(1,128)S(1)}, s32[1,2,1,512]{3,2,1,0:T(1,128)}, u32[]{:S(2)}) copy-start(s32[1,2,1,512]{3,2,1,0:T(1,128)} %param.23) | copy-start | bytes 12292
  2.5 14.3 %copy-start.8 = (s32[1,2,1,2,512]{4,3,2,1,0:T(2,128)S(1)}, s32[1,2,1,2,512]{4,3,2,1,0:T(2,128)}, u32[]{:S(2)}) copy-start(s32[1,2,1,2,512]{4,3,2,1,0:T(2,128)} %param.20) | copy-start | bytes 24580
  2.5 14.3 %copy-start.9 = (f32[1,2,1,2,512]{4,3,2,1,0:T(2,128)S(1)}, f32[1,2,1,2,512]{4,3,2,1,0:T(2,128)}, u32[]{:S(2)}) copy-start(f32[1,2,1,2,512]{4,3,2,1,0:T(2,128)} %param.21) | copy-start | bytes 24580
  2.5 14.3 %copy-start.10 = (f32[2,8,128]{2,1,0:T(8,128)S(1)}, f32[2,8,128]{2,1,0:T(8,128)}, u32[]{:S(2)}) copy-start(f32[2,8,128]{2,1,0:T(8,128)} %constant.33.clone.turn_ref) | copy-start | bytes 24580
  2.5 14.3 %copy-start.11 = (f32[1,2,1,512]{3,2,1,0:T(1,128)S(1)}, f32[1,2,1,512]{3,2,1,0:T(1,128)}, u32[]{:S(2)}) copy-start(f32[1,2,1,512]{3,2,1,0:T(1,128)} %param.22) | copy-start | bytes 12292
  2.5 25.1 %copy-start = (bf16[2,256,256]{2,1,0:T(8,128)(2,1)S(1)}, bf16[2,256,256]{2,1,0:T(8,128)(2,1)}, u32[]{:S(2)}) copy-start(bf16[2,256,256]{2,1,0:T(8,128)(2,1)} %constant.30.clone.inner_ref) | copy-start | bytes 786436
  16.8 10.8 %copy-start.3 = (bf16[2,128,128]{2,1,0:T(8,128)(2,1)S(1)}, bf16[2,128,128]{2,1,0:T(8,128)(2,1)}, u32[]{:S(2)}) copy-start(bf16[2,128,128]{2,1,0:T(8,128)(2,1)} %constant.32.clone.partial_ref) | copy-start | bytes 196612
  16.8 10.8 %copy-start.4 = (bf16[2,128,128]{2,1,0:T(8,128)(2,1)S(1)}, bf16[2,128,128]{2,1,0:T(8,128)(2,1)}, u32[]{:S(2)}) copy-start(bf16[2,128,128]{2,1,0:T(8,128)(2,1)} %constant.31.clone.outer_ref) | copy-start | bytes 196612
  16.8 10.8 %copy-start.5 = (f32[32,128]{1,0:T(8,128)S(1)}, f32[32,128]{1,0:T(8,128)}, u32[]{:S(2)}) copy-start(f32[32,128]{1,0:T(8,128)} %constant.24.clone.refs_1_.window_ref) | copy-start | bytes 49156
  18.4 9.3 %copy-start.1 = (f32[2,64,128]{2,1,0:T(8,128)S(1)}, f32[2,64,128]{2,1,0:T(8,128)}, u32[]{:S(2)}) copy-start(f32[2,64,128]{2,1,0:T(8,128)} %constant.26.clone.refs_6_.shift_ref) | copy-start | bytes 196612
  18.4 9.3 %copy-start.2 = (f32[2,64,128]{2,1,0:T(8,128)S(1)}, f32[2,64,128]{2,1,0:T(8,128)}, u32[]{:S(2)}) copy-start(f32[2,64,128]{2,1,0:T(8,128)} %constant.25.clone.refs_3_.turn_ref) | copy-start | bytes 196612
  27.6 0.7 %copy-start.13 = (s32[2,16]{1,0:T(2,128)S(1)}, s32[2,16]{1,0:T(2,128)}, u32[]{:S(2)}) copy-start(s32[2,16]{1,0:T(2,128)} %offsets_ref.1) | copy-start | bytes 388

commit v2 on v1

--- a/solution.py
+++ b/solution.py
@@ -14,6 +14,7 @@
 FACET_ROWS = 8
 LANES = 128
 HALF = LANES // 2
+MOST_STEPS = 32
 VMEM_LIMIT = 48 * 1024 * 1024
 F32 = jnp.float32
 BF16 = jnp.bfloat16
@@ -146,18 +147,18 @@
     return [e + o for e, o in zip(even, turned)] + [e - o for e, o in zip(even, turned)]
 
 
-def predict_kernel(*refs):
+def predict_kernel(*refs, outs):
     count = 8
+    sources, out_refs, targets = refs[:count], refs[count : count + outs], refs[count + outs :]
     copies = [
-        pltpu.make_async_copy(refs[i], refs[count + 1 + i], refs[-1].at[i]) for i in range(count)
+        pltpu.make_async_copy(sources[i], targets[i], refs[-1].at[i]) for i in range(count)
     ]
     for copy in copies:
         copy.start()
-    out_ref = refs[count]
     strips_ref, window_ref, outer_ref, turn_ref, inner_ref, offsets_ref, shift_ref, piece_ref = (
-        refs[count + 1 : 2 * count + 1]
-    )
-    real_ref, imag_ref, straight_ref, crossed_ref = refs[2 * count + 1 : -1]
+        targets[:count]
+    )
+    real_ref, imag_ref, straight_ref, crossed_ref, held_ref = targets[count:-1]
     columns, length = strips_ref.shape[1:]
     groups = length // LANES
     pairs = columns // 2
@@ -223,20 +224,34 @@
     kappa = iota((2 * CONTRIB, width), 0) % CONTRIB
     cutout = jnp.where(kappa >= residue, inside, beyond)
     piece = times_table(cutout.T, piece_ref)
-    out_ref[...] = (piece * straight_ref[...] + swap_halves(piece) * crossed_ref[...]).astype(BF16)
-
-
-def subgrid_kernel(
-    pieces_ref, cells_ref, values_ref, weights_ref, flags_ref, turn_ref, model_ref, back_ref,
-    out_ref, held_ref, *, columns, bands,
-):
+    piece = piece * straight_ref[...] + swap_halves(piece) * crossed_ref[...]
+    if outs == 1:
+        out_refs[0][...] = piece.astype(BF16)
+        return
+    held_ref[...] = piece
+    me = lax.axis_index("facet")
+    for step, out_ref in enumerate(out_refs):
+        rows = out_ref.shape[0]
+        begin = pl.multiple_of((me ^ step) * rows, rows)
+        out_ref[...] = held_ref[pl.ds(begin, rows), :].astype(BF16)
+
+
+def subgrid_kernel(*refs, columns, bands, facets, parts):
+    cells_ref, values_ref, weights_ref, flags_ref, turn_ref, model_ref, back_ref = refs[parts:-2]
+    out_ref, held_ref = refs[-2:]
     fronts, _, samples = cells_ref.shape
-    facets = pieces_ref.shape[0] // (fronts * columns)
     groups = facets // FACET_ROWS
     rows = groups * columns
     depth = FACET_ROWS * rows
     share = columns // bands
-    pieces = pieces_ref[...].astype(F32)
+    if parts == 1:
+        pieces = refs[0][...].astype(F32)
+    else:
+        me = lax.axis_index("facet")
+        for step, part_ref in enumerate(refs[:parts]):
+            begin = pl.multiple_of((me ^ step) * part_ref.shape[0], part_ref.shape[0])
+            held_ref[pl.ds(begin, part_ref.shape[0]), :] = part_ref[...].astype(F32)
+        pieces = held_ref[...]
 
     def block(facet, front):
         begin = (facet * fronts + front) * columns
@@ -388,7 +403,7 @@
         kernel,
         out_shape=out_shape,
         in_specs=[pl.BlockSpec(memory_space=space) for space in spaces],
-        out_specs=pl.BlockSpec(memory_space=pltpu.VMEM),
+        out_specs=jax.tree.map(lambda _: pl.BlockSpec(memory_space=pltpu.VMEM), out_shape),
         scratch_shapes=scratch,
         compiler_params=pltpu.CompilerParams(vmem_limit_bytes=VMEM_LIMIT),
         name=name,
@@ -412,23 +427,34 @@
     ]
     is_scalar = [array is offsets for array in fetched]
     fetched = [pltpu.with_memory_space_constraint(array, pltpu.HBM) for array in fetched]
+    parts = facets if facets <= MOST_STEPS and facets & (facets - 1) == 0 else 1
     pieces = kernel_call(
-        predict_kernel, "predict", jax.ShapeDtypeStruct((rows, LANES), BF16),
+        functools.partial(predict_kernel, outs=parts), "predict",
+        [jax.ShapeDtypeStruct((rows // parts, LANES), BF16)] * parts,
         [pltpu.HBM] * len(fetched),
         [
             (pltpu.SMEM if scalar else pltpu.VMEM)(array.shape, array.dtype)
             for array, scalar in zip(fetched, is_scalar)
         ]
         + [wide(held)] * 2
-        + [wide(rows)] * 2
+        + [wide(rows)] * 3
         + [pltpu.SemaphoreType.DMA((len(fetched),))],
         *fetched,
     )
-    arrived = lax.all_to_all(pieces, "facet", split_axis=0, concat_axis=0, tiled=True)
+    if parts == 1:
+        arrived = [lax.all_to_all(pieces[0], "facet", split_axis=0, concat_axis=0, tiled=True)]
+    else:
+        arrived = [pieces[0]] + [
+            lax.ppermute(pieces[step], "facet", [(i, i ^ step) for i in range(facets)])
+            for step in range(1, facets)
+        ]
     returned = kernel_call(
-        functools.partial(subgrid_kernel, columns=columns, bands=bands), "subgrid",
-        jax.ShapeDtypeStruct((rows, LANES), BF16), [pltpu.VMEM] * 8, [wide(rows)],
-        arrived, cells[0, :, 0], values[0, :, 0], weights[0], flags[0],
+        functools.partial(
+            subgrid_kernel, columns=columns, bands=bands, facets=facets, parts=parts
+        ),
+        "subgrid",
+        jax.ShapeDtypeStruct((rows, LANES), BF16), [pltpu.VMEM] * (7 + parts), [wide(rows)],
+        *arrived, cells[0, :, 0], values[0, :, 0], weights[0], flags[0],
         made["grid_turn"], made["model"], made["back"],
     )
     delivered = lax.all_to_all(

time: 30.8 us -> 44.5 us (1.44)
  starting transfers between devices: 0 us -> 22.1 us
  blocking collectives: 23.4 us -> 9.24 us
  waiting for transfers between devices: 0 us -> 5.63 us
    ppermute x0 -> x15, starting transfers between devices: none -> 22.1 us  [local(): lax.ppermute(pieces[step], 'facet', [(i, i ^ step) for i in range(facets)])]
    all_to_all x1 -> x0, blocking collectives: 14.2 us -> none  [local(): lax.all_to_all(pieces, 'facet', split_axis=0, concat_axis=0, tiled=True)]
    ppermute x0 -> x15, waiting for transfers between devices: none -> 5.63 us  [local(): lax.ppermute(pieces[step], 'facet', [(i, i ^ step) for i in range(facets)])]
  transfers between devices with their start and end apart: 0 -> 15, of which waited for: 0 -> 3; matrix products, arithmetic and copies ran while one was open for 0% -> 0% of each run, Pallas kernels for 0% -> 0%
where the time goes in v2:
time: 44.5 us; the launch traced here: 44.3 us
  starting transfers between devices  22.1 us (50%)
  blocking collectives  9.24 us (21%)
  Pallas kernels  6.41 us (14%)
  waiting for transfers between devices  5.63 us (13%)
  local copies, waits for them, and re-layouts  0.71 us (2%)
    ppermute x15, starting transfers between devices, local(): lax.ppermute(pieces[step], 'facet', [(i, i ^ step) for i in range(facets)])  22.1 us
    all_to_all x1, blocking collectives, local(): lax.all_to_all(returned, ('band', 'facet'), split_axis=0, concat_axis=0,...  9.24 us
    pallas_call x3, Pallas kernels, kernel_call(): pl.pallas_call(kernel, out_shape=out_shape, in_specs=[pl.BlockSpec(memory...  6.41 us
    ppermute x15, waiting for transfers between devices, local(): lax.ppermute(pieces[step], 'facet', [(i, i ^ step) for i in range(facets)])  5.63 us
  transfers between devices with their start and end apart: 15, of which 3 were waited for; matrix products, arithmetic and copies ran while one was open for 0% of the time, Pallas kernels for 0%

profile of v2, /device:TPU:0, one launch (start us, length us, event | category | flops | bytes accessed | tf_op | source)
XLA Modules:
  0.0 44.3 jit_solution(17453692442972501345)
XLA Ops:
  0.0 0.0 copy-start.11
  0.0 0.0 copy-start.12
  0.0 0.0 copy-start.4
  0.0 0.0 copy-start.5
  0.1 2.6 %predict.1 = (bf16[16,128]{1,0:T(8,128)(2,1)S(1)}, bf16[16,128]{1,0:T(8,128)(2,1)S(1)}, bf16[16,128]{1,0:T(8,128)(2,1)S(1)}, bf16[16,128]{1,0:T(8,128)(2,1)S(1)}...) custom-call(f32[2,8,4096]{2,1,0:T(8,128)} %bitcast.14, ...), custom_call_target="tpu_custom_call" | custom-call | tf_op jit(solution)/shard_map/predict/pallas_call | solution.py:402
  2.7 0.0 copy-start.2
  2.7 0.5 %collective-permute-start = (bf16[16,128]{1,0:T(8,128)(2,1)S(1)}, bf16[16,128]{1,0:T(8,128)(2,1)S(1)}, u32[]{:S(2)}, u32[]{:S(2)}) collective-permute-start(bf16[16,128]{1,0:T(8,128)(2,1)S(1)} %get-tuple-element.22), channel_id=1, source_target_pairs={{0,2},{2,0},{4,6},{6,4},{8,10},{10,8},{12,14},{14,12},{16,18},{18,... | collective-permute-start | bytes 12296 | tf_op jit(solution)/shard_map/ppermute | solution.py:448
  3.2 2.6 %collective-permute-start.1 = (bf16[16,128]{1,0:T(8,128)(2,1)S(1)}, bf16[16,128]{1,0:T(8,128)(2,1)S(1)}, u32[]{:S(2)}, u32[]{:S(2)}) collective-permute-start(bf16[16,128]{1,0:T(8,128)(2,1)S(1)} %get-tuple-element.23), channel_id=1, source_target_pairs={{0,4},{2,6},{4,0},{6,2},{8,12},{10,14},{12,8},{14,10},{16,20},{18,... | collective-permute-start | bytes 12296 | tf_op jit(solution)/shard_map/ppermute | solution.py:448
  5.7 0.1 collective-permute-start.2
  5.8 1.8 %collective-permute-start.3 = (bf16[16,128]{1,0:T(8,128)(2,1)S(1)}, bf16[16,128]{1,0:T(8,128)(2,1)S(1)}, u32[]{:S(2)}, u32[]{:S(2)}) collective-permute-start(bf16[16,128]{1,0:T(8,128)(2,1)S(1)} %get-tuple-element.25), channel_id=1, source_target_pairs={{0,8},{2,10},{4,12},{6,14},{8,0},{10,2},{12,4},{14,6},{16,24},{18,... | collective-permute-start | bytes 12296 | tf_op jit(solution)/shard_map/ppermute | solution.py:448
  7.6 0.0 collective-permute-start.4
  7.6 0.0 collective-permute-done.refs_1_
  7.7 2.6 %collective-permute-start.5 = (bf16[16,128]{1,0:T(8,128)(2,1)S(1)}, bf16[16,128]{1,0:T(8,128)(2,1)S(1)}, u32[]{:S(2)}, u32[]{:S(2)}) collective-permute-start(bf16[16,128]{1,0:T(8,128)(2,1)S(1)} %get-tuple-element.27), channel_id=1, source_target_pairs={{0,12},{2,14},{4,8},{6,10},{8,4},{10,6},{12,0},{14,2},{16,28},{18,... | collective-permute-start | bytes 12296 | tf_op jit(solution)/shard_map/ppermute | solution.py:448
  10.3 0.0 collective-permute-done.1.refs_2_
  10.3 0.1 collective-permute-start.6
  10.4 0.0 collective-permute-done.2.refs_3_
  10.4 2.7 %collective-permute-start.7 = (bf16[16,128]{1,0:T(8,128)(2,1)S(1)}, bf16[16,128]{1,0:T(8,128)(2,1)S(1)}, u32[]{:S(2)}, u32[]{:S(2)}) collective-permute-start(bf16[16,128]{1,0:T(8,128)(2,1)S(1)} %get-tuple-element.29), channel_id=1, source_target_pairs={{0,16},{2,18},{4,20},{6,22},{8,24},{10,26},{12,28},{14,30},{16,0},... | collective-permute-start | bytes 12296 | tf_op jit(solution)/shard_map/ppermute | solution.py:448
  13.0 0.0 collective-permute-done.3.refs_4_
  13.0 0.0 collective-permute-start.8
  13.1 0.0 collective-permute-done.4.refs_5_
  13.1 3.5 %collective-permute-start.9 = (bf16[16,128]{1,0:T(8,128)(2,1)S(1)}, bf16[16,128]{1,0:T(8,128)(2,1)S(1)}, u32[]{:S(2)}, u32[]{:S(2)}) collective-permute-start(bf16[16,128]{1,0:T(8,128)(2,1)S(1)} %get-tuple-element.31), channel_id=1, source_target_pairs={{0,20},{2,22},{4,16},{6,18},{8,28},{10,30},{12,24},{14,26},{16,4},... | collective-permute-start | bytes 12296 | tf_op jit(solution)/shard_map/ppermute | solution.py:448
  16.6 0.0 collective-permute-done.5.refs_6_
  16.6 0.1 collective-permute-start.10
  16.7 0.0 collective-permute-done.6.refs_7_
  16.7 3.6 %collective-permute-start.11 = (bf16[16,128]{1,0:T(8,128)(2,1)S(1)}, bf16[16,128]{1,0:T(8,128)(2,1)S(1)}, u32[]{:S(2)}, u32[]{:S(2)}) collective-permute-start(bf16[16,128]{1,0:T(8,128)(2,1)S(1)} %get-tuple-element.33), channel_id=1, source_target_pairs={{0,24},{2,26},{4,28},{6,30},{8,16},{10,18},{12,20},{14,22},{16,8},... | collective-permute-start | bytes 12296 | tf_op jit(solution)/shard_map/ppermute | solution.py:448
  20.3 0.0 collective-permute-done.7.refs_8_
  20.3 0.0 collective-permute-start.12
  20.3 0.0 collective-permute-done.8.refs_9_
  20.3 4.4 %collective-permute-start.13 = (bf16[16,128]{1,0:T(8,128)(2,1)S(1)}, bf16[16,128]{1,0:T(8,128)(2,1)S(1)}, u32[]{:S(2)}, u32[]{:S(2)}) collective-permute-start(bf16[16,128]{1,0:T(8,128)(2,1)S(1)} %get-tuple-element.35), channel_id=1, source_target_pairs={{0,28},{2,30},{4,24},{6,26},{8,20},{10,22},{12,16},{14,18},{16,12}... | collective-permute-start | bytes 12296 | tf_op jit(solution)/shard_map/ppermute | solution.py:448
  24.7 0.0 collective-permute-done.9.refs_10_
  24.7 0.1 collective-permute-start.14
  24.8 0.0 collective-permute-done.10.refs_11_
  24.8 0.0 collective-permute-done.11.refs_12_
  24.8 0.3 collective-permute-done.12.refs_13_
  25.1 1.5 %collective-permute-done.13.refs_14_ = bf16[16,128]{1,0:T(8,128)(2,1)S(1)} collective-permute-done((bf16[16,128]{1,0:T(8,128)(2,1)S(1)}, bf16[16,128]{1,0:T(8,128)(2,1)S(1)}, u32[]{:S(2)}, u32[]{:S(2)}) %collective-permute-start.13) | collective-permute-done | bytes 4128 | tf_op jit(solution)/shard_map/ppermute | solution.py:448
  26.6 3.8 %collective-permute-done.14.refs_15_ = bf16[16,128]{1,0:T(8,128)(2,1)S(1)} collective-permute-done((bf16[16,128]{1,0:T(8,128)(2,1)S(1)}, bf16[16,128]{1,0:T(8,128)(2,1)S(1)}, u32[]{:S(2)}, u32[]{:S(2)}) %collective-permute-start.14) | collective-permute-done | bytes 4128 | tf_op jit(solution)/shard_map/ppermute | solution.py:448
  30.4 0.0 copy-done.7
  30.5 0.0 copy-start.3
  30.5 1.6 %subgrid.1 = bf16[256,128]{1,0:T(8,128)(2,1)S(1)} custom-call(bf16[16,128]{1,0:T(8,128)(2,1)S(1)} %get-tuple-element.21.refs_0_, bf16[16,128]{1,0:T(8,128)(2,1)S(1)} %collective-permute-done.refs_1_, bf16[16,128]{1,0:T(8,128)(2,1)S(1)} %collective-permute-done.1.refs_2_, bf16[16,128]{1,0:T(8,128)(2,1)S(1)} %collective-permute-done.2.refs_3_, ...), custom_call_target="tpu_custom_call" | custom-call | tf_op jit(solution)/shard_map/subgrid/pallas_call | solution.py:402
  32.1 0.0 copy-start
  32.1 0.0 copy-start.1
  32.1 9.2 %all_to_all.11 = bf16[32,8,128]{2,1,0:T(8,128)(2,1)S(1)} all-to-all(bf16[32,8,128]{2,1,0:T(8,128)(2,1)S(1)} %bitcast.9), channel_id=1, replica_groups=mesh['facet'=16,'band'=2] {'band','facet'}, dimensions={0} | all-to-all | bytes 131072 | tf_op jit(solution)/shard_map/all_to_all | solution.py:460
  41.3 0.0 copy-done.5
  41.3 0.0 copy-done.3
  41.3 0.0 copy-done
  41.4 0.0 copy-done.1
  41.4 0.6 %copy-done.13 = s32[2,16]{1,0:T(2,128)S(1)} copy-done((s32[2,16]{1,0:T(2,128)S(1)}, s32[2,16]{1,0:T(2,128)}, u32[]{:S(2)}) %copy-start.13) | copy-done | bytes 152
  42.0 2.3 %lines.1 = f32[4,2,4096]{2,1,0:T(2,128)} custom-call(s32[2,16]{1,0:T(2,128)S(1)} %copy-done.13, bf16[256,128]{1,0:T(8,128)(2,1)S(1)} %bitcast.8, f32[32,128]{1,0:T(8,128)S(1)} %copy-done.5, f32[2,64,128]{2,1,0:T(8,128)S(1)} %copy-done.1, f32[2,64,128]{2,1,0:T(8,128)S(1)} %copy-done, bf16[2,128,128]{2,1,0:T(8,128)(2,1)S(1)} %copy-done.3, ...), custom_call_target="tpu_custom_call" | custom-call | tf_op jit(solution)/shard_map/lines/pallas_call | solution.py:402
  (14 shorter events, 0.0 us)
Async XLA Ops:
  0.0 30.4 %copy-start.6 = (bf16[2,128,128]{2,1,0:T(8,128)(2,1)S(1)}, bf16[2,128,128]{2,1,0:T(8,128)(2,1)}, u32[]{:S(2)}) copy-start(bf16[2,128,128]{2,1,0:T(8,128)(2,1)} %constant.35.clone.refs_22_) | copy-start | bytes 196612
  0.0 30.4 %copy-start.7 = (bf16[2,128,128]{2,1,0:T(8,128)(2,1)S(1)}, bf16[2,128,128]{2,1,0:T(8,128)(2,1)}, u32[]{:S(2)}) copy-start(bf16[2,128,128]{2,1,0:T(8,128)(2,1)} %constant.34.clone.refs_21_) | copy-start | bytes 196612
  0.0 30.4 %copy-start.8 = (s32[1,2,1,2,512]{4,3,2,1,0:T(2,128)S(1)}, s32[1,2,1,2,512]{4,3,2,1,0:T(2,128)}, u32[]{:S(2)}) copy-start(s32[1,2,1,2,512]{4,3,2,1,0:T(2,128)} %param.20) | copy-start | bytes 24580
  0.0 30.4 %copy-start.9 = (f32[1,2,1,2,512]{4,3,2,1,0:T(2,128)S(1)}, f32[1,2,1,2,512]{4,3,2,1,0:T(2,128)}, u32[]{:S(2)}) copy-start(f32[1,2,1,2,512]{4,3,2,1,0:T(2,128)} %param.21) | copy-start | bytes 24580
  0.0 30.4 %copy-start.10 = (f32[2,8,128]{2,1,0:T(8,128)S(1)}, f32[2,8,128]{2,1,0:T(8,128)}, u32[]{:S(2)}) copy-start(f32[2,8,128]{2,1,0:T(8,128)} %constant.33.clone.refs_20_) | copy-start | bytes 24580
  0.0 30.4 %copy-start.11 = (f32[1,2,1,512]{3,2,1,0:T(1,128)S(1)}, f32[1,2,1,512]{3,2,1,0:T(1,128)}, u32[]{:S(2)}) copy-start(f32[1,2,1,512]{3,2,1,0:T(1,128)} %param.22) | copy-start | bytes 12292
  0.0 30.4 %copy-start.12 = (s32[1,2,1,512]{3,2,1,0:T(1,128)S(1)}, s32[1,2,1,512]{3,2,1,0:T(1,128)}, u32[]{:S(2)}) copy-start(s32[1,2,1,512]{3,2,1,0:T(1,128)} %param.23) | copy-start | bytes 12292
  0.0 41.3 %copy-start.4 = (bf16[2,128,128]{2,1,0:T(8,128)(2,1)S(1)}, bf16[2,128,128]{2,1,0:T(8,128)(2,1)}, u32[]{:S(2)}) copy-start(bf16[2,128,128]{2,1,0:T(8,128)(2,1)} %constant.31.clone.outer_ref) | copy-start | bytes 196612
  0.0 41.3 %copy-start.5 = (f32[32,128]{1,0:T(8,128)S(1)}, f32[32,128]{1,0:T(8,128)}, u32[]{:S(2)}) copy-start(f32[32,128]{1,0:T(8,128)} %constant.24.clone.refs_1_.window_ref) | copy-start | bytes 49156
  2.7 38.7 %copy-start.2 = (bf16[2,256,256]{2,1,0:T(8,128)(2,1)S(1)}, bf16[2,256,256]{2,1,0:T(8,128)(2,1)}, u32[]{:S(2)}) copy-start(bf16[2,256,256]{2,1,0:T(8,128)(2,1)} %constant.30.clone.inner_ref) | copy-start | bytes 786436
  2.7 5.0 %collective-permute-start = (bf16[16,128]{1,0:T(8,128)(2,1)S(1)}, bf16[16,128]{1,0:T(8,128)(2,1)S(1)}, u32[]{:S(2)}, u32[]{:S(2)}) collective-permute-start(bf16[16,128]{1,0:T(8,128)(2,1)S(1)} %get-tuple-element.22), channel_id=1, source_target_pairs={{0,2},{2,0},{4,6},{6,4},{8,10},{10,8},{12,14},{14,12},{16,18},{18,... | collective-permute-start | bytes 12296 | tf_op jit(solution)/shard_map/ppermute | solution.py:448
  3.2 7.1 %collective-permute-start.1 = (bf16[16,128]{1,0:T(8,128)(2,1)S(1)}, bf16[16,128]{1,0:T(8,128)(2,1)S(1)}, u32[]{:S(2)}, u32[]{:S(2)}) collective-permute-start(bf16[16,128]{1,0:T(8,128)(2,1)S(1)} %get-tuple-element.23), channel_id=1, source_target_pairs={{0,4},{2,6},{4,0},{6,2},{8,12},{10,14},{12,8},{14,10},{16,20},{18,... | collective-permute-start | bytes 12296 | tf_op jit(solution)/shard_map/ppermute | solution.py:448
  5.7 4.6 %collective-permute-start.2 = (bf16[16,128]{1,0:T(8,128)(2,1)S(1)}, bf16[16,128]{1,0:T(8,128)(2,1)S(1)}, u32[]{:S(2)}, u32[]{:S(2)}) collective-permute-start(bf16[16,128]{1,0:T(8,128)(2,1)S(1)} %get-tuple-element.24), channel_id=1, source_target_pairs={{0,6},{2,4},{4,2},{6,0},{8,14},{10,12},{12,10},{14,8},{16,22},{18,... | collective-permute-start | bytes 12296 | tf_op jit(solution)/shard_map/ppermute | solution.py:448
  5.8 7.2 %collective-permute-start.3 = (bf16[16,128]{1,0:T(8,128)(2,1)S(1)}, bf16[16,128]{1,0:T(8,128)(2,1)S(1)}, u32[]{:S(2)}, u32[]{:S(2)}) collective-permute-start(bf16[16,128]{1,0:T(8,128)(2,1)S(1)} %get-tuple-element.25), channel_id=1, source_target_pairs={{0,8},{2,10},{4,12},{6,14},{8,0},{10,2},{12,4},{14,6},{16,24},{18,... | collective-permute-start | bytes 12296 | tf_op jit(solution)/shard_map/ppermute | solution.py:448
  7.6 5.4 %collective-permute-start.4 = (bf16[16,128]{1,0:T(8,128)(2,1)S(1)}, bf16[16,128]{1,0:T(8,128)(2,1)S(1)}, u32[]{:S(2)}, u32[]{:S(2)}) collective-permute-start(bf16[16,128]{1,0:T(8,128)(2,1)S(1)} %get-tuple-element.26), channel_id=1, source_target_pairs={{0,10},{2,8},{4,14},{6,12},{8,2},{10,0},{12,6},{14,4},{16,26},{18,... | collective-permute-start | bytes 12296 | tf_op jit(solution)/shard_map/ppermute | solution.py:448
  7.7 8.9 %collective-permute-start.5 = (bf16[16,128]{1,0:T(8,128)(2,1)S(1)}, bf16[16,128]{1,0:T(8,128)(2,1)S(1)}, u32[]{:S(2)}, u32[]{:S(2)}) collective-permute-start(bf16[16,128]{1,0:T(8,128)(2,1)S(1)} %get-tuple-element.27), channel_id=1, source_target_pairs={{0,12},{2,14},{4,8},{6,10},{8,4},{10,6},{12,0},{14,2},{16,28},{18,... | collective-permute-start | bytes 12296 | tf_op jit(solution)/shard_map/ppermute | solution.py:448
  10.3 6.4 %collective-permute-start.6 = (bf16[16,128]{1,0:T(8,128)(2,1)S(1)}, bf16[16,128]{1,0:T(8,128)(2,1)S(1)}, u32[]{:S(2)}, u32[]{:S(2)}) collective-permute-start(bf16[16,128]{1,0:T(8,128)(2,1)S(1)} %get-tuple-element.28), channel_id=1, source_target_pairs={{0,14},{2,12},{4,10},{6,8},{8,6},{10,4},{12,2},{14,0},{16,30},{18,... | collective-permute-start | bytes 12296 | tf_op jit(solution)/shard_map/ppermute | solution.py:448
  10.4 9.9 %collective-permute-start.7 = (bf16[16,128]{1,0:T(8,128)(2,1)S(1)}, bf16[16,128]{1,0:T(8,128)(2,1)S(1)}, u32[]{:S(2)}, u32[]{:S(2)}) collective-permute-start(bf16[16,128]{1,0:T(8,128)(2,1)S(1)} %get-tuple-element.29), channel_id=1, source_target_pairs={{0,16},{2,18},{4,20},{6,22},{8,24},{10,26},{12,28},{14,30},{16,0},... | collective-permute-start | bytes 12296 | tf_op jit(solution)/shard_map/ppermute | solution.py:448
  13.0 7.3 %collective-permute-start.8 = (bf16[16,128]{1,0:T(8,128)(2,1)S(1)}, bf16[16,128]{1,0:T(8,128)(2,1)S(1)}, u32[]{:S(2)}, u32[]{:S(2)}) collective-permute-start(bf16[16,128]{1,0:T(8,128)(2,1)S(1)} %get-tuple-element.30), channel_id=1, source_target_pairs={{0,18},{2,16},{4,22},{6,20},{8,26},{10,24},{12,30},{14,28},{16,2},... | collective-permute-start | bytes 12296 | tf_op jit(solution)/shard_map/ppermute | solution.py:448
  13.1 11.6 %collective-permute-start.9 = (bf16[16,128]{1,0:T(8,128)(2,1)S(1)}, bf16[16,128]{1,0:T(8,128)(2,1)S(1)}, u32[]{:S(2)}, u32[]{:S(2)}) collective-permute-start(bf16[16,128]{1,0:T(8,128)(2,1)S(1)} %get-tuple-element.31), channel_id=1, source_target_pairs={{0,20},{2,22},{4,16},{6,18},{8,28},{10,30},{12,24},{14,26},{16,4},... | collective-permute-start | bytes 12296 | tf_op jit(solution)/shard_map/ppermute | solution.py:448
  16.6 8.2 %collective-permute-start.10 = (bf16[16,128]{1,0:T(8,128)(2,1)S(1)}, bf16[16,128]{1,0:T(8,128)(2,1)S(1)}, u32[]{:S(2)}, u32[]{:S(2)}) collective-permute-start(bf16[16,128]{1,0:T(8,128)(2,1)S(1)} %get-tuple-element.32), channel_id=1, source_target_pairs={{0,22},{2,20},{4,18},{6,16},{8,30},{10,28},{12,26},{14,24},{16,6},... | collective-permute-start | bytes 12296 | tf_op jit(solution)/shard_map/ppermute | solution.py:448
  16.7 8.1 %collective-permute-start.11 = (bf16[16,128]{1,0:T(8,128)(2,1)S(1)}, bf16[16,128]{1,0:T(8,128)(2,1)S(1)}, u32[]{:S(2)}, u32[]{:S(2)}) collective-permute-start(bf16[16,128]{1,0:T(8,128)(2,1)S(1)} %get-tuple-element.33), channel_id=1, source_target_pairs={{0,24},{2,26},{4,28},{6,30},{8,16},{10,18},{12,20},{14,22},{16,8},... | collective-permute-start | bytes 12296 | tf_op jit(solution)/shard_map/ppermute | solution.py:448
  20.3 4.8 %collective-permute-start.12 = (bf16[16,128]{1,0:T(8,128)(2,1)S(1)}, bf16[16,128]{1,0:T(8,128)(2,1)S(1)}, u32[]{:S(2)}, u32[]{:S(2)}) collective-permute-start(bf16[16,128]{1,0:T(8,128)(2,1)S(1)} %get-tuple-element.34), channel_id=1, source_target_pairs={{0,26},{2,24},{4,30},{6,28},{8,18},{10,16},{12,22},{14,20},{16,10}... | collective-permute-start | bytes 12296 | tf_op jit(solution)/shard_map/ppermute | solution.py:448
  20.3 6.3 %collective-permute-start.13 = (bf16[16,128]{1,0:T(8,128)(2,1)S(1)}, bf16[16,128]{1,0:T(8,128)(2,1)S(1)}, u32[]{:S(2)}, u32[]{:S(2)}) collective-permute-start(bf16[16,128]{1,0:T(8,128)(2,1)S(1)} %get-tuple-element.35), channel_id=1, source_target_pairs={{0,28},{2,30},{4,24},{6,26},{8,20},{10,22},{12,16},{14,18},{16,12}... | collective-permute-start | bytes 12296 | tf_op jit(solution)/shard_map/ppermute | solution.py:448
  24.7 5.7 %collective-permute-start.14 = (bf16[16,128]{1,0:T(8,128)(2,1)S(1)}, bf16[16,128]{1,0:T(8,128)(2,1)S(1)}, u32[]{:S(2)}, u32[]{:S(2)}) collective-permute-start(bf16[16,128]{1,0:T(8,128)(2,1)S(1)} %get-tuple-element.36), channel_id=1, source_target_pairs={{0,30},{2,28},{4,26},{6,24},{8,22},{10,20},{12,18},{14,16},{16,14}... | collective-permute-start | bytes 12296 | tf_op jit(solution)/shard_map/ppermute | solution.py:448
  30.5 10.9 %copy-start.3 = (bf16[2,128,128]{2,1,0:T(8,128)(2,1)S(1)}, bf16[2,128,128]{2,1,0:T(8,128)(2,1)}, u32[]{:S(2)}) copy-start(bf16[2,128,128]{2,1,0:T(8,128)(2,1)} %constant.32.clone.partial_ref) | copy-start | bytes 196612
  32.1 9.3 %copy-start = (f32[2,64,128]{2,1,0:T(8,128)S(1)}, f32[2,64,128]{2,1,0:T(8,128)}, u32[]{:S(2)}) copy-start(f32[2,64,128]{2,1,0:T(8,128)} %constant.26.clone.refs_6_.shift_ref) | copy-start | bytes 196612
  32.1 9.3 %copy-start.1 = (f32[2,64,128]{2,1,0:T(8,128)S(1)}, f32[2,64,128]{2,1,0:T(8,128)}, u32[]{:S(2)}) copy-start(f32[2,64,128]{2,1,0:T(8,128)} %constant.25.clone.refs_3_.turn_ref) | copy-start | bytes 196612
  41.3 0.7 %copy-start.13 = (s32[2,16]{1,0:T(2,128)S(1)}, s32[2,16]{1,0:T(2,128)}, u32[]{:S(2)}) copy-start(s32[2,16]{1,0:T(2,128)} %offsets_ref.1) | copy-start | bytes 388

commit v3 on v1

--- a/solution.py
+++ b/solution.py
@@ -8,6 +8,7 @@
 from jax import lax
 from jax.experimental import pallas as pl
 from jax.experimental.pallas import tpu as pltpu
+from jax.sharding import Mesh
 from jax.sharding import PartitionSpec as P
 
 CONTRIB = 64
@@ -63,7 +64,7 @@
         outer_plus=high_low(from_left(phases(outer, short, blocks, 1))),
         partial=high_low(from_right(phases(short, short, CONTRIB, -1)).T * CONTRIB**-0.5),
         grid_turn=side_by_side(phases(np.arange(FACET_ROWS), short, subgrid_len, -1)),
-        model=high_low(from_right(phases(short, short, CONTRIB, -1)).T * subgrid_len**-0.5),
+        model=high_low(from_right(phases(short, short, CONTRIB, -1)) * subgrid_len**-0.5),
         back=high_low(from_right(phases(short, short, CONTRIB, 1)) * subgrid_len**-0.5),
     )
 
@@ -95,21 +96,31 @@
     return pltpu.roll(values, HALF, 1)
 
 
-def offsets_on_lanes(offsets_ref, columns):
+def place_offsets(offsets_ref):
     fronts, owners = offsets_ref.shape
-    lane = iota((1, fronts * owners * columns), 1)
+    groups = owners // FACET_ROWS
+    own = lax.axis_index("group")
+    return [
+        offsets_ref[t, lax.rem(own + step, groups) * FACET_ROWS + member]
+        for member in range(FACET_ROWS)
+        for step in range(groups)
+        for t in range(fronts)
+    ]
+
+
+def offsets_on_lanes(offsets, columns):
+    lane = iota((1, len(offsets) * columns), 1)
     spread = jnp.zeros_like(lane)
-    for place in range(fronts * owners):
+    for place, offset in enumerate(offsets):
         begin = place * columns
         here = (lane >= begin) & (lane < begin + columns)
-        spread = jnp.where(here, offsets_ref[place % fronts, place // fronts], spread)
+        spread = jnp.where(here, offset, spread)
     return lane, spread
 
 
-def place_shifts(offsets_ref, shift_ref, straight_ref, crossed_ref, columns):
-    fronts, owners = offsets_ref.shape
-    for place in range(fronts * owners):
-        residue = offsets_ref[place % fronts, place // fronts] % CONTRIB
+def place_shifts(offsets, shift_ref, straight_ref, crossed_ref, columns):
+    for place, offset in enumerate(offsets):
+        residue = offset % CONTRIB
         rows = pl.ds(place * columns, columns)
         straight_ref[rows, :] = jnp.broadcast_to(
             shift_ref[0, pl.ds(residue, 1), :], (columns, LANES)
@@ -180,7 +191,8 @@
         sections += [jnp.concatenate(even, axis=1), jnp.concatenate(odd, axis=1)]
     for copy in copies[2:]:
         copy.wait()
-    place_shifts(offsets_ref, shift_ref, straight_ref, crossed_ref, columns)
+    offsets = place_offsets(offsets_ref)
+    place_shifts(offsets, shift_ref, straight_ref, crossed_ref, columns)
     section = table_times(outer_ref, jnp.concatenate(sections, axis=0))
     turned = []
     for pair in range(pairs):
@@ -210,7 +222,7 @@
         axis=0,
     )
     blocks = length // CONTRIB
-    lane, spread = offsets_on_lanes(offsets_ref, columns)
+    lane, spread = offsets_on_lanes(offsets, columns)
     first_block, residue = spread // CONTRIB, spread % CONTRIB
     base = lane % columns * blocks
     width = lane.shape[1]
@@ -226,42 +238,37 @@
     out_ref[...] = (piece * straight_ref[...] + swap_halves(piece) * crossed_ref[...]).astype(BF16)
 
 
-def subgrid_kernel(
-    pieces_ref, cells_ref, values_ref, weights_ref, flags_ref, turn_ref, model_ref, back_ref,
-    out_ref, held_ref, *, columns, bands,
-):
-    fronts, _, samples = cells_ref.shape
-    facets = pieces_ref.shape[0] // (fronts * columns)
-    groups = facets // FACET_ROWS
-    rows = groups * columns
-    depth = FACET_ROWS * rows
+def subgrid_kernel(pieces_ref, turn_ref, model_ref, back_ref, *refs, columns, bands):
+    samples_refs, (out_ref, held_ref) = refs[:-2], refs[-2:]
+    groups = len(samples_refs) // 4
+    fronts, _, samples = samples_refs[0].shape
+    own = lax.axis_index("group")
+    rows = pieces_ref.shape[0] // FACET_ROWS
+    depth = FACET_ROWS * columns
     share = columns // bands
     pieces = pieces_ref[...].astype(F32)
-
-    def block(facet, front):
-        begin = (facet * fronts + front) * columns
-        return pieces[begin : begin + columns, :]
-
-    sky = [
-        jnp.concatenate(
-            [block(j * FACET_ROWS + i, t) for t in range(fronts) for j in range(groups)], axis=0
-        )
-        for i in range(FACET_ROWS)
-    ]
-    sky = turned_eighths(sky, -1.0)
+    sky = turned_eighths(
+        [pieces[i * rows : (i + 1) * rows, :] for i in range(FACET_ROWS)], -1.0
+    )
     sky = [
         value * turn_ref[0, i : i + 1, :] + swap_halves(value) * turn_ref[1, i : i + 1, :]
         for i, value in enumerate(sky)
     ]
+    spots = range(groups * fronts)
     stacked = jnp.concatenate(
-        [value[t * rows : (t + 1) * rows, :] for t in range(fronts) for value in sky], axis=0
-    )
-    model = table_times(model_ref, stacked, ((1,), (1,)))
+        [value[spot * columns : (spot + 1) * columns, :] for spot in spots for value in sky],
+        axis=0,
+    )
+    model = times_table(stacked, model_ref)
     grids = []
-    for t in range(fronts):
-        row, col = cells_ref[t, 0:1, :], cells_ref[t, 1:2, :]
-        pick = one_hot((depth, samples), col % FACET_ROWS * rows + row)
-        high, low = split(model[:, t * depth : (t + 1) * depth])
+    for spot in spots:
+        step, t = spot // fronts, spot % fronts
+        cells_ref, values_ref, weights_ref, flags_ref = samples_refs[4 * step : 4 * step + 4]
+        row, col = cells_ref[t, 0:1, :] - own * columns, cells_ref[t, 1:2, :]
+        inside = (row >= 0) & (row < columns)
+        target = jnp.where(inside, col % FACET_ROWS * columns + row, -1)
+        pick = one_hot((depth, samples), target)
+        high, low = split(model[spot * depth : (spot + 1) * depth, :].T)
         line = dot(high, pick) + dot(low, pick)
         mask = iota((HALF, samples), 0) == col // FACET_ROWS
         factor = weights_ref[t] * flags_ref[t].astype(F32)
@@ -285,8 +292,8 @@
     for i in range(FACET_ROWS):
         value = jnp.concatenate(
             [
-                back[t * depth + i * rows : t * depth + (i + 1) * rows, :]
-                for t in range(fronts)
+                back[spot * depth + i * columns : spot * depth + (i + 1) * columns, :]
+                for spot in spots
             ],
             axis=0,
         )
@@ -295,12 +302,11 @@
         )
     lines = turned_eighths(lines, 1.0)
     for i in range(FACET_ROWS):
-        for t in range(fronts):
-            for j in range(groups):
-                for b in range(bands):
-                    source = (t * groups + j) * columns + b * share
-                    target = ((b * facets + j * FACET_ROWS + i) * fronts + t) * share
-                    held_ref[target : target + share, :] = lines[i][source : source + share, :]
+        for spot in spots:
+            for b in range(bands):
+                source = spot * columns + b * share
+                target = ((b * FACET_ROWS + i) * len(spots) + spot) * share
+                held_ref[target : target + share, :] = lines[i][source : source + share, :]
     out_ref[...] = held_ref[...].astype(BF16)
 
 
@@ -312,14 +318,15 @@
     blocks = length // CONTRIB
     groups = length // LANES
     pairs = (columns + 1) // 2
-    place_shifts(offsets_ref, shift_ref, straight_ref, crossed_ref, columns)
+    offsets = place_offsets(offsets_ref)
+    place_shifts(offsets, shift_ref, straight_ref, crossed_ref, columns)
     width = pieces_ref.shape[0] // bands
     summed = pieces_ref[0:width, :].astype(F32)
     for b in range(1, bands):
         summed += pieces_ref[b * width : (b + 1) * width, :].astype(F32)
     summed = summed * straight_ref[...] - swap_halves(summed) * crossed_ref[...]
     residues = table_times(partial_ref, summed, ((1,), (1,)))
-    lane, spread = offsets_on_lanes(offsets_ref, columns)
+    lane, spread = offsets_on_lanes(offsets, columns)
     first_block, residue = spread // CONTRIB, spread % CONTRIB
     base = lane % columns * blocks
     kappa = iota((2 * CONTRIB, width), 0) % CONTRIB
@@ -399,11 +406,12 @@
     return pltpu.VMEM((rows, LANES), F32)
 
 
-def local(facets, bands, strips, offsets, cells, values, weights, flags):
+def local(groups, bands, strips, offsets, cells, values, weights, flags):
     columns, length = strips.shape[-2:]
     fronts = offsets.shape[0]
     share = columns // bands
     made = {key: jnp.asarray(value) for key, value in tables(length).items()}
+    facets = groups * FACET_ROWS
     rows = facets * fronts * columns
     held = length // LANES * columns
     fetched = [
@@ -424,15 +432,20 @@
         + [pltpu.SemaphoreType.DMA((len(fetched),))],
         *fetched,
     )
-    arrived = lax.all_to_all(pieces, "facet", split_axis=0, concat_axis=0, tiled=True)
+    samples = [cells[0, :, 0], values[0, :, 0], weights[0], flags[0]]
+    gathered = list(samples)
+    for step in range(1, groups):
+        moves = [((group + step) % groups, group) for group in range(groups)]
+        gathered += [lax.ppermute(array, "group", moves) for array in samples]
+    arrived = lax.all_to_all(pieces, "member", split_axis=0, concat_axis=0, tiled=True)
     returned = kernel_call(
         functools.partial(subgrid_kernel, columns=columns, bands=bands), "subgrid",
-        jax.ShapeDtypeStruct((rows, LANES), BF16), [pltpu.VMEM] * 8, [wide(rows)],
-        arrived, cells[0, :, 0], values[0, :, 0], weights[0], flags[0],
-        made["grid_turn"], made["model"], made["back"],
+        jax.ShapeDtypeStruct((rows, LANES), BF16), [pltpu.VMEM] * (4 + len(gathered)),
+        [wide(rows)],
+        arrived, made["grid_turn"], made["model"], made["back"], *gathered,
     )
     delivered = lax.all_to_all(
-        returned, ("band", "facet"), split_axis=0, concat_axis=0, tiled=True
+        returned, ("band", "member"), split_axis=0, concat_axis=0, tiled=True
     )
     width = facets * fronts * share
     lines = kernel_call(
@@ -446,18 +459,24 @@
 
 
 def solution(mesh):
+    bands = mesh.shape["band"]
+    groups = mesh.shape["facet"] // FACET_ROWS
+    split_mesh = Mesh(
+        mesh.devices.reshape(groups, FACET_ROWS, bands), ("group", "member", "band")
+    )
+    facet = ("group", "member")
     placed = (
-        P("band", "facet", None, None, None),
+        P("band", facet, None, None, None),
         P(),
-        P("band", None, "facet", None, None),
-        P("band", None, "facet", None, None),
-        P("band", None, "facet", None),
-        P("band", None, "facet", None),
+        P("band", None, facet, None, None),
+        P("band", None, facet, None, None),
+        P("band", None, facet, None),
+        P("band", None, facet, None),
     )
     return jax.shard_map(
-        functools.partial(local, mesh.shape["facet"], mesh.shape["band"]),
-        mesh=mesh,
+        functools.partial(local, groups, bands),
+        mesh=split_mesh,
         in_specs=placed,
-        out_specs=P("facet", "band", None, None),
+        out_specs=P(facet, "band", None, None),
         check_vma=False,
     )

time: 30.8 us -> 35 us (1.14)
  blocking collectives: 23.4 us -> 11 us
  starting transfers between devices: 0 us -> 11.3 us
  waiting for transfers between devices: 0 us -> 4.18 us
  Pallas kernels: 6.27 us -> 7.35 us
    all_to_all x2 -> x1, blocking collectives: 23.4 us -> 11 us  [local(): lax.all_to_all(returned, ('band', 'member'), split_axis=0, concat_axis=0,...]
    ppermute x0 -> x4, starting transfers between devices: none -> 5.91 us  [local(): gathered += [lax.ppermute(array, 'group', moves) for array in samples]]
    all_to_all x0 -> x1, starting transfers between devices: none -> 5.37 us  [local(): lax.all_to_all(pieces, 'member', split_axis=0, concat_axis=0, tiled=True)]
    ppermute x0 -> x4, waiting for transfers between devices: none -> 4.17 us  [local(): gathered += [lax.ppermute(array, 'group', moves) for array in samples]]
    pallas_call x3, Pallas kernels: 6.27 us -> 7.35 us  [kernel_call(): pl.pallas_call(kernel, out_shape=out_shape, in_specs=[pl.BlockSpec(memory...]
  transfers between devices with their start and end apart: 0 -> 5, of which waited for: 0 -> 2; matrix products, arithmetic and copies ran while one was open for 0% -> 0% of each run, Pallas kernels for 0% -> 0%
where the time goes in v3:
time: 35 us; the launch traced here: 34.7 us
  starting transfers between devices  11.3 us (32%)
  blocking collectives  11 us (31%)
  Pallas kernels  7.35 us (21%)
  waiting for transfers between devices  4.18 us (12%)
  local copies, waits for them, and re-layouts  0.71 us (2%)
    all_to_all x1, blocking collectives, local(): lax.all_to_all(returned, ('band', 'member'), split_axis=0, concat_axis=0,...  11 us
    pallas_call x3, Pallas kernels, kernel_call(): pl.pallas_call(kernel, out_shape=out_shape, in_specs=[pl.BlockSpec(memory...  7.35 us
    ppermute x4, starting transfers between devices, local(): gathered += [lax.ppermute(array, 'group', moves) for array in samples]  5.91 us
    all_to_all x1, starting transfers between devices, local(): lax.all_to_all(pieces, 'member', split_axis=0, concat_axis=0, tiled=True)  5.37 us
    ppermute x4, waiting for transfers between devices, local(): gathered += [lax.ppermute(array, 'group', moves) for array in samples]  4.17 us
    unnamed x28, local copies, waits for them, and re-layouts  0.71 us
  transfers between devices with their start and end apart: 5, of which 2 were waited for; matrix products, arithmetic and copies ran while one was open for 0% of the time, Pallas kernels for 0%

profile of v3, /device:TPU:0, one launch (start us, length us, event | category | flops | bytes accessed | tf_op | source)
XLA Modules:
  0.0 34.7 jit_solution(6211353991704646888)
XLA Ops:
  0.0 0.0 copy-start.8
  0.0 0.0 copy-start.9
  0.0 0.0 copy-start.12
  0.0 0.0 copy-start.6
  0.0 0.0 copy-start.10
  0.0 0.0 copy-start.7
  0.0 3.2 %predict.1 = bf16[256,128]{1,0:T(8,128)(2,1)} custom-call(f32[2,8,4096]{2,1,0:T(8,128)} %bitcast.21, f32[32,128]{1,0:T(8,128)} %constant.24.clone.refs_1_.window_ref, bf16[2,128,128]{2,1,0:T(8,128)(2,1)} %constant.27.clone.refs_2_, f32[2,64,128]{2,1,0:T(8,128)} %constant.25.clone.refs_3_.turn_ref, bf16[2,256,256]{2,1,0:T(8,128)(2,1)} %constant.28.clone.refs_4_, ...), custom_call_target="tpu_custom_call" | custom-call | tf_op jit(solution)/shard_map/predict/pallas_call | solution.py:394
  3.2 0.0 copy-start.11
  3.2 0.0 copy-start.5
  3.2 0.0 copy-start.4
  3.2 5.4 %all-to-all-start = ((bf16[8,32,128]{2,1,0:T(8,128)(2,1)}), bf16[8,32,128]{2,1,0:T(8,128)(2,1)S(1)}, u32[]{:S(2)}, u32[]{:S(2)}) async-start(bf16[8,32,128]{2,1,0:T(8,128)(2,1)} %bitcast.1), calls=%async_computation | async-start | bytes 131072 | tf_op jit(solution)/shard_map/all_to_all | solution.py:440
  8.6 0.0 copy-start
  8.6 0.0 copy-done.8
  8.6 2.7 %collective-permute-start = (s32[2,2,512]{2,1,0:T(2,128)S(1)}, s32[2,2,512]{2,1,0:T(2,128)S(1)}, u32[]{:S(2)}, u32[]{:S(2)}) collective-permute-start(s32[2,2,512]{2,1,0:T(2,128)S(1)} %bitcast.13), channel_id=1, source_target_pairs={{16,0},{0,16},{17,1},{1,17},{18,2},{2,18},{19,3},{3,19},{20,4},{4,... | collective-permute-start | bytes 24584 | tf_op jit(solution)/shard_map/ppermute | solution.py:439
  11.3 0.0 copy-done.9
  11.3 0.3 collective-permute-start.1
  11.6 0.0 copy-done.11
  11.6 2.6 %collective-permute-start.2 = (f32[2,1,512]{2,1,0:T(1,128)S(1)}, f32[2,1,512]{2,1,0:T(1,128)S(1)}, u32[]{:S(2)}, u32[]{:S(2)}) collective-permute-start(f32[2,1,512]{2,1,0:T(1,128)S(1)} %bitcast.17), channel_id=1, source_target_pairs={{16,0},{0,16},{17,1},{1,17},{18,2},{2,18},{19,3},{3,19},{20,4},{4,... | collective-permute-start | bytes 12296 | tf_op jit(solution)/shard_map/ppermute | solution.py:439
  14.2 0.0 copy-done.12
  14.2 0.3 collective-permute-start.3
  14.5 1.6 %collective-permute-done.2.refs_6_ = f32[2,1,512]{2,1,0:T(1,128)S(1)} collective-permute-done((f32[2,1,512]{2,1,0:T(1,128)S(1)}, f32[2,1,512]{2,1,0:T(1,128)S(1)}, u32[]{:S(2)}, u32[]{:S(2)}) %collective-permute-start.2) | collective-permute-done | bytes 4128 | tf_op jit(solution)/shard_map/ppermute | solution.py:439
  16.1 2.6 %collective-permute-done.3.refs_7_ = s32[2,1,512]{2,1,0:T(1,128)S(1)} collective-permute-done((s32[2,1,512]{2,1,0:T(1,128)S(1)}, s32[2,1,512]{2,1,0:T(1,128)S(1)}, u32[]{:S(2)}, u32[]{:S(2)}) %collective-permute-start.3) | collective-permute-done | bytes 4128 | tf_op jit(solution)/shard_map/ppermute | solution.py:439
  18.7 0.0 collective-permute-done.refs_4_
  18.7 0.0 collective-permute-done.1.refs_5_
  18.7 0.0 all-to-all-done
  18.7 0.0 copy-done.6
  18.7 0.0 copy-done.10
  18.7 0.0 copy-done.5
  18.8 0.0 copy-start.3
  18.8 1.9 %subgrid.1 = bf16[256,128]{1,0:T(8,128)(2,1)S(1)} custom-call(bf16[256,128]{1,0:T(8,128)(2,1)S(1)} %bitcast.10, f32[2,8,128]{2,1,0:T(8,128)S(1)} %copy-done.10, bf16[2,128,128]{2,1,0:T(8,128)(2,1)S(1)} %copy-done.6, bf16[2,128,128]{2,1,0:T(8,128)(2,1)S(1)} %copy-done.5, s32[2,2,512]{2,1,0:T(2,128)S(1)} %bitcast.14, f32[2,2,512]{2,1,0:T(2,128)S(1)} %bitcast.16, ...), custom_call_target="tpu_custom_call" | custom-call | tf_op jit(solution)/shard_map/subgrid/pallas_call | solution.py:394
  20.7 0.0 copy-start.1
  20.7 0.0 copy-start.2
  20.7 11.0 %all_to_all.22 = bf16[16,16,128]{2,1,0:T(8,128)(2,1)S(1)} all-to-all(bf16[16,16,128]{2,1,0:T(8,128)(2,1)S(1)} %bitcast.11), channel_id=1, replica_groups=mesh['group'=2,'member'=8,'band'=2] {'band','member'}, dimensions={0} | all-to-all | bytes 131072 | tf_op jit(solution)/shard_map/all_to_all | solution.py:447
  31.7 0.0 copy-start.13
  31.7 0.0 copy-done.7
  31.7 0.0 copy-done.4
  31.7 0.0 copy-done
  31.7 0.0 copy-done.3
  31.7 0.0 copy-done.1
  31.7 0.0 copy-done.2
  31.7 0.6 %copy-done.13 = s32[2,16]{1,0:T(2,128)S(1)} copy-done((s32[2,16]{1,0:T(2,128)S(1)}, s32[2,16]{1,0:T(2,128)}, u32[]{:S(2)}) %copy-start.13) | copy-done | bytes 152
  32.4 2.3 %lines.1 = f32[4,2,4096]{2,1,0:T(2,128)} custom-call(s32[2,16]{1,0:T(2,128)S(1)} %copy-done.13, bf16[256,128]{1,0:T(8,128)(2,1)S(1)} %bitcast.12, f32[32,128]{1,0:T(8,128)S(1)} %copy-done.7, f32[2,64,128]{2,1,0:T(8,128)S(1)} %copy-done.2, f32[2,64,128]{2,1,0:T(8,128)S(1)} %copy-done.1, bf16[2,128,128]{2,1,0:T(8,128)(2,1)S(1)} %copy-done.3, ...), custom_call_target="tpu_custom_call" | custom-call | tf_op jit(solution)/shard_map/lines/pallas_call | solution.py:394
Async XLA Ops:
  0.0 8.6 %copy-start.8 = (s32[1,2,1,2,512]{4,3,2,1,0:T(2,128)S(1)}, s32[1,2,1,2,512]{4,3,2,1,0:T(2,128)}, u32[]{:S(2)}) copy-start(s32[1,2,1,2,512]{4,3,2,1,0:T(2,128)} %param.20) | copy-start | bytes 24580
  0.0 11.3 %copy-start.9 = (f32[1,2,1,2,512]{4,3,2,1,0:T(2,128)S(1)}, f32[1,2,1,2,512]{4,3,2,1,0:T(2,128)}, u32[]{:S(2)}) copy-start(f32[1,2,1,2,512]{4,3,2,1,0:T(2,128)} %param.21) | copy-start | bytes 24580
  0.0 14.2 %copy-start.12 = (s32[1,2,1,512]{3,2,1,0:T(1,128)S(1)}, s32[1,2,1,512]{3,2,1,0:T(1,128)}, u32[]{:S(2)}) copy-start(s32[1,2,1,512]{3,2,1,0:T(1,128)} %param.23) | copy-start | bytes 12292
  0.0 18.7 %copy-start.6 = (bf16[2,128,128]{2,1,0:T(8,128)(2,1)S(1)}, bf16[2,128,128]{2,1,0:T(8,128)(2,1)}, u32[]{:S(2)}) copy-start(bf16[2,128,128]{2,1,0:T(8,128)(2,1)} %constant.34.clone.model_ref) | copy-start | bytes 196612
  0.0 18.7 %copy-start.10 = (f32[2,8,128]{2,1,0:T(8,128)S(1)}, f32[2,8,128]{2,1,0:T(8,128)}, u32[]{:S(2)}) copy-start(f32[2,8,128]{2,1,0:T(8,128)} %constant.33.clone.turn_ref) | copy-start | bytes 24580
  0.0 31.7 %copy-start.7 = (f32[32,128]{1,0:T(8,128)S(1)}, f32[32,128]{1,0:T(8,128)}, u32[]{:S(2)}) copy-start(f32[32,128]{1,0:T(8,128)} %constant.24.clone.refs_1_.window_ref) | copy-start | bytes 49156
  3.2 8.4 %copy-start.11 = (f32[1,2,1,512]{3,2,1,0:T(1,128)S(1)}, f32[1,2,1,512]{3,2,1,0:T(1,128)}, u32[]{:S(2)}) copy-start(f32[1,2,1,512]{3,2,1,0:T(1,128)} %param.22) | copy-start | bytes 12292
  3.2 15.5 %copy-start.5 = (bf16[2,128,128]{2,1,0:T(8,128)(2,1)S(1)}, bf16[2,128,128]{2,1,0:T(8,128)(2,1)}, u32[]{:S(2)}) copy-start(bf16[2,128,128]{2,1,0:T(8,128)(2,1)} %constant.35.clone.back_ref) | copy-start | bytes 196612
  3.2 28.5 %copy-start.4 = (bf16[2,128,128]{2,1,0:T(8,128)(2,1)S(1)}, bf16[2,128,128]{2,1,0:T(8,128)(2,1)}, u32[]{:S(2)}) copy-start(bf16[2,128,128]{2,1,0:T(8,128)(2,1)} %constant.31.clone.outer_ref) | copy-start | bytes 196612
  3.2 15.5 %all-to-all-start = ((bf16[8,32,128]{2,1,0:T(8,128)(2,1)}), bf16[8,32,128]{2,1,0:T(8,128)(2,1)S(1)}, u32[]{:S(2)}, u32[]{:S(2)}) async-start(bf16[8,32,128]{2,1,0:T(8,128)(2,1)} %bitcast.1), calls=%async_computation | async-start | bytes 131072 | tf_op jit(solution)/shard_map/all_to_all | solution.py:440
  8.6 23.1 %copy-start = (bf16[2,256,256]{2,1,0:T(8,128)(2,1)S(1)}, bf16[2,256,256]{2,1,0:T(8,128)(2,1)}, u32[]{:S(2)}) copy-start(bf16[2,256,256]{2,1,0:T(8,128)(2,1)} %constant.30.clone.inner_ref) | copy-start | bytes 786436
  8.6 10.1 %collective-permute-start = (s32[2,2,512]{2,1,0:T(2,128)S(1)}, s32[2,2,512]{2,1,0:T(2,128)S(1)}, u32[]{:S(2)}, u32[]{:S(2)}) collective-permute-start(s32[2,2,512]{2,1,0:T(2,128)S(1)} %bitcast.13), channel_id=1, source_target_pairs={{16,0},{0,16},{17,1},{1,17},{18,2},{2,18},{19,3},{3,19},{20,4},{4,... | collective-permute-start | bytes 24584 | tf_op jit(solution)/shard_map/ppermute | solution.py:439
  11.3 7.4 %collective-permute-start.1 = (f32[2,2,512]{2,1,0:T(2,128)S(1)}, f32[2,2,512]{2,1,0:T(2,128)S(1)}, u32[]{:S(2)}, u32[]{:S(2)}) collective-permute-start(f32[2,2,512]{2,1,0:T(2,128)S(1)} %bitcast.15), channel_id=1, source_target_pairs={{16,0},{0,16},{17,1},{1,17},{18,2},{2,18},{19,3},{3,19},{20,4},{4,... | collective-permute-start | bytes 24584 | tf_op jit(solution)/shard_map/ppermute | solution.py:439
  11.6 4.5 %collective-permute-start.2 = (f32[2,1,512]{2,1,0:T(1,128)S(1)}, f32[2,1,512]{2,1,0:T(1,128)S(1)}, u32[]{:S(2)}, u32[]{:S(2)}) collective-permute-start(f32[2,1,512]{2,1,0:T(1,128)S(1)} %bitcast.17), channel_id=1, source_target_pairs={{16,0},{0,16},{17,1},{1,17},{18,2},{2,18},{19,3},{3,19},{20,4},{4,... | collective-permute-start | bytes 12296 | tf_op jit(solution)/shard_map/ppermute | solution.py:439
  14.2 4.5 %collective-permute-start.3 = (s32[2,1,512]{2,1,0:T(1,128)S(1)}, s32[2,1,512]{2,1,0:T(1,128)S(1)}, u32[]{:S(2)}, u32[]{:S(2)}) collective-permute-start(s32[2,1,512]{2,1,0:T(1,128)S(1)} %bitcast.19), channel_id=1, source_target_pairs={{16,0},{0,16},{17,1},{1,17},{18,2},{2,18},{19,3},{3,19},{20,4},{4,... | collective-permute-start | bytes 12296 | tf_op jit(solution)/shard_map/ppermute | solution.py:439
  18.8 12.9 %copy-start.3 = (bf16[2,128,128]{2,1,0:T(8,128)(2,1)S(1)}, bf16[2,128,128]{2,1,0:T(8,128)(2,1)}, u32[]{:S(2)}) copy-start(bf16[2,128,128]{2,1,0:T(8,128)(2,1)} %constant.32.clone.partial_ref) | copy-start | bytes 196612
  20.7 11.0 %copy-start.1 = (f32[2,64,128]{2,1,0:T(8,128)S(1)}, f32[2,64,128]{2,1,0:T(8,128)}, u32[]{:S(2)}) copy-start(f32[2,64,128]{2,1,0:T(8,128)} %constant.26.clone.refs_6_.shift_ref) | copy-start | bytes 196612
  20.7 11.0 %copy-start.2 = (f32[2,64,128]{2,1,0:T(8,128)S(1)}, f32[2,64,128]{2,1,0:T(8,128)}, u32[]{:S(2)}) copy-start(f32[2,64,128]{2,1,0:T(8,128)} %constant.25.clone.refs_3_.turn_ref) | copy-start | bytes 196612
  31.7 0.7 %copy-start.13 = (s32[2,16]{1,0:T(2,128)S(1)}, s32[2,16]{1,0:T(2,128)}, u32[]{:S(2)}) copy-start(s32[2,16]{1,0:T(2,128)} %offsets_ref.1) | copy-start | bytes 388

commit v4 on v3

--- a/solution.py
+++ b/solution.py
@@ -13,6 +13,7 @@
 
 CONTRIB = 64
 FACET_ROWS = 8
+SUBGRID = FACET_ROWS * CONTRIB
 LANES = 128
 HALF = LANES // 2
 VMEM_LIMIT = 48 * 1024 * 1024
@@ -52,7 +53,6 @@
     window = 1.0 + 0.5 * np.cos(np.arange(length) * (2.0 * math.pi / length))
     turn = np.tile(phases(short, short, length, -1), (1, 2))
     pair = np.eye(2)
-    subgrid_len = FACET_ROWS * CONTRIB
     return dict(
         window=(window * length**-0.5).reshape(length // LANES, LANES).astype(np.float32),
         turn=np.stack([turn.real, turn.imag]).astype(np.float32),
@@ -63,9 +63,9 @@
         inner_plus=high_low(from_right(np.kron(pair, phases(short, short, CONTRIB, 1)))),
         outer_plus=high_low(from_left(phases(outer, short, blocks, 1))),
         partial=high_low(from_right(phases(short, short, CONTRIB, -1)).T * CONTRIB**-0.5),
-        grid_turn=side_by_side(phases(np.arange(FACET_ROWS), short, subgrid_len, -1)),
-        model=high_low(from_right(phases(short, short, CONTRIB, -1)) * subgrid_len**-0.5),
-        back=high_low(from_right(phases(short, short, CONTRIB, 1)) * subgrid_len**-0.5),
+        grid_turn=side_by_side(phases(np.arange(FACET_ROWS), short, SUBGRID, -1)),
+        model=high_low(from_right(phases(short, short, CONTRIB, -1)) * SUBGRID**-0.5),
+        back=high_low(from_right(phases(short, short, CONTRIB, 1)) * SUBGRID**-0.5),
     )
 
 
@@ -157,23 +157,48 @@
     return [e + o for e, o in zip(even, turned)] + [e - o for e, o in zip(even, turned)]
 
 
+def pack_samples(cells_ref, values_ref, weights_ref, flags_ref, out_ref):
+    for t in range(cells_ref.shape[0]):
+        rows = [
+            cells_ref[t, 0:1, :].astype(F32) * SUBGRID + cells_ref[t, 1:2, :].astype(F32),
+            weights_ref[t] * flags_ref[t].astype(F32),
+            values_ref[t],
+        ]
+        out_ref[4 * t : 4 * t + 4, :] = jnp.concatenate(rows, axis=0)
+
+
 def predict_kernel(*refs):
-    count = 8
+    count = 12
+    sources, outs, targets = refs[:count], refs[count : count + 2], refs[count + 2 :]
     copies = [
-        pltpu.make_async_copy(refs[i], refs[count + 1 + i], refs[-1].at[i]) for i in range(count)
+        pltpu.make_async_copy(sources[i], targets[i], refs[-1].at[i]) for i in range(count)
     ]
     for copy in copies:
         copy.start()
-    out_ref = refs[count]
-    strips_ref, window_ref, outer_ref, turn_ref, inner_ref, offsets_ref, shift_ref, piece_ref = (
-        refs[count + 1 : 2 * count + 1]
-    )
-    real_ref, imag_ref, straight_ref, crossed_ref = refs[2 * count + 1 : -1]
+    out_ref, packed_ref = outs
+    offsets_ref, shift_ref, strips_ref, window_ref = targets[:4]
+    outer_ref, turn_ref, inner_ref, piece_ref = targets[8:count]
+    real_ref, imag_ref, straight_ref, crossed_ref = targets[count:-1]
     columns, length = strips_ref.shape[1:]
     groups = length // LANES
     pairs = columns // 2
-    copies[0].wait()
-    copies[1].wait()
+    blocks = length // CONTRIB
+    for copy in copies[:2]:
+        copy.wait()
+    offsets = place_offsets(offsets_ref)
+    place_shifts(offsets, shift_ref, straight_ref, crossed_ref, columns)
+    lane, spread = offsets_on_lanes(offsets, columns)
+    first_block, residue = spread // CONTRIB, spread % CONTRIB
+    base = lane % columns * blocks
+    width = lane.shape[1]
+    shape = (columns * blocks, width)
+    pick_inside = one_hot(shape, base + first_block)
+    pick_beyond = one_hot(shape, base + (first_block + 1) % blocks)
+    for copy in copies[4:8]:
+        copy.wait()
+    pack_samples(*targets[4:8], packed_ref)
+    copies[2].wait()
+    copies[3].wait()
     window = window_ref[...]
     low_half = iota((groups, LANES), 1) < HALF
     sections = []
@@ -189,10 +214,8 @@
             even.append(jnp.where(low_half, first, swap_halves(second)))
             odd.append(jnp.where(low_half, swap_halves(first), second))
         sections += [jnp.concatenate(even, axis=1), jnp.concatenate(odd, axis=1)]
-    for copy in copies[2:]:
+    for copy in copies[8:]:
         copy.wait()
-    offsets = place_offsets(offsets_ref)
-    place_shifts(offsets, shift_ref, straight_ref, crossed_ref, columns)
     section = table_times(outer_ref, jnp.concatenate(sections, axis=0))
     turned = []
     for pair in range(pairs):
@@ -221,17 +244,9 @@
         ],
         axis=0,
     )
-    blocks = length // CONTRIB
-    lane, spread = offsets_on_lanes(offsets, columns)
-    first_block, residue = spread // CONTRIB, spread % CONTRIB
-    base = lane % columns * blocks
-    width = lane.shape[1]
-    shape = (columns * blocks, width)
     high, low = split(spectrum)
-    pick = one_hot(shape, base + first_block)
-    inside = dot(high, pick) + dot(low, pick)
-    pick = one_hot(shape, base + (first_block + 1) % blocks)
-    beyond = dot(high, pick) + dot(low, pick)
+    inside = dot(high, pick_inside) + dot(low, pick_inside)
+    beyond = dot(high, pick_beyond) + dot(low, pick_beyond)
     kappa = iota((2 * CONTRIB, width), 0) % CONTRIB
     cutout = jnp.where(kappa >= residue, inside, beyond)
     piece = times_table(cutout.T, piece_ref)
@@ -240,8 +255,8 @@
 
 def subgrid_kernel(pieces_ref, turn_ref, model_ref, back_ref, *refs, columns, bands):
     samples_refs, (out_ref, held_ref) = refs[:-2], refs[-2:]
-    groups = len(samples_refs) // 4
-    fronts, _, samples = samples_refs[0].shape
+    groups = len(samples_refs)
+    fronts, samples = samples_refs[0].shape[0] // 4, samples_refs[0].shape[1]
     own = lax.axis_index("group")
     rows = pieces_ref.shape[0] // FACET_ROWS
     depth = FACET_ROWS * columns
@@ -263,15 +278,15 @@
     grids = []
     for spot in spots:
         step, t = spot // fronts, spot % fronts
-        cells_ref, values_ref, weights_ref, flags_ref = samples_refs[4 * step : 4 * step + 4]
-        row, col = cells_ref[t, 0:1, :] - own * columns, cells_ref[t, 1:2, :]
+        sample = samples_refs[step][4 * t : 4 * t + 4, :]
+        cell = sample[0:1, :].astype(jnp.int32)
+        row, col = cell // SUBGRID - own * columns, cell % SUBGRID
         inside = (row >= 0) & (row < columns)
         target = jnp.where(inside, col % FACET_ROWS * columns + row, -1)
         pick = one_hot((depth, samples), target)
         high, low = split(model[spot * depth : (spot + 1) * depth, :].T)
         line = dot(high, pick) + dot(low, pick)
         mask = iota((HALF, samples), 0) == col // FACET_ROWS
-        factor = weights_ref[t] * flags_ref[t].astype(F32)
         highs, lows = [], []
         for part in range(2):
             predicted = jnp.sum(
@@ -279,7 +294,7 @@
                 axis=0,
                 keepdims=True,
             )
-            residual = factor * (values_ref[t, part : part + 1, :] - predicted)
+            residual = sample[1:2, :] * (sample[2 + part : 3 + part, :] - predicted)
             high = residual.astype(BF16).astype(F32)
             highs.append(jnp.where(mask, high, 0.0).astype(BF16))
             lows.append(jnp.where(mask, residual - high, 0.0).astype(BF16))
@@ -395,7 +410,7 @@
         kernel,
         out_shape=out_shape,
         in_specs=[pl.BlockSpec(memory_space=space) for space in spaces],
-        out_specs=pl.BlockSpec(memory_space=pltpu.VMEM),
+        out_specs=jax.tree.map(lambda _: pl.BlockSpec(memory_space=pltpu.VMEM), out_shape),
         scratch_shapes=scratch,
         compiler_params=pltpu.CompilerParams(vmem_limit_bytes=VMEM_LIMIT),
         name=name,
@@ -415,28 +430,29 @@
     rows = facets * fronts * columns
     held = length // LANES * columns
     fetched = [
-        strips[0, 0], made["window"], made["outer_minus"], made["turn"], made["inner_minus"],
-        offsets, made["shift"], made["piece"],
+        offsets, made["shift"], strips[0, 0], made["window"],
+        cells[0, :, 0], values[0, :, 0], weights[0], flags[0],
+        made["outer_minus"], made["turn"], made["inner_minus"], made["piece"],
     ]
-    is_scalar = [array is offsets for array in fetched]
-    fetched = [pltpu.with_memory_space_constraint(array, pltpu.HBM) for array in fetched]
-    pieces = kernel_call(
-        predict_kernel, "predict", jax.ShapeDtypeStruct((rows, LANES), BF16),
+    landing = [pltpu.VMEM(array.shape, array.dtype) for array in fetched]
+    landing[0] = pltpu.SMEM(offsets.shape, offsets.dtype)
+    pieces, packed = kernel_call(
+        predict_kernel, "predict",
+        [
+            jax.ShapeDtypeStruct((rows, LANES), BF16),
+            jax.ShapeDtypeStruct((4 * fronts, cells.shape[-1]), F32),
+        ],
         [pltpu.HBM] * len(fetched),
-        [
-            (pltpu.SMEM if scalar else pltpu.VMEM)(array.shape, array.dtype)
-            for array, scalar in zip(fetched, is_scalar)
-        ]
+        landing
         + [wide(held)] * 2
         + [wide(rows)] * 2
         + [pltpu.SemaphoreType.DMA((len(fetched),))],
-        *fetched,
-    )
-    samples = [cells[0, :, 0], values[0, :, 0], weights[0], flags[0]]
-    gathered = list(samples)
+        *[pltpu.with_memory_space_constraint(array, pltpu.HBM) for array in fetched],
+    )
+    gathered = [packed]
     for step in range(1, groups):
         moves = [((group + step) % groups, group) for group in range(groups)]
-        gathered += [lax.ppermute(array, "group", moves) for array in samples]
+        gathered.append(lax.ppermute(packed, "group", moves))
     arrived = lax.all_to_all(pieces, "member", split_axis=0, concat_axis=0, tiled=True)
     returned = kernel_call(
         functools.partial(subgrid_kernel, columns=columns, bands=bands), "subgrid",

time: 35 us -> 29.8 us (0.85)
  starting transfers between devices: 11.3 us -> 7.97 us
  waiting for transfers between devices: 4.18 us -> 2.26 us
    ppermute x4 -> x1, starting transfers between devices: 5.91 us -> 2.59 us  [local(): gathered.append(lax.ppermute(packed, 'group', moves))]
    ppermute x4 -> x1, waiting for transfers between devices: 4.17 us -> 2.05 us  [local(): gathered.append(lax.ppermute(packed, 'group', moves))]
    unnamed x28 -> x20, local copies, waits for them, and re-layouts: 0.71 us -> 0.69 us
  transfers between devices with their start and end apart: 5 -> 2, of which waited for: 2 -> 2; matrix products, arithmetic and copies ran while one was open for 0% -> 0% of each run, Pallas kernels for 0% -> 0%
where the time goes in v4:
time: 29.8 us; the launch traced here: 29.5 us
  blocking collectives  11 us (37%)
  starting transfers between devices  7.97 us (27%)
  Pallas kernels  7.44 us (25%)
  waiting for transfers between devices  2.26 us (8%)
  local copies, waits for them, and re-layouts  0.69 us (2%)
    all_to_all x1, blocking collectives, local(): lax.all_to_all(returned, ('band', 'member'), split_axis=0, concat_axis=0,...  11 us
    pallas_call x3, Pallas kernels, kernel_call(): pl.pallas_call(kernel, out_shape=out_shape, in_specs=[pl.BlockSpec(memory...  7.44 us
    all_to_all x1, starting transfers between devices, local(): lax.all_to_all(pieces, 'member', split_axis=0, concat_axis=0, tiled=True)  5.38 us
    ppermute x1, starting transfers between devices, local(): gathered.append(lax.ppermute(packed, 'group', moves))  2.59 us
    ppermute x1, waiting for transfers between devices, local(): gathered.append(lax.ppermute(packed, 'group', moves))  2.05 us
    unnamed x20, local copies, waits for them, and re-layouts  0.69 us
  transfers between devices with their start and end apart: 2, of which 2 were waited for; matrix products, arithmetic and copies ran while one was open for 0% of the time, Pallas kernels for 0%

profile of v4, /device:TPU:0, one launch (start us, length us, event | category | flops | bytes accessed | tf_op | source)
XLA Modules:
  0.0 29.5 jit_solution(16425071674525083405)
XLA Ops:
  0.0 0.0 copy-start.5
  0.0 0.0 copy-start.6
  0.0 0.0 copy-start.8
  0.0 3.3 %predict.1 = (bf16[256,128]{1,0:T(8,128)(2,1)}, f32[8,512]{1,0:T(8,128)S(1)}) custom-call(s32[2,16]{1,0:T(2,128)} %offsets_ref.1, f32[2,64,128]{2,1,0:T(8,128)} %constant.26.clone.refs_1_.shift_ref, f32[2,8,4096]{2,1,0:T(8,128)} %bitcast.13, f32[32,128]{1,0:T(8,128)} %constant.24.clone.refs_3_.window_ref, s32[2,2,512]{2,1,0:T(2,128)} %bitcast.14, ...), custom_call_target="tpu_custom_call" | custom-call | tf_op jit(solution)/shard_map/predict/pallas_call | solution.py:409
  3.3 0.0 copy-start.2
  3.3 5.4 %all-to-all-start = ((bf16[8,32,128]{2,1,0:T(8,128)(2,1)}), bf16[8,32,128]{2,1,0:T(8,128)(2,1)S(1)}, u32[]{:S(2)}, u32[]{:S(2)}) async-start(bf16[8,32,128]{2,1,0:T(8,128)(2,1)} %bitcast.5), calls=%async_computation | async-start | bytes 131072 | tf_op jit(solution)/shard_map/all_to_all | solution.py:456
  8.7 2.6 %collective-permute-start = (f32[8,512]{1,0:T(8,128)S(1)}, f32[8,512]{1,0:T(8,128)S(1)}, u32[]{:S(2)}, u32[]{:S(2)}) collective-permute-start(f32[8,512]{1,0:T(8,128)S(1)} %get-tuple-element.8.refs_0_), channel_id=1, source_target_pairs={{16,0},{0,16},{17,1},{1,17},{18,2},{2,18},{19,3},{3,19},{20,4},{4,... | collective-permute-start | bytes 49160 | tf_op jit(solution)/shard_map/ppermute | solution.py:455
  11.3 2.1 %collective-permute-done.refs_1_ = f32[8,512]{1,0:T(8,128)S(1)} collective-permute-done((f32[8,512]{1,0:T(8,128)S(1)}, f32[8,512]{1,0:T(8,128)S(1)}, u32[]{:S(2)}, u32[]{:S(2)}) %collective-permute-start) | collective-permute-done | bytes 16416 | tf_op jit(solution)/shard_map/ppermute | solution.py:455
  13.3 0.2 all-to-all-done
  13.5 0.0 copy-done.5
  13.5 0.0 copy-done.6
  13.5 0.0 copy-done.8
  13.5 0.0 copy-start.3
  13.5 0.0 copy-start.4
  13.6 0.0 copy-start.7
  13.6 1.9 %subgrid.1 = bf16[256,128]{1,0:T(8,128)(2,1)S(1)} custom-call(bf16[256,128]{1,0:T(8,128)(2,1)S(1)} %bitcast.10, f32[2,8,128]{2,1,0:T(8,128)S(1)} %copy-done.8, bf16[2,128,128]{2,1,0:T(8,128)(2,1)S(1)} %copy-done.6, bf16[2,128,128]{2,1,0:T(8,128)(2,1)S(1)} %copy-done.5, f32[8,512]{1,0:T(8,128)S(1)} %get-tuple-element.8.refs_0_, ...), custom_call_target="tpu_custom_call" | custom-call | tf_op jit(solution)/shard_map/subgrid/pallas_call | solution.py:409
  15.4 0.0 copy-start
  15.4 0.0 copy-start.1
  15.5 11.0 %all_to_all.22 = bf16[16,16,128]{2,1,0:T(8,128)(2,1)S(1)} all-to-all(bf16[16,16,128]{2,1,0:T(8,128)(2,1)S(1)} %bitcast.12), channel_id=1, replica_groups=mesh['group'=2,'member'=8,'band'=2] {'band','member'}, dimensions={0} | all-to-all | bytes 131072 | tf_op jit(solution)/shard_map/all_to_all | solution.py:463
  26.5 0.0 copy-start.9
  26.5 0.0 copy-done.2
  26.5 0.0 copy-done.3
  26.5 0.0 copy-done.4
  26.5 0.0 copy-done.7
  26.5 0.0 copy-done
  26.5 0.0 copy-done.1
  26.5 0.6 %copy-done.9 = s32[2,16]{1,0:T(2,128)S(1)} copy-done((s32[2,16]{1,0:T(2,128)S(1)}, s32[2,16]{1,0:T(2,128)}, u32[]{:S(2)}) %copy-start.9) | copy-done | bytes 152
  27.2 2.3 %lines.1 = f32[4,2,4096]{2,1,0:T(2,128)} custom-call(s32[2,16]{1,0:T(2,128)S(1)} %copy-done.9, bf16[256,128]{1,0:T(8,128)(2,1)S(1)} %bitcast.11, f32[32,128]{1,0:T(8,128)S(1)} %copy-done.7, f32[2,64,128]{2,1,0:T(8,128)S(1)} %copy-done.1, f32[2,64,128]{2,1,0:T(8,128)S(1)} %copy-done, bf16[2,128,128]{2,1,0:T(8,128)(2,1)S(1)} %copy-done.3, ...), custom_call_target="tpu_custom_call" | custom-call | tf_op jit(solution)/shard_map/lines/pallas_call | solution.py:409
Async XLA Ops:
  0.0 13.5 %copy-start.5 = (bf16[2,128,128]{2,1,0:T(8,128)(2,1)S(1)}, bf16[2,128,128]{2,1,0:T(8,128)(2,1)}, u32[]{:S(2)}) copy-start(bf16[2,128,128]{2,1,0:T(8,128)(2,1)} %constant.35.clone.back_ref) | copy-start | bytes 196612
  0.0 13.5 %copy-start.6 = (bf16[2,128,128]{2,1,0:T(8,128)(2,1)S(1)}, bf16[2,128,128]{2,1,0:T(8,128)(2,1)}, u32[]{:S(2)}) copy-start(bf16[2,128,128]{2,1,0:T(8,128)(2,1)} %constant.34.clone.model_ref) | copy-start | bytes 196612
  0.0 13.5 %copy-start.8 = (f32[2,8,128]{2,1,0:T(8,128)S(1)}, f32[2,8,128]{2,1,0:T(8,128)}, u32[]{:S(2)}) copy-start(f32[2,8,128]{2,1,0:T(8,128)} %constant.33.clone.turn_ref) | copy-start | bytes 24580
  3.3 23.2 %copy-start.2 = (bf16[2,256,256]{2,1,0:T(8,128)(2,1)S(1)}, bf16[2,256,256]{2,1,0:T(8,128)(2,1)}, u32[]{:S(2)}) copy-start(bf16[2,256,256]{2,1,0:T(8,128)(2,1)} %constant.30.clone.inner_ref) | copy-start | bytes 786436
  3.3 10.2 %all-to-all-start = ((bf16[8,32,128]{2,1,0:T(8,128)(2,1)}), bf16[8,32,128]{2,1,0:T(8,128)(2,1)S(1)}, u32[]{:S(2)}, u32[]{:S(2)}) async-start(bf16[8,32,128]{2,1,0:T(8,128)(2,1)} %bitcast.5), calls=%async_computation | async-start | bytes 131072 | tf_op jit(solution)/shard_map/all_to_all | solution.py:456
  8.7 4.6 %collective-permute-start = (f32[8,512]{1,0:T(8,128)S(1)}, f32[8,512]{1,0:T(8,128)S(1)}, u32[]{:S(2)}, u32[]{:S(2)}) collective-permute-start(f32[8,512]{1,0:T(8,128)S(1)} %get-tuple-element.8.refs_0_), channel_id=1, source_target_pairs={{16,0},{0,16},{17,1},{1,17},{18,2},{2,18},{19,3},{3,19},{20,4},{4,... | collective-permute-start | bytes 49160 | tf_op jit(solution)/shard_map/ppermute | solution.py:455
  13.5 13.0 %copy-start.3 = (bf16[2,128,128]{2,1,0:T(8,128)(2,1)S(1)}, bf16[2,128,128]{2,1,0:T(8,128)(2,1)}, u32[]{:S(2)}) copy-start(bf16[2,128,128]{2,1,0:T(8,128)(2,1)} %constant.32.clone.partial_ref) | copy-start | bytes 196612
  13.5 13.0 %copy-start.4 = (bf16[2,128,128]{2,1,0:T(8,128)(2,1)S(1)}, bf16[2,128,128]{2,1,0:T(8,128)(2,1)}, u32[]{:S(2)}) copy-start(bf16[2,128,128]{2,1,0:T(8,128)(2,1)} %constant.31.clone.outer_ref) | copy-start | bytes 196612
  13.6 13.0 %copy-start.7 = (f32[32,128]{1,0:T(8,128)S(1)}, f32[32,128]{1,0:T(8,128)}, u32[]{:S(2)}) copy-start(f32[32,128]{1,0:T(8,128)} %constant.24.clone.refs_3_.window_ref) | copy-start | bytes 49156
  15.4 11.1 %copy-start = (f32[2,64,128]{2,1,0:T(8,128)S(1)}, f32[2,64,128]{2,1,0:T(8,128)}, u32[]{:S(2)}) copy-start(f32[2,64,128]{2,1,0:T(8,128)} %constant.26.clone.refs_1_.shift_ref) | copy-start | bytes 196612
  15.4 11.1 %copy-start.1 = (f32[2,64,128]{2,1,0:T(8,128)S(1)}, f32[2,64,128]{2,1,0:T(8,128)}, u32[]{:S(2)}) copy-start(f32[2,64,128]{2,1,0:T(8,128)} %constant.25.clone.refs_9_.turn_ref) | copy-start | bytes 196612
  26.5 0.7 %copy-start.9 = (s32[2,16]{1,0:T(2,128)S(1)}, s32[2,16]{1,0:T(2,128)}, u32[]{:S(2)}) copy-start(s32[2,16]{1,0:T(2,128)} %offsets_ref.1) | copy-start | bytes 388

commit v5 on v4

--- a/solution.py
+++ b/solution.py
@@ -43,7 +43,23 @@
 def side_by_side(values):
     straight = np.concatenate([values.real, values.real], axis=-1)
     crossed = np.concatenate([-values.imag, values.imag], axis=-1)
-    return np.stack([straight, crossed]).astype(np.float32)
+    return np.stack([straight, crossed])
+
+
+def stack_tables(named):
+    places, blocks, begin = {}, [], 0
+    for name, table in named.items():
+        count = table.shape[1] // LANES
+        places[name] = (begin, table.shape[0], count)
+        blocks += [table[:, i * LANES : (i + 1) * LANES] for i in range(count)]
+        begin += table.shape[0] * count
+    return np.concatenate(blocks, axis=0), places
+
+
+def stack_pairs(named):
+    return stack_tables(
+        {(name, i): table for name, pair in named.items() for i, table in enumerate(pair)}
+    )
 
 
 def tables(length):
@@ -51,19 +67,33 @@
     short = np.arange(CONTRIB)
     outer = np.concatenate([np.arange(0, blocks, 2), np.arange(1, blocks, 2)])
     window = 1.0 + 0.5 * np.cos(np.arange(length) * (2.0 * math.pi / length))
+    window = (window * length**-0.5).reshape(length // LANES, LANES).astype(np.float32)
     turn = np.tile(phases(short, short, length, -1), (1, 2))
+    turn = np.stack([turn.real, turn.imag]).astype(np.float32)
     pair = np.eye(2)
+    shift = high_low(np.concatenate(side_by_side(phases(short, short, CONTRIB, -1)), axis=1))
+    outer_minus = from_left(phases(short, outer, blocks, -1))
+    inner_minus = from_right(np.kron(pair, phases(short, short, CONTRIB, -1)))
+    piece = from_right(phases(short, short, CONTRIB, 1)) * CONTRIB**-0.5
     return dict(
-        window=(window * length**-0.5).reshape(length // LANES, LANES).astype(np.float32),
-        turn=np.stack([turn.real, turn.imag]).astype(np.float32),
-        shift=side_by_side(phases(short, short, CONTRIB, -1)),
-        outer_minus=high_low(from_left(phases(short, outer, blocks, -1))),
-        inner_minus=high_low(from_right(np.kron(pair, phases(short, short, CONTRIB, -1)))),
-        piece=high_low(from_right(phases(short, short, CONTRIB, 1)) * CONTRIB**-0.5),
+        plain=stack_tables(dict(window=window, real=turn[0], imag=turn[1])),
+        paired=stack_pairs(
+            dict(
+                shift=shift,
+                outer=high_low(outer_minus),
+                inner=high_low(inner_minus),
+                piece=high_low(piece),
+            )
+        ),
+        window=window,
+        turn=turn,
+        shift=shift,
         inner_plus=high_low(from_right(np.kron(pair, phases(short, short, CONTRIB, 1)))),
         outer_plus=high_low(from_left(phases(outer, short, blocks, 1))),
         partial=high_low(from_right(phases(short, short, CONTRIB, -1)).T * CONTRIB**-0.5),
-        grid_turn=side_by_side(phases(np.arange(FACET_ROWS), short, SUBGRID, -1)),
+        grid_turn=side_by_side(phases(np.arange(FACET_ROWS), short, SUBGRID, -1)).astype(
+            np.float32
+        ),
         model=high_low(from_right(phases(short, short, CONTRIB, -1)) * SUBGRID**-0.5),
         back=high_low(from_right(phases(short, short, CONTRIB, 1)) * SUBGRID**-0.5),
     )
@@ -96,38 +126,32 @@
     return pltpu.roll(values, HALF, 1)
 
 
-def place_offsets(offsets_ref):
+def table_at(ref, place):
+    begin, rows, blocks = place
+    parts = [ref[begin + i * rows : begin + (i + 1) * rows, :] for i in range(blocks)]
+    return parts[0] if blocks == 1 else jnp.concatenate(parts, axis=1)
+
+
+def offsets_on_lanes(offsets_ref, columns):
     fronts, owners = offsets_ref.shape
     groups = owners // FACET_ROWS
     own = lax.axis_index("group")
-    return [
-        offsets_ref[t, lax.rem(own + step, groups) * FACET_ROWS + member]
-        for member in range(FACET_ROWS)
-        for step in range(groups)
-        for t in range(fronts)
-    ]
-
-
-def offsets_on_lanes(offsets, columns):
-    lane = iota((1, len(offsets) * columns), 1)
-    spread = jnp.zeros_like(lane)
-    for place, offset in enumerate(offsets):
-        begin = place * columns
-        here = (lane >= begin) & (lane < begin + columns)
-        spread = jnp.where(here, offset, spread)
-    return lane, spread
-
-
-def place_shifts(offsets, shift_ref, straight_ref, crossed_ref, columns):
-    for place, offset in enumerate(offsets):
-        residue = offset % CONTRIB
-        rows = pl.ds(place * columns, columns)
-        straight_ref[rows, :] = jnp.broadcast_to(
-            shift_ref[0, pl.ds(residue, 1), :], (columns, LANES)
-        )
-        crossed_ref[rows, :] = jnp.broadcast_to(
-            shift_ref[1, pl.ds(residue, 1), :], (columns, LANES)
-        )
+    begins = []
+    for step in range(groups):
+        group = own + step
+        begins.append(jnp.where(group >= groups, group - groups, group) * FACET_ROWS)
+    spread = iota((1, fronts * owners * columns), 1)
+    place_of = spread // columns
+    for place in range(fronts * owners):
+        t, step, member = place % fronts, place // fronts % groups, place // (fronts * groups)
+        spread = jnp.where(place_of == place, offsets_ref[t, begins[step] + member], spread)
+    return spread
+
+
+def shift_rows(residue, table):
+    pick = jnp.where(iota((CONTRIB, residue.shape[1]), 0) == residue, 1.0, 0.0).T.astype(BF16)
+    rows = dot(pick, table[0]) + dot(pick, table[1])
+    return rows[:, :LANES], rows[:, LANES:]
 
 
 def one_hot(shape, targets):
@@ -167,42 +191,38 @@
         out_ref[4 * t : 4 * t + 4, :] = jnp.concatenate(rows, axis=0)
 
 
-def predict_kernel(*refs):
-    count = 12
-    sources, outs, targets = refs[:count], refs[count : count + 2], refs[count + 2 :]
+def start_all(sources, targets, semaphores):
     copies = [
-        pltpu.make_async_copy(sources[i], targets[i], refs[-1].at[i]) for i in range(count)
+        pltpu.make_async_copy(source, target, semaphores.at[i])
+        for i, (source, target) in enumerate(zip(sources, targets))
     ]
     for copy in copies:
         copy.start()
-    out_ref, packed_ref = outs
-    offsets_ref, shift_ref, strips_ref, window_ref = targets[:4]
-    outer_ref, turn_ref, inner_ref, piece_ref = targets[8:count]
-    real_ref, imag_ref, straight_ref, crossed_ref = targets[count:-1]
+    return copies
+
+
+def predict(spread, copies, strips_ref, plain_ref, paired_ref, held_refs, out_ref, plain, paired):
     columns, length = strips_ref.shape[1:]
     groups = length // LANES
     pairs = columns // 2
     blocks = length // CONTRIB
-    for copy in copies[:2]:
-        copy.wait()
-    offsets = place_offsets(offsets_ref)
-    place_shifts(offsets, shift_ref, straight_ref, crossed_ref, columns)
-    lane, spread = offsets_on_lanes(offsets, columns)
+    width = spread.shape[1]
     first_block, residue = spread // CONTRIB, spread % CONTRIB
-    base = lane % columns * blocks
-    width = lane.shape[1]
+    base = iota(spread.shape, 1) % columns * blocks
     shape = (columns * blocks, width)
     pick_inside = one_hot(shape, base + first_block)
     pick_beyond = one_hot(shape, base + (first_block + 1) % blocks)
-    for copy in copies[4:8]:
+    for copy in copies:
         copy.wait()
-    pack_samples(*targets[4:8], packed_ref)
-    copies[2].wait()
-    copies[3].wait()
-    window = window_ref[...]
+
+    def pair_at(name):
+        return [table_at(paired_ref, paired[name, i]) for i in range(2)]
+
+    window = table_at(plain_ref, plain["window"])
+    turn_real, turn_imag = table_at(plain_ref, plain["real"]), table_at(plain_ref, plain["imag"])
     low_half = iota((groups, LANES), 1) < HALF
     sections = []
-    for part, held in enumerate((real_ref, imag_ref)):
+    for part, held in enumerate(held_refs):
         for group in range(groups):
             held[group * columns : (group + 1) * columns, :] = strips_ref[
                 part, :, group * LANES : (group + 1) * LANES
@@ -214,23 +234,18 @@
             even.append(jnp.where(low_half, first, swap_halves(second)))
             odd.append(jnp.where(low_half, swap_halves(first), second))
         sections += [jnp.concatenate(even, axis=1), jnp.concatenate(odd, axis=1)]
-    for copy in copies[8:]:
-        copy.wait()
-    section = table_times(outer_ref, jnp.concatenate(sections, axis=0))
+    section = table_times(pair_at("outer"), jnp.concatenate(sections, axis=0))
     turned = []
     for pair in range(pairs):
         lanes = slice(pair * LANES, (pair + 1) * LANES)
         real, imag = section[:CONTRIB, lanes], section[CONTRIB:, lanes]
         turned.append(
             jnp.concatenate(
-                [
-                    real * turn_ref[0] - imag * turn_ref[1],
-                    real * turn_ref[1] + imag * turn_ref[0],
-                ],
+                [real * turn_real - imag * turn_imag, real * turn_imag + imag * turn_real],
                 axis=1,
             )
         )
-    inner = times_table(jnp.concatenate(turned, axis=0), inner_ref)
+    inner = times_table(jnp.concatenate(turned, axis=0), pair_at("inner"))
     spectrum = jnp.concatenate(
         [
             jnp.concatenate(
@@ -249,8 +264,82 @@
     beyond = dot(high, pick_beyond) + dot(low, pick_beyond)
     kappa = iota((2 * CONTRIB, width), 0) % CONTRIB
     cutout = jnp.where(kappa >= residue, inside, beyond)
-    piece = times_table(cutout.T, piece_ref)
-    out_ref[...] = (piece * straight_ref[...] + swap_halves(piece) * crossed_ref[...]).astype(BF16)
+    piece = times_table(cutout.T, pair_at("piece"))
+    straight, crossed = shift_rows(residue, pair_at("shift"))
+    out_ref[...] = (piece * straight + swap_halves(piece) * crossed).astype(BF16)
+
+
+def in_first_half():
+    return 2 * lax.axis_index("group") < lax.axis_size("group")
+
+
+def early_kernel(
+    offsets, cells, values, weights, flags, strips, plain_table, paired_table,
+    out_ref, packed_ref, places_ref,
+    offsets_ref, cells_ref, values_ref, weights_ref, flags_ref, strips_ref, plain_ref, paired_ref,
+    real_ref, imag_ref, small_semaphores, semaphores, *, plain, paired, share,
+):
+    columns = strips_ref.shape[1]
+    small = start_all(
+        (offsets, cells, values, weights, flags),
+        (offsets_ref, cells_ref, values_ref, weights_ref, flags_ref),
+        small_semaphores,
+    )
+
+    def large():
+        sources, targets = (strips, plain_table, paired_table), (strips_ref, plain_ref, paired_ref)
+        return [
+            pltpu.make_async_copy(source, target, semaphores.at[i])
+            for i, (source, target) in enumerate(zip(sources, targets))
+        ]
+
+    @pl.when(in_first_half())
+    def _():
+        for copy in large():
+            copy.start()
+
+    for copy in small:
+        copy.wait()
+    for t in range(cells_ref.shape[0]):
+        rows = [
+            cells_ref[t, 0:1, :].astype(F32) * SUBGRID + cells_ref[t, 1:2, :].astype(F32),
+            weights_ref[t] * flags_ref[t].astype(F32),
+            values_ref[t],
+        ]
+        packed_ref[4 * t : 4 * t + 4, :] = jnp.concatenate(rows, axis=0)
+    places_ref[...] = offsets_on_lanes(offsets_ref, share)
+
+    @pl.when(in_first_half())
+    def _():
+        spread = offsets_on_lanes(offsets_ref, columns)
+        predict(
+            spread, large(), strips_ref, plain_ref, paired_ref, (real_ref, imag_ref), out_ref,
+            plain, paired,
+        )
+
+
+def late_kernel(
+    early_ref, offsets, strips, plain_table, paired_table, out_ref,
+    offsets_ref, strips_ref, plain_ref, paired_ref, real_ref, imag_ref, semaphores,
+    *, plain, paired,
+):
+    @pl.when(in_first_half())
+    def _():
+        out_ref[...] = early_ref[...]
+
+    @pl.when(jnp.logical_not(in_first_half()))
+    def _():
+        copies = start_all(
+            (offsets, strips, plain_table, paired_table),
+            (offsets_ref, strips_ref, plain_ref, paired_ref),
+            semaphores,
+        )
+        copies[0].wait()
+        spread = offsets_on_lanes(offsets_ref, strips_ref.shape[1])
+        predict(
+            spread, copies[1:], strips_ref, plain_ref, paired_ref, (real_ref, imag_ref), out_ref,
+            plain, paired,
+        )
 
 
 def subgrid_kernel(pieces_ref, turn_ref, model_ref, back_ref, *refs, columns, bands):
@@ -326,24 +415,23 @@
 
 
 def return_kernel(
-    offsets_ref, pieces_ref, window_ref, turn_ref, shift_ref, partial_ref, inner_ref, outer_ref,
-    out_ref, straight_ref, crossed_ref, *line_refs, bands,
+    places_ref, pieces_ref, window_ref, turn_ref, shift_ref, partial_ref, inner_ref, outer_ref,
+    out_ref, *line_refs, bands,
 ):
     columns, _, length = out_ref.shape
     blocks = length // CONTRIB
     groups = length // LANES
     pairs = (columns + 1) // 2
-    offsets = place_offsets(offsets_ref)
-    place_shifts(offsets, shift_ref, straight_ref, crossed_ref, columns)
+    spread = places_ref[...]
+    first_block, residue = spread // CONTRIB, spread % CONTRIB
+    straight, crossed = shift_rows(residue, shift_ref)
     width = pieces_ref.shape[0] // bands
     summed = pieces_ref[0:width, :].astype(F32)
     for b in range(1, bands):
         summed += pieces_ref[b * width : (b + 1) * width, :].astype(F32)
-    summed = summed * straight_ref[...] - swap_halves(summed) * crossed_ref[...]
+    summed = summed * straight - swap_halves(summed) * crossed
     residues = table_times(partial_ref, summed, ((1,), (1,)))
-    lane, spread = offsets_on_lanes(offsets, columns)
-    first_block, residue = spread // CONTRIB, spread % CONTRIB
-    base = lane % columns * blocks
+    base = iota(spread.shape, 1) % columns * blocks
     kappa = iota((2 * CONTRIB, width), 0) % CONTRIB
     inside = kappa >= residue
     both = jnp.concatenate(
@@ -425,29 +513,46 @@
     columns, length = strips.shape[-2:]
     fronts = offsets.shape[0]
     share = columns // bands
-    made = {key: jnp.asarray(value) for key, value in tables(length).items()}
     facets = groups * FACET_ROWS
     rows = facets * fronts * columns
+    width = facets * fronts * share
+    made = tables(length)
+    plain, plain_places = made.pop("plain")
+    paired, paired_places = made.pop("paired")
+    made = {key: jnp.asarray(value) for key, value in made.items()}
     held = length // LANES * columns
-    fetched = [
-        offsets, made["shift"], strips[0, 0], made["window"],
-        cells[0, :, 0], values[0, :, 0], weights[0], flags[0],
-        made["outer_minus"], made["turn"], made["inner_minus"], made["piece"],
-    ]
-    landing = [pltpu.VMEM(array.shape, array.dtype) for array in fetched]
-    landing[0] = pltpu.SMEM(offsets.shape, offsets.dtype)
-    pieces, packed = kernel_call(
-        predict_kernel, "predict",
+    small = [offsets, cells[0, :, 0], values[0, :, 0], weights[0], flags[0]]
+    large = [strips[0, 0], jnp.asarray(plain), jnp.asarray(paired)]
+
+    def landing(arrays):
+        return [
+            (pltpu.SMEM if array is offsets else pltpu.VMEM)(array.shape, array.dtype)
+            for array in arrays
+        ]
+
+    def in_hbm(arrays):
+        return [pltpu.with_memory_space_constraint(array, pltpu.HBM) for array in arrays]
+
+    def semaphores(count):
+        return pltpu.SemaphoreType.DMA((count,))
+
+    early, packed, places = kernel_call(
+        functools.partial(early_kernel, plain=plain_places, paired=paired_places, share=share),
+        "early",
         [
             jax.ShapeDtypeStruct((rows, LANES), BF16),
             jax.ShapeDtypeStruct((4 * fronts, cells.shape[-1]), F32),
+            jax.ShapeDtypeStruct((1, width), jnp.int32),
         ],
-        [pltpu.HBM] * len(fetched),
-        landing
-        + [wide(held)] * 2
-        + [wide(rows)] * 2
-        + [pltpu.SemaphoreType.DMA((len(fetched),))],
-        *[pltpu.with_memory_space_constraint(array, pltpu.HBM) for array in fetched],
+        [pltpu.HBM] * 8,
+        landing(small + large) + [wide(held)] * 2 + [semaphores(5), semaphores(3)],
+        *in_hbm(small + large),
+    )
+    pieces = kernel_call(
+        functools.partial(late_kernel, plain=plain_places, paired=paired_places), "late",
+        jax.ShapeDtypeStruct((rows, LANES), BF16), [pltpu.VMEM] + [pltpu.HBM] * 4,
+        landing([offsets] + large) + [wide(held)] * 2 + [semaphores(4)],
+        early, *in_hbm([offsets] + large),
     )
     gathered = [packed]
     for step in range(1, groups):
@@ -463,12 +568,11 @@
     delivered = lax.all_to_all(
         returned, ("band", "member"), split_axis=0, concat_axis=0, tiled=True
     )
-    width = facets * fronts * share
     lines = kernel_call(
         functools.partial(return_kernel, bands=bands), "lines",
-        jax.ShapeDtypeStruct((share, 2, length), F32), [pltpu.SMEM] + [pltpu.VMEM] * 7,
-        [wide(width)] * 2 + [wide(2 * length // LANES)] * share,
-        offsets, delivered, made["window"], made["turn"], made["shift"],
+        jax.ShapeDtypeStruct((share, 2, length), F32), [pltpu.VMEM] * 8,
+        [wide(2 * length // LANES)] * share,
+        places, delivered, made["window"], made["turn"], made["shift"],
         made["partial"], made["inner_plus"], made["outer_plus"],
     )
     return lines[None]

time: 29.8 us -> 29.5 us (0.990)
  starting transfers between devices: 7.97 us -> 8.7 us
  local copies, waits for them, and re-layouts: 0.69 us -> 0.06 us
  blocking collectives: 11 us -> 11.6 us
  waiting for transfers between devices: 2.26 us -> 1.72 us
  Pallas kernels: 7.44 us -> 7.02 us
    ppermute x1, starting transfers between devices: 2.59 us -> 3.32 us  [local(): gathered.append(lax.ppermute(packed, 'group', moves))]
    unnamed x20 -> x18, local copies, waits for them, and re-layouts: 0.69 us -> 0.06 us
    all_to_all x1, blocking collectives: 11 us -> 11.6 us  [local(): lax.all_to_all(returned, ('band', 'member'), split_axis=0, concat_axis=0,...]
    pallas_call x3 -> x4, Pallas kernels: 7.44 us -> 7.02 us  [kernel_call(): pl.pallas_call(kernel, out_shape=out_shape, in_specs=[pl.BlockSpec(memory...]
    ppermute x1, waiting for transfers between devices: 2.05 us -> 1.72 us  [local(): gathered.append(lax.ppermute(packed, 'group', moves))]
  transfers between devices with their start and end apart: 2 -> 2, of which waited for: 2 -> 1; matrix products, arithmetic and copies ran while one was open for 0% -> 0% of each run, Pallas kernels for 0% -> 0%
where the time goes in v5:
time: 29.5 us; the launch traced here: 29.2 us
  blocking collectives  11.6 us (39%)
  starting transfers between devices  8.7 us (29%)
  Pallas kernels  7.02 us (24%)
  waiting for transfers between devices  1.72 us (6%)
    all_to_all x1, blocking collectives, local(): lax.all_to_all(returned, ('band', 'member'), split_axis=0, concat_axis=0,...  11.6 us
    pallas_call x4, Pallas kernels, kernel_call(): pl.pallas_call(kernel, out_shape=out_shape, in_specs=[pl.BlockSpec(memory...  7.02 us
    all_to_all x1, starting transfers between devices, local(): lax.all_to_all(pieces, 'member', split_axis=0, concat_axis=0, tiled=True)  5.37 us
    ppermute x1, starting transfers between devices, local(): gathered.append(lax.ppermute(packed, 'group', moves))  3.32 us
    ppermute x1, waiting for transfers between devices, local(): gathered.append(lax.ppermute(packed, 'group', moves))  1.72 us
  transfers between devices with their start and end apart: 2, of which 1 were waited for; matrix products, arithmetic and copies ran while one was open for 0% of the time, Pallas kernels for 0%

profile of v5, /device:TPU:0, one launch (start us, length us, event | category | flops | bytes accessed | tf_op | source)
XLA Modules:
  0.0 29.2 jit_solution(1756853333309251963)
XLA Ops:
  0.0 2.6 %early.1 = (bf16[256,128]{1,0:T(8,128)(2,1)S(1)}, f32[8,512]{1,0:T(8,128)S(1)}, s32[1,128]{1,0:T(1,128)S(1)}) custom-call(s32[2,16]{1,0:T(2,128)} %offsets.3, s32[2,2,512]{2,1,0:T(2,128)} %bitcast.15, f32[2,2,512]{2,1,0:T(2,128)} %bitcast.16, f32[2,1,512]{2,1,0:T(1,128)} %bitcast.17, s32[2,1,512]{2,1,0:T(1,128)} %bitcast.18, f32[2,8,4096]{2,1,0:T(8,128)} %bitcast.13, ...), custom_call_target="tpu_custom_call" | custom-call | tf_op jit(solution)/shard_map/early/pallas_call | solution.py:497
  2.6 0.0 copy-start.5
  2.6 0.0 copy-start.6
  2.7 0.0 copy-start.8
  2.7 0.7 %late.1 = bf16[256,128]{1,0:T(8,128)(2,1)} custom-call(bf16[256,128]{1,0:T(8,128)(2,1)S(1)} %get-tuple-element.9.early_ref, s32[2,16]{1,0:T(2,128)} %offsets.3, f32[2,8,4096]{2,1,0:T(8,128)} %bitcast.14, f32[160,128]{1,0:T(8,128)} %constant.31.clone.plain_table, bf16[1792,128]{1,0:T(8,128)(2,1)} %constant.32.clone.paired_table), custom_call_target="tpu_custom_call" | custom-call | tf_op jit(solution)/shard_map/late/pallas_call | solution.py:497
  3.4 0.0 copy-start
  3.4 5.4 %all-to-all-start = ((bf16[8,32,128]{2,1,0:T(8,128)(2,1)}), bf16[8,32,128]{2,1,0:T(8,128)(2,1)S(1)}, u32[]{:S(2)}, u32[]{:S(2)}) async-start(bf16[8,32,128]{2,1,0:T(8,128)(2,1)} %bitcast.5), calls=%async_computation | async-start | bytes 131072 | tf_op jit(solution)/shard_map/all_to_all | solution.py:561
  8.8 3.3 %collective-permute-start = (f32[8,512]{1,0:T(8,128)S(1)}, f32[8,512]{1,0:T(8,128)S(1)}, u32[]{:S(2)}, u32[]{:S(2)}) collective-permute-start(f32[8,512]{1,0:T(8,128)S(1)} %get-tuple-element.10.refs_0_), channel_id=1, source_target_pairs={{16,0},{0,16},{17,1},{1,17},{18,2},{2,18},{19,3},{3,19},{20,4},{4,... | collective-permute-start | bytes 49160 | tf_op jit(solution)/shard_map/ppermute | solution.py:560
  12.1 1.7 %collective-permute-done.refs_1_ = f32[8,512]{1,0:T(8,128)S(1)} collective-permute-done((f32[8,512]{1,0:T(8,128)S(1)}, f32[8,512]{1,0:T(8,128)S(1)}, u32[]{:S(2)}, u32[]{:S(2)}) %collective-permute-start) | collective-permute-done | bytes 16416 | tf_op jit(solution)/shard_map/ppermute | solution.py:560
  13.8 0.0 all-to-all-done
  13.8 0.0 copy-done.5
  13.8 0.0 copy-done.6
  13.8 0.0 copy-done.8
  13.8 0.0 copy-start.3
  13.8 0.0 copy-start.4
  13.8 0.0 copy-start.7
  13.9 1.9 %subgrid.1 = bf16[256,128]{1,0:T(8,128)(2,1)S(1)} custom-call(bf16[256,128]{1,0:T(8,128)(2,1)S(1)} %bitcast.10, f32[2,8,128]{2,1,0:T(8,128)S(1)} %copy-done.8, bf16[2,128,128]{2,1,0:T(8,128)(2,1)S(1)} %copy-done.6, bf16[2,128,128]{2,1,0:T(8,128)(2,1)S(1)} %copy-done.5, f32[8,512]{1,0:T(8,128)S(1)} %get-tuple-element.10.refs_0_, ...), custom_call_target="tpu_custom_call" | custom-call | tf_op jit(solution)/shard_map/subgrid/pallas_call | solution.py:497
  15.7 0.0 copy-start.1
  15.7 0.0 copy-start.2
  15.7 11.6 %all_to_all.22 = bf16[16,16,128]{2,1,0:T(8,128)(2,1)S(1)} all-to-all(bf16[16,16,128]{2,1,0:T(8,128)(2,1)S(1)} %bitcast.12), channel_id=1, replica_groups=mesh['group'=2,'member'=8,'band'=2] {'band','member'}, dimensions={0} | all-to-all | bytes 131072 | tf_op jit(solution)/shard_map/all_to_all | solution.py:568
  27.3 0.0 copy-done
  27.3 0.0 copy-done.3
  27.3 0.0 copy-done.4
  27.3 0.0 copy-done.7
  27.3 0.0 copy-done.1
  27.4 0.0 copy-done.2
  27.4 1.8 %lines.1 = f32[4,2,4096]{2,1,0:T(2,128)} custom-call(s32[1,128]{1,0:T(1,128)S(1)} %get-tuple-element.8.places_ref, bf16[256,128]{1,0:T(8,128)(2,1)S(1)} %bitcast.11, f32[32,128]{1,0:T(8,128)S(1)} %copy-done.7, f32[2,64,128]{2,1,0:T(8,128)S(1)} %copy-done.4, bf16[2,64,256]{2,1,0:T(8,128)(2,1)S(1)} %copy-done.3, bf16[2,128,128]{2,1,0:T(8,128)(2,1)S(1)} %copy-done.1, ...), custom_call_target="tpu_custom_call" | custom-call | tf_op jit(solution)/shard_map/lines/pallas_call | solution.py:497
Async XLA Ops:
  2.6 11.2 %copy-start.5 = (bf16[2,128,128]{2,1,0:T(8,128)(2,1)S(1)}, bf16[2,128,128]{2,1,0:T(8,128)(2,1)}, u32[]{:S(2)}) copy-start(bf16[2,128,128]{2,1,0:T(8,128)(2,1)} %constant.30.clone.back_ref) | copy-start | bytes 196612
  2.6 11.2 %copy-start.6 = (bf16[2,128,128]{2,1,0:T(8,128)(2,1)S(1)}, bf16[2,128,128]{2,1,0:T(8,128)(2,1)}, u32[]{:S(2)}) copy-start(bf16[2,128,128]{2,1,0:T(8,128)(2,1)} %constant.29.clone.model_ref) | copy-start | bytes 196612
  2.7 11.1 %copy-start.8 = (f32[2,8,128]{2,1,0:T(8,128)S(1)}, f32[2,8,128]{2,1,0:T(8,128)}, u32[]{:S(2)}) copy-start(f32[2,8,128]{2,1,0:T(8,128)} %constant.28.clone.turn_ref) | copy-start | bytes 24580
  3.4 24.0 %copy-start = (bf16[2,256,256]{2,1,0:T(8,128)(2,1)S(1)}, bf16[2,256,256]{2,1,0:T(8,128)(2,1)}, u32[]{:S(2)}) copy-start(bf16[2,256,256]{2,1,0:T(8,128)(2,1)} %constant.25.clone.inner_ref) | copy-start | bytes 786436
  3.4 10.4 %all-to-all-start = ((bf16[8,32,128]{2,1,0:T(8,128)(2,1)}), bf16[8,32,128]{2,1,0:T(8,128)(2,1)S(1)}, u32[]{:S(2)}, u32[]{:S(2)}) async-start(bf16[8,32,128]{2,1,0:T(8,128)(2,1)} %bitcast.5), calls=%async_computation | async-start | bytes 131072 | tf_op jit(solution)/shard_map/all_to_all | solution.py:561
  8.8 5.0 %collective-permute-start = (f32[8,512]{1,0:T(8,128)S(1)}, f32[8,512]{1,0:T(8,128)S(1)}, u32[]{:S(2)}, u32[]{:S(2)}) collective-permute-start(f32[8,512]{1,0:T(8,128)S(1)} %get-tuple-element.10.refs_0_), channel_id=1, source_target_pairs={{16,0},{0,16},{17,1},{1,17},{18,2},{2,18},{19,3},{3,19},{20,4},{4,... | collective-permute-start | bytes 49160 | tf_op jit(solution)/shard_map/ppermute | solution.py:560
  13.8 13.5 %copy-start.3 = (bf16[2,64,256]{2,1,0:T(8,128)(2,1)S(1)}, bf16[2,64,256]{2,1,0:T(8,128)(2,1)}, u32[]{:S(2)}) copy-start(bf16[2,64,256]{2,1,0:T(8,128)(2,1)} %constant.24.clone.shift_ref) | copy-start | bytes 196612
  13.8 13.5 %copy-start.4 = (f32[2,64,128]{2,1,0:T(8,128)S(1)}, f32[2,64,128]{2,1,0:T(8,128)}, u32[]{:S(2)}) copy-start(f32[2,64,128]{2,1,0:T(8,128)} %constant.23.clone.turn_ref) | copy-start | bytes 196612
  13.8 13.5 %copy-start.7 = (f32[32,128]{1,0:T(8,128)S(1)}, f32[32,128]{1,0:T(8,128)}, u32[]{:S(2)}) copy-start(f32[32,128]{1,0:T(8,128)} %constant.22.clone.window_ref) | copy-start | bytes 49156
  15.7 11.6 %copy-start.1 = (bf16[2,128,128]{2,1,0:T(8,128)(2,1)S(1)}, bf16[2,128,128]{2,1,0:T(8,128)(2,1)}, u32[]{:S(2)}) copy-start(bf16[2,128,128]{2,1,0:T(8,128)(2,1)} %constant.27.clone.partial_ref) | copy-start | bytes 196612
  15.7 11.6 %copy-start.2 = (bf16[2,128,128]{2,1,0:T(8,128)(2,1)S(1)}, bf16[2,128,128]{2,1,0:T(8,128)(2,1)}, u32[]{:S(2)}) copy-start(bf16[2,128,128]{2,1,0:T(8,128)(2,1)} %constant.26.clone.outer_ref) | copy-start | bytes 196612

commit v6 on v5

--- a/solution.py
+++ b/solution.py
@@ -16,6 +16,8 @@
 SUBGRID = FACET_ROWS * CONTRIB
 LANES = 128
 HALF = LANES // 2
+LATE_FLOPS = 10**10
+PREPARE_FLOPS = 2 * 10**10
 VMEM_LIMIT = 48 * 1024 * 1024
 F32 = jnp.float32
 BF16 = jnp.bfloat16
@@ -342,30 +344,13 @@
         )
 
 
-def subgrid_kernel(pieces_ref, turn_ref, model_ref, back_ref, *refs, columns, bands):
-    samples_refs, (out_ref, held_ref) = refs[:-2], refs[-2:]
-    groups = len(samples_refs)
+def prepare_kernel(places_ref, shift_ref, *refs, columns, share, blocks):
+    samples_refs, outs = refs[:-5], refs[-5:]
+    value_ref, weight_ref, put_ref, straight_ref, crossed_ref = outs
     fronts, samples = samples_refs[0].shape[0] // 4, samples_refs[0].shape[1]
     own = lax.axis_index("group")
-    rows = pieces_ref.shape[0] // FACET_ROWS
     depth = FACET_ROWS * columns
-    share = columns // bands
-    pieces = pieces_ref[...].astype(F32)
-    sky = turned_eighths(
-        [pieces[i * rows : (i + 1) * rows, :] for i in range(FACET_ROWS)], -1.0
-    )
-    sky = [
-        value * turn_ref[0, i : i + 1, :] + swap_halves(value) * turn_ref[1, i : i + 1, :]
-        for i, value in enumerate(sky)
-    ]
-    spots = range(groups * fronts)
-    stacked = jnp.concatenate(
-        [value[spot * columns : (spot + 1) * columns, :] for spot in spots for value in sky],
-        axis=0,
-    )
-    model = times_table(stacked, model_ref)
-    grids = []
-    for spot in spots:
+    for spot in range(len(samples_refs) * fronts):
         step, t = spot // fronts, spot % fronts
         sample = samples_refs[step][4 * t : 4 * t + 4, :]
         cell = sample[0:1, :].astype(jnp.int32)
@@ -373,25 +358,50 @@
         inside = (row >= 0) & (row < columns)
         target = jnp.where(inside, col % FACET_ROWS * columns + row, -1)
         pick = one_hot((depth, samples), target)
-        high, low = split(model[spot * depth : (spot + 1) * depth, :].T)
-        line = dot(high, pick) + dot(low, pick)
         mask = iota((HALF, samples), 0) == col // FACET_ROWS
+        factor = sample[1:2, :]
         highs, lows = [], []
-        for part in range(2):
-            predicted = jnp.sum(
-                jnp.where(mask, line[part * HALF : (part + 1) * HALF, :], 0.0),
-                axis=0,
-                keepdims=True,
-            )
-            residual = sample[1:2, :] * (sample[2 + part : 3 + part, :] - predicted)
-            high = residual.astype(BF16).astype(F32)
+        for term in (factor * sample[2:3, :], factor * sample[3:4, :], factor):
+            high = term.astype(BF16).astype(F32)
             highs.append(jnp.where(mask, high, 0.0).astype(BF16))
-            lows.append(jnp.where(mask, residual - high, 0.0).astype(BF16))
-        grids.append(
-            dot(pick, jnp.concatenate(highs, axis=0), ((1,), (1,)))
-            + dot(pick, jnp.concatenate(lows, axis=0), ((1,), (1,)))
+            lows.append(jnp.where(mask, term - high, 0.0).astype(BF16))
+        highs, lows = highs + highs[2:], lows + lows[2:]
+        grid = dot(pick, jnp.concatenate(highs, axis=0), ((1,), (1,))) + dot(
+            pick, jnp.concatenate(lows, axis=0), ((1,), (1,))
         )
-    back = times_table(jnp.concatenate(grids, axis=0), back_ref)
+        rows = slice(spot * depth, (spot + 1) * depth)
+        value_ref[rows, :] = grid[:, :LANES]
+        weight_ref[rows, :] = grid[:, LANES:]
+    spread = places_ref[...]
+    first_block, residue = spread // CONTRIB, spread % CONTRIB
+    straight_ref[...], crossed_ref[...] = shift_rows(residue, shift_ref)
+    base = iota(spread.shape, 1) % share * blocks
+    targets = jnp.concatenate([base + first_block, base + (first_block + 1) % blocks], axis=1)
+    put_ref[...] = one_hot(put_ref.shape, targets)
+
+
+def subgrid_kernel(
+    pieces_ref, value_ref, weight_ref, turn_ref, model_ref, back_ref, out_ref, held_ref,
+    *, columns, bands,
+):
+    rows = pieces_ref.shape[0] // FACET_ROWS
+    spots = range(rows // columns)
+    depth = FACET_ROWS * columns
+    share = columns // bands
+    pieces = pieces_ref[...].astype(F32)
+    sky = turned_eighths(
+        [pieces[i * rows : (i + 1) * rows, :] for i in range(FACET_ROWS)], -1.0
+    )
+    sky = [
+        value * turn_ref[0, i : i + 1, :] + swap_halves(value) * turn_ref[1, i : i + 1, :]
+        for i, value in enumerate(sky)
+    ]
+    stacked = jnp.concatenate(
+        [value[spot * columns : (spot + 1) * columns, :] for spot in spots for value in sky],
+        axis=0,
+    )
+    grid = value_ref[...] - weight_ref[...] * times_table(stacked, model_ref)
+    back = times_table(grid, back_ref)
     lines = []
     for i in range(FACET_ROWS):
         value = jnp.concatenate(
@@ -415,32 +425,25 @@
 
 
 def return_kernel(
-    places_ref, pieces_ref, window_ref, turn_ref, shift_ref, partial_ref, inner_ref, outer_ref,
-    out_ref, *line_refs, bands,
+    places_ref, pieces_ref, straight_ref, crossed_ref, put_ref, window_ref, turn_ref, partial_ref,
+    inner_ref, outer_ref, out_ref, *line_refs, bands,
 ):
     columns, _, length = out_ref.shape
     blocks = length // CONTRIB
     groups = length // LANES
     pairs = (columns + 1) // 2
-    spread = places_ref[...]
-    first_block, residue = spread // CONTRIB, spread % CONTRIB
-    straight, crossed = shift_rows(residue, shift_ref)
     width = pieces_ref.shape[0] // bands
     summed = pieces_ref[0:width, :].astype(F32)
     for b in range(1, bands):
         summed += pieces_ref[b * width : (b + 1) * width, :].astype(F32)
-    summed = summed * straight - swap_halves(summed) * crossed
+    summed = summed * straight_ref[...] - swap_halves(summed) * crossed_ref[...]
     residues = table_times(partial_ref, summed, ((1,), (1,)))
-    base = iota(spread.shape, 1) % columns * blocks
     kappa = iota((2 * CONTRIB, width), 0) % CONTRIB
-    inside = kappa >= residue
+    inside = kappa >= places_ref[...] % CONTRIB
     both = jnp.concatenate(
         [jnp.where(inside, residues, 0.0), jnp.where(inside, 0.0, residues)], axis=1
     )
-    targets = jnp.concatenate(
-        [base + first_block, base + (first_block + 1) % blocks], axis=1
-    )
-    put = one_hot((2 * pairs * blocks, 2 * width), targets)
+    put = put_ref[...]
     high, low = split(both)
     spectrum = dot(high, put, ((1,), (1,))) + dot(low, put, ((1,), (1,)))
     inner = times_table(
@@ -493,7 +496,7 @@
             ]
 
 
-def kernel_call(kernel, name, out_shape, spaces, scratch, *operands):
+def kernel_call(kernel, name, out_shape, spaces, scratch, *operands, flops=0):
     return pl.pallas_call(
         kernel,
         out_shape=out_shape,
@@ -501,6 +504,9 @@
         out_specs=jax.tree.map(lambda _: pl.BlockSpec(memory_space=pltpu.VMEM), out_shape),
         scratch_shapes=scratch,
         compiler_params=pltpu.CompilerParams(vmem_limit_bytes=VMEM_LIMIT),
+        cost_estimate=pl.CostEstimate(flops=flops, bytes_accessed=0, transcendentals=0)
+        if flops
+        else None,
         name=name,
     )(*operands)
 
@@ -552,27 +558,35 @@
         functools.partial(late_kernel, plain=plain_places, paired=paired_places), "late",
         jax.ShapeDtypeStruct((rows, LANES), BF16), [pltpu.VMEM] + [pltpu.HBM] * 4,
         landing([offsets] + large) + [wide(held)] * 2 + [semaphores(4)],
-        early, *in_hbm([offsets] + large),
+        early, *in_hbm([offsets] + large), flops=LATE_FLOPS,
     )
     gathered = [packed]
     for step in range(1, groups):
         moves = [((group + step) % groups, group) for group in range(groups)]
         gathered.append(lax.ppermute(packed, "group", moves))
     arrived = lax.all_to_all(pieces, "member", split_axis=0, concat_axis=0, tiled=True)
+    blocks = length // CONTRIB
+    value, weight, put, straight, crossed = kernel_call(
+        functools.partial(prepare_kernel, columns=columns, share=share, blocks=blocks), "prepare",
+        [jax.ShapeDtypeStruct((rows, LANES), F32)] * 2
+        + [jax.ShapeDtypeStruct(((share + share % 2) * blocks, 2 * width), BF16)]
+        + [jax.ShapeDtypeStruct((width, LANES), F32)] * 2,
+        [pltpu.VMEM] * (2 + len(gathered)), [],
+        places, made["shift"], *gathered, flops=PREPARE_FLOPS,
+    )
     returned = kernel_call(
         functools.partial(subgrid_kernel, columns=columns, bands=bands), "subgrid",
-        jax.ShapeDtypeStruct((rows, LANES), BF16), [pltpu.VMEM] * (4 + len(gathered)),
-        [wide(rows)],
-        arrived, made["grid_turn"], made["model"], made["back"], *gathered,
+        jax.ShapeDtypeStruct((rows, LANES), BF16), [pltpu.VMEM] * 6, [wide(rows)],
+        arrived, value, weight, made["grid_turn"], made["model"], made["back"],
     )
     delivered = lax.all_to_all(
         returned, ("band", "member"), split_axis=0, concat_axis=0, tiled=True
     )
     lines = kernel_call(
         functools.partial(return_kernel, bands=bands), "lines",
-        jax.ShapeDtypeStruct((share, 2, length), F32), [pltpu.VMEM] * 8,
+        jax.ShapeDtypeStruct((share, 2, length), F32), [pltpu.VMEM] * 10,
         [wide(2 * length // LANES)] * share,
-        places, delivered, made["window"], made["turn"], made["shift"],
+        places, delivered, straight, crossed, put, made["window"], made["turn"],
         made["partial"], made["inner_plus"], made["outer_plus"],
     )
     return lines[None]

time: 29.5 us -> 26.8 us (0.908)
  the two profiles are of different devices: /device:TPU:0 before, /device:TPU:16 now
where the time goes in v6:
time: 26.8 us; the launch traced here: 26.4 us
  blocking collectives  8.83 us (33%)
  Pallas kernels  7.42 us (28%)
  starting transfers between devices  6.11 us (23%)
  waiting for transfers between devices  3.89 us (15%)
    all_to_all x1, blocking collectives, local(): lax.all_to_all(returned, ('band', 'member'), split_axis=0, concat_axis=0,...  8.83 us
    pallas_call x5, Pallas kernels, kernel_call(): pl.pallas_call(kernel, out_shape=out_shape, in_specs=[pl.BlockSpec(memory...  7.42 us
    all_to_all x1, starting transfers between devices, local(): lax.all_to_all(pieces, 'member', split_axis=0, concat_axis=0, tiled=True)  5.37 us
    all_to_all x1, waiting for transfers between devices, local(): lax.all_to_all(pieces, 'member', split_axis=0, concat_axis=0, tiled=True)  3.89 us
    ppermute x1, starting transfers between devices, local(): gathered.append(lax.ppermute(packed, 'group', moves))  0.73 us
  transfers between devices with their start and end apart: 2, of which 1 were waited for; matrix products, arithmetic and copies ran while one was open for 0% of the time, Pallas kernels for 15%

profile of v6, /device:TPU:16, one launch (start us, length us, event | category | flops | bytes accessed | tf_op | source)
XLA Modules:
  0.0 26.4 jit_solution(4844720436591018860)
XLA Ops:
  0.0 0.8 %early.1 = (bf16[256,128]{1,0:T(8,128)(2,1)S(1)}, f32[8,512]{1,0:T(8,128)S(1)}, s32[1,128]{1,0:T(1,128)S(1)}) custom-call(s32[2,16]{1,0:T(2,128)} %offsets.3, s32[2,2,512]{2,1,0:T(2,128)} %bitcast.15, f32[2,2,512]{2,1,0:T(2,128)} %bitcast.16, f32[2,1,512]{2,1,0:T(1,128)} %bitcast.17, s32[2,1,512]{2,1,0:T(1,128)} %bitcast.18, f32[2,8,4096]{2,1,0:T(8,128)} %bitcast.13, ...), custom_call_target="tpu_custom_call" | custom-call | tf_op jit(solution)/shard_map/early/pallas_call | solution.py:500
  0.9 0.7 %collective-permute-start = (f32[8,512]{1,0:T(8,128)S(1)}, f32[8,512]{1,0:T(8,128)S(1)}, u32[]{:S(2)}, u32[]{:S(2)}) collective-permute-start(f32[8,512]{1,0:T(8,128)S(1)} %get-tuple-element.15.refs_0_), channel_id=1, source_target_pairs={{16,0},{0,16},{17,1},{1,17},{18,2},{2,18},{19,3},{3,19},{20,4},{4,... | collective-permute-start | bytes 49160 | tf_op jit(solution)/shard_map/ppermute | solution.py:566
  1.6 3.2 %late.1 = bf16[256,128]{1,0:T(8,128)(2,1)} custom-call(bf16[256,128]{1,0:T(8,128)(2,1)S(1)} %get-tuple-element.14.early_ref, s32[2,16]{1,0:T(2,128)} %offsets.3, f32[2,8,4096]{2,1,0:T(8,128)} %bitcast.14, f32[160,128]{1,0:T(8,128)} %constant.31.clone.plain_table, bf16[1792,128]{1,0:T(8,128)(2,1)} %constant.32.clone.paired_table), custom_call_target="tpu_custom_call" | custom-call | flops 10000000000 | tf_op jit(solution)/shard_map/late/pallas_call | solution.py:500
  4.8 0.0 copy-start.8
  4.8 5.4 %all-to-all-start = ((bf16[8,32,128]{2,1,0:T(8,128)(2,1)}), bf16[8,32,128]{2,1,0:T(8,128)(2,1)S(1)}, u32[]{:S(2)}, u32[]{:S(2)}) async-start(bf16[8,32,128]{2,1,0:T(8,128)(2,1)} %bitcast.5), calls=%async_computation | async-start | bytes 131072 | tf_op jit(solution)/shard_map/all_to_all | solution.py:567
  10.1 0.0 collective-permute-done.refs_1_
  10.1 0.0 copy-done.8
  10.2 0.0 copy-start.4
  10.2 0.0 copy-start.5
  10.2 0.0 copy-start.7
  10.2 0.0 copy-start.3
  10.2 0.0 copy-start.6
  10.2 0.9 %prepare.1 = (f32[256,128]{1,0:T(8,128)S(1)}, f32[256,128]{1,0:T(8,128)S(1)}, bf16[256,256]{1,0:T(8,128)(2,1)S(1)}, f32[128,128]{1,0:T(8,128)S(1)}, f32[128,128]{1,0:T(8,128)S(1)}) custom-call(s32[1,128]{1,0:T(1,128)S(1)} %get-tuple-element.13.places_ref, bf16[2,64,256]{2,1,0:T(8,128)(2,1)S(1)} %copy-done.8, f32[8,512]{1,0:T(8,128)S(1)} %get-tuple-element.15.refs_0_, ...), custom_call_target="tpu_custom_call" | custom-call | flops 20000000000 | tf_op jit(solution)/shard_map/prepare/pallas_call | solution.py:500
  11.1 3.9 %all-to-all-done = bf16[8,32,128]{2,1,0:T(8,128)(2,1)S(1)} async-done(((bf16[8,32,128]{2,1,0:T(8,128)(2,1)}), bf16[8,32,128]{2,1,0:T(8,128)(2,1)S(1)}, u32[]{:S(2)}, u32[]{:S(2)}) %all-to-all-start) | async-done | bytes 65568 | tf_op jit(solution)/shard_map/all_to_all | solution.py:567
  15.0 0.0 copy-done.4
  15.0 0.0 copy-done.5
  15.0 0.0 copy-done.7
  15.0 0.0 copy-start
  15.0 0.9 %subgrid.1 = bf16[256,128]{1,0:T(8,128)(2,1)S(1)} custom-call(bf16[256,128]{1,0:T(8,128)(2,1)S(1)} %bitcast.11, f32[256,128]{1,0:T(8,128)S(1)} %get-tuple-element.16.value_ref, f32[256,128]{1,0:T(8,128)S(1)} %get-tuple-element.17.weight_ref, f32[2,8,128]{2,1,0:T(8,128)S(1)} %copy-done.7, bf16[2,128,128]{2,1,0:T(8,128)(2,1)S(1)} %copy-done.5, ...), custom_call_target="tpu_custom_call" | custom-call | tf_op jit(solution)/shard_map/subgrid/pallas_call | solution.py:500
  15.9 0.0 copy-start.1
  15.9 0.0 copy-start.2
  15.9 8.8 %all_to_all.22 = bf16[16,16,128]{2,1,0:T(8,128)(2,1)S(1)} all-to-all(bf16[16,16,128]{2,1,0:T(8,128)(2,1)S(1)} %bitcast.12), channel_id=1, replica_groups=mesh['group'=2,'member'=8,'band'=2] {'band','member'}, dimensions={0} | all-to-all | bytes 131072 | tf_op jit(solution)/shard_map/all_to_all | solution.py:582
  24.7 0.0 copy-done.3
  24.7 0.0 copy-done.6
  24.7 0.0 copy-done
  24.7 0.0 copy-done.1
  24.7 0.0 copy-done.2
  24.7 1.7 %lines.1 = f32[4,2,4096]{2,1,0:T(2,128)} custom-call(s32[1,128]{1,0:T(1,128)S(1)} %get-tuple-element.13.places_ref, bf16[256,128]{1,0:T(8,128)(2,1)S(1)} %bitcast.10, f32[128,128]{1,0:T(8,128)S(1)} %get-tuple-element.18.straight_ref, f32[128,128]{1,0:T(8,128)S(1)} %get-tuple-element.19.crossed_ref, bf16[256,256]{1,0:T(8,128)(2,1)S(1)} %get-tuple-element.20.put_ref, ...), custom_call_target="tpu_custom_call" | custom-call | tf_op jit(solution)/shard_map/lines/pallas_call | solution.py:500
Async XLA Ops:
  0.9 9.3 %collective-permute-start = (f32[8,512]{1,0:T(8,128)S(1)}, f32[8,512]{1,0:T(8,128)S(1)}, u32[]{:S(2)}, u32[]{:S(2)}) collective-permute-start(f32[8,512]{1,0:T(8,128)S(1)} %get-tuple-element.15.refs_0_), channel_id=1, source_target_pairs={{16,0},{0,16},{17,1},{1,17},{18,2},{2,18},{19,3},{3,19},{20,4},{4,... | collective-permute-start | bytes 49160 | tf_op jit(solution)/shard_map/ppermute | solution.py:566
  4.8 5.4 %copy-start.8 = (bf16[2,64,256]{2,1,0:T(8,128)(2,1)S(1)}, bf16[2,64,256]{2,1,0:T(8,128)(2,1)}, u32[]{:S(2)}) copy-start(bf16[2,64,256]{2,1,0:T(8,128)(2,1)} %constant.24.clone.shift_ref) | copy-start | bytes 196612
  4.8 10.2 %all-to-all-start = ((bf16[8,32,128]{2,1,0:T(8,128)(2,1)}), bf16[8,32,128]{2,1,0:T(8,128)(2,1)S(1)}, u32[]{:S(2)}, u32[]{:S(2)}) async-start(bf16[8,32,128]{2,1,0:T(8,128)(2,1)} %bitcast.5), calls=%async_computation | async-start | bytes 131072 | tf_op jit(solution)/shard_map/all_to_all | solution.py:567
  10.2 4.8 %copy-start.4 = (bf16[2,128,128]{2,1,0:T(8,128)(2,1)S(1)}, bf16[2,128,128]{2,1,0:T(8,128)(2,1)}, u32[]{:S(2)}) copy-start(bf16[2,128,128]{2,1,0:T(8,128)(2,1)} %constant.30.clone.back_ref) | copy-start | bytes 196612
  10.2 4.8 %copy-start.5 = (bf16[2,128,128]{2,1,0:T(8,128)(2,1)S(1)}, bf16[2,128,128]{2,1,0:T(8,128)(2,1)}, u32[]{:S(2)}) copy-start(bf16[2,128,128]{2,1,0:T(8,128)(2,1)} %constant.29.clone.model_ref) | copy-start | bytes 196612
  10.2 4.8 %copy-start.7 = (f32[2,8,128]{2,1,0:T(8,128)S(1)}, f32[2,8,128]{2,1,0:T(8,128)}, u32[]{:S(2)}) copy-start(f32[2,8,128]{2,1,0:T(8,128)} %constant.28.clone.turn_ref) | copy-start | bytes 24580
  10.2 14.5 %copy-start.3 = (f32[2,64,128]{2,1,0:T(8,128)S(1)}, f32[2,64,128]{2,1,0:T(8,128)}, u32[]{:S(2)}) copy-start(f32[2,64,128]{2,1,0:T(8,128)} %constant.23.clone.turn_ref) | copy-start | bytes 196612
  10.2 14.5 %copy-start.6 = (f32[32,128]{1,0:T(8,128)S(1)}, f32[32,128]{1,0:T(8,128)}, u32[]{:S(2)}) copy-start(f32[32,128]{1,0:T(8,128)} %constant.22.clone.window_ref) | copy-start | bytes 49156
  15.0 9.7 %copy-start = (bf16[2,256,256]{2,1,0:T(8,128)(2,1)S(1)}, bf16[2,256,256]{2,1,0:T(8,128)(2,1)}, u32[]{:S(2)}) copy-start(bf16[2,256,256]{2,1,0:T(8,128)(2,1)} %constant.25.clone.inner_ref) | copy-start | bytes 786436
  15.9 8.9 %copy-start.1 = (bf16[2,128,128]{2,1,0:T(8,128)(2,1)S(1)}, bf16[2,128,128]{2,1,0:T(8,128)(2,1)}, u32[]{:S(2)}) copy-start(bf16[2,128,128]{2,1,0:T(8,128)(2,1)} %constant.27.clone.partial_ref) | copy-start | bytes 196612
  15.9 8.9 %copy-start.2 = (bf16[2,128,128]{2,1,0:T(8,128)(2,1)S(1)}, bf16[2,128,128]{2,1,0:T(8,128)(2,1)}, u32[]{:S(2)}) copy-start(bf16[2,128,128]{2,1,0:T(8,128)(2,1)} %constant.26.clone.outer_ref) | copy-start | bytes 196612

commit v7 on v6

--- a/solution.py
+++ b/solution.py
@@ -16,8 +16,8 @@
 SUBGRID = FACET_ROWS * CONTRIB
 LANES = 128
 HALF = LANES // 2
-LATE_FLOPS = 10**10
-PREPARE_FLOPS = 2 * 10**10
+PREDICT_FLOPS = 10**10
+PREPARE_FLOPS = 10**8
 VMEM_LIMIT = 48 * 1024 * 1024
 F32 = jnp.float32
 BF16 = jnp.bfloat16
@@ -275,33 +275,7 @@
     return 2 * lax.axis_index("group") < lax.axis_size("group")
 
 
-def early_kernel(
-    offsets, cells, values, weights, flags, strips, plain_table, paired_table,
-    out_ref, packed_ref, places_ref,
-    offsets_ref, cells_ref, values_ref, weights_ref, flags_ref, strips_ref, plain_ref, paired_ref,
-    real_ref, imag_ref, small_semaphores, semaphores, *, plain, paired, share,
-):
-    columns = strips_ref.shape[1]
-    small = start_all(
-        (offsets, cells, values, weights, flags),
-        (offsets_ref, cells_ref, values_ref, weights_ref, flags_ref),
-        small_semaphores,
-    )
-
-    def large():
-        sources, targets = (strips, plain_table, paired_table), (strips_ref, plain_ref, paired_ref)
-        return [
-            pltpu.make_async_copy(source, target, semaphores.at[i])
-            for i, (source, target) in enumerate(zip(sources, targets))
-        ]
-
-    @pl.when(in_first_half())
-    def _():
-        for copy in large():
-            copy.start()
-
-    for copy in small:
-        copy.wait()
+def pack_rows(cells_ref, values_ref, weights_ref, flags_ref, packed_ref):
     for t in range(cells_ref.shape[0]):
         rows = [
             cells_ref[t, 0:1, :].astype(F32) * SUBGRID + cells_ref[t, 1:2, :].astype(F32),
@@ -309,50 +283,53 @@
             values_ref[t],
         ]
         packed_ref[4 * t : 4 * t + 4, :] = jnp.concatenate(rows, axis=0)
-    places_ref[...] = offsets_on_lanes(offsets_ref, share)
+
+
+def pack_kernel(*refs):
+    sources, packed_ref, targets, semaphores = refs[:4], refs[4], refs[5:9], refs[9]
 
     @pl.when(in_first_half())
     def _():
-        spread = offsets_on_lanes(offsets_ref, columns)
-        predict(
-            spread, large(), strips_ref, plain_ref, paired_ref, (real_ref, imag_ref), out_ref,
-            plain, paired,
-        )
-
-
-def late_kernel(
-    early_ref, offsets, strips, plain_table, paired_table, out_ref,
-    offsets_ref, strips_ref, plain_ref, paired_ref, real_ref, imag_ref, semaphores,
-    *, plain, paired,
-):
-    @pl.when(in_first_half())
-    def _():
-        out_ref[...] = early_ref[...]
+        packed_ref[...] = jnp.zeros_like(packed_ref)
 
     @pl.when(jnp.logical_not(in_first_half()))
     def _():
-        copies = start_all(
-            (offsets, strips, plain_table, paired_table),
-            (offsets_ref, strips_ref, plain_ref, paired_ref),
-            semaphores,
-        )
-        copies[0].wait()
-        spread = offsets_on_lanes(offsets_ref, strips_ref.shape[1])
-        predict(
-            spread, copies[1:], strips_ref, plain_ref, paired_ref, (real_ref, imag_ref), out_ref,
-            plain, paired,
-        )
+        for copy in start_all(sources, targets, semaphores):
+            copy.wait()
+        pack_rows(*targets, packed_ref)
+
+
+def predict_kernel(*refs, plain, paired, share):
+    sources, outs, targets, refs = refs[:8], refs[8:11], refs[11:19], refs[19:]
+    out_ref, packed_ref, places_ref = outs
+    offsets_ref, samples_refs = targets[0], targets[1:5]
+    strips_ref, plain_ref, paired_ref = targets[5:8]
+    copies = start_all(sources, targets, refs[2])
+    copies[0].wait()
+    spread = offsets_on_lanes(offsets_ref, strips_ref.shape[1])
+    places_ref[...] = offsets_on_lanes(offsets_ref, share)
+    for copy in copies[1:5]:
+        copy.wait()
+    pack_rows(*samples_refs, packed_ref)
+    predict(
+        spread, copies[5:], strips_ref, plain_ref, paired_ref, refs[:2], out_ref, plain, paired
+    )
 
 
 def prepare_kernel(places_ref, shift_ref, *refs, columns, share, blocks):
     samples_refs, outs = refs[:-5], refs[-5:]
     value_ref, weight_ref, put_ref, straight_ref, crossed_ref = outs
     fronts, samples = samples_refs[0].shape[0] // 4, samples_refs[0].shape[1]
+    groups = (len(samples_refs) + 1) // 2
     own = lax.axis_index("group")
     depth = FACET_ROWS * columns
-    for spot in range(len(samples_refs) * fronts):
+    for spot in range(groups * fronts):
         step, t = spot // fronts, spot % fronts
-        sample = samples_refs[step][4 * t : 4 * t + 4, :]
+        rows = slice(4 * t, 4 * t + 4)
+        if step == 0:
+            sample = samples_refs[0][rows, :]
+        else:
+            sample = samples_refs[2 * step - 1][rows, :] + samples_refs[2 * step][rows, :]
         cell = sample[0:1, :].astype(jnp.int32)
         row, col = cell // SUBGRID - own * columns, cell % SUBGRID
         inside = (row >= 0) & (row < columns)
@@ -542,28 +519,30 @@
     def semaphores(count):
         return pltpu.SemaphoreType.DMA((count,))
 
-    early, packed, places = kernel_call(
-        functools.partial(early_kernel, plain=plain_places, paired=paired_places, share=share),
-        "early",
+    shape = jax.ShapeDtypeStruct((4 * fronts, cells.shape[-1]), F32)
+    first = kernel_call(
+        pack_kernel, "pack", shape, [pltpu.HBM] * 4,
+        landing(small[1:]) + [semaphores(4)], *in_hbm(small[1:]),
+    )
+    pieces, packed, places = kernel_call(
+        functools.partial(predict_kernel, plain=plain_places, paired=paired_places, share=share),
+        "predict",
         [
             jax.ShapeDtypeStruct((rows, LANES), BF16),
-            jax.ShapeDtypeStruct((4 * fronts, cells.shape[-1]), F32),
+            shape,
             jax.ShapeDtypeStruct((1, width), jnp.int32),
         ],
         [pltpu.HBM] * 8,
-        landing(small + large) + [wide(held)] * 2 + [semaphores(5), semaphores(3)],
-        *in_hbm(small + large),
-    )
-    pieces = kernel_call(
-        functools.partial(late_kernel, plain=plain_places, paired=paired_places), "late",
-        jax.ShapeDtypeStruct((rows, LANES), BF16), [pltpu.VMEM] + [pltpu.HBM] * 4,
-        landing([offsets] + large) + [wide(held)] * 2 + [semaphores(4)],
-        early, *in_hbm([offsets] + large), flops=LATE_FLOPS,
+        landing(small + large) + [wide(held)] * 2 + [semaphores(8)],
+        *in_hbm(small + large), flops=PREDICT_FLOPS,
     )
     gathered = [packed]
     for step in range(1, groups):
         moves = [((group + step) % groups, group) for group in range(groups)]
-        gathered.append(lax.ppermute(packed, "group", moves))
+        gathered += [
+            lax.ppermute(first, "group", [move for move in moves if 2 * move[0] >= groups]),
+            lax.ppermute(packed, "group", [move for move in moves if 2 * move[0] < groups]),
+        ]
     arrived = lax.all_to_all(pieces, "member", split_axis=0, concat_axis=0, tiled=True)
     blocks = length // CONTRIB
     value, weight, put, straight, crossed = kernel_call(

time: 26.8 us -> 31.8 us (1.19)
  the two profiles are of different devices: /device:TPU:16 before, /device:TPU:0 now
where the time goes in v7:
time: 31.8 us; the launch traced here: 31.5 us
  starting transfers between devices  12.1 us (38%)
  blocking collectives  11 us (35%)
  Pallas kernels  6.72 us (21%)
  waiting for transfers between devices  1.42 us (4%)
    all_to_all x1, blocking collectives, local(): lax.all_to_all(returned, ('band', 'member'), split_axis=0, concat_axis=0,...  11 us
    pallas_call x5, Pallas kernels, kernel_call(): pl.pallas_call(kernel, out_shape=out_shape, in_specs=[pl.BlockSpec(memory...  6.72 us
    ppermute x1, starting transfers between devices, local(): lax.ppermute(packed, 'group', [move for move in moves if 2 * move[0] < gr...  5.44 us
    all_to_all x1, starting transfers between devices, local(): lax.all_to_all(pieces, 'member', split_axis=0, concat_axis=0, tiled=True)  5.37 us
    ppermute x1, waiting for transfers between devices, local(): lax.ppermute(packed, 'group', [move for move in moves if 2 * move[0] < gr...  1.41 us
    ppermute x1, starting transfers between devices, local(): lax.ppermute(first, 'group', [move for move in moves if 2 * move[0] >= gr...  1.29 us
  transfers between devices with their start and end apart: 3, of which 1 were waited for; matrix products, arithmetic and copies ran while one was open for 0% of the time, Pallas kernels for 3%

profile of v7, /device:TPU:0, one launch (start us, length us, event | category | flops | bytes accessed | tf_op | source)
XLA Modules:
  0.0 31.5 jit_solution(2732247747085494743)
XLA Ops:
  0.0 3.3 %predict.1 = (bf16[256,128]{1,0:T(8,128)(2,1)}, f32[8,512]{1,0:T(8,128)S(1)}, s32[1,128]{1,0:T(1,128)S(1)}) custom-call(s32[2,16]{1,0:T(2,128)} %refs_0_.1, s32[2,2,512]{2,1,0:T(2,128)} %bitcast.13, f32[2,2,512]{2,1,0:T(2,128)} %bitcast.15, f32[2,1,512]{2,1,0:T(1,128)} %bitcast.17, s32[2,1,512]{2,1,0:T(1,128)} %bitcast.19, f32[2,8,4096]{2,1,0:T(8,128)} %bitcast.21, ...), custom_call_target="tpu_custom_call" | custom-call | flops 10000000000 | tf_op jit(solution)/shard_map/predict/pallas_call | solution.py:477
  3.3 0.0 copy-start.8
  3.3 5.4 %all-to-all-start = ((bf16[8,32,128]{2,1,0:T(8,128)(2,1)}), bf16[8,32,128]{2,1,0:T(8,128)(2,1)S(1)}, u32[]{:S(2)}, u32[]{:S(2)}) async-start(bf16[8,32,128]{2,1,0:T(8,128)(2,1)} %bitcast.5), calls=%async_computation | async-start | bytes 131072 | tf_op jit(solution)/shard_map/all_to_all | solution.py:546
  8.7 1.3 %collective-permute-start = (f32[8,512]{1,0:T(8,128)S(1)}, f32[8,512]{1,0:T(8,128)S(1)}, u32[]{:S(2)}, u32[]{:S(2)}) collective-permute-start(f32[8,512]{1,0:T(8,128)S(1)} %pack.1), channel_id=1, source_target_pairs={{16,0},{17,1},{18,2},{19,3},{20,4},{21,5},{22,6},{23,7},{24,8},{25... | collective-permute-start | bytes 49160 | tf_op jit(solution)/shard_map/ppermute | solution.py:543
  10.0 5.4 %collective-permute-start.1 = (f32[8,512]{1,0:T(8,128)S(1)}, f32[8,512]{1,0:T(8,128)S(1)}, u32[]{:S(2)}, u32[]{:S(2)}) collective-permute-start(f32[8,512]{1,0:T(8,128)S(1)} %get-tuple-element.15.refs_0_), channel_id=1, source_target_pairs={{0,16},{1,17},{2,18},{3,19},{4,20},{5,21},{6,22},{7,23},{8,24},{9,... | collective-permute-start | bytes 49160 | tf_op jit(solution)/shard_map/ppermute | solution.py:544
  15.4 0.0 collective-permute-done.refs_1_
  15.5 1.4 %collective-permute-done.1.refs_2_ = f32[8,512]{1,0:T(8,128)S(1)} collective-permute-done((f32[8,512]{1,0:T(8,128)S(1)}, f32[8,512]{1,0:T(8,128)S(1)}, u32[]{:S(2)}, u32[]{:S(2)}) %collective-permute-start.1) | collective-permute-done | bytes 16416 | tf_op jit(solution)/shard_map/ppermute | solution.py:544
  16.9 0.0 copy-done.8
  16.9 0.0 copy-start.4
  16.9 0.0 copy-start.5
  16.9 0.0 copy-start.7
  16.9 0.9 %prepare.1 = (f32[256,128]{1,0:T(8,128)S(1)}, f32[256,128]{1,0:T(8,128)S(1)}, bf16[256,256]{1,0:T(8,128)(2,1)S(1)}, f32[128,128]{1,0:T(8,128)S(1)}, f32[128,128]{1,0:T(8,128)S(1)}) custom-call(s32[1,128]{1,0:T(1,128)S(1)} %get-tuple-element.13.places_ref, bf16[2,64,256]{2,1,0:T(8,128)(2,1)S(1)} %copy-done.8, f32[8,512]{1,0:T(8,128)S(1)} %get-tuple-element.15.refs_0_, ...), custom_call_target="tpu_custom_call" | custom-call | flops 100000000 | tf_op jit(solution)/shard_map/prepare/pallas_call | solution.py:477
  17.8 0.0 all-to-all-done
  17.8 0.0 copy-done.4
  17.8 0.0 copy-done.5
  17.8 0.0 copy-done.7
  17.8 0.0 copy-start
  17.8 0.0 copy-start.3
  17.8 0.0 copy-start.6
  17.8 0.9 %subgrid.1 = bf16[256,128]{1,0:T(8,128)(2,1)S(1)} custom-call(bf16[256,128]{1,0:T(8,128)(2,1)S(1)} %bitcast.11, f32[256,128]{1,0:T(8,128)S(1)} %get-tuple-element.16.value_ref, f32[256,128]{1,0:T(8,128)S(1)} %get-tuple-element.17.weight_ref, f32[2,8,128]{2,1,0:T(8,128)S(1)} %copy-done.7, bf16[2,128,128]{2,1,0:T(8,128)(2,1)S(1)} %copy-done.5, ...), custom_call_target="tpu_custom_call" | custom-call | tf_op jit(solution)/shard_map/subgrid/pallas_call | solution.py:477
  18.7 0.0 copy-start.1
  18.7 0.0 copy-start.2
  18.7 11.0 %all_to_all.22 = bf16[16,16,128]{2,1,0:T(8,128)(2,1)S(1)} all-to-all(bf16[16,16,128]{2,1,0:T(8,128)(2,1)S(1)} %bitcast.12), channel_id=1, replica_groups=mesh['group'=2,'member'=8,'band'=2] {'band','member'}, dimensions={0} | all-to-all | bytes 131072 | tf_op jit(solution)/shard_map/all_to_all | solution.py:561
  29.7 0.0 copy-done
  29.7 0.0 copy-done.3
  29.7 0.0 copy-done.6
  29.8 0.0 copy-done.1
  29.8 0.0 copy-done.2
  29.8 1.7 %lines.1 = f32[4,2,4096]{2,1,0:T(2,128)} custom-call(s32[1,128]{1,0:T(1,128)S(1)} %get-tuple-element.13.places_ref, bf16[256,128]{1,0:T(8,128)(2,1)S(1)} %bitcast.10, f32[128,128]{1,0:T(8,128)S(1)} %get-tuple-element.18.straight_ref, f32[128,128]{1,0:T(8,128)S(1)} %get-tuple-element.19.crossed_ref, bf16[256,256]{1,0:T(8,128)(2,1)S(1)} %get-tuple-element.20.put_ref, ...), custom_call_target="tpu_custom_call" | custom-call | tf_op jit(solution)/shard_map/lines/pallas_call | solution.py:477
  (1 shorter events, 0.0 us)
Async XLA Ops:
  3.3 13.6 %copy-start.8 = (bf16[2,64,256]{2,1,0:T(8,128)(2,1)S(1)}, bf16[2,64,256]{2,1,0:T(8,128)(2,1)}, u32[]{:S(2)}) copy-start(bf16[2,64,256]{2,1,0:T(8,128)(2,1)} %constant.24.clone.shift_ref) | copy-start | bytes 196612
  3.3 14.5 %all-to-all-start = ((bf16[8,32,128]{2,1,0:T(8,128)(2,1)}), bf16[8,32,128]{2,1,0:T(8,128)(2,1)S(1)}, u32[]{:S(2)}, u32[]{:S(2)}) async-start(bf16[8,32,128]{2,1,0:T(8,128)(2,1)} %bitcast.5), calls=%async_computation | async-start | bytes 131072 | tf_op jit(solution)/shard_map/all_to_all | solution.py:546
  8.7 6.8 %collective-permute-start = (f32[8,512]{1,0:T(8,128)S(1)}, f32[8,512]{1,0:T(8,128)S(1)}, u32[]{:S(2)}, u32[]{:S(2)}) collective-permute-start(f32[8,512]{1,0:T(8,128)S(1)} %pack.1), channel_id=1, source_target_pairs={{16,0},{17,1},{18,2},{19,3},{20,4},{21,5},{22,6},{23,7},{24,8},{25... | collective-permute-start | bytes 49160 | tf_op jit(solution)/shard_map/ppermute | solution.py:543
  10.0 6.9 %collective-permute-start.1 = (f32[8,512]{1,0:T(8,128)S(1)}, f32[8,512]{1,0:T(8,128)S(1)}, u32[]{:S(2)}, u32[]{:S(2)}) collective-permute-start(f32[8,512]{1,0:T(8,128)S(1)} %get-tuple-element.15.refs_0_), channel_id=1, source_target_pairs={{0,16},{1,17},{2,18},{3,19},{4,20},{5,21},{6,22},{7,23},{8,24},{9,... | collective-permute-start | bytes 49160 | tf_op jit(solution)/shard_map/ppermute | solution.py:544
  16.9 0.9 %copy-start.4 = (bf16[2,128,128]{2,1,0:T(8,128)(2,1)S(1)}, bf16[2,128,128]{2,1,0:T(8,128)(2,1)}, u32[]{:S(2)}) copy-start(bf16[2,128,128]{2,1,0:T(8,128)(2,1)} %constant.30.clone.back_ref) | copy-start | bytes 196612
  16.9 0.9 %copy-start.5 = (bf16[2,128,128]{2,1,0:T(8,128)(2,1)S(1)}, bf16[2,128,128]{2,1,0:T(8,128)(2,1)}, u32[]{:S(2)}) copy-start(bf16[2,128,128]{2,1,0:T(8,128)(2,1)} %constant.29.clone.model_ref) | copy-start | bytes 196612
  16.9 0.9 %copy-start.7 = (f32[2,8,128]{2,1,0:T(8,128)S(1)}, f32[2,8,128]{2,1,0:T(8,128)}, u32[]{:S(2)}) copy-start(f32[2,8,128]{2,1,0:T(8,128)} %constant.28.clone.turn_ref) | copy-start | bytes 24580
  17.8 11.9 %copy-start = (bf16[2,256,256]{2,1,0:T(8,128)(2,1)S(1)}, bf16[2,256,256]{2,1,0:T(8,128)(2,1)}, u32[]{:S(2)}) copy-start(bf16[2,256,256]{2,1,0:T(8,128)(2,1)} %constant.25.clone.inner_ref) | copy-start | bytes 786436
  17.8 11.9 %copy-start.3 = (f32[2,64,128]{2,1,0:T(8,128)S(1)}, f32[2,64,128]{2,1,0:T(8,128)}, u32[]{:S(2)}) copy-start(f32[2,64,128]{2,1,0:T(8,128)} %constant.23.clone.turn_ref) | copy-start | bytes 196612
  17.8 11.9 %copy-start.6 = (f32[32,128]{1,0:T(8,128)S(1)}, f32[32,128]{1,0:T(8,128)}, u32[]{:S(2)}) copy-start(f32[32,128]{1,0:T(8,128)} %constant.22.clone.window_ref) | copy-start | bytes 49156
  18.7 11.1 %copy-start.1 = (bf16[2,128,128]{2,1,0:T(8,128)(2,1)S(1)}, bf16[2,128,128]{2,1,0:T(8,128)(2,1)}, u32[]{:S(2)}) copy-start(bf16[2,128,128]{2,1,0:T(8,128)(2,1)} %constant.27.clone.partial_ref) | copy-start | bytes 196612
  18.7 11.1 %copy-start.2 = (bf16[2,128,128]{2,1,0:T(8,128)(2,1)S(1)}, bf16[2,128,128]{2,1,0:T(8,128)(2,1)}, u32[]{:S(2)}) copy-start(bf16[2,128,128]{2,1,0:T(8,128)(2,1)} %constant.26.clone.outer_ref) | copy-start | bytes 196612

commit v8 on v6

--- a/solution.py
+++ b/solution.py
@@ -124,6 +124,14 @@
     return lax.broadcasted_iota(jnp.int32, shape, dimension)
 
 
+def over(values, size):
+    return lax.shift_right_logical(values, jnp.full_like(values, size.bit_length() - 1))
+
+
+def within(values, size):
+    return values & (size - 1)
+
+
 def swap_halves(values):
     return pltpu.roll(values, HALF, 1)
 
@@ -143,7 +151,7 @@
         group = own + step
         begins.append(jnp.where(group >= groups, group - groups, group) * FACET_ROWS)
     spread = iota((1, fronts * owners * columns), 1)
-    place_of = spread // columns
+    place_of = over(spread, columns)
     for place in range(fronts * owners):
         t, step, member = place % fronts, place // fronts % groups, place // (fronts * groups)
         spread = jnp.where(place_of == place, offsets_ref[t, begins[step] + member], spread)
@@ -209,11 +217,11 @@
     pairs = columns // 2
     blocks = length // CONTRIB
     width = spread.shape[1]
-    first_block, residue = spread // CONTRIB, spread % CONTRIB
-    base = iota(spread.shape, 1) % columns * blocks
+    first_block, residue = over(spread, CONTRIB), within(spread, CONTRIB)
+    base = within(iota(spread.shape, 1), columns) * blocks
     shape = (columns * blocks, width)
     pick_inside = one_hot(shape, base + first_block)
-    pick_beyond = one_hot(shape, base + (first_block + 1) % blocks)
+    pick_beyond = one_hot(shape, base + within(first_block + 1, blocks))
     for copy in copies:
         copy.wait()
 
@@ -264,7 +272,7 @@
     high, low = split(spectrum)
     inside = dot(high, pick_inside) + dot(low, pick_inside)
     beyond = dot(high, pick_beyond) + dot(low, pick_beyond)
-    kappa = iota((2 * CONTRIB, width), 0) % CONTRIB
+    kappa = within(iota((2 * CONTRIB, width), 0), CONTRIB)
     cutout = jnp.where(kappa >= residue, inside, beyond)
     piece = times_table(cutout.T, pair_at("piece"))
     straight, crossed = shift_rows(residue, pair_at("shift"))
@@ -354,11 +362,11 @@
         step, t = spot // fronts, spot % fronts
         sample = samples_refs[step][4 * t : 4 * t + 4, :]
         cell = sample[0:1, :].astype(jnp.int32)
-        row, col = cell // SUBGRID - own * columns, cell % SUBGRID
+        row, col = over(cell, SUBGRID) - own * columns, within(cell, SUBGRID)
         inside = (row >= 0) & (row < columns)
-        target = jnp.where(inside, col % FACET_ROWS * columns + row, -1)
+        target = jnp.where(inside, within(col, FACET_ROWS) * columns + row, -1)
         pick = one_hot((depth, samples), target)
-        mask = iota((HALF, samples), 0) == col // FACET_ROWS
+        mask = iota((HALF, samples), 0) == over(col, FACET_ROWS)
         factor = sample[1:2, :]
         highs, lows = [], []
         for term in (factor * sample[2:3, :], factor * sample[3:4, :], factor):
@@ -373,10 +381,10 @@
         value_ref[rows, :] = grid[:, :LANES]
         weight_ref[rows, :] = grid[:, LANES:]
     spread = places_ref[...]
-    first_block, residue = spread // CONTRIB, spread % CONTRIB
+    first_block, residue = over(spread, CONTRIB), within(spread, CONTRIB)
     straight_ref[...], crossed_ref[...] = shift_rows(residue, shift_ref)
-    base = iota(spread.shape, 1) % share * blocks
-    targets = jnp.concatenate([base + first_block, base + (first_block + 1) % blocks], axis=1)
+    base = within(iota(spread.shape, 1), share) * blocks
+    targets = jnp.concatenate([base + first_block, base + within(first_block + 1, blocks)], axis=1)
     put_ref[...] = one_hot(put_ref.shape, targets)
 
 
@@ -438,8 +446,8 @@
         summed += pieces_ref[b * width : (b + 1) * width, :].astype(F32)
     summed = summed * straight_ref[...] - swap_halves(summed) * crossed_ref[...]
     residues = table_times(partial_ref, summed, ((1,), (1,)))
-    kappa = iota((2 * CONTRIB, width), 0) % CONTRIB
-    inside = kappa >= places_ref[...] % CONTRIB
+    kappa = within(iota((2 * CONTRIB, width), 0), CONTRIB)
+    inside = kappa >= within(places_ref[...], CONTRIB)
     both = jnp.concatenate(
         [jnp.where(inside, residues, 0.0), jnp.where(inside, 0.0, residues)], axis=1
     )
@@ -556,7 +564,7 @@
     )
     pieces = kernel_call(
         functools.partial(late_kernel, plain=plain_places, paired=paired_places), "late",
-        jax.ShapeDtypeStruct((rows, LANES), BF16), [pltpu.VMEM] + [pltpu.HBM] * 4,
+        pltpu.VMEM((rows, LANES), BF16), [pltpu.VMEM] + [pltpu.HBM] * 4,
         landing([offsets] + large) + [wide(held)] * 2 + [semaphores(4)],
         early, *in_hbm([offsets] + large), flops=LATE_FLOPS,
     )

time: 26.8 us -> 26.8 us (level)
  no operation moved by 1% of the time
where the time goes in v8:
time: 26.8 us; the launch traced here: 26.4 us
  blocking collectives  8.83 us (33%)
  Pallas kernels  7.39 us (28%)
  starting transfers between devices  6.11 us (23%)
  waiting for transfers between devices  3.92 us (15%)
    all_to_all x1, blocking collectives, local(): lax.all_to_all(returned, ('band', 'member'), split_axis=0, concat_axis=0,...  8.83 us
    pallas_call x5, Pallas kernels, kernel_call(): pl.pallas_call(kernel, out_shape=out_shape, in_specs=[pl.BlockSpec(memory...  7.39 us
    all_to_all x1, starting transfers between devices, local(): lax.all_to_all(pieces, 'member', split_axis=0, concat_axis=0, tiled=True)  5.37 us
    all_to_all x1, waiting for transfers between devices, local(): lax.all_to_all(pieces, 'member', split_axis=0, concat_axis=0, tiled=True)  3.92 us
    ppermute x1, starting transfers between devices, local(): gathered.append(lax.ppermute(packed, 'group', moves))  0.74 us
  transfers between devices with their start and end apart: 2, of which 1 were waited for; matrix products, arithmetic and copies ran while one was open for 0% of the time, Pallas kernels for 15%

profile of v8, /device:TPU:16, one launch (start us, length us, event | category | flops | bytes accessed | tf_op | source)
XLA Modules:
  0.0 26.4 jit_solution(18048531299618519750)
XLA Ops:
  0.0 0.8 %early.1 = (bf16[256,128]{1,0:T(8,128)(2,1)S(1)}, f32[8,512]{1,0:T(8,128)S(1)}, s32[1,128]{1,0:T(1,128)S(1)}) custom-call(s32[2,16]{1,0:T(2,128)} %offsets.3, s32[2,2,512]{2,1,0:T(2,128)} %bitcast.15, f32[2,2,512]{2,1,0:T(2,128)} %bitcast.16, f32[2,1,512]{2,1,0:T(1,128)} %bitcast.17, s32[2,1,512]{2,1,0:T(1,128)} %bitcast.18, f32[2,8,4096]{2,1,0:T(8,128)} %bitcast.13, ...), custom_call_target="tpu_custom_call" | custom-call | tf_op jit(solution)/shard_map/early/pallas_call | solution.py:508
  0.9 0.7 %collective-permute-start = (f32[8,512]{1,0:T(8,128)S(1)}, f32[8,512]{1,0:T(8,128)S(1)}, u32[]{:S(2)}, u32[]{:S(2)}) collective-permute-start(f32[8,512]{1,0:T(8,128)S(1)} %get-tuple-element.15.refs_0_), channel_id=1, source_target_pairs={{16,0},{0,16},{17,1},{1,17},{18,2},{2,18},{19,3},{3,19},{20,4},{4,... | collective-permute-start | bytes 49160 | tf_op jit(solution)/shard_map/ppermute | solution.py:574
  1.6 3.2 %late.1 = bf16[256,128]{1,0:T(8,128)(2,1)} custom-call(bf16[256,128]{1,0:T(8,128)(2,1)S(1)} %get-tuple-element.14.early_ref, s32[2,16]{1,0:T(2,128)} %offsets.3, f32[2,8,4096]{2,1,0:T(8,128)} %bitcast.14, f32[160,128]{1,0:T(8,128)} %constant.31.clone.plain_table, bf16[1792,128]{1,0:T(8,128)(2,1)} %constant.32.clone.paired_table), custom_call_target="tpu_custom_call" | custom-call | flops 10000000000 | tf_op jit(solution)/shard_map/late/pallas_call | solution.py:508
  4.8 0.0 copy-start.8
  4.8 5.4 %all-to-all-start = ((bf16[8,32,128]{2,1,0:T(8,128)(2,1)}), bf16[8,32,128]{2,1,0:T(8,128)(2,1)S(1)}, u32[]{:S(2)}, u32[]{:S(2)}) async-start(bf16[8,32,128]{2,1,0:T(8,128)(2,1)} %bitcast.5), calls=%async_computation | async-start | bytes 131072 | tf_op jit(solution)/shard_map/all_to_all | solution.py:575
  10.1 0.0 collective-permute-done.refs_1_
  10.1 0.0 copy-done.8
  10.2 0.0 copy-start.4
  10.2 0.0 copy-start.5
  10.2 0.0 copy-start.7
  10.2 0.0 copy-start.3
  10.2 0.0 copy-start.6
  10.2 0.8 %prepare.1 = (f32[256,128]{1,0:T(8,128)S(1)}, f32[256,128]{1,0:T(8,128)S(1)}, bf16[256,256]{1,0:T(8,128)(2,1)S(1)}, f32[128,128]{1,0:T(8,128)S(1)}, f32[128,128]{1,0:T(8,128)S(1)}) custom-call(s32[1,128]{1,0:T(1,128)S(1)} %get-tuple-element.13.places_ref, bf16[2,64,256]{2,1,0:T(8,128)(2,1)S(1)} %copy-done.8, f32[8,512]{1,0:T(8,128)S(1)} %get-tuple-element.15.refs_0_, ...), custom_call_target="tpu_custom_call" | custom-call | flops 20000000000 | tf_op jit(solution)/shard_map/prepare/pallas_call | solution.py:508
  11.1 3.9 %all-to-all-done = bf16[8,32,128]{2,1,0:T(8,128)(2,1)S(1)} async-done(((bf16[8,32,128]{2,1,0:T(8,128)(2,1)}), bf16[8,32,128]{2,1,0:T(8,128)(2,1)S(1)}, u32[]{:S(2)}, u32[]{:S(2)}) %all-to-all-start) | async-done | bytes 65568 | tf_op jit(solution)/shard_map/all_to_all | solution.py:575
  15.0 0.0 copy-done.4
  15.0 0.0 copy-done.5
  15.0 0.0 copy-done.7
  15.0 0.0 copy-start
  15.0 0.9 %subgrid.1 = bf16[256,128]{1,0:T(8,128)(2,1)S(1)} custom-call(bf16[256,128]{1,0:T(8,128)(2,1)S(1)} %bitcast.11, f32[256,128]{1,0:T(8,128)S(1)} %get-tuple-element.16.value_ref, f32[256,128]{1,0:T(8,128)S(1)} %get-tuple-element.17.weight_ref, f32[2,8,128]{2,1,0:T(8,128)S(1)} %copy-done.7, bf16[2,128,128]{2,1,0:T(8,128)(2,1)S(1)} %copy-done.5, ...), custom_call_target="tpu_custom_call" | custom-call | tf_op jit(solution)/shard_map/subgrid/pallas_call | solution.py:508
  15.9 0.0 copy-start.1
  15.9 0.0 copy-start.2
  15.9 8.8 %all_to_all.22 = bf16[16,16,128]{2,1,0:T(8,128)(2,1)S(1)} all-to-all(bf16[16,16,128]{2,1,0:T(8,128)(2,1)S(1)} %bitcast.12), channel_id=1, replica_groups=mesh['group'=2,'member'=8,'band'=2] {'band','member'}, dimensions={0} | all-to-all | bytes 131072 | tf_op jit(solution)/shard_map/all_to_all | solution.py:590
  24.7 0.0 copy-done.3
  24.7 0.0 copy-done.6
  24.7 0.0 copy-done
  24.7 0.0 copy-done.1
  24.7 0.0 copy-done.2
  24.7 1.7 %lines.1 = f32[4,2,4096]{2,1,0:T(2,128)} custom-call(s32[1,128]{1,0:T(1,128)S(1)} %get-tuple-element.13.places_ref, bf16[256,128]{1,0:T(8,128)(2,1)S(1)} %bitcast.10, f32[128,128]{1,0:T(8,128)S(1)} %get-tuple-element.18.straight_ref, f32[128,128]{1,0:T(8,128)S(1)} %get-tuple-element.19.crossed_ref, bf16[256,256]{1,0:T(8,128)(2,1)S(1)} %get-tuple-element.20.put_ref, ...), custom_call_target="tpu_custom_call" | custom-call | tf_op jit(solution)/shard_map/lines/pallas_call | solution.py:508
Async XLA Ops:
  0.9 9.3 %collective-permute-start = (f32[8,512]{1,0:T(8,128)S(1)}, f32[8,512]{1,0:T(8,128)S(1)}, u32[]{:S(2)}, u32[]{:S(2)}) collective-permute-start(f32[8,512]{1,0:T(8,128)S(1)} %get-tuple-element.15.refs_0_), channel_id=1, source_target_pairs={{16,0},{0,16},{17,1},{1,17},{18,2},{2,18},{19,3},{3,19},{20,4},{4,... | collective-permute-start | bytes 49160 | tf_op jit(solution)/shard_map/ppermute | solution.py:574
  4.8 5.4 %copy-start.8 = (bf16[2,64,256]{2,1,0:T(8,128)(2,1)S(1)}, bf16[2,64,256]{2,1,0:T(8,128)(2,1)}, u32[]{:S(2)}) copy-start(bf16[2,64,256]{2,1,0:T(8,128)(2,1)} %constant.24.clone.shift_ref) | copy-start | bytes 196612
  4.8 10.2 %all-to-all-start = ((bf16[8,32,128]{2,1,0:T(8,128)(2,1)}), bf16[8,32,128]{2,1,0:T(8,128)(2,1)S(1)}, u32[]{:S(2)}, u32[]{:S(2)}) async-start(bf16[8,32,128]{2,1,0:T(8,128)(2,1)} %bitcast.5), calls=%async_computation | async-start | bytes 131072 | tf_op jit(solution)/shard_map/all_to_all | solution.py:575
  10.2 4.8 %copy-start.4 = (bf16[2,128,128]{2,1,0:T(8,128)(2,1)S(1)}, bf16[2,128,128]{2,1,0:T(8,128)(2,1)}, u32[]{:S(2)}) copy-start(bf16[2,128,128]{2,1,0:T(8,128)(2,1)} %constant.30.clone.back_ref) | copy-start | bytes 196612
  10.2 4.8 %copy-start.5 = (bf16[2,128,128]{2,1,0:T(8,128)(2,1)S(1)}, bf16[2,128,128]{2,1,0:T(8,128)(2,1)}, u32[]{:S(2)}) copy-start(bf16[2,128,128]{2,1,0:T(8,128)(2,1)} %constant.29.clone.model_ref) | copy-start | bytes 196612
  10.2 4.8 %copy-start.7 = (f32[2,8,128]{2,1,0:T(8,128)S(1)}, f32[2,8,128]{2,1,0:T(8,128)}, u32[]{:S(2)}) copy-start(f32[2,8,128]{2,1,0:T(8,128)} %constant.28.clone.turn_ref) | copy-start | bytes 24580
  10.2 14.5 %copy-start.3 = (f32[2,64,128]{2,1,0:T(8,128)S(1)}, f32[2,64,128]{2,1,0:T(8,128)}, u32[]{:S(2)}) copy-start(f32[2,64,128]{2,1,0:T(8,128)} %constant.23.clone.turn_ref) | copy-start | bytes 196612
  10.2 14.5 %copy-start.6 = (f32[32,128]{1,0:T(8,128)S(1)}, f32[32,128]{1,0:T(8,128)}, u32[]{:S(2)}) copy-start(f32[32,128]{1,0:T(8,128)} %constant.22.clone.window_ref) | copy-start | bytes 49156
  15.0 9.7 %copy-start = (bf16[2,256,256]{2,1,0:T(8,128)(2,1)S(1)}, bf16[2,256,256]{2,1,0:T(8,128)(2,1)}, u32[]{:S(2)}) copy-start(bf16[2,256,256]{2,1,0:T(8,128)(2,1)} %constant.25.clone.inner_ref) | copy-start | bytes 786436
  15.9 8.9 %copy-start.1 = (bf16[2,128,128]{2,1,0:T(8,128)(2,1)S(1)}, bf16[2,128,128]{2,1,0:T(8,128)(2,1)}, u32[]{:S(2)}) copy-start(bf16[2,128,128]{2,1,0:T(8,128)(2,1)} %constant.27.clone.partial_ref) | copy-start | bytes 196612
  15.9 8.9 %copy-start.2 = (bf16[2,128,128]{2,1,0:T(8,128)(2,1)S(1)}, bf16[2,128,128]{2,1,0:T(8,128)(2,1)}, u32[]{:S(2)}) copy-start(bf16[2,128,128]{2,1,0:T(8,128)(2,1)} %constant.26.clone.outer_ref) | copy-start | bytes 196612

commit v9 on v8

--- a/solution.py
+++ b/solution.py
@@ -14,6 +14,8 @@
 CONTRIB = 64
 FACET_ROWS = 8
 SUBGRID = FACET_ROWS * CONTRIB
+SEND_ORDER = tuple(reversed(range(FACET_ROWS)))
+RETURN_ORDER = tuple(range(FACET_ROWS))
 LANES = 128
 HALF = LANES // 2
 LATE_FLOPS = 10**10
@@ -142,7 +144,7 @@
     return parts[0] if blocks == 1 else jnp.concatenate(parts, axis=1)
 
 
-def offsets_on_lanes(offsets_ref, columns):
+def offsets_on_lanes(offsets_ref, columns, order):
     fronts, owners = offsets_ref.shape
     groups = owners // FACET_ROWS
     own = lax.axis_index("group")
@@ -153,7 +155,8 @@
     spread = iota((1, fronts * owners * columns), 1)
     place_of = over(spread, columns)
     for place in range(fronts * owners):
-        t, step, member = place % fronts, place // fronts % groups, place // (fronts * groups)
+        t, step, spot = place % fronts, place // fronts % groups, place // (fronts * groups)
+        member = order[spot]
         spread = jnp.where(place_of == place, offsets_ref[t, begins[step] + member], spread)
     return spread
 
@@ -317,11 +320,11 @@
             values_ref[t],
         ]
         packed_ref[4 * t : 4 * t + 4, :] = jnp.concatenate(rows, axis=0)
-    places_ref[...] = offsets_on_lanes(offsets_ref, share)
+    places_ref[...] = offsets_on_lanes(offsets_ref, share, RETURN_ORDER)
 
     @pl.when(in_first_half())
     def _():
-        spread = offsets_on_lanes(offsets_ref, columns)
+        spread = offsets_on_lanes(offsets_ref, columns, SEND_ORDER)
         predict(
             spread, large(), strips_ref, plain_ref, paired_ref, (real_ref, imag_ref), out_ref,
             plain, paired,
@@ -345,7 +348,7 @@
             semaphores,
         )
         copies[0].wait()
-        spread = offsets_on_lanes(offsets_ref, strips_ref.shape[1])
+        spread = offsets_on_lanes(offsets_ref, strips_ref.shape[1], SEND_ORDER)
         predict(
             spread, copies[1:], strips_ref, plain_ref, paired_ref, (real_ref, imag_ref), out_ref,
             plain, paired,
@@ -398,7 +401,11 @@
     share = columns // bands
     pieces = pieces_ref[...].astype(F32)
     sky = turned_eighths(
-        [pieces[i * rows : (i + 1) * rows, :] for i in range(FACET_ROWS)], -1.0
+        [
+            pieces[spot * rows : (spot + 1) * rows, :]
+            for spot in (SEND_ORDER.index(i) for i in range(FACET_ROWS))
+        ],
+        -1.0,
     )
     sky = [
         value * turn_ref[0, i : i + 1, :] + swap_halves(value) * turn_ref[1, i : i + 1, :]
@@ -427,7 +434,8 @@
         for spot in spots:
             for b in range(bands):
                 source = spot * columns + b * share
-                target = ((b * FACET_ROWS + i) * len(spots) + spot) * share
+                place = b * FACET_ROWS + RETURN_ORDER.index(i)
+                target = (place * len(spots) + spot) * share
                 held_ref[target : target + share, :] = lines[i][source : source + share, :]
     out_ref[...] = held_ref[...].astype(BF16)
 
@@ -564,7 +572,7 @@
     )
     pieces = kernel_call(
         functools.partial(late_kernel, plain=plain_places, paired=paired_places), "late",
-        pltpu.VMEM((rows, LANES), BF16), [pltpu.VMEM] + [pltpu.HBM] * 4,
+        jax.ShapeDtypeStruct((rows, LANES), BF16), [pltpu.VMEM] + [pltpu.HBM] * 4,
         landing([offsets] + large) + [wide(held)] * 2 + [semaphores(4)],
         early, *in_hbm([offsets] + large), flops=LATE_FLOPS,
     )
@@ -572,7 +580,10 @@
     for step in range(1, groups):
         moves = [((group + step) % groups, group) for group in range(groups)]
         gathered.append(lax.ppermute(packed, "group", moves))
-    arrived = lax.all_to_all(pieces, "member", split_axis=0, concat_axis=0, tiled=True)
+    arrived = lax.all_to_all(
+        pieces, "member", split_axis=0, concat_axis=0, tiled=True,
+        axis_index_groups=[list(SEND_ORDER)],
+    )
     blocks = length // CONTRIB
     value, weight, put, straight, crossed = kernel_call(
         functools.partial(prepare_kernel, columns=columns, share=share, blocks=blocks), "prepare",
@@ -588,7 +599,10 @@
         arrived, value, weight, made["grid_turn"], made["model"], made["back"],
     )
     delivered = lax.all_to_all(
-        returned, ("band", "member"), split_axis=0, concat_axis=0, tiled=True
+        returned, ("band", "member"), split_axis=0, concat_axis=0, tiled=True,
+        axis_index_groups=[
+            [b * FACET_ROWS + member for b in range(bands) for member in RETURN_ORDER]
+        ],
     )
     lines = kernel_call(
         functools.partial(return_kernel, bands=bands), "lines",

time: 26.8 us -> 27.2 us (1.015)
  waiting for transfers between devices: 3.92 us -> 1.78 us
  blocking collectives: 8.83 us -> 10.2 us
  starting transfers between devices: 6.11 us -> 7.32 us
    all_to_all x1, waiting for transfers between devices: 3.92 us -> 1.77 us  [local(): lax.all_to_all(pieces, 'member', split_axis=0, concat_axis=0, tiled=True,...]
    all_to_all x1, blocking collectives: 8.83 us -> 10.2 us  [local(): lax.all_to_all(returned, ('band', 'member'), split_axis=0, concat_axis=0,...]
    all_to_all x1, starting transfers between devices: 5.37 us -> 6.59 us  [local(): lax.all_to_all(pieces, 'member', split_axis=0, concat_axis=0, tiled=True,...]
where the time goes in v9:
time: 27.2 us; the launch traced here: 26.9 us
  blocking collectives  10.2 us (38%)
  Pallas kernels  7.4 us (27%)
  starting transfers between devices  7.32 us (27%)
  waiting for transfers between devices  1.78 us (7%)
    all_to_all x1, blocking collectives, local(): lax.all_to_all(returned, ('band', 'member'), split_axis=0, concat_axis=0,...  10.2 us
    pallas_call x5, Pallas kernels, kernel_call(): pl.pallas_call(kernel, out_shape=out_shape, in_specs=[pl.BlockSpec(memory...  7.4 us
    all_to_all x1, starting transfers between devices, local(): lax.all_to_all(pieces, 'member', split_axis=0, concat_axis=0, tiled=True,...  6.59 us
    all_to_all x1, waiting for transfers between devices, local(): lax.all_to_all(pieces, 'member', split_axis=0, concat_axis=0, tiled=True,...  1.77 us
    ppermute x1, starting transfers between devices, local(): gathered.append(lax.ppermute(packed, 'group', moves))  0.73 us
  transfers between devices with their start and end apart: 2, of which 1 were waited for; matrix products, arithmetic and copies ran while one was open for 0% of the time, Pallas kernels for 15%

profile of v9, /device:TPU:16, one launch (start us, length us, event | category | flops | bytes accessed | tf_op | source)
XLA Modules:
  0.0 26.9 jit_solution(16607148191384778857)
XLA Ops:
  0.0 0.8 %early.1 = (bf16[256,128]{1,0:T(8,128)(2,1)S(1)}, f32[8,512]{1,0:T(8,128)S(1)}, s32[1,128]{1,0:T(1,128)S(1)}) custom-call(s32[2,16]{1,0:T(2,128)} %offsets.3, s32[2,2,512]{2,1,0:T(2,128)} %bitcast.15, f32[2,2,512]{2,1,0:T(2,128)} %bitcast.16, f32[2,1,512]{2,1,0:T(1,128)} %bitcast.17, s32[2,1,512]{2,1,0:T(1,128)} %bitcast.18, f32[2,8,4096]{2,1,0:T(8,128)} %bitcast.13, ...), custom_call_target="tpu_custom_call" | custom-call | tf_op jit(solution)/shard_map/early/pallas_call | solution.py:516
  0.9 0.7 %collective-permute-start = (f32[8,512]{1,0:T(8,128)S(1)}, f32[8,512]{1,0:T(8,128)S(1)}, u32[]{:S(2)}, u32[]{:S(2)}) collective-permute-start(f32[8,512]{1,0:T(8,128)S(1)} %get-tuple-element.15.refs_0_), channel_id=1, source_target_pairs={{16,0},{0,16},{17,1},{1,17},{18,2},{2,18},{19,3},{3,19},{20,4},{4,... | collective-permute-start | bytes 49160 | tf_op jit(solution)/shard_map/ppermute | solution.py:582
  1.6 3.2 %late.1 = bf16[256,128]{1,0:T(8,128)(2,1)} custom-call(bf16[256,128]{1,0:T(8,128)(2,1)S(1)} %get-tuple-element.14.early_ref, s32[2,16]{1,0:T(2,128)} %offsets.3, f32[2,8,4096]{2,1,0:T(8,128)} %bitcast.14, f32[160,128]{1,0:T(8,128)} %constant.31.clone.plain_table, bf16[1792,128]{1,0:T(8,128)(2,1)} %constant.32.clone.paired_table), custom_call_target="tpu_custom_call" | custom-call | flops 10000000000 | tf_op jit(solution)/shard_map/late/pallas_call | solution.py:516
  4.8 0.0 copy-start.8
  4.8 6.6 %all-to-all-start = ((bf16[8,32,128]{2,1,0:T(8,128)(2,1)}), bf16[8,32,128]{2,1,0:T(8,128)(2,1)S(1)}, u32[]{:S(2)}, u32[]{:S(2)}) async-start(bf16[8,32,128]{2,1,0:T(8,128)(2,1)} %bitcast.5), calls=%async_computation | async-start | bytes 131072 | tf_op jit(solution)/shard_map/all_to_all | solution.py:583
  11.4 0.0 collective-permute-done.refs_1_
  11.4 0.0 copy-done.8
  11.4 0.0 copy-start.4
  11.4 0.0 copy-start.5
  11.4 0.0 copy-start.7
  11.4 0.0 copy-start.3
  11.4 0.0 copy-start.6
  11.4 0.8 %prepare.1 = (f32[256,128]{1,0:T(8,128)S(1)}, f32[256,128]{1,0:T(8,128)S(1)}, bf16[256,256]{1,0:T(8,128)(2,1)S(1)}, f32[128,128]{1,0:T(8,128)S(1)}, f32[128,128]{1,0:T(8,128)S(1)}) custom-call(s32[1,128]{1,0:T(1,128)S(1)} %get-tuple-element.13.places_ref, bf16[2,64,256]{2,1,0:T(8,128)(2,1)S(1)} %copy-done.8, f32[8,512]{1,0:T(8,128)S(1)} %get-tuple-element.15.refs_0_, ...), custom_call_target="tpu_custom_call" | custom-call | flops 20000000000 | tf_op jit(solution)/shard_map/prepare/pallas_call | solution.py:516
  12.3 1.8 %all-to-all-done = bf16[8,32,128]{2,1,0:T(8,128)(2,1)S(1)} async-done(((bf16[8,32,128]{2,1,0:T(8,128)(2,1)}), bf16[8,32,128]{2,1,0:T(8,128)(2,1)S(1)}, u32[]{:S(2)}, u32[]{:S(2)}) %all-to-all-start) | async-done | bytes 65568 | tf_op jit(solution)/shard_map/all_to_all | solution.py:583
  14.0 0.0 copy-done.4
  14.0 0.0 copy-done.5
  14.1 0.0 copy-done.7
  14.1 0.0 copy-start
  14.1 0.9 %subgrid.1 = bf16[256,128]{1,0:T(8,128)(2,1)S(1)} custom-call(bf16[256,128]{1,0:T(8,128)(2,1)S(1)} %bitcast.11, f32[256,128]{1,0:T(8,128)S(1)} %get-tuple-element.16.value_ref, f32[256,128]{1,0:T(8,128)S(1)} %get-tuple-element.17.weight_ref, f32[2,8,128]{2,1,0:T(8,128)S(1)} %copy-done.7, bf16[2,128,128]{2,1,0:T(8,128)(2,1)S(1)} %copy-done.5, ...), custom_call_target="tpu_custom_call" | custom-call | tf_op jit(solution)/shard_map/subgrid/pallas_call | solution.py:516
  14.9 0.0 copy-start.1
  14.9 0.0 copy-start.2
  15.0 10.2 %all_to_all.22 = bf16[16,16,128]{2,1,0:T(8,128)(2,1)S(1)} all-to-all(bf16[16,16,128]{2,1,0:T(8,128)(2,1)S(1)} %bitcast.12), channel_id=1, replica_groups={{0,2,4,6,8,10,12,14,1,3,5,7,9,11,13,15},{16,18,20,22,24,26,28,30,17,19,..., dimensions={0} | all-to-all | bytes 131072 | tf_op jit(solution)/shard_map/all_to_all | solution.py:601
  25.2 0.0 copy-done.3
  25.2 0.0 copy-done.6
  25.2 0.0 copy-done
  25.2 0.0 copy-done.1
  25.2 0.0 copy-done.2
  25.2 1.7 %lines.1 = f32[4,2,4096]{2,1,0:T(2,128)} custom-call(s32[1,128]{1,0:T(1,128)S(1)} %get-tuple-element.13.places_ref, bf16[256,128]{1,0:T(8,128)(2,1)S(1)} %bitcast.10, f32[128,128]{1,0:T(8,128)S(1)} %get-tuple-element.18.straight_ref, f32[128,128]{1,0:T(8,128)S(1)} %get-tuple-element.19.crossed_ref, bf16[256,256]{1,0:T(8,128)(2,1)S(1)} %get-tuple-element.20.put_ref, ...), custom_call_target="tpu_custom_call" | custom-call | tf_op jit(solution)/shard_map/lines/pallas_call | solution.py:516
Async XLA Ops:
  0.9 10.5 %collective-permute-start = (f32[8,512]{1,0:T(8,128)S(1)}, f32[8,512]{1,0:T(8,128)S(1)}, u32[]{:S(2)}, u32[]{:S(2)}) collective-permute-start(f32[8,512]{1,0:T(8,128)S(1)} %get-tuple-element.15.refs_0_), channel_id=1, source_target_pairs={{16,0},{0,16},{17,1},{1,17},{18,2},{2,18},{19,3},{3,19},{20,4},{4,... | collective-permute-start | bytes 49160 | tf_op jit(solution)/shard_map/ppermute | solution.py:582
  4.8 6.6 %copy-start.8 = (bf16[2,64,256]{2,1,0:T(8,128)(2,1)S(1)}, bf16[2,64,256]{2,1,0:T(8,128)(2,1)}, u32[]{:S(2)}) copy-start(bf16[2,64,256]{2,1,0:T(8,128)(2,1)} %constant.24.clone.shift_ref) | copy-start | bytes 196612
  4.8 9.3 %all-to-all-start = ((bf16[8,32,128]{2,1,0:T(8,128)(2,1)}), bf16[8,32,128]{2,1,0:T(8,128)(2,1)S(1)}, u32[]{:S(2)}, u32[]{:S(2)}) async-start(bf16[8,32,128]{2,1,0:T(8,128)(2,1)} %bitcast.5), calls=%async_computation | async-start | bytes 131072 | tf_op jit(solution)/shard_map/all_to_all | solution.py:583
  11.4 2.7 %copy-start.4 = (bf16[2,128,128]{2,1,0:T(8,128)(2,1)S(1)}, bf16[2,128,128]{2,1,0:T(8,128)(2,1)}, u32[]{:S(2)}) copy-start(bf16[2,128,128]{2,1,0:T(8,128)(2,1)} %constant.30.clone.back_ref) | copy-start | bytes 196612
  11.4 2.7 %copy-start.5 = (bf16[2,128,128]{2,1,0:T(8,128)(2,1)S(1)}, bf16[2,128,128]{2,1,0:T(8,128)(2,1)}, u32[]{:S(2)}) copy-start(bf16[2,128,128]{2,1,0:T(8,128)(2,1)} %constant.29.clone.model_ref) | copy-start | bytes 196612
  11.4 2.7 %copy-start.7 = (f32[2,8,128]{2,1,0:T(8,128)S(1)}, f32[2,8,128]{2,1,0:T(8,128)}, u32[]{:S(2)}) copy-start(f32[2,8,128]{2,1,0:T(8,128)} %constant.28.clone.turn_ref) | copy-start | bytes 24580
  11.4 13.8 %copy-start.3 = (f32[2,64,128]{2,1,0:T(8,128)S(1)}, f32[2,64,128]{2,1,0:T(8,128)}, u32[]{:S(2)}) copy-start(f32[2,64,128]{2,1,0:T(8,128)} %constant.23.clone.turn_ref) | copy-start | bytes 196612
  11.4 13.8 %copy-start.6 = (f32[32,128]{1,0:T(8,128)S(1)}, f32[32,128]{1,0:T(8,128)}, u32[]{:S(2)}) copy-start(f32[32,128]{1,0:T(8,128)} %constant.22.clone.window_ref) | copy-start | bytes 49156
  14.1 11.1 %copy-start = (bf16[2,256,256]{2,1,0:T(8,128)(2,1)S(1)}, bf16[2,256,256]{2,1,0:T(8,128)(2,1)}, u32[]{:S(2)}) copy-start(bf16[2,256,256]{2,1,0:T(8,128)(2,1)} %constant.25.clone.inner_ref) | copy-start | bytes 786436
  14.9 10.3 %copy-start.1 = (bf16[2,128,128]{2,1,0:T(8,128)(2,1)S(1)}, bf16[2,128,128]{2,1,0:T(8,128)(2,1)}, u32[]{:S(2)}) copy-start(bf16[2,128,128]{2,1,0:T(8,128)(2,1)} %constant.27.clone.partial_ref) | copy-start | bytes 196612
  14.9 10.3 %copy-start.2 = (bf16[2,128,128]{2,1,0:T(8,128)(2,1)S(1)}, bf16[2,128,128]{2,1,0:T(8,128)(2,1)}, u32[]{:S(2)}) copy-start(bf16[2,128,128]{2,1,0:T(8,128)(2,1)} %constant.26.clone.outer_ref) | copy-start | bytes 196612

commit v10 on v9

--- a/solution.py
+++ b/solution.py
@@ -15,7 +15,7 @@
 FACET_ROWS = 8
 SUBGRID = FACET_ROWS * CONTRIB
 SEND_ORDER = tuple(reversed(range(FACET_ROWS)))
-RETURN_ORDER = tuple(range(FACET_ROWS))
+RETURN_ORDER = tuple(reversed(range(FACET_ROWS)))
 LANES = 128
 HALF = LANES // 2
 LATE_FLOPS = 10**10
@@ -434,7 +434,7 @@
         for spot in spots:
             for b in range(bands):
                 source = spot * columns + b * share
-                place = b * FACET_ROWS + RETURN_ORDER.index(i)
+                place = (bands - 1 - b) * FACET_ROWS + RETURN_ORDER.index(i)
                 target = (place * len(spots) + spot) * share
                 held_ref[target : target + share, :] = lines[i][source : source + share, :]
     out_ref[...] = held_ref[...].astype(BF16)
@@ -601,7 +601,7 @@
     delivered = lax.all_to_all(
         returned, ("band", "member"), split_axis=0, concat_axis=0, tiled=True,
         axis_index_groups=[
-            [b * FACET_ROWS + member for b in range(bands) for member in RETURN_ORDER]
+            [b * FACET_ROWS + member for b in reversed(range(bands)) for member in RETURN_ORDER]
         ],
     )
     lines = kernel_call(

time: 27.2 us -> 25.4 us (0.934)
  the two profiles are of different devices: /device:TPU:16 before, /device:TPU:19 now
where the time goes in v10:
time: 25.4 us; the launch traced here: 25 us
  blocking collectives  8.34 us (33%)
  Pallas kernels  7.41 us (29%)
  starting transfers between devices  6.62 us (26%)
  waiting for transfers between devices  2.49 us (10%)
    all_to_all x1, blocking collectives, local(): lax.all_to_all(returned, ('band', 'member'), split_axis=0, concat_axis=0,...  8.34 us
    pallas_call x5, Pallas kernels, kernel_call(): pl.pallas_call(kernel, out_shape=out_shape, in_specs=[pl.BlockSpec(memory...  7.41 us
    all_to_all x1, starting transfers between devices, local(): lax.all_to_all(pieces, 'member', split_axis=0, concat_axis=0, tiled=True,...  4.71 us
    all_to_all x1, waiting for transfers between devices, local(): lax.all_to_all(pieces, 'member', split_axis=0, concat_axis=0, tiled=True,...  2.48 us
    ppermute x1, starting transfers between devices, local(): gathered.append(lax.ppermute(packed, 'group', moves))  1.9 us
  transfers between devices with their start and end apart: 2, of which 1 were waited for; matrix products, arithmetic and copies ran while one was open for 0% of the time, Pallas kernels for 16%

profile of v10, /device:TPU:19, one launch (start us, length us, event | category | flops | bytes accessed | tf_op | source)
XLA Modules:
  0.0 25.0 jit_solution(3499772391176035976)
XLA Ops:
  0.0 0.8 %early.1 = (bf16[256,128]{1,0:T(8,128)(2,1)S(1)}, f32[8,512]{1,0:T(8,128)S(1)}, s32[1,128]{1,0:T(1,128)S(1)}) custom-call(s32[2,16]{1,0:T(2,128)} %offsets.3, s32[2,2,512]{2,1,0:T(2,128)} %bitcast.15, f32[2,2,512]{2,1,0:T(2,128)} %bitcast.16, f32[2,1,512]{2,1,0:T(1,128)} %bitcast.17, s32[2,1,512]{2,1,0:T(1,128)} %bitcast.18, f32[2,8,4096]{2,1,0:T(8,128)} %bitcast.13, ...), custom_call_target="tpu_custom_call" | custom-call | tf_op jit(solution)/shard_map/early/pallas_call | solution.py:516
  0.9 1.9 %collective-permute-start = (f32[8,512]{1,0:T(8,128)S(1)}, f32[8,512]{1,0:T(8,128)S(1)}, u32[]{:S(2)}, u32[]{:S(2)}) collective-permute-start(f32[8,512]{1,0:T(8,128)S(1)} %get-tuple-element.15.refs_0_), channel_id=1, source_target_pairs={{16,0},{0,16},{17,1},{1,17},{18,2},{2,18},{19,3},{3,19},{20,4},{4,... | collective-permute-start | bytes 49160 | tf_op jit(solution)/shard_map/ppermute | solution.py:582
  2.8 3.2 %late.1 = bf16[256,128]{1,0:T(8,128)(2,1)} custom-call(bf16[256,128]{1,0:T(8,128)(2,1)S(1)} %get-tuple-element.14.early_ref, s32[2,16]{1,0:T(2,128)} %offsets.3, f32[2,8,4096]{2,1,0:T(8,128)} %bitcast.14, f32[160,128]{1,0:T(8,128)} %constant.31.clone.plain_table, bf16[1792,128]{1,0:T(8,128)(2,1)} %constant.32.clone.paired_table), custom_call_target="tpu_custom_call" | custom-call | flops 10000000000 | tf_op jit(solution)/shard_map/late/pallas_call | solution.py:516
  5.9 0.0 copy-start.8
  5.9 4.7 %all-to-all-start = ((bf16[8,32,128]{2,1,0:T(8,128)(2,1)}), bf16[8,32,128]{2,1,0:T(8,128)(2,1)S(1)}, u32[]{:S(2)}, u32[]{:S(2)}) async-start(bf16[8,32,128]{2,1,0:T(8,128)(2,1)} %bitcast.5), calls=%async_computation | async-start | bytes 131072 | tf_op jit(solution)/shard_map/all_to_all | solution.py:583
  10.7 0.0 collective-permute-done.refs_1_
  10.7 0.0 copy-done.8
  10.7 0.0 copy-start.4
  10.7 0.0 copy-start.5
  10.7 0.0 copy-start.7
  10.7 0.0 copy-start.3
  10.7 0.0 copy-start.6
  10.7 0.8 %prepare.1 = (f32[256,128]{1,0:T(8,128)S(1)}, f32[256,128]{1,0:T(8,128)S(1)}, bf16[256,256]{1,0:T(8,128)(2,1)S(1)}, f32[128,128]{1,0:T(8,128)S(1)}, f32[128,128]{1,0:T(8,128)S(1)}) custom-call(s32[1,128]{1,0:T(1,128)S(1)} %get-tuple-element.13.places_ref, bf16[2,64,256]{2,1,0:T(8,128)(2,1)S(1)} %copy-done.8, f32[8,512]{1,0:T(8,128)S(1)} %get-tuple-element.15.refs_0_, ...), custom_call_target="tpu_custom_call" | custom-call | flops 20000000000 | tf_op jit(solution)/shard_map/prepare/pallas_call | solution.py:516
  11.6 2.5 %all-to-all-done = bf16[8,32,128]{2,1,0:T(8,128)(2,1)S(1)} async-done(((bf16[8,32,128]{2,1,0:T(8,128)(2,1)}), bf16[8,32,128]{2,1,0:T(8,128)(2,1)S(1)}, u32[]{:S(2)}, u32[]{:S(2)}) %all-to-all-start) | async-done | bytes 65568 | tf_op jit(solution)/shard_map/all_to_all | solution.py:583
  14.1 0.0 copy-done.4
  14.1 0.0 copy-done.5
  14.1 0.0 copy-done.7
  14.1 0.0 copy-start
  14.1 0.9 %subgrid.1 = bf16[256,128]{1,0:T(8,128)(2,1)S(1)} custom-call(bf16[256,128]{1,0:T(8,128)(2,1)S(1)} %bitcast.11, f32[256,128]{1,0:T(8,128)S(1)} %get-tuple-element.16.value_ref, f32[256,128]{1,0:T(8,128)S(1)} %get-tuple-element.17.weight_ref, f32[2,8,128]{2,1,0:T(8,128)S(1)} %copy-done.7, bf16[2,128,128]{2,1,0:T(8,128)(2,1)S(1)} %copy-done.5, ...), custom_call_target="tpu_custom_call" | custom-call | tf_op jit(solution)/shard_map/subgrid/pallas_call | solution.py:516
  14.9 0.0 copy-start.1
  15.0 0.0 copy-start.2
  15.0 8.3 %all_to_all.22 = bf16[16,16,128]{2,1,0:T(8,128)(2,1)S(1)} all-to-all(bf16[16,16,128]{2,1,0:T(8,128)(2,1)S(1)} %bitcast.12), channel_id=1, replica_groups={{15,13,11,9,7,5,3,1,14,12,10,8,6,4,2,0},{31,29,27,25,23,21,19,17,30,28,..., dimensions={0} | all-to-all | bytes 131072 | tf_op jit(solution)/shard_map/all_to_all | solution.py:601
  23.3 0.0 copy-done.3
  23.3 0.0 copy-done.6
  23.3 0.0 copy-done
  23.3 0.0 copy-done.1
  23.3 0.0 copy-done.2
  23.3 1.7 %lines.1 = f32[4,2,4096]{2,1,0:T(2,128)} custom-call(s32[1,128]{1,0:T(1,128)S(1)} %get-tuple-element.13.places_ref, bf16[256,128]{1,0:T(8,128)(2,1)S(1)} %bitcast.10, f32[128,128]{1,0:T(8,128)S(1)} %get-tuple-element.18.straight_ref, f32[128,128]{1,0:T(8,128)S(1)} %get-tuple-element.19.crossed_ref, bf16[256,256]{1,0:T(8,128)(2,1)S(1)} %get-tuple-element.20.put_ref, ...), custom_call_target="tpu_custom_call" | custom-call | tf_op jit(solution)/shard_map/lines/pallas_call | solution.py:516
Async XLA Ops:
  0.9 9.8 %collective-permute-start = (f32[8,512]{1,0:T(8,128)S(1)}, f32[8,512]{1,0:T(8,128)S(1)}, u32[]{:S(2)}, u32[]{:S(2)}) collective-permute-start(f32[8,512]{1,0:T(8,128)S(1)} %get-tuple-element.15.refs_0_), channel_id=1, source_target_pairs={{16,0},{0,16},{17,1},{1,17},{18,2},{2,18},{19,3},{3,19},{20,4},{4,... | collective-permute-start | bytes 49160 | tf_op jit(solution)/shard_map/ppermute | solution.py:582
  5.9 4.7 %copy-start.8 = (bf16[2,64,256]{2,1,0:T(8,128)(2,1)S(1)}, bf16[2,64,256]{2,1,0:T(8,128)(2,1)}, u32[]{:S(2)}) copy-start(bf16[2,64,256]{2,1,0:T(8,128)(2,1)} %constant.24.clone.shift_ref) | copy-start | bytes 196612
  5.9 8.1 %all-to-all-start = ((bf16[8,32,128]{2,1,0:T(8,128)(2,1)}), bf16[8,32,128]{2,1,0:T(8,128)(2,1)S(1)}, u32[]{:S(2)}, u32[]{:S(2)}) async-start(bf16[8,32,128]{2,1,0:T(8,128)(2,1)} %bitcast.5), calls=%async_computation | async-start | bytes 131072 | tf_op jit(solution)/shard_map/all_to_all | solution.py:583
  10.7 3.4 %copy-start.4 = (bf16[2,128,128]{2,1,0:T(8,128)(2,1)S(1)}, bf16[2,128,128]{2,1,0:T(8,128)(2,1)}, u32[]{:S(2)}) copy-start(bf16[2,128,128]{2,1,0:T(8,128)(2,1)} %constant.30.clone.back_ref) | copy-start | bytes 196612
  10.7 3.4 %copy-start.5 = (bf16[2,128,128]{2,1,0:T(8,128)(2,1)S(1)}, bf16[2,128,128]{2,1,0:T(8,128)(2,1)}, u32[]{:S(2)}) copy-start(bf16[2,128,128]{2,1,0:T(8,128)(2,1)} %constant.29.clone.model_ref) | copy-start | bytes 196612
  10.7 3.4 %copy-start.7 = (f32[2,8,128]{2,1,0:T(8,128)S(1)}, f32[2,8,128]{2,1,0:T(8,128)}, u32[]{:S(2)}) copy-start(f32[2,8,128]{2,1,0:T(8,128)} %constant.28.clone.turn_ref) | copy-start | bytes 24580
  10.7 12.6 %copy-start.3 = (f32[2,64,128]{2,1,0:T(8,128)S(1)}, f32[2,64,128]{2,1,0:T(8,128)}, u32[]{:S(2)}) copy-start(f32[2,64,128]{2,1,0:T(8,128)} %constant.23.clone.turn_ref) | copy-start | bytes 196612
  10.7 12.6 %copy-start.6 = (f32[32,128]{1,0:T(8,128)S(1)}, f32[32,128]{1,0:T(8,128)}, u32[]{:S(2)}) copy-start(f32[32,128]{1,0:T(8,128)} %constant.22.clone.window_ref) | copy-start | bytes 49156
  14.1 9.2 %copy-start = (bf16[2,256,256]{2,1,0:T(8,128)(2,1)S(1)}, bf16[2,256,256]{2,1,0:T(8,128)(2,1)}, u32[]{:S(2)}) copy-start(bf16[2,256,256]{2,1,0:T(8,128)(2,1)} %constant.25.clone.inner_ref) | copy-start | bytes 786436
  14.9 8.4 %copy-start.1 = (bf16[2,128,128]{2,1,0:T(8,128)(2,1)S(1)}, bf16[2,128,128]{2,1,0:T(8,128)(2,1)}, u32[]{:S(2)}) copy-start(bf16[2,128,128]{2,1,0:T(8,128)(2,1)} %constant.27.clone.partial_ref) | copy-start | bytes 196612
  15.0 8.4 %copy-start.2 = (bf16[2,128,128]{2,1,0:T(8,128)(2,1)S(1)}, bf16[2,128,128]{2,1,0:T(8,128)(2,1)}, u32[]{:S(2)}) copy-start(bf16[2,128,128]{2,1,0:T(8,128)(2,1)} %constant.26.clone.outer_ref) | copy-start | bytes 196612

commit v11 on v10

--- a/solution.py
+++ b/solution.py
@@ -112,14 +112,21 @@
     return lax.dot_general(left, right, (dims, ((), ())), preferred_element_type=F32)
 
 
-def times_table(values, table, dims=((1,), (0,))):
-    high, low = split(values)
-    return dot(high, table[0], dims) + dot(low, table[0], dims) + dot(high, table[1], dims)
+def dot_split(values, right):
+    rows = values.shape[0]
+    both = dot(jnp.concatenate(split(values), axis=0), right)
+    return both[:rows] + both[rows:]
+
+
+def times_table(values, table):
+    return dot_split(values, table[0]) + dot(values.astype(BF16), table[1])
 
 
 def table_times(table, values, dims=((1,), (0,))):
     high, low = split(values)
-    return dot(table[0], high, dims) + dot(table[0], low, dims) + dot(table[1], high, dims)
+    rows = table[0].shape[0]
+    both = dot(jnp.concatenate([table[0], table[1]], axis=0), high, dims)
+    return both[:rows] + both[rows:] + dot(table[0], low, dims)
 
 
 def iota(shape, dimension):
@@ -225,7 +232,7 @@
     shape = (columns * blocks, width)
     pick_inside = one_hot(shape, base + first_block)
     pick_beyond = one_hot(shape, base + within(first_block + 1, blocks))
-    for copy in copies:
+    for copy in copies[:2]:
         copy.wait()
 
     def pair_at(name):
@@ -247,6 +254,8 @@
             even.append(jnp.where(low_half, first, swap_halves(second)))
             odd.append(jnp.where(low_half, swap_halves(first), second))
         sections += [jnp.concatenate(even, axis=1), jnp.concatenate(odd, axis=1)]
+    for copy in copies[2:]:
+        copy.wait()
     section = table_times(pair_at("outer"), jnp.concatenate(sections, axis=0))
     turned = []
     for pair in range(pairs):
@@ -272,9 +281,8 @@
         ],
         axis=0,
     )
-    high, low = split(spectrum)
-    inside = dot(high, pick_inside) + dot(low, pick_inside)
-    beyond = dot(high, pick_beyond) + dot(low, pick_beyond)
+    inside = dot_split(spectrum, pick_inside)
+    beyond = dot_split(spectrum, pick_beyond)
     kappa = within(iota((2 * CONTRIB, width), 0), CONTRIB)
     cutout = jnp.where(kappa >= residue, inside, beyond)
     piece = times_table(cutout.T, pair_at("piece"))
@@ -288,29 +296,18 @@
 
 def early_kernel(
     offsets, cells, values, weights, flags, strips, plain_table, paired_table,
-    out_ref, packed_ref, places_ref,
-    offsets_ref, cells_ref, values_ref, weights_ref, flags_ref, strips_ref, plain_ref, paired_ref,
-    real_ref, imag_ref, small_semaphores, semaphores, *, plain, paired, share,
+    out_ref, packed_ref, places_ref, spread_ref, strips_ref, plain_ref, paired_ref,
+    offsets_ref, cells_ref, values_ref, weights_ref, flags_ref, real_ref, imag_ref,
+    small_semaphores, semaphores, *, plain, paired, share,
 ):
-    columns = strips_ref.shape[1]
     small = start_all(
         (offsets, cells, values, weights, flags),
         (offsets_ref, cells_ref, values_ref, weights_ref, flags_ref),
         small_semaphores,
     )
-
-    def large():
-        sources, targets = (strips, plain_table, paired_table), (strips_ref, plain_ref, paired_ref)
-        return [
-            pltpu.make_async_copy(source, target, semaphores.at[i])
-            for i, (source, target) in enumerate(zip(sources, targets))
-        ]
-
-    @pl.when(in_first_half())
-    def _():
-        for copy in large():
-            copy.start()
-
+    large = start_all(
+        (strips, plain_table, paired_table), (strips_ref, plain_ref, paired_ref), semaphores
+    )
     for copy in small:
         copy.wait()
     for t in range(cells_ref.shape[0]):
@@ -321,19 +318,23 @@
         ]
         packed_ref[4 * t : 4 * t + 4, :] = jnp.concatenate(rows, axis=0)
     places_ref[...] = offsets_on_lanes(offsets_ref, share, RETURN_ORDER)
+    spread_ref[...] = offsets_on_lanes(offsets_ref, strips_ref.shape[1], SEND_ORDER)
 
     @pl.when(in_first_half())
     def _():
-        spread = offsets_on_lanes(offsets_ref, columns, SEND_ORDER)
         predict(
-            spread, large(), strips_ref, plain_ref, paired_ref, (real_ref, imag_ref), out_ref,
-            plain, paired,
+            spread_ref[...], large, strips_ref, plain_ref, paired_ref, (real_ref, imag_ref),
+            out_ref, plain, paired,
         )
 
+    @pl.when(jnp.logical_not(in_first_half()))
+    def _():
+        for copy in large:
+            copy.wait()
+
 
 def late_kernel(
-    early_ref, offsets, strips, plain_table, paired_table, out_ref,
-    offsets_ref, strips_ref, plain_ref, paired_ref, real_ref, imag_ref, semaphores,
+    early_ref, spread_ref, strips_ref, plain_ref, paired_ref, out_ref, real_ref, imag_ref,
     *, plain, paired,
 ):
     @pl.when(in_first_half())
@@ -342,15 +343,8 @@
 
     @pl.when(jnp.logical_not(in_first_half()))
     def _():
-        copies = start_all(
-            (offsets, strips, plain_table, paired_table),
-            (offsets_ref, strips_ref, plain_ref, paired_ref),
-            semaphores,
-        )
-        copies[0].wait()
-        spread = offsets_on_lanes(offsets_ref, strips_ref.shape[1], SEND_ORDER)
         predict(
-            spread, copies[1:], strips_ref, plain_ref, paired_ref, (real_ref, imag_ref), out_ref,
+            spread_ref[...], (), strips_ref, plain_ref, paired_ref, (real_ref, imag_ref), out_ref,
             plain, paired,
         )
 
@@ -558,23 +552,24 @@
     def semaphores(count):
         return pltpu.SemaphoreType.DMA((count,))
 
-    early, packed, places = kernel_call(
+    early, packed, places, *fetched = kernel_call(
         functools.partial(early_kernel, plain=plain_places, paired=paired_places, share=share),
         "early",
         [
             jax.ShapeDtypeStruct((rows, LANES), BF16),
             jax.ShapeDtypeStruct((4 * fronts, cells.shape[-1]), F32),
             jax.ShapeDtypeStruct((1, width), jnp.int32),
-        ],
+            jax.ShapeDtypeStruct((1, rows), jnp.int32),
+        ]
+        + [jax.ShapeDtypeStruct(array.shape, array.dtype) for array in large],
         [pltpu.HBM] * 8,
-        landing(small + large) + [wide(held)] * 2 + [semaphores(5), semaphores(3)],
+        landing(small) + [wide(held)] * 2 + [semaphores(5), semaphores(3)],
         *in_hbm(small + large),
     )
     pieces = kernel_call(
         functools.partial(late_kernel, plain=plain_places, paired=paired_places), "late",
-        jax.ShapeDtypeStruct((rows, LANES), BF16), [pltpu.VMEM] + [pltpu.HBM] * 4,
-        landing([offsets] + large) + [wide(held)] * 2 + [semaphores(4)],
-        early, *in_hbm([offsets] + large), flops=LATE_FLOPS,
+        jax.ShapeDtypeStruct((rows, LANES), BF16), [pltpu.VMEM] * 5, [wide(held)] * 2,
+        early, *fetched, flops=LATE_FLOPS,
     )
     gathered = [packed]
     for step in range(1, groups):

time: 25.4 us -> 24.8 us (0.976)
  the two profiles are of different devices: /device:TPU:19 before, /device:TPU:0 now
where the time goes in v11:
time: 24.8 us; the launch traced here: 24.5 us
  blocking collectives  8.11 us (33%)
  starting transfers between devices  7.9 us (32%)
  Pallas kernels  6.55 us (26%)
  waiting for transfers between devices  1.79 us (7%)
    all_to_all x1, blocking collectives, local(): lax.all_to_all(returned, ('band', 'member'), split_axis=0, concat_axis=0,...  8.11 us
    pallas_call x5, Pallas kernels, kernel_call(): pl.pallas_call(kernel, out_shape=out_shape, in_specs=[pl.BlockSpec(memory...  6.55 us
    all_to_all x1, starting transfers between devices, local(): lax.all_to_all(pieces, 'member', split_axis=0, concat_axis=0, tiled=True,...  5.12 us
    ppermute x1, starting transfers between devices, local(): gathered.append(lax.ppermute(packed, 'group', moves))  2.79 us
    all_to_all x1, waiting for transfers between devices, local(): lax.all_to_all(pieces, 'member', split_axis=0, concat_axis=0, tiled=True,...  1.79 us
  transfers between devices with their start and end apart: 2, of which 1 were waited for; matrix products, arithmetic and copies ran while one was open for 0% of the time, Pallas kernels for 6%

profile of v11, /device:TPU:0, one launch (start us, length us, event | category | flops | bytes accessed | tf_op | source)
XLA Modules:
  0.0 24.5 jit_solution(16127059509994507740)
XLA Ops:
  0.0 2.6 %early.1 = (bf16[256,128]{1,0:T(8,128)(2,1)S(1)}, f32[8,512]{1,0:T(8,128)S(1)}, s32[1,128]{1,0:T(1,128)S(1)}, s32[1,256]{1,0:T(1,128)S(1)}, f32[2,8,4096]{2,1,0:...) custom-call(s32[2,16]{1,0:T(2,128)} %offsets.1, s32[2,2,512]{2,1,0:T(2,128)} %bitcast.14, ...), custom_call_target="tpu_custom_call" | custom-call | tf_op jit(solution)/shard_map/early/pallas_call | solution.py:510
  2.6 2.8 %collective-permute-start = (f32[8,512]{1,0:T(8,128)S(1)}, f32[8,512]{1,0:T(8,128)S(1)}, u32[]{:S(2)}, u32[]{:S(2)}) collective-permute-start(f32[8,512]{1,0:T(8,128)S(1)} %get-tuple-element.23.refs_0_), channel_id=1, source_target_pairs={{16,0},{0,16},{17,1},{1,17},{18,2},{2,18},{19,3},{3,19},{20,4},{4,... | collective-permute-start | bytes 49160 | tf_op jit(solution)/shard_map/ppermute | solution.py:577
  5.4 0.6 %late.1 = bf16[256,128]{1,0:T(8,128)(2,1)} custom-call(bf16[256,128]{1,0:T(8,128)(2,1)S(1)} %get-tuple-element.18.early_ref, s32[1,256]{1,0:T(1,128)S(1)} %get-tuple-element.19.spread_ref, f32[2,8,4096]{2,1,0:T(8,128)S(1)} %get-tuple-element.20.strips_ref, f32[160,128]{1,0:T(8,128)S(1)} %get-tuple-element.21.plain_ref, ...), custom_call_target="tpu_custom_call" | custom-call | flops 10000000000 | tf_op jit(solution)/shard_map/late/pallas_call | solution.py:510
  6.0 0.0 copy-start.8
  6.0 5.1 %all-to-all-start = ((bf16[8,32,128]{2,1,0:T(8,128)(2,1)}), bf16[8,32,128]{2,1,0:T(8,128)(2,1)S(1)}, u32[]{:S(2)}, u32[]{:S(2)}) async-start(bf16[8,32,128]{2,1,0:T(8,128)(2,1)} %bitcast.5), calls=%async_computation | async-start | bytes 131072 | tf_op jit(solution)/shard_map/all_to_all | solution.py:578
  11.1 0.0 collective-permute-done.refs_1_
  11.1 0.0 copy-done.8
  11.1 0.0 copy-start.4
  11.2 0.0 copy-start.5
  11.2 0.0 copy-start.7
  11.2 0.0 copy-start.3
  11.2 0.0 copy-start.6
  11.2 0.8 %prepare.1 = (f32[256,128]{1,0:T(8,128)S(1)}, f32[256,128]{1,0:T(8,128)S(1)}, bf16[256,256]{1,0:T(8,128)(2,1)S(1)}, f32[128,128]{1,0:T(8,128)S(1)}, f32[128,128]{1,0:T(8,128)S(1)}) custom-call(s32[1,128]{1,0:T(1,128)S(1)} %get-tuple-element.17.places_ref, bf16[2,64,256]{2,1,0:T(8,128)(2,1)S(1)} %copy-done.8, f32[8,512]{1,0:T(8,128)S(1)} %get-tuple-element.23.refs_0_, ...), custom_call_target="tpu_custom_call" | custom-call | flops 20000000000 | tf_op jit(solution)/shard_map/prepare/pallas_call | solution.py:510
  12.1 1.8 %all-to-all-done = bf16[8,32,128]{2,1,0:T(8,128)(2,1)S(1)} async-done(((bf16[8,32,128]{2,1,0:T(8,128)(2,1)}), bf16[8,32,128]{2,1,0:T(8,128)(2,1)S(1)}, u32[]{:S(2)}, u32[]{:S(2)}) %all-to-all-start) | async-done | bytes 65568 | tf_op jit(solution)/shard_map/all_to_all | solution.py:578
  13.8 0.0 copy-done.4
  13.8 0.0 copy-done.5
  13.8 0.0 copy-done.7
  13.9 0.0 copy-start
  13.9 0.8 %subgrid.1 = bf16[256,128]{1,0:T(8,128)(2,1)S(1)} custom-call(bf16[256,128]{1,0:T(8,128)(2,1)S(1)} %bitcast.11, f32[256,128]{1,0:T(8,128)S(1)} %get-tuple-element.24.value_ref, f32[256,128]{1,0:T(8,128)S(1)} %get-tuple-element.25.weight_ref, f32[2,8,128]{2,1,0:T(8,128)S(1)} %copy-done.7, bf16[2,128,128]{2,1,0:T(8,128)(2,1)S(1)} %copy-done.5, ...), custom_call_target="tpu_custom_call" | custom-call | tf_op jit(solution)/shard_map/subgrid/pallas_call | solution.py:510
  14.7 0.0 copy-start.1
  14.7 0.0 copy-start.2
  14.7 8.1 %all_to_all.22 = bf16[16,16,128]{2,1,0:T(8,128)(2,1)S(1)} all-to-all(bf16[16,16,128]{2,1,0:T(8,128)(2,1)S(1)} %bitcast.12), channel_id=1, replica_groups={{15,13,11,9,7,5,3,1,14,12,10,8,6,4,2,0},{31,29,27,25,23,21,19,17,30,28,..., dimensions={0} | all-to-all | bytes 131072 | tf_op jit(solution)/shard_map/all_to_all | solution.py:596
  22.9 0.0 copy-done.3
  22.9 0.0 copy-done.6
  22.9 0.0 copy-done
  22.9 0.0 copy-done.1
  22.9 0.0 copy-done.2
  22.9 1.6 %lines.1 = f32[4,2,4096]{2,1,0:T(2,128)} custom-call(s32[1,128]{1,0:T(1,128)S(1)} %get-tuple-element.17.places_ref, bf16[256,128]{1,0:T(8,128)(2,1)S(1)} %bitcast.10, f32[128,128]{1,0:T(8,128)S(1)} %get-tuple-element.26.straight_ref, f32[128,128]{1,0:T(8,128)S(1)} %get-tuple-element.27.crossed_ref, bf16[256,256]{1,0:T(8,128)(2,1)S(1)} %get-tuple-element.28.put_ref, ...), custom_call_target="tpu_custom_call" | custom-call | tf_op jit(solution)/shard_map/lines/pallas_call | solution.py:510
Async XLA Ops:
  2.6 8.5 %collective-permute-start = (f32[8,512]{1,0:T(8,128)S(1)}, f32[8,512]{1,0:T(8,128)S(1)}, u32[]{:S(2)}, u32[]{:S(2)}) collective-permute-start(f32[8,512]{1,0:T(8,128)S(1)} %get-tuple-element.23.refs_0_), channel_id=1, source_target_pairs={{16,0},{0,16},{17,1},{1,17},{18,2},{2,18},{19,3},{3,19},{20,4},{4,... | collective-permute-start | bytes 49160 | tf_op jit(solution)/shard_map/ppermute | solution.py:577
  6.0 5.1 %copy-start.8 = (bf16[2,64,256]{2,1,0:T(8,128)(2,1)S(1)}, bf16[2,64,256]{2,1,0:T(8,128)(2,1)}, u32[]{:S(2)}) copy-start(bf16[2,64,256]{2,1,0:T(8,128)(2,1)} %constant.24.clone.shift_ref) | copy-start | bytes 196612
  6.0 7.8 %all-to-all-start = ((bf16[8,32,128]{2,1,0:T(8,128)(2,1)}), bf16[8,32,128]{2,1,0:T(8,128)(2,1)S(1)}, u32[]{:S(2)}, u32[]{:S(2)}) async-start(bf16[8,32,128]{2,1,0:T(8,128)(2,1)} %bitcast.5), calls=%async_computation | async-start | bytes 131072 | tf_op jit(solution)/shard_map/all_to_all | solution.py:578
  11.1 2.7 %copy-start.4 = (bf16[2,128,128]{2,1,0:T(8,128)(2,1)S(1)}, bf16[2,128,128]{2,1,0:T(8,128)(2,1)}, u32[]{:S(2)}) copy-start(bf16[2,128,128]{2,1,0:T(8,128)(2,1)} %constant.30.clone.back_ref) | copy-start | bytes 196612
  11.2 2.7 %copy-start.5 = (bf16[2,128,128]{2,1,0:T(8,128)(2,1)S(1)}, bf16[2,128,128]{2,1,0:T(8,128)(2,1)}, u32[]{:S(2)}) copy-start(bf16[2,128,128]{2,1,0:T(8,128)(2,1)} %constant.29.clone.model_ref) | copy-start | bytes 196612
  11.2 2.7 %copy-start.7 = (f32[2,8,128]{2,1,0:T(8,128)S(1)}, f32[2,8,128]{2,1,0:T(8,128)}, u32[]{:S(2)}) copy-start(f32[2,8,128]{2,1,0:T(8,128)} %constant.28.clone.turn_ref) | copy-start | bytes 24580
  11.2 11.7 %copy-start.3 = (f32[2,64,128]{2,1,0:T(8,128)S(1)}, f32[2,64,128]{2,1,0:T(8,128)}, u32[]{:S(2)}) copy-start(f32[2,64,128]{2,1,0:T(8,128)} %constant.23.clone.turn_ref) | copy-start | bytes 196612
  11.2 11.7 %copy-start.6 = (f32[32,128]{1,0:T(8,128)S(1)}, f32[32,128]{1,0:T(8,128)}, u32[]{:S(2)}) copy-start(f32[32,128]{1,0:T(8,128)} %constant.22.clone.window_ref) | copy-start | bytes 49156
  13.9 9.0 %copy-start = (bf16[2,256,256]{2,1,0:T(8,128)(2,1)S(1)}, bf16[2,256,256]{2,1,0:T(8,128)(2,1)}, u32[]{:S(2)}) copy-start(bf16[2,256,256]{2,1,0:T(8,128)(2,1)} %constant.25.clone.inner_ref) | copy-start | bytes 786436
  14.7 8.2 %copy-start.1 = (bf16[2,128,128]{2,1,0:T(8,128)(2,1)S(1)}, bf16[2,128,128]{2,1,0:T(8,128)(2,1)}, u32[]{:S(2)}) copy-start(bf16[2,128,128]{2,1,0:T(8,128)(2,1)} %constant.27.clone.partial_ref) | copy-start | bytes 196612
  14.7 8.1 %copy-start.2 = (bf16[2,128,128]{2,1,0:T(8,128)(2,1)S(1)}, bf16[2,128,128]{2,1,0:T(8,128)(2,1)}, u32[]{:S(2)}) copy-start(bf16[2,128,128]{2,1,0:T(8,128)(2,1)} %constant.26.clone.outer_ref) | copy-start | bytes 196612

commit v12 on v11

--- a/solution.py
+++ b/solution.py
@@ -18,6 +18,7 @@
 RETURN_ORDER = tuple(reversed(range(FACET_ROWS)))
 LANES = 128
 HALF = LANES // 2
+EARLY_FLOPS = 10**10
 LATE_FLOPS = 10**10
 PREPARE_FLOPS = 2 * 10**10
 VMEM_LIMIT = 48 * 1024 * 1024
@@ -296,18 +297,28 @@
 
 def early_kernel(
     offsets, cells, values, weights, flags, strips, plain_table, paired_table,
-    out_ref, packed_ref, places_ref, spread_ref, strips_ref, plain_ref, paired_ref,
-    offsets_ref, cells_ref, values_ref, weights_ref, flags_ref, real_ref, imag_ref,
-    small_semaphores, semaphores, *, plain, paired, share,
+    out_ref, packed_ref, places_ref, spread_ref,
+    offsets_ref, cells_ref, values_ref, weights_ref, flags_ref, strips_ref, plain_ref, paired_ref,
+    real_ref, imag_ref, small_semaphores, semaphores, *, plain, paired, share,
 ):
     small = start_all(
         (offsets, cells, values, weights, flags),
         (offsets_ref, cells_ref, values_ref, weights_ref, flags_ref),
         small_semaphores,
     )
-    large = start_all(
-        (strips, plain_table, paired_table), (strips_ref, plain_ref, paired_ref), semaphores
-    )
+
+    def large():
+        sources, targets = (strips, plain_table, paired_table), (strips_ref, plain_ref, paired_ref)
+        return [
+            pltpu.make_async_copy(source, target, semaphores.at[i])
+            for i, (source, target) in enumerate(zip(sources, targets))
+        ]
+
+    @pl.when(in_first_half())
+    def _():
+        for copy in large():
+            copy.start()
+
     for copy in small:
         copy.wait()
     for t in range(cells_ref.shape[0]):
@@ -323,14 +334,9 @@
     @pl.when(in_first_half())
     def _():
         predict(
-            spread_ref[...], large, strips_ref, plain_ref, paired_ref, (real_ref, imag_ref),
+            spread_ref[...], large(), strips_ref, plain_ref, paired_ref, (real_ref, imag_ref),
             out_ref, plain, paired,
         )
-
-    @pl.when(jnp.logical_not(in_first_half()))
-    def _():
-        for copy in large:
-            copy.wait()
 
 
 def late_kernel(
@@ -552,7 +558,7 @@
     def semaphores(count):
         return pltpu.SemaphoreType.DMA((count,))
 
-    early, packed, places, *fetched = kernel_call(
+    early, packed, places, spread = kernel_call(
         functools.partial(early_kernel, plain=plain_places, paired=paired_places, share=share),
         "early",
         [
@@ -560,16 +566,15 @@
             jax.ShapeDtypeStruct((4 * fronts, cells.shape[-1]), F32),
             jax.ShapeDtypeStruct((1, width), jnp.int32),
             jax.ShapeDtypeStruct((1, rows), jnp.int32),
-        ]
-        + [jax.ShapeDtypeStruct(array.shape, array.dtype) for array in large],
+        ],
         [pltpu.HBM] * 8,
-        landing(small) + [wide(held)] * 2 + [semaphores(5), semaphores(3)],
-        *in_hbm(small + large),
+        landing(small + large) + [wide(held)] * 2 + [semaphores(5), semaphores(3)],
+        *in_hbm(small + large), flops=EARLY_FLOPS,
     )
     pieces = kernel_call(
         functools.partial(late_kernel, plain=plain_places, paired=paired_places), "late",
         jax.ShapeDtypeStruct((rows, LANES), BF16), [pltpu.VMEM] * 5, [wide(held)] * 2,
-        early, *fetched, flops=LATE_FLOPS,
+        early, spread, *large, flops=LATE_FLOPS,
     )
     gathered = [packed]
     for step in range(1, groups):

time: 24.8 us -> 24.6 us (level)
  starting transfers between devices: 7.9 us -> 7.54 us
    ppermute x1, starting transfers between devices: 2.79 us -> 2.42 us  [local(): gathered.append(lax.ppermute(packed, 'group', moves))]
where the time goes in v12:
time: 24.6 us; the launch traced here: 24.2 us
  blocking collectives  8.11 us (33%)
  starting transfers between devices  7.54 us (31%)
  Pallas kernels  6.62 us (27%)
  waiting for transfers between devices  1.79 us (7%)
    all_to_all x1, blocking collectives, local(): lax.all_to_all(returned, ('band', 'member'), split_axis=0, concat_axis=0,...  8.11 us
    pallas_call x5, Pallas kernels, kernel_call(): pl.pallas_call(kernel, out_shape=out_shape, in_specs=[pl.BlockSpec(memory...  6.62 us
    all_to_all x1, starting transfers between devices, local(): lax.all_to_all(pieces, 'member', split_axis=0, concat_axis=0, tiled=True,...  5.12 us
    ppermute x1, starting transfers between devices, local(): gathered.append(lax.ppermute(packed, 'group', moves))  2.42 us
    all_to_all x1, waiting for transfers between devices, local(): lax.all_to_all(pieces, 'member', split_axis=0, concat_axis=0, tiled=True,...  1.79 us
  transfers between devices with their start and end apart: 2, of which 1 were waited for; matrix products, arithmetic and copies ran while one was open for 0% of the time, Pallas kernels for 6%

profile of v12, /device:TPU:0, one launch (start us, length us, event | category | flops | bytes accessed | tf_op | source)
XLA Modules:
  0.0 24.2 jit_solution(4964622603857934865)
XLA Ops:
  0.0 0.0 copy-start.8
  0.0 0.0 copy-start.9
  0.0 0.0 copy-start.10
  0.0 2.6 %early.1 = (bf16[256,128]{1,0:T(8,128)(2,1)S(1)}, f32[8,512]{1,0:T(8,128)S(1)}, s32[1,128]{1,0:T(1,128)S(1)}, s32[1,256]{1,0:T(1,128)S(1)}) custom-call(s32[2,16]{1,0:T(2,128)} %offsets.1, s32[2,2,512]{2,1,0:T(2,128)} %bitcast.15, f32[2,2,512]{2,1,0:T(2,128)} %bitcast.16, f32[2,1,512]{2,1,0:T(1,128)} %bitcast.17, s32[2,1,512]{2,1,0:T(1,128)} %bitcast.18, ...), custom_call_target="tpu_custom_call" | custom-call | flops 10000000000 | tf_op jit(solution)/shard_map/early/pallas_call | solution.py:516
  2.7 2.4 %collective-permute-start = (f32[8,512]{1,0:T(8,128)S(1)}, f32[8,512]{1,0:T(8,128)S(1)}, u32[]{:S(2)}, u32[]{:S(2)}) collective-permute-start(f32[8,512]{1,0:T(8,128)S(1)} %get-tuple-element.17.refs_0_), channel_id=1, source_target_pairs={{16,0},{0,16},{17,1},{1,17},{18,2},{2,18},{19,3},{3,19},{20,4},{4,... | collective-permute-start | bytes 49160 | tf_op jit(solution)/shard_map/ppermute | solution.py:582
  5.1 0.0 copy-done.8
  5.1 0.0 copy-done.9
  5.1 0.0 copy-done.10
  5.1 0.6 %late.1 = bf16[256,128]{1,0:T(8,128)(2,1)} custom-call(bf16[256,128]{1,0:T(8,128)(2,1)S(1)} %get-tuple-element.15.early_ref, s32[1,256]{1,0:T(1,128)S(1)} %get-tuple-element.16.spread_ref, f32[2,8,4096]{2,1,0:T(8,128)S(1)} %bitcast.14, f32[160,128]{1,0:T(8,128)S(1)} %copy-done.10, bf16[1792,128]{1,0:T(8,128)(2,1)S(1)} %copy-done.9), custom_call_target="tpu_custom_call" | custom-call | flops 10000000000 | tf_op jit(solution)/shard_map/late/pallas_call | solution.py:516
  5.7 0.0 copy-start.11
  5.7 5.1 %all-to-all-start = ((bf16[8,32,128]{2,1,0:T(8,128)(2,1)}), bf16[8,32,128]{2,1,0:T(8,128)(2,1)S(1)}, u32[]{:S(2)}, u32[]{:S(2)}) async-start(bf16[8,32,128]{2,1,0:T(8,128)(2,1)} %bitcast.5), calls=%async_computation | async-start | bytes 131072 | tf_op jit(solution)/shard_map/all_to_all | solution.py:583
  10.9 0.0 collective-permute-done.refs_1_
  10.9 0.0 copy-done.11
  10.9 0.0 copy-start.4
  10.9 0.0 copy-start.5
  10.9 0.0 copy-start.7
  10.9 0.0 copy-start.3
  10.9 0.0 copy-start.6
  10.9 0.8 %prepare.1 = (f32[256,128]{1,0:T(8,128)S(1)}, f32[256,128]{1,0:T(8,128)S(1)}, bf16[256,256]{1,0:T(8,128)(2,1)S(1)}, f32[128,128]{1,0:T(8,128)S(1)}, f32[128,128]{1,0:T(8,128)S(1)}) custom-call(s32[1,128]{1,0:T(1,128)S(1)} %get-tuple-element.14.places_ref, bf16[2,64,256]{2,1,0:T(8,128)(2,1)S(1)} %copy-done.11, f32[8,512]{1,0:T(8,128)S(1)} %get-tuple-element.17.refs_0_, ...), custom_call_target="tpu_custom_call" | custom-call | flops 20000000000 | tf_op jit(solution)/shard_map/prepare/pallas_call | solution.py:516
  11.8 1.8 %all-to-all-done = bf16[8,32,128]{2,1,0:T(8,128)(2,1)S(1)} async-done(((bf16[8,32,128]{2,1,0:T(8,128)(2,1)}), bf16[8,32,128]{2,1,0:T(8,128)(2,1)S(1)}, u32[]{:S(2)}, u32[]{:S(2)}) %all-to-all-start) | async-done | bytes 65568 | tf_op jit(solution)/shard_map/all_to_all | solution.py:583
  13.6 0.0 copy-done.4
  13.6 0.0 copy-done.5
  13.6 0.0 copy-done.7
  13.6 0.0 copy-start
  13.6 0.8 %subgrid.1 = bf16[256,128]{1,0:T(8,128)(2,1)S(1)} custom-call(bf16[256,128]{1,0:T(8,128)(2,1)S(1)} %bitcast.11, f32[256,128]{1,0:T(8,128)S(1)} %get-tuple-element.18.value_ref, f32[256,128]{1,0:T(8,128)S(1)} %get-tuple-element.19.weight_ref, f32[2,8,128]{2,1,0:T(8,128)S(1)} %copy-done.7, bf16[2,128,128]{2,1,0:T(8,128)(2,1)S(1)} %copy-done.5, ...), custom_call_target="tpu_custom_call" | custom-call | tf_op jit(solution)/shard_map/subgrid/pallas_call | solution.py:516
  14.4 0.0 copy-start.1
  14.5 0.0 copy-start.2
  14.5 8.1 %all_to_all.22 = bf16[16,16,128]{2,1,0:T(8,128)(2,1)S(1)} all-to-all(bf16[16,16,128]{2,1,0:T(8,128)(2,1)S(1)} %bitcast.12), channel_id=1, replica_groups={{15,13,11,9,7,5,3,1,14,12,10,8,6,4,2,0},{31,29,27,25,23,21,19,17,30,28,..., dimensions={0} | all-to-all | bytes 131072 | tf_op jit(solution)/shard_map/all_to_all | solution.py:601
  22.6 0.0 copy-done.3
  22.6 0.0 copy-done.6
  22.6 0.0 copy-done
  22.6 0.0 copy-done.1
  22.6 0.0 copy-done.2
  22.6 1.6 %lines.1 = f32[4,2,4096]{2,1,0:T(2,128)} custom-call(s32[1,128]{1,0:T(1,128)S(1)} %get-tuple-element.14.places_ref, bf16[256,128]{1,0:T(8,128)(2,1)S(1)} %bitcast.10, f32[128,128]{1,0:T(8,128)S(1)} %get-tuple-element.20.straight_ref, f32[128,128]{1,0:T(8,128)S(1)} %get-tuple-element.21.crossed_ref, bf16[256,256]{1,0:T(8,128)(2,1)S(1)} %get-tuple-element.22.put_ref, ...), custom_call_target="tpu_custom_call" | custom-call | tf_op jit(solution)/shard_map/lines/pallas_call | solution.py:516
Async XLA Ops:
  0.0 5.1 %copy-start.8 = (f32[1,1,2,8,4096]{4,3,2,1,0:T(8,128)S(1)}, f32[1,1,2,8,4096]{4,3,2,1,0:T(8,128)}, u32[]{:S(2)}) copy-start(f32[1,1,2,8,4096]{4,3,2,1,0:T(8,128)} %param.17) | copy-start | bytes 786436
  0.0 5.1 %copy-start.9 = (bf16[1792,128]{1,0:T(8,128)(2,1)S(1)}, bf16[1792,128]{1,0:T(8,128)(2,1)}, u32[]{:S(2)}) copy-start(bf16[1792,128]{1,0:T(8,128)(2,1)} %constant.32.clone.paired_table.paired_ref) | copy-start | bytes 1376260
  0.0 5.1 %copy-start.10 = (f32[160,128]{1,0:T(8,128)S(1)}, f32[160,128]{1,0:T(8,128)}, u32[]{:S(2)}) copy-start(f32[160,128]{1,0:T(8,128)} %constant.31.clone.plain_table.plain_ref) | copy-start | bytes 245764
  2.7 8.2 %collective-permute-start = (f32[8,512]{1,0:T(8,128)S(1)}, f32[8,512]{1,0:T(8,128)S(1)}, u32[]{:S(2)}, u32[]{:S(2)}) collective-permute-start(f32[8,512]{1,0:T(8,128)S(1)} %get-tuple-element.17.refs_0_), channel_id=1, source_target_pairs={{16,0},{0,16},{17,1},{1,17},{18,2},{2,18},{19,3},{3,19},{20,4},{4,... | collective-permute-start | bytes 49160 | tf_op jit(solution)/shard_map/ppermute | solution.py:582
  5.7 5.1 %copy-start.11 = (bf16[2,64,256]{2,1,0:T(8,128)(2,1)S(1)}, bf16[2,64,256]{2,1,0:T(8,128)(2,1)}, u32[]{:S(2)}) copy-start(bf16[2,64,256]{2,1,0:T(8,128)(2,1)} %constant.24.clone.shift_ref) | copy-start | bytes 196612
  5.7 7.8 %all-to-all-start = ((bf16[8,32,128]{2,1,0:T(8,128)(2,1)}), bf16[8,32,128]{2,1,0:T(8,128)(2,1)S(1)}, u32[]{:S(2)}, u32[]{:S(2)}) async-start(bf16[8,32,128]{2,1,0:T(8,128)(2,1)} %bitcast.5), calls=%async_computation | async-start | bytes 131072 | tf_op jit(solution)/shard_map/all_to_all | solution.py:583
  10.9 2.7 %copy-start.4 = (bf16[2,128,128]{2,1,0:T(8,128)(2,1)S(1)}, bf16[2,128,128]{2,1,0:T(8,128)(2,1)}, u32[]{:S(2)}) copy-start(bf16[2,128,128]{2,1,0:T(8,128)(2,1)} %constant.30.clone.back_ref) | copy-start | bytes 196612
  10.9 2.7 %copy-start.5 = (bf16[2,128,128]{2,1,0:T(8,128)(2,1)S(1)}, bf16[2,128,128]{2,1,0:T(8,128)(2,1)}, u32[]{:S(2)}) copy-start(bf16[2,128,128]{2,1,0:T(8,128)(2,1)} %constant.29.clone.model_ref) | copy-start | bytes 196612
  10.9 2.7 %copy-start.7 = (f32[2,8,128]{2,1,0:T(8,128)S(1)}, f32[2,8,128]{2,1,0:T(8,128)}, u32[]{:S(2)}) copy-start(f32[2,8,128]{2,1,0:T(8,128)} %constant.28.clone.turn_ref) | copy-start | bytes 24580
  10.9 11.7 %copy-start.3 = (f32[2,64,128]{2,1,0:T(8,128)S(1)}, f32[2,64,128]{2,1,0:T(8,128)}, u32[]{:S(2)}) copy-start(f32[2,64,128]{2,1,0:T(8,128)} %constant.23.clone.turn_ref) | copy-start | bytes 196612
  10.9 11.7 %copy-start.6 = (f32[32,128]{1,0:T(8,128)S(1)}, f32[32,128]{1,0:T(8,128)}, u32[]{:S(2)}) copy-start(f32[32,128]{1,0:T(8,128)} %constant.22.clone.window_ref) | copy-start | bytes 49156
  13.6 9.0 %copy-start = (bf16[2,256,256]{2,1,0:T(8,128)(2,1)S(1)}, bf16[2,256,256]{2,1,0:T(8,128)(2,1)}, u32[]{:S(2)}) copy-start(bf16[2,256,256]{2,1,0:T(8,128)(2,1)} %constant.25.clone.inner_ref) | copy-start | bytes 786436
  14.4 8.2 %copy-start.1 = (bf16[2,128,128]{2,1,0:T(8,128)(2,1)S(1)}, bf16[2,128,128]{2,1,0:T(8,128)(2,1)}, u32[]{:S(2)}) copy-start(bf16[2,128,128]{2,1,0:T(8,128)(2,1)} %constant.27.clone.partial_ref) | copy-start | bytes 196612
  14.5 8.1 %copy-start.2 = (bf16[2,128,128]{2,1,0:T(8,128)(2,1)S(1)}, bf16[2,128,128]{2,1,0:T(8,128)(2,1)}, u32[]{:S(2)}) copy-start(bf16[2,128,128]{2,1,0:T(8,128)(2,1)} %constant.26.clone.outer_ref) | copy-start | bytes 196612

commit v13 on v12

--- a/solution.py
+++ b/solution.py
@@ -14,8 +14,8 @@
 CONTRIB = 64
 FACET_ROWS = 8
 SUBGRID = FACET_ROWS * CONTRIB
-SEND_ORDER = tuple(reversed(range(FACET_ROWS)))
-RETURN_ORDER = tuple(reversed(range(FACET_ROWS)))
+SEND_ORDER = (FACET_ROWS - 1, *range(FACET_ROWS - 1))
+PLACE_ORDER = tuple(range(FACET_ROWS))
 LANES = 128
 HALF = LANES // 2
 EARLY_FLOPS = 10**10
@@ -102,6 +102,11 @@
         model=high_low(from_right(phases(short, short, CONTRIB, -1)) * SUBGRID**-0.5),
         back=high_low(from_right(phases(short, short, CONTRIB, 1)) * SUBGRID**-0.5),
     )
+
+
+def return_order(bands):
+    order = [(b, member) for b in range(bands) for member in PLACE_ORDER]
+    return order[-1:] + order[:-1]
 
 
 def split(values):
@@ -328,7 +333,7 @@
             values_ref[t],
         ]
         packed_ref[4 * t : 4 * t + 4, :] = jnp.concatenate(rows, axis=0)
-    places_ref[...] = offsets_on_lanes(offsets_ref, share, RETURN_ORDER)
+    places_ref[...] = offsets_on_lanes(offsets_ref, share, PLACE_ORDER)
     spread_ref[...] = offsets_on_lanes(offsets_ref, strips_ref.shape[1], SEND_ORDER)
 
     @pl.when(in_first_half())
@@ -434,7 +439,7 @@
         for spot in spots:
             for b in range(bands):
                 source = spot * columns + b * share
-                place = (bands - 1 - b) * FACET_ROWS + RETURN_ORDER.index(i)
+                place = return_order(bands).index((b, i))
                 target = (place * len(spots) + spot) * share
                 held_ref[target : target + share, :] = lines[i][source : source + share, :]
     out_ref[...] = held_ref[...].astype(BF16)
@@ -449,9 +454,16 @@
     groups = length // LANES
     pairs = (columns + 1) // 2
     width = pieces_ref.shape[0] // bands
-    summed = pieces_ref[0:width, :].astype(F32)
+    pieces = pieces_ref[...].astype(F32)
+    order, rows = return_order(bands), width // FACET_ROWS
+
+    def of_band(b):
+        begins = [order.index((b, member)) * rows for member in PLACE_ORDER]
+        return jnp.concatenate([pieces[begin : begin + rows, :] for begin in begins], axis=0)
+
+    summed = of_band(0)
     for b in range(1, bands):
-        summed += pieces_ref[b * width : (b + 1) * width, :].astype(F32)
+        summed += of_band(b)
     summed = summed * straight_ref[...] - swap_halves(summed) * crossed_ref[...]
     residues = table_times(partial_ref, summed, ((1,), (1,)))
     kappa = within(iota((2 * CONTRIB, width), 0), CONTRIB)
@@ -601,7 +613,7 @@
     delivered = lax.all_to_all(
         returned, ("band", "member"), split_axis=0, concat_axis=0, tiled=True,
         axis_index_groups=[
-            [b * FACET_ROWS + member for b in reversed(range(bands)) for member in RETURN_ORDER]
+            [b * FACET_ROWS + member for b, member in return_order(bands)]
         ],
     )
     lines = kernel_call(

time: 24.6 us -> 24.1 us (0.980)
  blocking collectives: 8.11 us -> 7.66 us
    all_to_all x1, blocking collectives: 8.11 us -> 7.66 us  [local(): lax.all_to_all(returned, ('band', 'member'), split_axis=0, concat_axis=0,...]
where the time goes in v13:
time: 24.1 us; the launch traced here: 23.8 us
  blocking collectives  7.66 us (32%)
  starting transfers between devices  7.47 us (31%)
  Pallas kernels  6.62 us (27%)
  waiting for transfers between devices  1.86 us (8%)
    all_to_all x1, blocking collectives, local(): lax.all_to_all(returned, ('band', 'member'), split_axis=0, concat_axis=0,...  7.66 us
    pallas_call x5, Pallas kernels, kernel_call(): pl.pallas_call(kernel, out_shape=out_shape, in_specs=[pl.BlockSpec(memory...  6.62 us
    all_to_all x1, starting transfers between devices, local(): lax.all_to_all(pieces, 'member', split_axis=0, concat_axis=0, tiled=True,...  5.05 us
    ppermute x1, starting transfers between devices, local(): gathered.append(lax.ppermute(packed, 'group', moves))  2.42 us
    all_to_all x1, waiting for transfers between devices, local(): lax.all_to_all(pieces, 'member', split_axis=0, concat_axis=0, tiled=True,...  1.85 us
  transfers between devices with their start and end apart: 2, of which 1 were waited for; matrix products, arithmetic and copies ran while one was open for 0% of the time, Pallas kernels for 6%

profile of v13, /device:TPU:0, one launch (start us, length us, event | category | flops | bytes accessed | tf_op | source)
XLA Modules:
  0.0 23.8 jit_solution(2390799026282836350)
XLA Ops:
  0.0 0.0 copy-start.8
  0.0 0.0 copy-start.9
  0.0 0.0 copy-start.10
  0.0 2.6 %early.1 = (bf16[256,128]{1,0:T(8,128)(2,1)S(1)}, f32[8,512]{1,0:T(8,128)S(1)}, s32[1,128]{1,0:T(1,128)S(1)}, s32[1,256]{1,0:T(1,128)S(1)}) custom-call(s32[2,16]{1,0:T(2,128)} %offsets.1, s32[2,2,512]{2,1,0:T(2,128)} %bitcast.15, f32[2,2,512]{2,1,0:T(2,128)} %bitcast.16, f32[2,1,512]{2,1,0:T(1,128)} %bitcast.17, s32[2,1,512]{2,1,0:T(1,128)} %bitcast.18, ...), custom_call_target="tpu_custom_call" | custom-call | flops 10000000000 | tf_op jit(solution)/shard_map/early/pallas_call | solution.py:528
  2.7 2.4 %collective-permute-start = (f32[8,512]{1,0:T(8,128)S(1)}, f32[8,512]{1,0:T(8,128)S(1)}, u32[]{:S(2)}, u32[]{:S(2)}) collective-permute-start(f32[8,512]{1,0:T(8,128)S(1)} %get-tuple-element.17.refs_0_), channel_id=1, source_target_pairs={{16,0},{0,16},{17,1},{1,17},{18,2},{2,18},{19,3},{3,19},{20,4},{4,... | collective-permute-start | bytes 49160 | tf_op jit(solution)/shard_map/ppermute | solution.py:594
  5.1 0.0 copy-done.8
  5.1 0.0 copy-done.9
  5.1 0.0 copy-done.10
  5.1 0.6 %late.1 = bf16[256,128]{1,0:T(8,128)(2,1)} custom-call(bf16[256,128]{1,0:T(8,128)(2,1)S(1)} %get-tuple-element.15.early_ref, s32[1,256]{1,0:T(1,128)S(1)} %get-tuple-element.16.spread_ref, f32[2,8,4096]{2,1,0:T(8,128)S(1)} %bitcast.14, f32[160,128]{1,0:T(8,128)S(1)} %copy-done.10, bf16[1792,128]{1,0:T(8,128)(2,1)S(1)} %copy-done.9), custom_call_target="tpu_custom_call" | custom-call | flops 10000000000 | tf_op jit(solution)/shard_map/late/pallas_call | solution.py:528
  5.7 0.0 copy-start.11
  5.7 5.0 %all-to-all-start = ((bf16[8,32,128]{2,1,0:T(8,128)(2,1)}), bf16[8,32,128]{2,1,0:T(8,128)(2,1)S(1)}, u32[]{:S(2)}, u32[]{:S(2)}) async-start(bf16[8,32,128]{2,1,0:T(8,128)(2,1)} %bitcast.5), calls=%async_computation | async-start | bytes 131072 | tf_op jit(solution)/shard_map/all_to_all | solution.py:595
  10.8 0.0 collective-permute-done.refs_1_
  10.8 0.0 copy-done.11
  10.8 0.0 copy-start.4
  10.8 0.0 copy-start.5
  10.8 0.0 copy-start.7
  10.8 0.0 copy-start.3
  10.8 0.0 copy-start.6
  10.9 0.8 %prepare.1 = (f32[256,128]{1,0:T(8,128)S(1)}, f32[256,128]{1,0:T(8,128)S(1)}, bf16[256,256]{1,0:T(8,128)(2,1)S(1)}, f32[128,128]{1,0:T(8,128)S(1)}, f32[128,128]{1,0:T(8,128)S(1)}) custom-call(s32[1,128]{1,0:T(1,128)S(1)} %get-tuple-element.14.places_ref, bf16[2,64,256]{2,1,0:T(8,128)(2,1)S(1)} %copy-done.11, f32[8,512]{1,0:T(8,128)S(1)} %get-tuple-element.17.refs_0_, ...), custom_call_target="tpu_custom_call" | custom-call | flops 20000000000 | tf_op jit(solution)/shard_map/prepare/pallas_call | solution.py:528
  11.7 1.9 %all-to-all-done = bf16[8,32,128]{2,1,0:T(8,128)(2,1)S(1)} async-done(((bf16[8,32,128]{2,1,0:T(8,128)(2,1)}), bf16[8,32,128]{2,1,0:T(8,128)(2,1)S(1)}, u32[]{:S(2)}, u32[]{:S(2)}) %all-to-all-start) | async-done | bytes 65568 | tf_op jit(solution)/shard_map/all_to_all | solution.py:595
  13.6 0.0 copy-done.4
  13.6 0.0 copy-done.5
  13.6 0.0 copy-done.7
  13.6 0.0 copy-start
  13.6 0.8 %subgrid.1 = bf16[256,128]{1,0:T(8,128)(2,1)S(1)} custom-call(bf16[256,128]{1,0:T(8,128)(2,1)S(1)} %bitcast.11, f32[256,128]{1,0:T(8,128)S(1)} %get-tuple-element.18.value_ref, f32[256,128]{1,0:T(8,128)S(1)} %get-tuple-element.19.weight_ref, f32[2,8,128]{2,1,0:T(8,128)S(1)} %copy-done.7, bf16[2,128,128]{2,1,0:T(8,128)(2,1)S(1)} %copy-done.5, ...), custom_call_target="tpu_custom_call" | custom-call | tf_op jit(solution)/shard_map/subgrid/pallas_call | solution.py:528
  14.4 0.0 copy-start.1
  14.5 0.0 copy-start.2
  14.5 7.7 %all_to_all.22 = bf16[16,16,128]{2,1,0:T(8,128)(2,1)S(1)} all-to-all(bf16[16,16,128]{2,1,0:T(8,128)(2,1)S(1)} %bitcast.12), channel_id=1, replica_groups={{15,0,2,4,6,8,10,12,14,1,3,5,7,9,11,13},{31,16,18,20,22,24,26,28,30,17,..., dimensions={0} | all-to-all | bytes 131072 | tf_op jit(solution)/shard_map/all_to_all | solution.py:613
  22.1 0.0 copy-done.3
  22.1 0.0 copy-done.6
  22.1 0.0 copy-done
  22.1 0.0 copy-done.1
  22.1 0.0 copy-done.2
  22.2 1.6 %lines.1 = f32[4,2,4096]{2,1,0:T(2,128)} custom-call(s32[1,128]{1,0:T(1,128)S(1)} %get-tuple-element.14.places_ref, bf16[256,128]{1,0:T(8,128)(2,1)S(1)} %bitcast.10, f32[128,128]{1,0:T(8,128)S(1)} %get-tuple-element.20.straight_ref, f32[128,128]{1,0:T(8,128)S(1)} %get-tuple-element.21.crossed_ref, bf16[256,256]{1,0:T(8,128)(2,1)S(1)} %get-tuple-element.22.put_ref, ...), custom_call_target="tpu_custom_call" | custom-call | tf_op jit(solution)/shard_map/lines/pallas_call | solution.py:528
Async XLA Ops:
  0.0 5.1 %copy-start.8 = (f32[1,1,2,8,4096]{4,3,2,1,0:T(8,128)S(1)}, f32[1,1,2,8,4096]{4,3,2,1,0:T(8,128)}, u32[]{:S(2)}) copy-start(f32[1,1,2,8,4096]{4,3,2,1,0:T(8,128)} %param.17) | copy-start | bytes 786436
  0.0 5.1 %copy-start.9 = (bf16[1792,128]{1,0:T(8,128)(2,1)S(1)}, bf16[1792,128]{1,0:T(8,128)(2,1)}, u32[]{:S(2)}) copy-start(bf16[1792,128]{1,0:T(8,128)(2,1)} %constant.32.clone.paired_table.paired_ref) | copy-start | bytes 1376260
  0.0 5.1 %copy-start.10 = (f32[160,128]{1,0:T(8,128)S(1)}, f32[160,128]{1,0:T(8,128)}, u32[]{:S(2)}) copy-start(f32[160,128]{1,0:T(8,128)} %constant.31.clone.plain_table.plain_ref) | copy-start | bytes 245764
  2.7 8.1 %collective-permute-start = (f32[8,512]{1,0:T(8,128)S(1)}, f32[8,512]{1,0:T(8,128)S(1)}, u32[]{:S(2)}, u32[]{:S(2)}) collective-permute-start(f32[8,512]{1,0:T(8,128)S(1)} %get-tuple-element.17.refs_0_), channel_id=1, source_target_pairs={{16,0},{0,16},{17,1},{1,17},{18,2},{2,18},{19,3},{3,19},{20,4},{4,... | collective-permute-start | bytes 49160 | tf_op jit(solution)/shard_map/ppermute | solution.py:594
  5.7 5.1 %copy-start.11 = (bf16[2,64,256]{2,1,0:T(8,128)(2,1)S(1)}, bf16[2,64,256]{2,1,0:T(8,128)(2,1)}, u32[]{:S(2)}) copy-start(bf16[2,64,256]{2,1,0:T(8,128)(2,1)} %constant.24.clone.shift_ref) | copy-start | bytes 196612
  5.7 7.8 %all-to-all-start = ((bf16[8,32,128]{2,1,0:T(8,128)(2,1)}), bf16[8,32,128]{2,1,0:T(8,128)(2,1)S(1)}, u32[]{:S(2)}, u32[]{:S(2)}) async-start(bf16[8,32,128]{2,1,0:T(8,128)(2,1)} %bitcast.5), calls=%async_computation | async-start | bytes 131072 | tf_op jit(solution)/shard_map/all_to_all | solution.py:595
  10.8 2.8 %copy-start.4 = (bf16[2,128,128]{2,1,0:T(8,128)(2,1)S(1)}, bf16[2,128,128]{2,1,0:T(8,128)(2,1)}, u32[]{:S(2)}) copy-start(bf16[2,128,128]{2,1,0:T(8,128)(2,1)} %constant.30.clone.back_ref) | copy-start | bytes 196612
  10.8 2.8 %copy-start.5 = (bf16[2,128,128]{2,1,0:T(8,128)(2,1)S(1)}, bf16[2,128,128]{2,1,0:T(8,128)(2,1)}, u32[]{:S(2)}) copy-start(bf16[2,128,128]{2,1,0:T(8,128)(2,1)} %constant.29.clone.model_ref) | copy-start | bytes 196612
  10.8 2.7 %copy-start.7 = (f32[2,8,128]{2,1,0:T(8,128)S(1)}, f32[2,8,128]{2,1,0:T(8,128)}, u32[]{:S(2)}) copy-start(f32[2,8,128]{2,1,0:T(8,128)} %constant.28.clone.turn_ref) | copy-start | bytes 24580
  10.8 11.3 %copy-start.3 = (f32[2,64,128]{2,1,0:T(8,128)S(1)}, f32[2,64,128]{2,1,0:T(8,128)}, u32[]{:S(2)}) copy-start(f32[2,64,128]{2,1,0:T(8,128)} %constant.23.clone.turn_ref) | copy-start | bytes 196612
  10.8 11.3 %copy-start.6 = (f32[32,128]{1,0:T(8,128)S(1)}, f32[32,128]{1,0:T(8,128)}, u32[]{:S(2)}) copy-start(f32[32,128]{1,0:T(8,128)} %constant.22.clone.window_ref) | copy-start | bytes 49156
  13.6 8.6 %copy-start = (bf16[2,256,256]{2,1,0:T(8,128)(2,1)S(1)}, bf16[2,256,256]{2,1,0:T(8,128)(2,1)}, u32[]{:S(2)}) copy-start(bf16[2,256,256]{2,1,0:T(8,128)(2,1)} %constant.25.clone.inner_ref) | copy-start | bytes 786436
  14.4 7.7 %copy-start.1 = (bf16[2,128,128]{2,1,0:T(8,128)(2,1)S(1)}, bf16[2,128,128]{2,1,0:T(8,128)(2,1)}, u32[]{:S(2)}) copy-start(bf16[2,128,128]{2,1,0:T(8,128)(2,1)} %constant.27.clone.partial_ref) | copy-start | bytes 196612
  14.5 7.7 %copy-start.2 = (bf16[2,128,128]{2,1,0:T(8,128)(2,1)S(1)}, bf16[2,128,128]{2,1,0:T(8,128)(2,1)}, u32[]{:S(2)}) copy-start(bf16[2,128,128]{2,1,0:T(8,128)(2,1)} %constant.26.clone.outer_ref) | copy-start | bytes 196612

commit v14 on v13

--- a/solution.py
+++ b/solution.py
@@ -14,7 +14,7 @@
 CONTRIB = 64
 FACET_ROWS = 8
 SUBGRID = FACET_ROWS * CONTRIB
-SEND_ORDER = (FACET_ROWS - 1, *range(FACET_ROWS - 1))
+SEND_ORDER = tuple(FACET_ROWS - 1 - (i ^ (i >> 1)) for i in range(FACET_ROWS))
 PLACE_ORDER = tuple(range(FACET_ROWS))
 LANES = 128
 HALF = LANES // 2
@@ -105,8 +105,8 @@
 
 
 def return_order(bands):
-    order = [(b, member) for b in range(bands) for member in PLACE_ORDER]
-    return order[-1:] + order[:-1]
+    last = bands * FACET_ROWS - 1
+    return [divmod(last - (i ^ (i >> 1)), FACET_ROWS) for i in range(last + 1)]
 
 
 def split(values):
@@ -306,12 +306,6 @@
     offsets_ref, cells_ref, values_ref, weights_ref, flags_ref, strips_ref, plain_ref, paired_ref,
     real_ref, imag_ref, small_semaphores, semaphores, *, plain, paired, share,
 ):
-    small = start_all(
-        (offsets, cells, values, weights, flags),
-        (offsets_ref, cells_ref, values_ref, weights_ref, flags_ref),
-        small_semaphores,
-    )
-
     def large():
         sources, targets = (strips, plain_table, paired_table), (strips_ref, plain_ref, paired_ref)
         return [
@@ -324,6 +318,11 @@
         for copy in large():
             copy.start()
 
+    small = start_all(
+        (offsets, cells, values, weights, flags),
+        (offsets_ref, cells_ref, values_ref, weights_ref, flags_ref),
+        small_semaphores,
+    )
     for copy in small:
         copy.wait()
     for t in range(cells_ref.shape[0]):
@@ -447,7 +446,7 @@
 
 def return_kernel(
     places_ref, pieces_ref, straight_ref, crossed_ref, put_ref, window_ref, turn_ref, partial_ref,
-    inner_ref, outer_ref, out_ref, *line_refs, bands,
+    inner_ref, outer_ref, result, out_ref, semaphores, *line_refs, bands,
 ):
     columns, _, length = out_ref.shape
     blocks = length // CONTRIB
@@ -504,32 +503,43 @@
     )
     window = window_ref[...]
     low_half = iota((groups, LANES), 1) < HALF
-    for part in range(2):
-        for pair in range(pairs):
-            lanes = slice(pair * LANES, (pair + 1) * LANES)
+    copies = []
+    for pair in range(pairs):
+        lanes = slice(pair * LANES, (pair + 1) * LANES)
+        held = [column for column in (2 * pair, 2 * pair + 1) if column < columns]
+        for part in range(2):
             begin = part * blocks
             even = lines[begin : begin + groups, lanes]
             odd = lines[begin + groups : begin + blocks, lanes]
-            line_refs[2 * pair][pl.ds(part, groups, stride=2), :] = (
-                jnp.where(low_half, even, swap_halves(odd)) * window
+            both = (
+                jnp.where(low_half, even, swap_halves(odd)),
+                jnp.where(low_half, swap_halves(even), odd),
             )
-            if 2 * pair + 1 < columns:
-                line_refs[2 * pair + 1][pl.ds(part, groups, stride=2), :] = (
-                    jnp.where(low_half, swap_halves(even), odd) * window
+            for column, line in zip(held, both):
+                line_refs[column][pl.ds(part, groups, stride=2), :] = line * window
+        for column in held:
+            for group in range(groups):
+                out_ref[column, :, group * LANES : (group + 1) * LANES] = line_refs[column][
+                    2 * group : 2 * group + 2, :
+                ]
+            copies.append(
+                pltpu.make_async_copy(
+                    out_ref.at[column], result.at[column], semaphores.at[column]
                 )
-    for column in range(columns):
-        for group in range(groups):
-            out_ref[column, :, group * LANES : (group + 1) * LANES] = line_refs[column][
-                2 * group : 2 * group + 2, :
-            ]
-
-
-def kernel_call(kernel, name, out_shape, spaces, scratch, *operands, flops=0):
+            )
+            copies[-1].start()
+    for copy in copies:
+        copy.wait()
+
+
+def kernel_call(
+    kernel, name, out_shape, spaces, scratch, *operands, flops=0, out_space=pltpu.VMEM
+):
     return pl.pallas_call(
         kernel,
         out_shape=out_shape,
         in_specs=[pl.BlockSpec(memory_space=space) for space in spaces],
-        out_specs=jax.tree.map(lambda _: pl.BlockSpec(memory_space=pltpu.VMEM), out_shape),
+        out_specs=jax.tree.map(lambda _: pl.BlockSpec(memory_space=out_space), out_shape),
         scratch_shapes=scratch,
         compiler_params=pltpu.CompilerParams(vmem_limit_bytes=VMEM_LIMIT),
         cost_estimate=pl.CostEstimate(flops=flops, bytes_accessed=0, transcendentals=0)
@@ -619,9 +629,10 @@
     lines = kernel_call(
         functools.partial(return_kernel, bands=bands), "lines",
         jax.ShapeDtypeStruct((share, 2, length), F32), [pltpu.VMEM] * 10,
-        [wide(2 * length // LANES)] * share,
+        [pltpu.VMEM((share, 2, length), F32), semaphores(share)]
+        + [wide(2 * length // LANES)] * share,
         places, delivered, straight, crossed, put, made["window"], made["turn"],
-        made["partial"], made["inner_plus"], made["outer_plus"],
+        made["partial"], made["inner_plus"], made["outer_plus"], out_space=pltpu.HBM,
     )
     return lines[None]
 

time: 24.1 us -> 24.4 us (1.012)
  no operation moved by 1% of the time
where the time goes in v14:
time: 24.4 us; the launch traced here: 24 us
  blocking collectives  7.71 us (32%)
  starting transfers between devices  7.52 us (31%)
  Pallas kernels  6.64 us (27%)
  waiting for transfers between devices  1.98 us (8%)
    all_to_all x1, blocking collectives, local(): lax.all_to_all(returned, ('band', 'member'), split_axis=0, concat_axis=0,...  7.71 us
    pallas_call x5, Pallas kernels, kernel_call(): pl.pallas_call(kernel, out_shape=out_shape, in_specs=[pl.BlockSpec(memory...  6.64 us
    all_to_all x1, starting transfers between devices, local(): lax.all_to_all(pieces, 'member', split_axis=0, concat_axis=0, tiled=True,...  5.1 us
    ppermute x1, starting transfers between devices, local(): gathered.append(lax.ppermute(packed, 'group', moves))  2.42 us
    all_to_all x1, waiting for transfers between devices, local(): lax.all_to_all(pieces, 'member', split_axis=0, concat_axis=0, tiled=True,...  1.98 us
  transfers between devices with their start and end apart: 2, of which 1 were waited for; matrix products, arithmetic and copies ran while one was open for 0% of the time, Pallas kernels for 6%

profile of v14, /device:TPU:0, one launch (start us, length us, event | category | flops | bytes accessed | tf_op | source)
XLA Modules:
  0.0 24.0 jit_solution(16073855858309378731)
XLA Ops:
  0.0 0.0 copy-start.8
  0.0 0.0 copy-start.9
  0.0 0.0 copy-start.10
  0.0 2.6 %early.1 = (bf16[256,128]{1,0:T(8,128)(2,1)S(1)}, f32[8,512]{1,0:T(8,128)S(1)}, s32[1,128]{1,0:T(1,128)S(1)}, s32[1,256]{1,0:T(1,128)S(1)}) custom-call(s32[2,16]{1,0:T(2,128)} %offsets.1, s32[2,2,512]{2,1,0:T(2,128)} %bitcast.15, f32[2,2,512]{2,1,0:T(2,128)} %bitcast.16, f32[2,1,512]{2,1,0:T(1,128)} %bitcast.17, s32[2,1,512]{2,1,0:T(1,128)} %bitcast.18, ...), custom_call_target="tpu_custom_call" | custom-call | flops 10000000000 | tf_op jit(solution)/shard_map/early/pallas_call | solution.py:538
  2.7 2.4 %collective-permute-start = (f32[8,512]{1,0:T(8,128)S(1)}, f32[8,512]{1,0:T(8,128)S(1)}, u32[]{:S(2)}, u32[]{:S(2)}) collective-permute-start(f32[8,512]{1,0:T(8,128)S(1)} %get-tuple-element.17.refs_0_), channel_id=1, source_target_pairs={{16,0},{0,16},{17,1},{1,17},{18,2},{2,18},{19,3},{3,19},{20,4},{4,... | collective-permute-start | bytes 49160 | tf_op jit(solution)/shard_map/ppermute | solution.py:604
  5.1 0.0 copy-done.8
  5.1 0.0 copy-done.9
  5.1 0.0 copy-done.10
  5.1 0.6 %late.1 = bf16[256,128]{1,0:T(8,128)(2,1)} custom-call(bf16[256,128]{1,0:T(8,128)(2,1)S(1)} %get-tuple-element.15.early_ref, s32[1,256]{1,0:T(1,128)S(1)} %get-tuple-element.16.spread_ref, f32[2,8,4096]{2,1,0:T(8,128)S(1)} %bitcast.14, f32[160,128]{1,0:T(8,128)S(1)} %copy-done.10, bf16[1792,128]{1,0:T(8,128)(2,1)S(1)} %copy-done.9), custom_call_target="tpu_custom_call" | custom-call | flops 10000000000 | tf_op jit(solution)/shard_map/late/pallas_call | solution.py:538
  5.7 0.0 copy-start.11
  5.7 5.1 %all-to-all-start = ((bf16[8,32,128]{2,1,0:T(8,128)(2,1)}), bf16[8,32,128]{2,1,0:T(8,128)(2,1)S(1)}, u32[]{:S(2)}, u32[]{:S(2)}) async-start(bf16[8,32,128]{2,1,0:T(8,128)(2,1)} %bitcast.5), calls=%async_computation | async-start | bytes 131072 | tf_op jit(solution)/shard_map/all_to_all | solution.py:605
  10.8 0.0 collective-permute-done.refs_1_
  10.8 0.0 copy-done.11
  10.9 0.0 copy-start.4
  10.9 0.0 copy-start.5
  10.9 0.0 copy-start.7
  10.9 0.0 copy-start.3
  10.9 0.0 copy-start.6
  10.9 0.8 %prepare.1 = (f32[256,128]{1,0:T(8,128)S(1)}, f32[256,128]{1,0:T(8,128)S(1)}, bf16[256,256]{1,0:T(8,128)(2,1)S(1)}, f32[128,128]{1,0:T(8,128)S(1)}, f32[128,128]{1,0:T(8,128)S(1)}) custom-call(s32[1,128]{1,0:T(1,128)S(1)} %get-tuple-element.14.places_ref, bf16[2,64,256]{2,1,0:T(8,128)(2,1)S(1)} %copy-done.11, f32[8,512]{1,0:T(8,128)S(1)} %get-tuple-element.17.refs_0_, ...), custom_call_target="tpu_custom_call" | custom-call | flops 20000000000 | tf_op jit(solution)/shard_map/prepare/pallas_call | solution.py:538
  11.8 2.0 %all-to-all-done = bf16[8,32,128]{2,1,0:T(8,128)(2,1)S(1)} async-done(((bf16[8,32,128]{2,1,0:T(8,128)(2,1)}), bf16[8,32,128]{2,1,0:T(8,128)(2,1)S(1)}, u32[]{:S(2)}, u32[]{:S(2)}) %all-to-all-start) | async-done | bytes 65568 | tf_op jit(solution)/shard_map/all_to_all | solution.py:605
  13.7 0.0 copy-done.4
  13.7 0.0 copy-done.5
  13.7 0.0 copy-done.7
  13.7 0.0 copy-start
  13.8 0.8 %subgrid.1 = bf16[256,128]{1,0:T(8,128)(2,1)S(1)} custom-call(bf16[256,128]{1,0:T(8,128)(2,1)S(1)} %bitcast.11, f32[256,128]{1,0:T(8,128)S(1)} %get-tuple-element.18.value_ref, f32[256,128]{1,0:T(8,128)S(1)} %get-tuple-element.19.weight_ref, f32[2,8,128]{2,1,0:T(8,128)S(1)} %copy-done.7, bf16[2,128,128]{2,1,0:T(8,128)(2,1)S(1)} %copy-done.5, ...), custom_call_target="tpu_custom_call" | custom-call | tf_op jit(solution)/shard_map/subgrid/pallas_call | solution.py:538
  14.6 0.0 copy-start.1
  14.6 0.0 copy-start.2
  14.6 7.7 %all_to_all.22 = bf16[16,16,128]{2,1,0:T(8,128)(2,1)S(1)} all-to-all(bf16[16,16,128]{2,1,0:T(8,128)(2,1)S(1)} %bitcast.12), channel_id=1, replica_groups={{15,13,9,11,3,1,5,7,6,4,0,2,10,8,12,14},{31,29,25,27,19,17,21,23,22,20,..., dimensions={0} | all-to-all | bytes 131072 | tf_op jit(solution)/shard_map/all_to_all | solution.py:623
  22.3 0.0 copy-done.3
  22.4 0.0 copy-done.6
  22.4 0.0 copy-done
  22.4 0.0 copy-done.1
  22.4 0.0 copy-done.2
  22.4 1.7 %lines.1 = f32[4,2,4096]{2,1,0:T(2,128)} custom-call(s32[1,128]{1,0:T(1,128)S(1)} %get-tuple-element.14.places_ref, bf16[256,128]{1,0:T(8,128)(2,1)S(1)} %bitcast.10, f32[128,128]{1,0:T(8,128)S(1)} %get-tuple-element.20.straight_ref, f32[128,128]{1,0:T(8,128)S(1)} %get-tuple-element.21.crossed_ref, bf16[256,256]{1,0:T(8,128)(2,1)S(1)} %get-tuple-element.22.put_ref, ...), custom_call_target="tpu_custom_call" | custom-call | tf_op jit(solution)/shard_map/lines/pallas_call | solution.py:538
Async XLA Ops:
  0.0 5.1 %copy-start.8 = (f32[1,1,2,8,4096]{4,3,2,1,0:T(8,128)S(1)}, f32[1,1,2,8,4096]{4,3,2,1,0:T(8,128)}, u32[]{:S(2)}) copy-start(f32[1,1,2,8,4096]{4,3,2,1,0:T(8,128)} %param.17) | copy-start | bytes 786436
  0.0 5.1 %copy-start.9 = (bf16[1792,128]{1,0:T(8,128)(2,1)S(1)}, bf16[1792,128]{1,0:T(8,128)(2,1)}, u32[]{:S(2)}) copy-start(bf16[1792,128]{1,0:T(8,128)(2,1)} %constant.32.clone.paired_table.paired_ref) | copy-start | bytes 1376260
  0.0 5.1 %copy-start.10 = (f32[160,128]{1,0:T(8,128)S(1)}, f32[160,128]{1,0:T(8,128)}, u32[]{:S(2)}) copy-start(f32[160,128]{1,0:T(8,128)} %constant.31.clone.plain_table.plain_ref) | copy-start | bytes 245764
  2.7 8.2 %collective-permute-start = (f32[8,512]{1,0:T(8,128)S(1)}, f32[8,512]{1,0:T(8,128)S(1)}, u32[]{:S(2)}, u32[]{:S(2)}) collective-permute-start(f32[8,512]{1,0:T(8,128)S(1)} %get-tuple-element.17.refs_0_), channel_id=1, source_target_pairs={{16,0},{0,16},{17,1},{1,17},{18,2},{2,18},{19,3},{3,19},{20,4},{4,... | collective-permute-start | bytes 49160 | tf_op jit(solution)/shard_map/ppermute | solution.py:604
  5.7 5.1 %copy-start.11 = (bf16[2,64,256]{2,1,0:T(8,128)(2,1)S(1)}, bf16[2,64,256]{2,1,0:T(8,128)(2,1)}, u32[]{:S(2)}) copy-start(bf16[2,64,256]{2,1,0:T(8,128)(2,1)} %constant.24.clone.shift_ref) | copy-start | bytes 196612
  5.7 8.0 %all-to-all-start = ((bf16[8,32,128]{2,1,0:T(8,128)(2,1)}), bf16[8,32,128]{2,1,0:T(8,128)(2,1)S(1)}, u32[]{:S(2)}, u32[]{:S(2)}) async-start(bf16[8,32,128]{2,1,0:T(8,128)(2,1)} %bitcast.5), calls=%async_computation | async-start | bytes 131072 | tf_op jit(solution)/shard_map/all_to_all | solution.py:605
  10.9 2.9 %copy-start.4 = (bf16[2,128,128]{2,1,0:T(8,128)(2,1)S(1)}, bf16[2,128,128]{2,1,0:T(8,128)(2,1)}, u32[]{:S(2)}) copy-start(bf16[2,128,128]{2,1,0:T(8,128)(2,1)} %constant.30.clone.back_ref) | copy-start | bytes 196612
  10.9 2.9 %copy-start.5 = (bf16[2,128,128]{2,1,0:T(8,128)(2,1)S(1)}, bf16[2,128,128]{2,1,0:T(8,128)(2,1)}, u32[]{:S(2)}) copy-start(bf16[2,128,128]{2,1,0:T(8,128)(2,1)} %constant.29.clone.model_ref) | copy-start | bytes 196612
  10.9 2.9 %copy-start.7 = (f32[2,8,128]{2,1,0:T(8,128)S(1)}, f32[2,8,128]{2,1,0:T(8,128)}, u32[]{:S(2)}) copy-start(f32[2,8,128]{2,1,0:T(8,128)} %constant.28.clone.turn_ref) | copy-start | bytes 24580
  10.9 11.5 %copy-start.3 = (f32[2,64,128]{2,1,0:T(8,128)S(1)}, f32[2,64,128]{2,1,0:T(8,128)}, u32[]{:S(2)}) copy-start(f32[2,64,128]{2,1,0:T(8,128)} %constant.23.clone.turn_ref) | copy-start | bytes 196612
  10.9 11.5 %copy-start.6 = (f32[32,128]{1,0:T(8,128)S(1)}, f32[32,128]{1,0:T(8,128)}, u32[]{:S(2)}) copy-start(f32[32,128]{1,0:T(8,128)} %constant.22.clone.window_ref) | copy-start | bytes 49156
  13.7 8.6 %copy-start = (bf16[2,256,256]{2,1,0:T(8,128)(2,1)S(1)}, bf16[2,256,256]{2,1,0:T(8,128)(2,1)}, u32[]{:S(2)}) copy-start(bf16[2,256,256]{2,1,0:T(8,128)(2,1)} %constant.25.clone.inner_ref) | copy-start | bytes 786436
  14.6 7.8 %copy-start.1 = (bf16[2,128,128]{2,1,0:T(8,128)(2,1)S(1)}, bf16[2,128,128]{2,1,0:T(8,128)(2,1)}, u32[]{:S(2)}) copy-start(bf16[2,128,128]{2,1,0:T(8,128)(2,1)} %constant.27.clone.partial_ref) | copy-start | bytes 196612
  14.6 7.7 %copy-start.2 = (bf16[2,128,128]{2,1,0:T(8,128)(2,1)S(1)}, bf16[2,128,128]{2,1,0:T(8,128)(2,1)}, u32[]{:S(2)}) copy-start(bf16[2,128,128]{2,1,0:T(8,128)(2,1)} %constant.26.clone.outer_ref) | copy-start | bytes 196612

commit v15 on v13

--- a/solution.py
+++ b/solution.py
@@ -160,18 +160,23 @@
 def offsets_on_lanes(offsets_ref, columns, order):
     fronts, owners = offsets_ref.shape
     groups = owners // FACET_ROWS
-    own = lax.axis_index("group")
-    begins = []
-    for step in range(groups):
-        group = own + step
-        begins.append(jnp.where(group >= groups, group - groups, group) * FACET_ROWS)
-    spread = iota((1, fronts * owners * columns), 1)
-    place_of = over(spread, columns)
-    for place in range(fronts * owners):
-        t, step, spot = place % fronts, place // fronts % groups, place // (fronts * groups)
-        member = order[spot]
-        spread = jnp.where(place_of == place, offsets_ref[t, begins[step] + member], spread)
-    return spread
+    place = over(iota((1, fronts * owners * columns), 1), columns)
+    front = within(place, fronts)
+    group = within(over(place, fronts) + lax.axis_index("group"), groups)
+    spot = over(place, fronts * groups)
+    member = jnp.zeros_like(spot)
+    for i, value in enumerate(order):
+        member = jnp.where(spot == i, value, member)
+    owner = group * FACET_ROWS + member
+    pick = one_hot((owners, place.shape[1]), owner)
+    offsets = offsets_ref[...]
+    blocks = dot(over(offsets, CONTRIB).astype(F32).astype(BF16), pick)
+    residues = dot(within(offsets, CONTRIB).astype(F32).astype(BF16), pick)
+    spread = jnp.zeros_like(place, dtype=F32)
+    for t in range(fronts):
+        here = blocks[t : t + 1, :] * CONTRIB + residues[t : t + 1, :]
+        spread = jnp.where(front == t, here, spread)
+    return spread.astype(jnp.int32)
 
 
 def shift_rows(residue, table):
@@ -234,10 +239,11 @@
     blocks = length // CONTRIB
     width = spread.shape[1]
     first_block, residue = over(spread, CONTRIB), within(spread, CONTRIB)
-    base = within(iota(spread.shape, 1), columns) * blocks
-    shape = (columns * blocks, width)
-    pick_inside = one_hot(shape, base + first_block)
-    pick_beyond = one_hot(shape, base + within(first_block + 1, blocks))
+    column = within(iota(spread.shape, 1), columns)
+    kappa = iota((CONTRIB, width), 0)
+    block = within(first_block + jnp.where(kappa < residue, 1, 0), blocks)
+    source = within(column, 2) * blocks + block
+    pair_of = over(column, 2)
     for copy in copies[:2]:
         copy.wait()
 
@@ -274,23 +280,22 @@
             )
         )
     inner = times_table(jnp.concatenate(turned, axis=0), pair_at("inner"))
-    spectrum = jnp.concatenate(
-        [
-            jnp.concatenate(
-                [
-                    inner[pair * CONTRIB : (pair + 1) * CONTRIB, part * LANES : (part + 1) * LANES]
-                    for pair in range(pairs)
-                ],
-                axis=1,
-            )
-            for part in range(2)
-        ],
-        axis=0,
-    )
-    inside = dot_split(spectrum, pick_inside)
-    beyond = dot_split(spectrum, pick_beyond)
-    kappa = within(iota((2 * CONTRIB, width), 0), CONTRIB)
-    cutout = jnp.where(kappa >= residue, inside, beyond)
+    cutouts = []
+    for part in range(2):
+        tiles = []
+        for tile in range(width // LANES):
+            lanes = slice(tile * LANES, (tile + 1) * LANES)
+            chosen = None
+            for pair in range(pairs):
+                rows = inner[pair * CONTRIB : (pair + 1) * CONTRIB, part * LANES : (part + 1) * LANES]
+                found = jnp.take_along_axis(
+                    rows, source[:, lanes], axis=1, mode="promise_in_bounds"
+                )
+                here = pair_of[:, lanes] == pair
+                chosen = found if chosen is None else jnp.where(here, found, chosen)
+            tiles.append(chosen)
+        cutouts.append(jnp.concatenate(tiles, axis=1))
+    cutout = jnp.concatenate(cutouts, axis=0)
     piece = times_table(cutout.T, pair_at("piece"))
     straight, crossed = shift_rows(residue, pair_at("shift"))
     out_ref[...] = (piece * straight + swap_halves(piece) * crossed).astype(BF16)
@@ -301,19 +306,19 @@
 
 
 def early_kernel(
-    offsets, cells, values, weights, flags, strips, plain_table, paired_table,
-    out_ref, packed_ref, places_ref, spread_ref,
-    offsets_ref, cells_ref, values_ref, weights_ref, flags_ref, strips_ref, plain_ref, paired_ref,
-    real_ref, imag_ref, small_semaphores, semaphores, *, plain, paired, share,
+    cells, values, weights, flags, offsets, strips, plain_table, paired_table, out_ref, packed_ref,
+    cells_ref, values_ref, weights_ref, flags_ref, offsets_ref, strips_ref, plain_ref, paired_ref,
+    real_ref, imag_ref, small_semaphores, semaphores, *, plain, paired,
 ):
     small = start_all(
-        (offsets, cells, values, weights, flags),
-        (offsets_ref, cells_ref, values_ref, weights_ref, flags_ref),
+        (cells, values, weights, flags),
+        (cells_ref, values_ref, weights_ref, flags_ref),
         small_semaphores,
     )
 
     def large():
-        sources, targets = (strips, plain_table, paired_table), (strips_ref, plain_ref, paired_ref)
+        sources = (offsets, strips, plain_table, paired_table)
+        targets = (offsets_ref, strips_ref, plain_ref, paired_ref)
         return [
             pltpu.make_async_copy(source, target, semaphores.at[i])
             for i, (source, target) in enumerate(zip(sources, targets))
@@ -333,19 +338,19 @@
             values_ref[t],
         ]
         packed_ref[4 * t : 4 * t + 4, :] = jnp.concatenate(rows, axis=0)
-    places_ref[...] = offsets_on_lanes(offsets_ref, share, PLACE_ORDER)
-    spread_ref[...] = offsets_on_lanes(offsets_ref, strips_ref.shape[1], SEND_ORDER)
 
     @pl.when(in_first_half())
     def _():
+        copies = large()
+        copies[0].wait()
         predict(
-            spread_ref[...], large(), strips_ref, plain_ref, paired_ref, (real_ref, imag_ref),
-            out_ref, plain, paired,
+            offsets_on_lanes(offsets_ref, strips_ref.shape[1], SEND_ORDER), copies[1:],
+            strips_ref, plain_ref, paired_ref, (real_ref, imag_ref), out_ref, plain, paired,
         )
 
 
 def late_kernel(
-    early_ref, spread_ref, strips_ref, plain_ref, paired_ref, out_ref, real_ref, imag_ref,
+    early_ref, offsets_ref, strips_ref, plain_ref, paired_ref, out_ref, real_ref, imag_ref,
     *, plain, paired,
 ):
     @pl.when(in_first_half())
@@ -355,14 +360,14 @@
     @pl.when(jnp.logical_not(in_first_half()))
     def _():
         predict(
-            spread_ref[...], (), strips_ref, plain_ref, paired_ref, (real_ref, imag_ref), out_ref,
-            plain, paired,
+            offsets_on_lanes(offsets_ref, strips_ref.shape[1], SEND_ORDER), (),
+            strips_ref, plain_ref, paired_ref, (real_ref, imag_ref), out_ref, plain, paired,
         )
 
 
-def prepare_kernel(places_ref, shift_ref, *refs, columns, share, blocks):
-    samples_refs, outs = refs[:-5], refs[-5:]
-    value_ref, weight_ref, put_ref, straight_ref, crossed_ref = outs
+def prepare_kernel(offsets_ref, shift_ref, *refs, columns, share, blocks):
+    samples_refs, outs = refs[:-6], refs[-6:]
+    value_ref, weight_ref, put_ref, straight_ref, crossed_ref, places_ref = outs
     fronts, samples = samples_refs[0].shape[0] // 4, samples_refs[0].shape[1]
     own = lax.axis_index("group")
     depth = FACET_ROWS * columns
@@ -388,7 +393,8 @@
         rows = slice(spot * depth, (spot + 1) * depth)
         value_ref[rows, :] = grid[:, :LANES]
         weight_ref[rows, :] = grid[:, LANES:]
-    spread = places_ref[...]
+    spread = offsets_on_lanes(offsets_ref, share, PLACE_ORDER)
+    places_ref[...] = spread
     first_block, residue = over(spread, CONTRIB), within(spread, CONTRIB)
     straight_ref[...], crossed_ref[...] = shift_rows(residue, shift_ref)
     base = within(iota(spread.shape, 1), share) * blocks
@@ -555,14 +561,11 @@
     paired, paired_places = made.pop("paired")
     made = {key: jnp.asarray(value) for key, value in made.items()}
     held = length // LANES * columns
-    small = [offsets, cells[0, :, 0], values[0, :, 0], weights[0], flags[0]]
+    small = [cells[0, :, 0], values[0, :, 0], weights[0], flags[0]]
     large = [strips[0, 0], jnp.asarray(plain), jnp.asarray(paired)]
 
     def landing(arrays):
-        return [
-            (pltpu.SMEM if array is offsets else pltpu.VMEM)(array.shape, array.dtype)
-            for array in arrays
-        ]
+        return [pltpu.VMEM(array.shape, array.dtype) for array in arrays]
 
     def in_hbm(arrays):
         return [pltpu.with_memory_space_constraint(array, pltpu.HBM) for array in arrays]
@@ -570,23 +573,20 @@
     def semaphores(count):
         return pltpu.SemaphoreType.DMA((count,))
 
-    early, packed, places, spread = kernel_call(
-        functools.partial(early_kernel, plain=plain_places, paired=paired_places, share=share),
-        "early",
+    early, packed = kernel_call(
+        functools.partial(early_kernel, plain=plain_places, paired=paired_places), "early",
         [
             jax.ShapeDtypeStruct((rows, LANES), BF16),
             jax.ShapeDtypeStruct((4 * fronts, cells.shape[-1]), F32),
-            jax.ShapeDtypeStruct((1, width), jnp.int32),
-            jax.ShapeDtypeStruct((1, rows), jnp.int32),
         ],
         [pltpu.HBM] * 8,
-        landing(small + large) + [wide(held)] * 2 + [semaphores(5), semaphores(3)],
-        *in_hbm(small + large), flops=EARLY_FLOPS,
+        landing(small + [offsets] + large) + [wide(held)] * 2 + [semaphores(4), semaphores(4)],
+        *in_hbm(small + [offsets] + large), flops=EARLY_FLOPS,
     )
     pieces = kernel_call(
         functools.partial(late_kernel, plain=plain_places, paired=paired_places), "late",
         jax.ShapeDtypeStruct((rows, LANES), BF16), [pltpu.VMEM] * 5, [wide(held)] * 2,
-        early, spread, *large, flops=LATE_FLOPS,
+        early, offsets, *large, flops=LATE_FLOPS,
     )
     gathered = [packed]
     for step in range(1, groups):
@@ -597,13 +597,14 @@
         axis_index_groups=[list(SEND_ORDER)],
     )
     blocks = length // CONTRIB
-    value, weight, put, straight, crossed = kernel_call(
+    value, weight, put, straight, crossed, places = kernel_call(
         functools.partial(prepare_kernel, columns=columns, share=share, blocks=blocks), "prepare",
         [jax.ShapeDtypeStruct((rows, LANES), F32)] * 2
         + [jax.ShapeDtypeStruct(((share + share % 2) * blocks, 2 * width), BF16)]
-        + [jax.ShapeDtypeStruct((width, LANES), F32)] * 2,
+        + [jax.ShapeDtypeStruct((width, LANES), F32)] * 2
+        + [jax.ShapeDtypeStruct((1, width), jnp.int32)],
         [pltpu.VMEM] * (2 + len(gathered)), [],
-        places, made["shift"], *gathered, flops=PREPARE_FLOPS,
+        offsets, made["shift"], *gathered, flops=PREPARE_FLOPS,
     )
     returned = kernel_call(
         functools.partial(subgrid_kernel, columns=columns, bands=bands), "subgrid",

time: 24.1 us -> 24.1 us (level)
  transfers between devices with their start and end apart: 2 -> 2, of which waited for: 1 -> 1; matrix products, arithmetic and copies ran while one was open for 0% -> 0% of each run, Pallas kernels for 6% -> 7%
where the time goes in v15:
time: 24.1 us; the launch traced here: 23.8 us
  blocking collectives  7.7 us (32%)
  starting transfers between devices  7.41 us (31%)
  Pallas kernels  6.86 us (28%)
  waiting for transfers between devices  1.62 us (7%)
    all_to_all x1, blocking collectives, local(): lax.all_to_all(returned, ('band', 'member'), split_axis=0, concat_axis=0,...  7.7 us
    pallas_call x5, Pallas kernels, kernel_call(): pl.pallas_call(kernel, out_shape=out_shape, in_specs=[pl.BlockSpec(memory...  6.86 us
    all_to_all x1, starting transfers between devices, local(): lax.all_to_all(pieces, 'member', split_axis=0, concat_axis=0, tiled=True,...  5.09 us
    ppermute x1, starting transfers between devices, local(): gathered.append(lax.ppermute(packed, 'group', moves))  2.33 us
    all_to_all x1, waiting for transfers between devices, local(): lax.all_to_all(pieces, 'member', split_axis=0, concat_axis=0, tiled=True,...  1.62 us
  transfers between devices with their start and end apart: 2, of which 1 were waited for; matrix products, arithmetic and copies ran while one was open for 0% of the time, Pallas kernels for 7%

profile of v15, /device:TPU:0, one launch (start us, length us, event | category | flops | bytes accessed | tf_op | source)
XLA Modules:
  0.0 23.8 jit_solution(5202005293838624000)
XLA Ops:
  0.0 0.0 copy-start.8
  0.0 0.0 copy-start.10
  0.0 0.0 copy-start.11
  0.0 2.7 %early.1 = (bf16[256,128]{1,0:T(8,128)(2,1)S(1)}, f32[8,512]{1,0:T(8,128)S(1)}) custom-call(s32[2,2,512]{2,1,0:T(2,128)} %bitcast.15, f32[2,2,512]{2,1,0:T(2,128)} %bitcast.16, f32[2,1,512]{2,1,0:T(1,128)} %bitcast.17, s32[2,1,512]{2,1,0:T(1,128)} %bitcast.18, s32[2,16]{1,0:T(2,128)} %offsets_ref.3, f32[2,8,4096]{2,1,0:T(8,128)} %bitcast.13, ...), custom_call_target="tpu_custom_call" | custom-call | flops 10000000000 | tf_op jit(solution)/shard_map/early/pallas_call | solution.py:534
  2.7 0.0 copy-start.9
  2.7 2.3 %collective-permute-start = (f32[8,512]{1,0:T(8,128)S(1)}, f32[8,512]{1,0:T(8,128)S(1)}, u32[]{:S(2)}, u32[]{:S(2)}) collective-permute-start(f32[8,512]{1,0:T(8,128)S(1)} %get-tuple-element.13.refs_0_), channel_id=1, source_target_pairs={{16,0},{0,16},{17,1},{1,17},{18,2},{2,18},{19,3},{3,19},{20,4},{4,... | collective-permute-start | bytes 49160 | tf_op jit(solution)/shard_map/ppermute | solution.py:594
  5.0 0.0 copy-done.8
  5.0 0.0 copy-done.10
  5.0 0.0 copy-done.11
  5.0 0.0 copy-done.9
  5.0 0.7 %late.1 = bf16[256,128]{1,0:T(8,128)(2,1)} custom-call(bf16[256,128]{1,0:T(8,128)(2,1)S(1)} %get-tuple-element.15.early_ref, s32[2,16]{1,0:T(2,128)S(1)} %copy-done.9, f32[2,8,4096]{2,1,0:T(8,128)S(1)} %bitcast.14, f32[160,128]{1,0:T(8,128)S(1)} %copy-done.11, bf16[1792,128]{1,0:T(8,128)(2,1)S(1)} %copy-done.10), custom_call_target="tpu_custom_call" | custom-call | flops 10000000000 | tf_op jit(solution)/shard_map/late/pallas_call | solution.py:534
  5.7 0.0 copy-start.12
  5.7 5.1 %all-to-all-start = ((bf16[8,32,128]{2,1,0:T(8,128)(2,1)}), bf16[8,32,128]{2,1,0:T(8,128)(2,1)S(1)}, u32[]{:S(2)}, u32[]{:S(2)}) async-start(bf16[8,32,128]{2,1,0:T(8,128)(2,1)} %bitcast.5), calls=%async_computation | async-start | bytes 131072 | tf_op jit(solution)/shard_map/all_to_all | solution.py:595
  10.8 0.0 copy-start.4
  10.8 0.0 copy-start.5
  10.8 0.0 collective-permute-done.refs_1_
  10.8 0.0 copy-done.12
  10.8 0.0 copy-start.7
  10.8 0.0 copy-start.3
  10.8 0.0 copy-start.6
  10.8 1.0 %prepare.1 = (f32[256,128]{1,0:T(8,128)S(1)}, f32[256,128]{1,0:T(8,128)S(1)}, bf16[256,256]{1,0:T(8,128)(2,1)S(1)}, f32[128,128]{1,0:T(8,128)S(1)}, f32[128,128]{1,0:T(8,128)S(1)}, /*index=5*/s32[1,128]{1,0:T(1,128)S(1)}) custom-call(s32[2,16]{1,0:T(2,128)S(1)} %copy-done.9, bf16[2,64,256]{2,1,0:T(8,128)(2,1)S(1)} %copy-done.12, ...), custom_call_target="tpu_custom_call" | custom-call | flops 20000000000 | tf_op jit(solution)/shard_map/prepare/pallas_call | solution.py:534
  11.9 1.6 %all-to-all-done = bf16[8,32,128]{2,1,0:T(8,128)(2,1)S(1)} async-done(((bf16[8,32,128]{2,1,0:T(8,128)(2,1)}), bf16[8,32,128]{2,1,0:T(8,128)(2,1)S(1)}, u32[]{:S(2)}, u32[]{:S(2)}) %all-to-all-start) | async-done | bytes 65568 | tf_op jit(solution)/shard_map/all_to_all | solution.py:595
  13.5 0.0 copy-done.4
  13.5 0.0 copy-done.5
  13.5 0.0 copy-done.7
  13.5 0.0 copy-start
  13.5 0.8 %subgrid.1 = bf16[256,128]{1,0:T(8,128)(2,1)S(1)} custom-call(bf16[256,128]{1,0:T(8,128)(2,1)S(1)} %bitcast.11, f32[256,128]{1,0:T(8,128)S(1)} %get-tuple-element.16.value_ref, f32[256,128]{1,0:T(8,128)S(1)} %get-tuple-element.17.weight_ref, f32[2,8,128]{2,1,0:T(8,128)S(1)} %copy-done.7, bf16[2,128,128]{2,1,0:T(8,128)(2,1)S(1)} %copy-done.5, ...), custom_call_target="tpu_custom_call" | custom-call | tf_op jit(solution)/shard_map/subgrid/pallas_call | solution.py:534
  14.4 0.0 copy-start.1
  14.4 0.0 copy-start.2
  14.4 7.7 %all_to_all.22 = bf16[16,16,128]{2,1,0:T(8,128)(2,1)S(1)} all-to-all(bf16[16,16,128]{2,1,0:T(8,128)(2,1)S(1)} %bitcast.12), channel_id=1, replica_groups={{15,0,2,4,6,8,10,12,14,1,3,5,7,9,11,13},{31,16,18,20,22,24,26,28,30,17,..., dimensions={0} | all-to-all | bytes 131072 | tf_op jit(solution)/shard_map/all_to_all | solution.py:614
  22.1 0.0 copy-done.3
  22.1 0.0 copy-done.6
  22.1 0.0 copy-done
  22.1 0.0 copy-done.1
  22.1 0.0 copy-done.2
  22.1 1.6 %lines.1 = f32[4,2,4096]{2,1,0:T(2,128)} custom-call(s32[1,128]{1,0:T(1,128)S(1)} %get-tuple-element.14.places_ref, bf16[256,128]{1,0:T(8,128)(2,1)S(1)} %bitcast.10, f32[128,128]{1,0:T(8,128)S(1)} %get-tuple-element.18.straight_ref, f32[128,128]{1,0:T(8,128)S(1)} %get-tuple-element.19.crossed_ref, bf16[256,256]{1,0:T(8,128)(2,1)S(1)} %get-tuple-element.20.put_ref, ...), custom_call_target="tpu_custom_call" | custom-call | tf_op jit(solution)/shard_map/lines/pallas_call | solution.py:534
Async XLA Ops:
  0.0 5.0 %copy-start.8 = (f32[1,1,2,8,4096]{4,3,2,1,0:T(8,128)S(1)}, f32[1,1,2,8,4096]{4,3,2,1,0:T(8,128)}, u32[]{:S(2)}) copy-start(f32[1,1,2,8,4096]{4,3,2,1,0:T(8,128)} %param.17) | copy-start | bytes 786436
  0.0 5.0 %copy-start.10 = (bf16[1792,128]{1,0:T(8,128)(2,1)S(1)}, bf16[1792,128]{1,0:T(8,128)(2,1)}, u32[]{:S(2)}) copy-start(bf16[1792,128]{1,0:T(8,128)(2,1)} %constant.32.clone.paired_table.paired_ref) | copy-start | bytes 1376260
  0.0 5.0 %copy-start.11 = (f32[160,128]{1,0:T(8,128)S(1)}, f32[160,128]{1,0:T(8,128)}, u32[]{:S(2)}) copy-start(f32[160,128]{1,0:T(8,128)} %constant.31.clone.plain_table.plain_ref) | copy-start | bytes 245764
  2.7 2.3 %copy-start.9 = (s32[2,16]{1,0:T(2,128)S(1)}, s32[2,16]{1,0:T(2,128)}, u32[]{:S(2)}) copy-start(s32[2,16]{1,0:T(2,128)} %offsets_ref.3) | copy-start | bytes 388
  2.7 8.1 %collective-permute-start = (f32[8,512]{1,0:T(8,128)S(1)}, f32[8,512]{1,0:T(8,128)S(1)}, u32[]{:S(2)}, u32[]{:S(2)}) collective-permute-start(f32[8,512]{1,0:T(8,128)S(1)} %get-tuple-element.13.refs_0_), channel_id=1, source_target_pairs={{16,0},{0,16},{17,1},{1,17},{18,2},{2,18},{19,3},{3,19},{20,4},{4,... | collective-permute-start | bytes 49160 | tf_op jit(solution)/shard_map/ppermute | solution.py:594
  5.7 5.1 %copy-start.12 = (bf16[2,64,256]{2,1,0:T(8,128)(2,1)S(1)}, bf16[2,64,256]{2,1,0:T(8,128)(2,1)}, u32[]{:S(2)}) copy-start(bf16[2,64,256]{2,1,0:T(8,128)(2,1)} %constant.24.clone.shift_ref) | copy-start | bytes 196612
  5.7 7.8 %all-to-all-start = ((bf16[8,32,128]{2,1,0:T(8,128)(2,1)}), bf16[8,32,128]{2,1,0:T(8,128)(2,1)S(1)}, u32[]{:S(2)}, u32[]{:S(2)}) async-start(bf16[8,32,128]{2,1,0:T(8,128)(2,1)} %bitcast.5), calls=%async_computation | async-start | bytes 131072 | tf_op jit(solution)/shard_map/all_to_all | solution.py:595
  10.8 2.7 %copy-start.4 = (bf16[2,128,128]{2,1,0:T(8,128)(2,1)S(1)}, bf16[2,128,128]{2,1,0:T(8,128)(2,1)}, u32[]{:S(2)}) copy-start(bf16[2,128,128]{2,1,0:T(8,128)(2,1)} %constant.30.clone.back_ref) | copy-start | bytes 196612
  10.8 2.7 %copy-start.5 = (bf16[2,128,128]{2,1,0:T(8,128)(2,1)S(1)}, bf16[2,128,128]{2,1,0:T(8,128)(2,1)}, u32[]{:S(2)}) copy-start(bf16[2,128,128]{2,1,0:T(8,128)(2,1)} %constant.29.clone.model_ref) | copy-start | bytes 196612
  10.8 2.7 %copy-start.7 = (f32[2,8,128]{2,1,0:T(8,128)S(1)}, f32[2,8,128]{2,1,0:T(8,128)}, u32[]{:S(2)}) copy-start(f32[2,8,128]{2,1,0:T(8,128)} %constant.28.clone.turn_ref) | copy-start | bytes 24580
  10.8 11.3 %copy-start.3 = (f32[2,64,128]{2,1,0:T(8,128)S(1)}, f32[2,64,128]{2,1,0:T(8,128)}, u32[]{:S(2)}) copy-start(f32[2,64,128]{2,1,0:T(8,128)} %constant.23.clone.turn_ref) | copy-start | bytes 196612
  10.8 11.3 %copy-start.6 = (f32[32,128]{1,0:T(8,128)S(1)}, f32[32,128]{1,0:T(8,128)}, u32[]{:S(2)}) copy-start(f32[32,128]{1,0:T(8,128)} %constant.22.clone.window_ref) | copy-start | bytes 49156
  13.5 8.6 %copy-start = (bf16[2,256,256]{2,1,0:T(8,128)(2,1)S(1)}, bf16[2,256,256]{2,1,0:T(8,128)(2,1)}, u32[]{:S(2)}) copy-start(bf16[2,256,256]{2,1,0:T(8,128)(2,1)} %constant.25.clone.inner_ref) | copy-start | bytes 786436
  14.4 7.7 %copy-start.1 = (bf16[2,128,128]{2,1,0:T(8,128)(2,1)S(1)}, bf16[2,128,128]{2,1,0:T(8,128)(2,1)}, u32[]{:S(2)}) copy-start(bf16[2,128,128]{2,1,0:T(8,128)(2,1)} %constant.27.clone.partial_ref) | copy-start | bytes 196612
  14.4 7.7 %copy-start.2 = (bf16[2,128,128]{2,1,0:T(8,128)(2,1)S(1)}, bf16[2,128,128]{2,1,0:T(8,128)(2,1)}, u32[]{:S(2)}) copy-start(bf16[2,128,128]{2,1,0:T(8,128)(2,1)} %constant.26.clone.outer_ref) | copy-start | bytes 196612

commit v16 on v15

--- a/solution.py
+++ b/solution.py
@@ -18,6 +18,7 @@
 PLACE_ORDER = tuple(range(FACET_ROWS))
 LANES = 128
 HALF = LANES // 2
+PADDED_ROWS = 64
 EARLY_FLOPS = 10**10
 LATE_FLOPS = 10**10
 PREPARE_FLOPS = 2 * 10**10
@@ -368,7 +369,7 @@
 def prepare_kernel(offsets_ref, shift_ref, *refs, columns, share, blocks):
     samples_refs, outs = refs[:-6], refs[-6:]
     value_ref, weight_ref, put_ref, straight_ref, crossed_ref, places_ref = outs
-    fronts, samples = samples_refs[0].shape[0] // 4, samples_refs[0].shape[1]
+    fronts, samples = offsets_ref.shape[0], samples_refs[0].shape[1]
     own = lax.axis_index("group")
     depth = FACET_ROWS * columns
     for spot in range(len(samples_refs) * fronts):
@@ -577,7 +578,7 @@
         functools.partial(early_kernel, plain=plain_places, paired=paired_places), "early",
         [
             jax.ShapeDtypeStruct((rows, LANES), BF16),
-            jax.ShapeDtypeStruct((4 * fronts, cells.shape[-1]), F32),
+            jax.ShapeDtypeStruct((PADDED_ROWS, cells.shape[-1]), F32),
         ],
         [pltpu.HBM] * 8,
         landing(small + [offsets] + large) + [wide(held)] * 2 + [semaphores(4), semaphores(4)],
@@ -596,6 +597,7 @@
         pieces, "member", split_axis=0, concat_axis=0, tiled=True,
         axis_index_groups=[list(SEND_ORDER)],
     )
+    gathered, arrived = lax.optimization_barrier((gathered, arrived))
     blocks = length // CONTRIB
     value, weight, put, straight, crossed, places = kernel_call(
         functools.partial(prepare_kernel, columns=columns, share=share, blocks=blocks), "prepare",

time: 24.1 us -> 24.8 us (1.029)
  blocking collectives: 7.7 us -> 15.7 us
  starting transfers between devices: 7.41 us -> 2.33 us
  waiting for transfers between devices: 1.62 us -> 0.01 us
  Pallas kernels: 6.86 us -> 6.23 us
    all_to_all x0 -> x1, blocking collectives: none -> 7.6 us  [local(): lax.all_to_all(pieces, 'member', split_axis=0, concat_axis=0, tiled=True,...]
    all_to_all x1 -> x0, starting transfers between devices: 5.09 us -> none  [local(): lax.all_to_all(pieces, 'member', split_axis=0, concat_axis=0, tiled=True,...]
    all_to_all x1 -> x0, waiting for transfers between devices: 1.62 us -> none  [local(): lax.all_to_all(pieces, 'member', split_axis=0, concat_axis=0, tiled=True,...]
    pallas_call x5, Pallas kernels: 6.86 us -> 6.23 us  [kernel_call(): pl.pallas_call(kernel, out_shape=out_shape, in_specs=[pl.BlockSpec(memory...]
    all_to_all x1, blocking collectives: 7.7 us -> 8.14 us  [local(): lax.all_to_all(returned, ('band', 'member'), split_axis=0, concat_axis=0,...]
  transfers between devices with their start and end apart: 2 -> 1, of which waited for: 1 -> 0; matrix products, arithmetic and copies ran while one was open for 0% -> 0% of each run, Pallas kernels for 7% -> 0%
where the time goes in v16:
time: 24.8 us; the launch traced here: 24.5 us
  blocking collectives  15.7 us (63%)
  Pallas kernels  6.23 us (25%)
  starting transfers between devices  2.33 us (9%)
    all_to_all x1, blocking collectives, local(): lax.all_to_all(returned, ('band', 'member'), split_axis=0, concat_axis=0,...  8.14 us
    all_to_all x1, blocking collectives, local(): lax.all_to_all(pieces, 'member', split_axis=0, concat_axis=0, tiled=True,...  7.6 us
    pallas_call x5, Pallas kernels, kernel_call(): pl.pallas_call(kernel, out_shape=out_shape, in_specs=[pl.BlockSpec(memory...  6.23 us
    ppermute x1, starting transfers between devices, local(): gathered.append(lax.ppermute(packed, 'group', moves))  2.33 us
  transfers between devices with their start and end apart: 1, of which 0 were waited for; matrix products, arithmetic and copies ran while one was open for 0% of the time, Pallas kernels for 0%

profile of v16, /device:TPU:0, one launch (start us, length us, event | category | flops | bytes accessed | tf_op | source)
XLA Modules:
  0.0 24.5 jit_solution(6431253701084053227)
XLA Ops:
  0.0 0.0 copy-start.8
  0.0 0.0 copy-start.10
  0.0 0.0 copy-start.11
  0.0 2.7 %early.1 = (bf16[256,128]{1,0:T(8,128)(2,1)S(1)}, f32[64,512]{1,0:T(8,128)S(1)}) custom-call(s32[2,2,512]{2,1,0:T(2,128)} %bitcast.16, f32[2,2,512]{2,1,0:T(2,128)} %bitcast.17, f32[2,1,512]{2,1,0:T(1,128)} %bitcast.18, s32[2,1,512]{2,1,0:T(1,128)} %bitcast.19, s32[2,16]{1,0:T(2,128)} %offsets_ref.3, f32[2,8,4096]{2,1,0:T(8,128)} %bitcast.14, ...), custom_call_target="tpu_custom_call" | custom-call | flops 10000000000 | tf_op jit(solution)/shard_map/early/pallas_call | solution.py:535
  2.7 0.0 copy-start.9
  2.7 2.3 %collective-permute-start = (f32[64,512]{1,0:T(8,128)S(1)}, f32[64,512]{1,0:T(8,128)S(1)}, u32[]{:S(2)}, u32[]{:S(2)}) collective-permute-start(f32[64,512]{1,0:T(8,128)S(1)} %get-tuple-element.18.refs_0_), channel_id=1, source_target_pairs={{16,0},{0,16},{17,1},{1,17},{18,2},{2,18},{19,3},{3,19},{20,4},{4,... | collective-permute-start | bytes 393224 | tf_op jit(solution)/shard_map/ppermute | solution.py:595
  5.0 0.0 copy-done.8
  5.0 0.0 copy-done.10
  5.0 0.0 copy-done.11
  5.0 0.0 copy-done.9
  5.1 0.0 copy-start.12
  5.1 7.6 %all_to_all.23 = bf16[8,32,128]{2,1,0:T(8,128)(2,1)S(1)} all-to-all(bf16[8,32,128]{2,1,0:T(8,128)(2,1)S(1)} %bitcast.13), channel_id=1, replica_groups={{14,0,2,4,6,8,10,12},{15,1,3,5,7,9,11,13},{30,16,18,20,22,24,26,28},{31..., dimensions={0} | all-to-all | bytes 131072 | tf_op jit(solution)/shard_map/all_to_all | solution.py:596
  12.7 0.0 collective-permute-done.refs_1_
  12.7 0.0 copy-done.12
  12.7 0.0 copy-start.4
  12.7 0.0 copy-start.5
  12.7 0.0 copy-start.7
  12.7 0.0 copy-start.3
  12.7 0.0 copy-start.6
  12.7 1.1 %prepare.1 = (f32[256,128]{1,0:T(8,128)S(1)}, f32[256,128]{1,0:T(8,128)S(1)}, bf16[256,256]{1,0:T(8,128)(2,1)S(1)}, f32[128,128]{1,0:T(8,128)S(1)}, f32[128,128]{1,0:T(8,128)S(1)}, /*index=5*/s32[1,128]{1,0:T(1,128)S(1)}) custom-call(s32[2,16]{1,0:T(2,128)S(1)} %copy-done.9, bf16[2,64,256]{2,1,0:T(8,128)(2,1)S(1)} %copy-done.12, ...), custom_call_target="tpu_custom_call" | custom-call | flops 20000000000 | tf_op jit(solution)/shard_map/prepare/pallas_call | solution.py:535
  13.8 0.0 copy-done.4
  13.8 0.0 copy-done.5
  13.8 0.0 copy-done.7
  13.8 0.0 copy-start
  13.8 0.8 %subgrid.1 = bf16[256,128]{1,0:T(8,128)(2,1)S(1)} custom-call(bf16[256,128]{1,0:T(8,128)(2,1)S(1)} %bitcast.11, f32[256,128]{1,0:T(8,128)S(1)} %get-tuple-element.22.value_ref, f32[256,128]{1,0:T(8,128)S(1)} %get-tuple-element.23.weight_ref, f32[2,8,128]{2,1,0:T(8,128)S(1)} %copy-done.7, bf16[2,128,128]{2,1,0:T(8,128)(2,1)S(1)} %copy-done.5, ...), custom_call_target="tpu_custom_call" | custom-call | tf_op jit(solution)/shard_map/subgrid/pallas_call | solution.py:535
  14.7 0.0 copy-start.1
  14.7 0.0 copy-start.2
  14.7 8.1 %all_to_all.24 = bf16[16,16,128]{2,1,0:T(8,128)(2,1)S(1)} all-to-all(bf16[16,16,128]{2,1,0:T(8,128)(2,1)S(1)} %bitcast.12), channel_id=1, replica_groups={{15,0,2,4,6,8,10,12,14,1,3,5,7,9,11,13},{31,16,18,20,22,24,26,28,30,17,..., dimensions={0} | all-to-all | bytes 131072 | tf_op jit(solution)/shard_map/all_to_all | solution.py:616
  22.9 0.0 copy-done.3
  22.9 0.0 copy-done.6
  22.9 0.0 copy-done
  22.9 0.0 copy-done.1
  22.9 0.0 copy-done.2
  22.9 1.6 %lines.1 = f32[4,2,4096]{2,1,0:T(2,128)} custom-call(s32[1,128]{1,0:T(1,128)S(1)} %get-tuple-element.20.places_ref, bf16[256,128]{1,0:T(8,128)(2,1)S(1)} %bitcast.10, f32[128,128]{1,0:T(8,128)S(1)} %get-tuple-element.24.straight_ref, f32[128,128]{1,0:T(8,128)S(1)} %get-tuple-element.25.crossed_ref, bf16[256,256]{1,0:T(8,128)(2,1)S(1)} %get-tuple-element.26.put_ref, ...), custom_call_target="tpu_custom_call" | custom-call | tf_op jit(solution)/shard_map/lines/pallas_call | solution.py:535
  (1 shorter events, 0.0 us)
Async XLA Ops:
  0.0 5.0 %copy-start.8 = (f32[1,1,2,8,4096]{4,3,2,1,0:T(8,128)S(1)}, f32[1,1,2,8,4096]{4,3,2,1,0:T(8,128)}, u32[]{:S(2)}) copy-start(f32[1,1,2,8,4096]{4,3,2,1,0:T(8,128)} %param.17) | copy-start | bytes 786436
  0.0 5.0 %copy-start.10 = (bf16[1792,128]{1,0:T(8,128)(2,1)S(1)}, bf16[1792,128]{1,0:T(8,128)(2,1)}, u32[]{:S(2)}) copy-start(bf16[1792,128]{1,0:T(8,128)(2,1)} %constant.32.clone.paired_table.paired_ref) | copy-start | bytes 1376260
  0.0 5.0 %copy-start.11 = (f32[160,128]{1,0:T(8,128)S(1)}, f32[160,128]{1,0:T(8,128)}, u32[]{:S(2)}) copy-start(f32[160,128]{1,0:T(8,128)} %constant.31.clone.plain_table.plain_ref) | copy-start | bytes 245764
  2.7 2.3 %copy-start.9 = (s32[2,16]{1,0:T(2,128)S(1)}, s32[2,16]{1,0:T(2,128)}, u32[]{:S(2)}) copy-start(s32[2,16]{1,0:T(2,128)} %offsets_ref.3) | copy-start | bytes 388
  2.7 10.0 %collective-permute-start = (f32[64,512]{1,0:T(8,128)S(1)}, f32[64,512]{1,0:T(8,128)S(1)}, u32[]{:S(2)}, u32[]{:S(2)}) collective-permute-start(f32[64,512]{1,0:T(8,128)S(1)} %get-tuple-element.18.refs_0_), channel_id=1, source_target_pairs={{16,0},{0,16},{17,1},{1,17},{18,2},{2,18},{19,3},{3,19},{20,4},{4,... | collective-permute-start | bytes 393224 | tf_op jit(solution)/shard_map/ppermute | solution.py:595
  5.1 7.6 %copy-start.12 = (bf16[2,64,256]{2,1,0:T(8,128)(2,1)S(1)}, bf16[2,64,256]{2,1,0:T(8,128)(2,1)}, u32[]{:S(2)}) copy-start(bf16[2,64,256]{2,1,0:T(8,128)(2,1)} %constant.24.clone.shift_ref) | copy-start | bytes 196612
  12.7 1.1 %copy-start.4 = (bf16[2,128,128]{2,1,0:T(8,128)(2,1)S(1)}, bf16[2,128,128]{2,1,0:T(8,128)(2,1)}, u32[]{:S(2)}) copy-start(bf16[2,128,128]{2,1,0:T(8,128)(2,1)} %constant.30.clone.back_ref) | copy-start | bytes 196612
  12.7 1.1 %copy-start.5 = (bf16[2,128,128]{2,1,0:T(8,128)(2,1)S(1)}, bf16[2,128,128]{2,1,0:T(8,128)(2,1)}, u32[]{:S(2)}) copy-start(bf16[2,128,128]{2,1,0:T(8,128)(2,1)} %constant.29.clone.model_ref) | copy-start | bytes 196612
  12.7 1.1 %copy-start.7 = (f32[2,8,128]{2,1,0:T(8,128)S(1)}, f32[2,8,128]{2,1,0:T(8,128)}, u32[]{:S(2)}) copy-start(f32[2,8,128]{2,1,0:T(8,128)} %constant.28.clone.turn_ref) | copy-start | bytes 24580
  12.7 10.1 %copy-start.3 = (f32[2,64,128]{2,1,0:T(8,128)S(1)}, f32[2,64,128]{2,1,0:T(8,128)}, u32[]{:S(2)}) copy-start(f32[2,64,128]{2,1,0:T(8,128)} %constant.23.clone.turn_ref) | copy-start | bytes 196612
  12.7 10.1 %copy-start.6 = (f32[32,128]{1,0:T(8,128)S(1)}, f32[32,128]{1,0:T(8,128)}, u32[]{:S(2)}) copy-start(f32[32,128]{1,0:T(8,128)} %constant.22.clone.window_ref) | copy-start | bytes 49156
  13.8 9.0 %copy-start = (bf16[2,256,256]{2,1,0:T(8,128)(2,1)S(1)}, bf16[2,256,256]{2,1,0:T(8,128)(2,1)}, u32[]{:S(2)}) copy-start(bf16[2,256,256]{2,1,0:T(8,128)(2,1)} %constant.25.clone.inner_ref) | copy-start | bytes 786436
  14.7 8.2 %copy-start.1 = (bf16[2,128,128]{2,1,0:T(8,128)(2,1)S(1)}, bf16[2,128,128]{2,1,0:T(8,128)(2,1)}, u32[]{:S(2)}) copy-start(bf16[2,128,128]{2,1,0:T(8,128)(2,1)} %constant.27.clone.partial_ref) | copy-start | bytes 196612
  14.7 8.2 %copy-start.2 = (bf16[2,128,128]{2,1,0:T(8,128)(2,1)S(1)}, bf16[2,128,128]{2,1,0:T(8,128)(2,1)}, u32[]{:S(2)}) copy-start(bf16[2,128,128]{2,1,0:T(8,128)(2,1)} %constant.26.clone.outer_ref) | copy-start | bytes 196612

commit v17 on v16

--- a/solution.py
+++ b/solution.py
@@ -18,7 +18,7 @@
 PLACE_ORDER = tuple(range(FACET_ROWS))
 LANES = 128
 HALF = LANES // 2
-PADDED_ROWS = 64
+PADDED_ROWS = 8
 EARLY_FLOPS = 10**10
 LATE_FLOPS = 10**10
 PREPARE_FLOPS = 2 * 10**10

time: 24.8 us -> 27 us (1.089)
  blocking collectives: 15.7 us -> 7.31 us
  starting transfers between devices: 2.33 us -> 9.07 us
  waiting for transfers between devices: 0.01 us -> 2.53 us
  local copies, waits for them, and re-layouts: 0.08 us -> 0.71 us
  Pallas kernels: 6.23 us -> 6.85 us
    all_to_all x1 -> x0, blocking collectives: 7.6 us -> none  [local(): lax.all_to_all(pieces, 'member', split_axis=0, concat_axis=0, tiled=True,...]
    all_to_all x0 -> x1, starting transfers between devices: none -> 6.78 us  [local(): lax.all_to_all(pieces, 'member', split_axis=0, concat_axis=0, tiled=True,...]
    ppermute x1, waiting for transfers between devices: 0.01 us -> 2.52 us  [local(): gathered.append(lax.ppermute(packed, 'group', moves))]
    all_to_all x1, blocking collectives: 8.14 us -> 7.31 us  [local(): lax.all_to_all(returned, ('band', 'member'), split_axis=0, concat_axis=0,...]
    unnamed x26, local copies, waits for them, and re-layouts: 0.08 us -> 0.71 us
    pallas_call x5, Pallas kernels: 6.23 us -> 6.85 us  [kernel_call(): pl.pallas_call(kernel, out_shape=out_shape, in_specs=[pl.BlockSpec(memory...]
  transfers between devices with their start and end apart: 1 -> 2, of which waited for: 0 -> 1; matrix products, arithmetic and copies ran while one was open for 0% -> 0% of each run, Pallas kernels for 0% -> 0%
where the time goes in v17:
time: 27 us; the launch traced here: 26.6 us
  starting transfers between devices  9.07 us (34%)
  blocking collectives  7.31 us (27%)
  Pallas kernels  6.85 us (25%)
  waiting for transfers between devices  2.53 us (9%)
  local copies, waits for them, and re-layouts  0.71 us (3%)
    all_to_all x1, blocking collectives, local(): lax.all_to_all(returned, ('band', 'member'), split_axis=0, concat_axis=0,...  7.31 us
    pallas_call x5, Pallas kernels, kernel_call(): pl.pallas_call(kernel, out_shape=out_shape, in_specs=[pl.BlockSpec(memory...  6.85 us
    all_to_all x1, starting transfers between devices, local(): lax.all_to_all(pieces, 'member', split_axis=0, concat_axis=0, tiled=True,...  6.78 us
    ppermute x1, waiting for transfers between devices, local(): gathered.append(lax.ppermute(packed, 'group', moves))  2.52 us
    ppermute x1, starting transfers between devices, local(): gathered.append(lax.ppermute(packed, 'group', moves))  2.29 us
    unnamed x26, local copies, waits for them, and re-layouts  0.71 us
  transfers between devices with their start and end apart: 2, of which 1 were waited for; matrix products, arithmetic and copies ran while one was open for 0% of the time, Pallas kernels for 0%

profile of v17, /device:TPU:0, one launch (start us, length us, event | category | flops | bytes accessed | tf_op | source)
XLA Modules:
  0.0 26.6 jit_solution(8308679563319300391)
XLA Ops:
  0.0 0.0 copy-start.8
  0.0 0.0 copy-start.10
  0.0 0.0 copy-start.11
  0.0 2.7 %early.1 = (bf16[256,128]{1,0:T(8,128)(2,1)S(1)}, f32[8,512]{1,0:T(8,128)S(1)}) custom-call(s32[2,2,512]{2,1,0:T(2,128)} %bitcast.15, f32[2,2,512]{2,1,0:T(2,128)} %bitcast.16, f32[2,1,512]{2,1,0:T(1,128)} %bitcast.17, s32[2,1,512]{2,1,0:T(1,128)} %bitcast.18, s32[2,16]{1,0:T(2,128)} %offsets_ref.3, f32[2,8,4096]{2,1,0:T(8,128)} %bitcast.13, ...), custom_call_target="tpu_custom_call" | custom-call | flops 10000000000 | tf_op jit(solution)/shard_map/early/pallas_call | solution.py:535
  2.7 0.0 copy-start.9
  2.7 0.0 copy-done.8
  2.7 0.0 copy-done.10
  2.7 0.0 copy-done.11
  2.7 0.6 %copy-done.9 = s32[2,16]{1,0:T(2,128)S(1)} copy-done((s32[2,16]{1,0:T(2,128)S(1)}, s32[2,16]{1,0:T(2,128)}, u32[]{:S(2)}) %copy-start.9) | copy-done | bytes 152
  3.4 0.6 %late.1 = bf16[256,128]{1,0:T(8,128)(2,1)} custom-call(bf16[256,128]{1,0:T(8,128)(2,1)S(1)} %get-tuple-element.17.early_ref, s32[2,16]{1,0:T(2,128)S(1)} %copy-done.9, f32[2,8,4096]{2,1,0:T(8,128)S(1)} %bitcast.14, f32[160,128]{1,0:T(8,128)S(1)} %copy-done.11, bf16[1792,128]{1,0:T(8,128)(2,1)S(1)} %copy-done.10), custom_call_target="tpu_custom_call" | custom-call | flops 10000000000 | tf_op jit(solution)/shard_map/late/pallas_call | solution.py:535
  4.0 0.0 copy-start.12
  4.0 6.8 %all-to-all-start = ((bf16[8,32,128]{2,1,0:T(8,128)(2,1)}), bf16[8,32,128]{2,1,0:T(8,128)(2,1)S(1)}, u32[]{:S(2)}, u32[]{:S(2)}) async-start(bf16[8,32,128]{2,1,0:T(8,128)(2,1)} %bitcast.5), calls=%async_computation | async-start | bytes 131072 | tf_op jit(solution)/shard_map/all_to_all | solution.py:596
  10.8 2.3 %collective-permute-start = (f32[8,512]{1,0:T(8,128)S(1)}, f32[8,512]{1,0:T(8,128)S(1)}, u32[]{:S(2)}, u32[]{:S(2)}) collective-permute-start(f32[8,512]{1,0:T(8,128)S(1)} %get-tuple-element.18.refs_0_), channel_id=1, source_target_pairs={{16,0},{0,16},{17,1},{1,17},{18,2},{2,18},{19,3},{3,19},{20,4},{4,... | collective-permute-start | bytes 49160 | tf_op jit(solution)/shard_map/ppermute | solution.py:595
  13.1 2.5 %collective-permute-done.refs_1_ = f32[8,512]{1,0:T(8,128)S(1)} collective-permute-done((f32[8,512]{1,0:T(8,128)S(1)}, f32[8,512]{1,0:T(8,128)S(1)}, u32[]{:S(2)}, u32[]{:S(2)}) %collective-permute-start) | collective-permute-done | bytes 16416 | tf_op jit(solution)/shard_map/ppermute | solution.py:595
  15.6 0.0 all-to-all-done
  15.6 0.0 copy-done.12
  15.6 0.0 copy-start.4
  15.6 0.0 copy-start.5
  15.6 0.0 copy-start.7
  15.6 0.0 copy-start.3
  15.6 0.0 copy-start.6
  15.7 1.0 %prepare.1 = (f32[256,128]{1,0:T(8,128)S(1)}, f32[256,128]{1,0:T(8,128)S(1)}, bf16[256,256]{1,0:T(8,128)(2,1)S(1)}, f32[128,128]{1,0:T(8,128)S(1)}, f32[128,128]{1,0:T(8,128)S(1)}, /*index=5*/s32[1,128]{1,0:T(1,128)S(1)}) custom-call(s32[2,16]{1,0:T(2,128)S(1)} %copy-done.9, bf16[2,64,256]{2,1,0:T(8,128)(2,1)S(1)} %copy-done.12, ...), custom_call_target="tpu_custom_call" | custom-call | flops 20000000000 | tf_op jit(solution)/shard_map/prepare/pallas_call | solution.py:535
  16.7 0.0 copy-done.4
  16.7 0.0 copy-done.5
  16.7 0.0 copy-done.7
  16.7 0.0 copy-start
  16.8 0.8 %subgrid.1 = bf16[256,128]{1,0:T(8,128)(2,1)S(1)} custom-call(bf16[256,128]{1,0:T(8,128)(2,1)S(1)} %bitcast.11, f32[256,128]{1,0:T(8,128)S(1)} %get-tuple-element.22.value_ref, f32[256,128]{1,0:T(8,128)S(1)} %get-tuple-element.23.weight_ref, f32[2,8,128]{2,1,0:T(8,128)S(1)} %copy-done.7, bf16[2,128,128]{2,1,0:T(8,128)(2,1)S(1)} %copy-done.5, ...), custom_call_target="tpu_custom_call" | custom-call | tf_op jit(solution)/shard_map/subgrid/pallas_call | solution.py:535
  17.6 0.0 copy-start.1
  17.6 0.0 copy-start.2
  17.6 7.3 %all_to_all.23 = bf16[16,16,128]{2,1,0:T(8,128)(2,1)S(1)} all-to-all(bf16[16,16,128]{2,1,0:T(8,128)(2,1)S(1)} %bitcast.12), channel_id=1, replica_groups={{15,0,2,4,6,8,10,12,14,1,3,5,7,9,11,13},{31,16,18,20,22,24,26,28,30,17,..., dimensions={0} | all-to-all | bytes 131072 | tf_op jit(solution)/shard_map/all_to_all | solution.py:616
  24.9 0.0 copy-done.3
  25.0 0.0 copy-done.6
  25.0 0.0 copy-done
  25.0 0.0 copy-done.1
  25.0 0.0 copy-done.2
  25.0 1.6 %lines.1 = f32[4,2,4096]{2,1,0:T(2,128)} custom-call(s32[1,128]{1,0:T(1,128)S(1)} %get-tuple-element.20.places_ref, bf16[256,128]{1,0:T(8,128)(2,1)S(1)} %bitcast.10, f32[128,128]{1,0:T(8,128)S(1)} %get-tuple-element.24.straight_ref, f32[128,128]{1,0:T(8,128)S(1)} %get-tuple-element.25.crossed_ref, bf16[256,256]{1,0:T(8,128)(2,1)S(1)} %get-tuple-element.26.put_ref, ...), custom_call_target="tpu_custom_call" | custom-call | tf_op jit(solution)/shard_map/lines/pallas_call | solution.py:535
Async XLA Ops:
  0.0 2.7 %copy-start.8 = (f32[1,1,2,8,4096]{4,3,2,1,0:T(8,128)S(1)}, f32[1,1,2,8,4096]{4,3,2,1,0:T(8,128)}, u32[]{:S(2)}) copy-start(f32[1,1,2,8,4096]{4,3,2,1,0:T(8,128)} %param.17) | copy-start | bytes 786436
  0.0 2.7 %copy-start.10 = (bf16[1792,128]{1,0:T(8,128)(2,1)S(1)}, bf16[1792,128]{1,0:T(8,128)(2,1)}, u32[]{:S(2)}) copy-start(bf16[1792,128]{1,0:T(8,128)(2,1)} %constant.32.clone.paired_table.paired_ref) | copy-start | bytes 1376260
  0.0 2.7 %copy-start.11 = (f32[160,128]{1,0:T(8,128)S(1)}, f32[160,128]{1,0:T(8,128)}, u32[]{:S(2)}) copy-start(f32[160,128]{1,0:T(8,128)} %constant.31.clone.plain_table.plain_ref) | copy-start | bytes 245764
  2.7 0.7 %copy-start.9 = (s32[2,16]{1,0:T(2,128)S(1)}, s32[2,16]{1,0:T(2,128)}, u32[]{:S(2)}) copy-start(s32[2,16]{1,0:T(2,128)} %offsets_ref.3) | copy-start | bytes 388
  4.0 11.6 %copy-start.12 = (bf16[2,64,256]{2,1,0:T(8,128)(2,1)S(1)}, bf16[2,64,256]{2,1,0:T(8,128)(2,1)}, u32[]{:S(2)}) copy-start(bf16[2,64,256]{2,1,0:T(8,128)(2,1)} %constant.24.clone.shift_ref) | copy-start | bytes 196612
  4.0 11.6 %all-to-all-start = ((bf16[8,32,128]{2,1,0:T(8,128)(2,1)}), bf16[8,32,128]{2,1,0:T(8,128)(2,1)S(1)}, u32[]{:S(2)}, u32[]{:S(2)}) async-start(bf16[8,32,128]{2,1,0:T(8,128)(2,1)} %bitcast.5), calls=%async_computation | async-start | bytes 131072 | tf_op jit(solution)/shard_map/all_to_all | solution.py:596
  10.8 4.8 %collective-permute-start = (f32[8,512]{1,0:T(8,128)S(1)}, f32[8,512]{1,0:T(8,128)S(1)}, u32[]{:S(2)}, u32[]{:S(2)}) collective-permute-start(f32[8,512]{1,0:T(8,128)S(1)} %get-tuple-element.18.refs_0_), channel_id=1, source_target_pairs={{16,0},{0,16},{17,1},{1,17},{18,2},{2,18},{19,3},{3,19},{20,4},{4,... | collective-permute-start | bytes 49160 | tf_op jit(solution)/shard_map/ppermute | solution.py:595
  15.6 1.1 %copy-start.4 = (bf16[2,128,128]{2,1,0:T(8,128)(2,1)S(1)}, bf16[2,128,128]{2,1,0:T(8,128)(2,1)}, u32[]{:S(2)}) copy-start(bf16[2,128,128]{2,1,0:T(8,128)(2,1)} %constant.30.clone.back_ref) | copy-start | bytes 196612
  15.6 1.1 %copy-start.5 = (bf16[2,128,128]{2,1,0:T(8,128)(2,1)S(1)}, bf16[2,128,128]{2,1,0:T(8,128)(2,1)}, u32[]{:S(2)}) copy-start(bf16[2,128,128]{2,1,0:T(8,128)(2,1)} %constant.29.clone.model_ref) | copy-start | bytes 196612
  15.6 1.1 %copy-start.7 = (f32[2,8,128]{2,1,0:T(8,128)S(1)}, f32[2,8,128]{2,1,0:T(8,128)}, u32[]{:S(2)}) copy-start(f32[2,8,128]{2,1,0:T(8,128)} %constant.28.clone.turn_ref) | copy-start | bytes 24580
  15.6 9.3 %copy-start.3 = (f32[2,64,128]{2,1,0:T(8,128)S(1)}, f32[2,64,128]{2,1,0:T(8,128)}, u32[]{:S(2)}) copy-start(f32[2,64,128]{2,1,0:T(8,128)} %constant.23.clone.turn_ref) | copy-start | bytes 196612
  15.6 9.3 %copy-start.6 = (f32[32,128]{1,0:T(8,128)S(1)}, f32[32,128]{1,0:T(8,128)}, u32[]{:S(2)}) copy-start(f32[32,128]{1,0:T(8,128)} %constant.22.clone.window_ref) | copy-start | bytes 49156
  16.7 8.2 %copy-start = (bf16[2,256,256]{2,1,0:T(8,128)(2,1)S(1)}, bf16[2,256,256]{2,1,0:T(8,128)(2,1)}, u32[]{:S(2)}) copy-start(bf16[2,256,256]{2,1,0:T(8,128)(2,1)} %constant.25.clone.inner_ref) | copy-start | bytes 786436
  17.6 7.4 %copy-start.1 = (bf16[2,128,128]{2,1,0:T(8,128)(2,1)S(1)}, bf16[2,128,128]{2,1,0:T(8,128)(2,1)}, u32[]{:S(2)}) copy-start(bf16[2,128,128]{2,1,0:T(8,128)(2,1)} %constant.27.clone.partial_ref) | copy-start | bytes 196612
  17.6 7.3 %copy-start.2 = (bf16[2,128,128]{2,1,0:T(8,128)(2,1)S(1)}, bf16[2,128,128]{2,1,0:T(8,128)(2,1)}, u32[]{:S(2)}) copy-start(bf16[2,128,128]{2,1,0:T(8,128)(2,1)} %constant.26.clone.outer_ref) | copy-start | bytes 196612

commit v18 on v17

--- a/solution.py
+++ b/solution.py
@@ -18,7 +18,7 @@
 PLACE_ORDER = tuple(range(FACET_ROWS))
 LANES = 128
 HALF = LANES // 2
-PADDED_ROWS = 8
+PADDED_ROWS = 32
 EARLY_FLOPS = 10**10
 LATE_FLOPS = 10**10
 PREPARE_FLOPS = 2 * 10**10

time: 27 us -> 28.6 us (1.059)
  waiting for transfers between devices: 2.53 us -> 4.16 us
    ppermute x1, waiting for transfers between devices: 2.52 us -> 4.16 us  [local(): gathered.append(lax.ppermute(packed, 'group', moves))]
where the time goes in v18:
time: 28.6 us; the launch traced here: 28.3 us
  starting transfers between devices  9.07 us (32%)
  blocking collectives  7.31 us (26%)
  Pallas kernels  6.84 us (24%)
  waiting for transfers between devices  4.16 us (15%)
  local copies, waits for them, and re-layouts  0.71 us (2%)
    all_to_all x1, blocking collectives, local(): lax.all_to_all(returned, ('band', 'member'), split_axis=0, concat_axis=0,...  7.31 us
    pallas_call x5, Pallas kernels, kernel_call(): pl.pallas_call(kernel, out_shape=out_shape, in_specs=[pl.BlockSpec(memory...  6.84 us
    all_to_all x1, starting transfers between devices, local(): lax.all_to_all(pieces, 'member', split_axis=0, concat_axis=0, tiled=True,...  6.78 us
    ppermute x1, waiting for transfers between devices, local(): gathered.append(lax.ppermute(packed, 'group', moves))  4.16 us
    ppermute x1, starting transfers between devices, local(): gathered.append(lax.ppermute(packed, 'group', moves))  2.29 us
    unnamed x26, local copies, waits for them, and re-layouts  0.71 us
  transfers between devices with their start and end apart: 2, of which 1 were waited for; matrix products, arithmetic and copies ran while one was open for 0% of the time, Pallas kernels for 0%

profile of v18, /device:TPU:0, one launch (start us, length us, event | category | flops | bytes accessed | tf_op | source)
XLA Modules:
  0.0 28.3 jit_solution(179324926293457422)
XLA Ops:
  0.0 0.0 copy-start.8
  0.0 0.0 copy-start.10
  0.0 0.0 copy-start.11
  0.0 2.7 %early.1 = (bf16[256,128]{1,0:T(8,128)(2,1)S(1)}, f32[32,512]{1,0:T(8,128)S(1)}) custom-call(s32[2,2,512]{2,1,0:T(2,128)} %bitcast.15, f32[2,2,512]{2,1,0:T(2,128)} %bitcast.16, f32[2,1,512]{2,1,0:T(1,128)} %bitcast.17, s32[2,1,512]{2,1,0:T(1,128)} %bitcast.18, s32[2,16]{1,0:T(2,128)} %offsets_ref.3, f32[2,8,4096]{2,1,0:T(8,128)} %bitcast.13, ...), custom_call_target="tpu_custom_call" | custom-call | flops 10000000000 | tf_op jit(solution)/shard_map/early/pallas_call | solution.py:535
  2.7 0.0 copy-start.9
  2.7 0.0 copy-done.8
  2.7 0.0 copy-done.10
  2.7 0.0 copy-done.11
  2.7 0.6 %copy-done.9 = s32[2,16]{1,0:T(2,128)S(1)} copy-done((s32[2,16]{1,0:T(2,128)S(1)}, s32[2,16]{1,0:T(2,128)}, u32[]{:S(2)}) %copy-start.9) | copy-done | bytes 152
  3.4 0.6 %late.1 = bf16[256,128]{1,0:T(8,128)(2,1)} custom-call(bf16[256,128]{1,0:T(8,128)(2,1)S(1)} %get-tuple-element.17.early_ref, s32[2,16]{1,0:T(2,128)S(1)} %copy-done.9, f32[2,8,4096]{2,1,0:T(8,128)S(1)} %bitcast.14, f32[160,128]{1,0:T(8,128)S(1)} %copy-done.11, bf16[1792,128]{1,0:T(8,128)(2,1)S(1)} %copy-done.10), custom_call_target="tpu_custom_call" | custom-call | flops 10000000000 | tf_op jit(solution)/shard_map/late/pallas_call | solution.py:535
  4.0 0.0 copy-start.12
  4.0 6.8 %all-to-all-start = ((bf16[8,32,128]{2,1,0:T(8,128)(2,1)}), bf16[8,32,128]{2,1,0:T(8,128)(2,1)S(1)}, u32[]{:S(2)}, u32[]{:S(2)}) async-start(bf16[8,32,128]{2,1,0:T(8,128)(2,1)} %bitcast.5), calls=%async_computation | async-start | bytes 131072 | tf_op jit(solution)/shard_map/all_to_all | solution.py:596
  10.8 2.3 %collective-permute-start = (f32[32,512]{1,0:T(8,128)S(1)}, f32[32,512]{1,0:T(8,128)S(1)}, u32[]{:S(2)}, u32[]{:S(2)}) collective-permute-start(f32[32,512]{1,0:T(8,128)S(1)} %get-tuple-element.18.refs_0_), channel_id=1, source_target_pairs={{16,0},{0,16},{17,1},{1,17},{18,2},{2,18},{19,3},{3,19},{20,4},{4,... | collective-permute-start | bytes 196616 | tf_op jit(solution)/shard_map/ppermute | solution.py:595
  13.1 4.2 %collective-permute-done.refs_1_ = f32[32,512]{1,0:T(8,128)S(1)} collective-permute-done((f32[32,512]{1,0:T(8,128)S(1)}, f32[32,512]{1,0:T(8,128)S(1)}, u32[]{:S(2)}, u32[]{:S(2)}) %collective-permute-start) | collective-permute-done | bytes 65568 | tf_op jit(solution)/shard_map/ppermute | solution.py:595
  17.2 0.0 all-to-all-done
  17.2 0.0 copy-done.12
  17.2 0.0 copy-start.4
  17.2 0.0 copy-start.5
  17.3 0.0 copy-start.7
  17.3 0.0 copy-start.3
  17.3 0.0 copy-start.6
  17.3 1.1 %prepare.1 = (f32[256,128]{1,0:T(8,128)S(1)}, f32[256,128]{1,0:T(8,128)S(1)}, bf16[256,256]{1,0:T(8,128)(2,1)S(1)}, f32[128,128]{1,0:T(8,128)S(1)}, f32[128,128]{1,0:T(8,128)S(1)}, /*index=5*/s32[1,128]{1,0:T(1,128)S(1)}) custom-call(s32[2,16]{1,0:T(2,128)S(1)} %copy-done.9, bf16[2,64,256]{2,1,0:T(8,128)(2,1)S(1)} %copy-done.12, ...), custom_call_target="tpu_custom_call" | custom-call | flops 20000000000 | tf_op jit(solution)/shard_map/prepare/pallas_call | solution.py:535
  18.4 0.0 copy-done.4
  18.4 0.0 copy-done.5
  18.4 0.0 copy-done.7
  18.4 0.0 copy-start
  18.4 0.8 %subgrid.1 = bf16[256,128]{1,0:T(8,128)(2,1)S(1)} custom-call(bf16[256,128]{1,0:T(8,128)(2,1)S(1)} %bitcast.11, f32[256,128]{1,0:T(8,128)S(1)} %get-tuple-element.22.value_ref, f32[256,128]{1,0:T(8,128)S(1)} %get-tuple-element.23.weight_ref, f32[2,8,128]{2,1,0:T(8,128)S(1)} %copy-done.7, bf16[2,128,128]{2,1,0:T(8,128)(2,1)S(1)} %copy-done.5, ...), custom_call_target="tpu_custom_call" | custom-call | tf_op jit(solution)/shard_map/subgrid/pallas_call | solution.py:535
  19.2 0.0 copy-start.1
  19.3 0.0 copy-start.2
  19.3 7.3 %all_to_all.23 = bf16[16,16,128]{2,1,0:T(8,128)(2,1)S(1)} all-to-all(bf16[16,16,128]{2,1,0:T(8,128)(2,1)S(1)} %bitcast.12), channel_id=1, replica_groups={{15,0,2,4,6,8,10,12,14,1,3,5,7,9,11,13},{31,16,18,20,22,24,26,28,30,17,..., dimensions={0} | all-to-all | bytes 131072 | tf_op jit(solution)/shard_map/all_to_all | solution.py:616
  26.6 0.0 copy-done.3
  26.6 0.0 copy-done.6
  26.6 0.0 copy-done
  26.6 0.0 copy-done.1
  26.6 0.0 copy-done.2
  26.6 1.6 %lines.1 = f32[4,2,4096]{2,1,0:T(2,128)} custom-call(s32[1,128]{1,0:T(1,128)S(1)} %get-tuple-element.20.places_ref, bf16[256,128]{1,0:T(8,128)(2,1)S(1)} %bitcast.10, f32[128,128]{1,0:T(8,128)S(1)} %get-tuple-element.24.straight_ref, f32[128,128]{1,0:T(8,128)S(1)} %get-tuple-element.25.crossed_ref, bf16[256,256]{1,0:T(8,128)(2,1)S(1)} %get-tuple-element.26.put_ref, ...), custom_call_target="tpu_custom_call" | custom-call | tf_op jit(solution)/shard_map/lines/pallas_call | solution.py:535
Async XLA Ops:
  0.0 2.7 %copy-start.8 = (f32[1,1,2,8,4096]{4,3,2,1,0:T(8,128)S(1)}, f32[1,1,2,8,4096]{4,3,2,1,0:T(8,128)}, u32[]{:S(2)}) copy-start(f32[1,1,2,8,4096]{4,3,2,1,0:T(8,128)} %param.17) | copy-start | bytes 786436
  0.0 2.7 %copy-start.10 = (bf16[1792,128]{1,0:T(8,128)(2,1)S(1)}, bf16[1792,128]{1,0:T(8,128)(2,1)}, u32[]{:S(2)}) copy-start(bf16[1792,128]{1,0:T(8,128)(2,1)} %constant.32.clone.paired_table.paired_ref) | copy-start | bytes 1376260
  0.0 2.7 %copy-start.11 = (f32[160,128]{1,0:T(8,128)S(1)}, f32[160,128]{1,0:T(8,128)}, u32[]{:S(2)}) copy-start(f32[160,128]{1,0:T(8,128)} %constant.31.clone.plain_table.plain_ref) | copy-start | bytes 245764
  2.7 0.7 %copy-start.9 = (s32[2,16]{1,0:T(2,128)S(1)}, s32[2,16]{1,0:T(2,128)}, u32[]{:S(2)}) copy-start(s32[2,16]{1,0:T(2,128)} %offsets_ref.3) | copy-start | bytes 388
  4.0 13.2 %copy-start.12 = (bf16[2,64,256]{2,1,0:T(8,128)(2,1)S(1)}, bf16[2,64,256]{2,1,0:T(8,128)(2,1)}, u32[]{:S(2)}) copy-start(bf16[2,64,256]{2,1,0:T(8,128)(2,1)} %constant.24.clone.shift_ref) | copy-start | bytes 196612
  4.0 13.2 %all-to-all-start = ((bf16[8,32,128]{2,1,0:T(8,128)(2,1)}), bf16[8,32,128]{2,1,0:T(8,128)(2,1)S(1)}, u32[]{:S(2)}, u32[]{:S(2)}) async-start(bf16[8,32,128]{2,1,0:T(8,128)(2,1)} %bitcast.5), calls=%async_computation | async-start | bytes 131072 | tf_op jit(solution)/shard_map/all_to_all | solution.py:596
  10.8 6.5 %collective-permute-start = (f32[32,512]{1,0:T(8,128)S(1)}, f32[32,512]{1,0:T(8,128)S(1)}, u32[]{:S(2)}, u32[]{:S(2)}) collective-permute-start(f32[32,512]{1,0:T(8,128)S(1)} %get-tuple-element.18.refs_0_), channel_id=1, source_target_pairs={{16,0},{0,16},{17,1},{1,17},{18,2},{2,18},{19,3},{3,19},{20,4},{4,... | collective-permute-start | bytes 196616 | tf_op jit(solution)/shard_map/ppermute | solution.py:595
  17.2 1.1 %copy-start.4 = (bf16[2,128,128]{2,1,0:T(8,128)(2,1)S(1)}, bf16[2,128,128]{2,1,0:T(8,128)(2,1)}, u32[]{:S(2)}) copy-start(bf16[2,128,128]{2,1,0:T(8,128)(2,1)} %constant.30.clone.back_ref) | copy-start | bytes 196612
  17.2 1.1 %copy-start.5 = (bf16[2,128,128]{2,1,0:T(8,128)(2,1)S(1)}, bf16[2,128,128]{2,1,0:T(8,128)(2,1)}, u32[]{:S(2)}) copy-start(bf16[2,128,128]{2,1,0:T(8,128)(2,1)} %constant.29.clone.model_ref) | copy-start | bytes 196612
  17.3 1.1 %copy-start.7 = (f32[2,8,128]{2,1,0:T(8,128)S(1)}, f32[2,8,128]{2,1,0:T(8,128)}, u32[]{:S(2)}) copy-start(f32[2,8,128]{2,1,0:T(8,128)} %constant.28.clone.turn_ref) | copy-start | bytes 24580
  17.3 9.3 %copy-start.3 = (f32[2,64,128]{2,1,0:T(8,128)S(1)}, f32[2,64,128]{2,1,0:T(8,128)}, u32[]{:S(2)}) copy-start(f32[2,64,128]{2,1,0:T(8,128)} %constant.23.clone.turn_ref) | copy-start | bytes 196612
  17.3 9.3 %copy-start.6 = (f32[32,128]{1,0:T(8,128)S(1)}, f32[32,128]{1,0:T(8,128)}, u32[]{:S(2)}) copy-start(f32[32,128]{1,0:T(8,128)} %constant.22.clone.window_ref) | copy-start | bytes 49156
  18.4 8.2 %copy-start = (bf16[2,256,256]{2,1,0:T(8,128)(2,1)S(1)}, bf16[2,256,256]{2,1,0:T(8,128)(2,1)}, u32[]{:S(2)}) copy-start(bf16[2,256,256]{2,1,0:T(8,128)(2,1)} %constant.25.clone.inner_ref) | copy-start | bytes 786436
  19.2 7.4 %copy-start.1 = (bf16[2,128,128]{2,1,0:T(8,128)(2,1)S(1)}, bf16[2,128,128]{2,1,0:T(8,128)(2,1)}, u32[]{:S(2)}) copy-start(bf16[2,128,128]{2,1,0:T(8,128)(2,1)} %constant.27.clone.partial_ref) | copy-start | bytes 196612
  19.3 7.3 %copy-start.2 = (bf16[2,128,128]{2,1,0:T(8,128)(2,1)S(1)}, bf16[2,128,128]{2,1,0:T(8,128)(2,1)}, u32[]{:S(2)}) copy-start(bf16[2,128,128]{2,1,0:T(8,128)(2,1)} %constant.26.clone.outer_ref) | copy-start | bytes 196612

commit v19 on v18

--- a/solution.py
+++ b/solution.py
@@ -18,7 +18,7 @@
 PLACE_ORDER = tuple(range(FACET_ROWS))
 LANES = 128
 HALF = LANES // 2
-PADDED_ROWS = 32
+PADDED_ROWS = 40
 EARLY_FLOPS = 10**10
 LATE_FLOPS = 10**10
 PREPARE_FLOPS = 2 * 10**10

time: 28.6 us -> 29.3 us (1.024)
  waiting for transfers between devices: 4.16 us -> 4.86 us
    ppermute x1, waiting for transfers between devices: 4.16 us -> 4.86 us  [local(): gathered.append(lax.ppermute(packed, 'group', moves))]
where the time goes in v19:
time: 29.3 us; the launch traced here: 29 us
  starting transfers between devices  9.07 us (31%)
  blocking collectives  7.31 us (25%)
  Pallas kernels  6.84 us (23%)
  waiting for transfers between devices  4.86 us (17%)
  local copies, waits for them, and re-layouts  0.71 us (2%)
    all_to_all x1, blocking collectives, local(): lax.all_to_all(returned, ('band', 'member'), split_axis=0, concat_axis=0,...  7.31 us
    pallas_call x5, Pallas kernels, kernel_call(): pl.pallas_call(kernel, out_shape=out_shape, in_specs=[pl.BlockSpec(memory...  6.84 us
    all_to_all x1, starting transfers between devices, local(): lax.all_to_all(pieces, 'member', split_axis=0, concat_axis=0, tiled=True,...  6.78 us
    ppermute x1, waiting for transfers between devices, local(): gathered.append(lax.ppermute(packed, 'group', moves))  4.86 us
    ppermute x1, starting transfers between devices, local(): gathered.append(lax.ppermute(packed, 'group', moves))  2.29 us
    unnamed x26, local copies, waits for them, and re-layouts  0.71 us
  transfers between devices with their start and end apart: 2, of which 1 were waited for; matrix products, arithmetic and copies ran while one was open for 0% of the time, Pallas kernels for 0%

profile of v19, /device:TPU:0, one launch (start us, length us, event | category | flops | bytes accessed | tf_op | source)
XLA Modules:
  0.0 29.0 jit_solution(7709356828966747208)
XLA Ops:
  0.0 0.0 copy-start.8
  0.0 0.0 copy-start.10
  0.0 0.0 copy-start.11
  0.0 2.7 %early.1 = (bf16[256,128]{1,0:T(8,128)(2,1)S(1)}, f32[40,512]{1,0:T(8,128)S(1)}) custom-call(s32[2,2,512]{2,1,0:T(2,128)} %bitcast.15, f32[2,2,512]{2,1,0:T(2,128)} %bitcast.16, f32[2,1,512]{2,1,0:T(1,128)} %bitcast.17, s32[2,1,512]{2,1,0:T(1,128)} %bitcast.18, s32[2,16]{1,0:T(2,128)} %offsets_ref.3, f32[2,8,4096]{2,1,0:T(8,128)} %bitcast.13, ...), custom_call_target="tpu_custom_call" | custom-call | flops 10000000000 | tf_op jit(solution)/shard_map/early/pallas_call | solution.py:535
  2.7 0.0 copy-start.9
  2.7 0.0 copy-done.8
  2.7 0.0 copy-done.10
  2.7 0.0 copy-done.11
  2.7 0.6 %copy-done.9 = s32[2,16]{1,0:T(2,128)S(1)} copy-done((s32[2,16]{1,0:T(2,128)S(1)}, s32[2,16]{1,0:T(2,128)}, u32[]{:S(2)}) %copy-start.9) | copy-done | bytes 152
  3.4 0.6 %late.1 = bf16[256,128]{1,0:T(8,128)(2,1)} custom-call(bf16[256,128]{1,0:T(8,128)(2,1)S(1)} %get-tuple-element.17.early_ref, s32[2,16]{1,0:T(2,128)S(1)} %copy-done.9, f32[2,8,4096]{2,1,0:T(8,128)S(1)} %bitcast.14, f32[160,128]{1,0:T(8,128)S(1)} %copy-done.11, bf16[1792,128]{1,0:T(8,128)(2,1)S(1)} %copy-done.10), custom_call_target="tpu_custom_call" | custom-call | flops 10000000000 | tf_op jit(solution)/shard_map/late/pallas_call | solution.py:535
  4.0 0.0 copy-start.12
  4.0 6.8 %all-to-all-start = ((bf16[8,32,128]{2,1,0:T(8,128)(2,1)}), bf16[8,32,128]{2,1,0:T(8,128)(2,1)S(1)}, u32[]{:S(2)}, u32[]{:S(2)}) async-start(bf16[8,32,128]{2,1,0:T(8,128)(2,1)} %bitcast.5), calls=%async_computation | async-start | bytes 131072 | tf_op jit(solution)/shard_map/all_to_all | solution.py:596
  10.8 2.3 %collective-permute-start = (f32[40,512]{1,0:T(8,128)S(1)}, f32[40,512]{1,0:T(8,128)S(1)}, u32[]{:S(2)}, u32[]{:S(2)}) collective-permute-start(f32[40,512]{1,0:T(8,128)S(1)} %get-tuple-element.18.refs_0_), channel_id=1, source_target_pairs={{16,0},{0,16},{17,1},{1,17},{18,2},{2,18},{19,3},{3,19},{20,4},{4,... | collective-permute-start | bytes 245768 | tf_op jit(solution)/shard_map/ppermute | solution.py:595
  13.1 4.9 %collective-permute-done.refs_1_ = f32[40,512]{1,0:T(8,128)S(1)} collective-permute-done((f32[40,512]{1,0:T(8,128)S(1)}, f32[40,512]{1,0:T(8,128)S(1)}, u32[]{:S(2)}, u32[]{:S(2)}) %collective-permute-start) | collective-permute-done | bytes 81952 | tf_op jit(solution)/shard_map/ppermute | solution.py:595
  17.9 0.0 all-to-all-done
  17.9 0.0 copy-done.12
  17.9 0.0 copy-start.4
  17.9 0.0 copy-start.5
  18.0 0.0 copy-start.7
  18.0 0.0 copy-start.3
  18.0 0.0 copy-start.6
  18.0 1.1 %prepare.1 = (f32[256,128]{1,0:T(8,128)S(1)}, f32[256,128]{1,0:T(8,128)S(1)}, bf16[256,256]{1,0:T(8,128)(2,1)S(1)}, f32[128,128]{1,0:T(8,128)S(1)}, f32[128,128]{1,0:T(8,128)S(1)}, /*index=5*/s32[1,128]{1,0:T(1,128)S(1)}) custom-call(s32[2,16]{1,0:T(2,128)S(1)} %copy-done.9, bf16[2,64,256]{2,1,0:T(8,128)(2,1)S(1)} %copy-done.12, ...), custom_call_target="tpu_custom_call" | custom-call | flops 20000000000 | tf_op jit(solution)/shard_map/prepare/pallas_call | solution.py:535
  19.1 0.0 copy-done.4
  19.1 0.0 copy-done.5
  19.1 0.0 copy-done.7
  19.1 0.0 copy-start
  19.1 0.8 %subgrid.1 = bf16[256,128]{1,0:T(8,128)(2,1)S(1)} custom-call(bf16[256,128]{1,0:T(8,128)(2,1)S(1)} %bitcast.11, f32[256,128]{1,0:T(8,128)S(1)} %get-tuple-element.22.value_ref, f32[256,128]{1,0:T(8,128)S(1)} %get-tuple-element.23.weight_ref, f32[2,8,128]{2,1,0:T(8,128)S(1)} %copy-done.7, bf16[2,128,128]{2,1,0:T(8,128)(2,1)S(1)} %copy-done.5, ...), custom_call_target="tpu_custom_call" | custom-call | tf_op jit(solution)/shard_map/subgrid/pallas_call | solution.py:535
  19.9 0.0 copy-start.1
  20.0 0.0 copy-start.2
  20.0 7.3 %all_to_all.23 = bf16[16,16,128]{2,1,0:T(8,128)(2,1)S(1)} all-to-all(bf16[16,16,128]{2,1,0:T(8,128)(2,1)S(1)} %bitcast.12), channel_id=1, replica_groups={{15,0,2,4,6,8,10,12,14,1,3,5,7,9,11,13},{31,16,18,20,22,24,26,28,30,17,..., dimensions={0} | all-to-all | bytes 131072 | tf_op jit(solution)/shard_map/all_to_all | solution.py:616
  27.3 0.0 copy-done.3
  27.3 0.0 copy-done.6
  27.3 0.0 copy-done
  27.3 0.0 copy-done.1
  27.3 0.0 copy-done.2
  27.3 1.6 %lines.1 = f32[4,2,4096]{2,1,0:T(2,128)} custom-call(s32[1,128]{1,0:T(1,128)S(1)} %get-tuple-element.20.places_ref, bf16[256,128]{1,0:T(8,128)(2,1)S(1)} %bitcast.10, f32[128,128]{1,0:T(8,128)S(1)} %get-tuple-element.24.straight_ref, f32[128,128]{1,0:T(8,128)S(1)} %get-tuple-element.25.crossed_ref, bf16[256,256]{1,0:T(8,128)(2,1)S(1)} %get-tuple-element.26.put_ref, ...), custom_call_target="tpu_custom_call" | custom-call | tf_op jit(solution)/shard_map/lines/pallas_call | solution.py:535
Async XLA Ops:
  0.0 2.7 %copy-start.8 = (f32[1,1,2,8,4096]{4,3,2,1,0:T(8,128)S(1)}, f32[1,1,2,8,4096]{4,3,2,1,0:T(8,128)}, u32[]{:S(2)}) copy-start(f32[1,1,2,8,4096]{4,3,2,1,0:T(8,128)} %param.17) | copy-start | bytes 786436
  0.0 2.7 %copy-start.10 = (bf16[1792,128]{1,0:T(8,128)(2,1)S(1)}, bf16[1792,128]{1,0:T(8,128)(2,1)}, u32[]{:S(2)}) copy-start(bf16[1792,128]{1,0:T(8,128)(2,1)} %constant.32.clone.paired_table.paired_ref) | copy-start | bytes 1376260
  0.0 2.7 %copy-start.11 = (f32[160,128]{1,0:T(8,128)S(1)}, f32[160,128]{1,0:T(8,128)}, u32[]{:S(2)}) copy-start(f32[160,128]{1,0:T(8,128)} %constant.31.clone.plain_table.plain_ref) | copy-start | bytes 245764
  2.7 0.7 %copy-start.9 = (s32[2,16]{1,0:T(2,128)S(1)}, s32[2,16]{1,0:T(2,128)}, u32[]{:S(2)}) copy-start(s32[2,16]{1,0:T(2,128)} %offsets_ref.3) | copy-start | bytes 388
  4.0 13.9 %copy-start.12 = (bf16[2,64,256]{2,1,0:T(8,128)(2,1)S(1)}, bf16[2,64,256]{2,1,0:T(8,128)(2,1)}, u32[]{:S(2)}) copy-start(bf16[2,64,256]{2,1,0:T(8,128)(2,1)} %constant.24.clone.shift_ref) | copy-start | bytes 196612
  4.0 13.9 %all-to-all-start = ((bf16[8,32,128]{2,1,0:T(8,128)(2,1)}), bf16[8,32,128]{2,1,0:T(8,128)(2,1)S(1)}, u32[]{:S(2)}, u32[]{:S(2)}) async-start(bf16[8,32,128]{2,1,0:T(8,128)(2,1)} %bitcast.5), calls=%async_computation | async-start | bytes 131072 | tf_op jit(solution)/shard_map/all_to_all | solution.py:596
  10.8 7.2 %collective-permute-start = (f32[40,512]{1,0:T(8,128)S(1)}, f32[40,512]{1,0:T(8,128)S(1)}, u32[]{:S(2)}, u32[]{:S(2)}) collective-permute-start(f32[40,512]{1,0:T(8,128)S(1)} %get-tuple-element.18.refs_0_), channel_id=1, source_target_pairs={{16,0},{0,16},{17,1},{1,17},{18,2},{2,18},{19,3},{3,19},{20,4},{4,... | collective-permute-start | bytes 245768 | tf_op jit(solution)/shard_map/ppermute | solution.py:595
  17.9 1.1 %copy-start.4 = (bf16[2,128,128]{2,1,0:T(8,128)(2,1)S(1)}, bf16[2,128,128]{2,1,0:T(8,128)(2,1)}, u32[]{:S(2)}) copy-start(bf16[2,128,128]{2,1,0:T(8,128)(2,1)} %constant.30.clone.back_ref) | copy-start | bytes 196612
  17.9 1.1 %copy-start.5 = (bf16[2,128,128]{2,1,0:T(8,128)(2,1)S(1)}, bf16[2,128,128]{2,1,0:T(8,128)(2,1)}, u32[]{:S(2)}) copy-start(bf16[2,128,128]{2,1,0:T(8,128)(2,1)} %constant.29.clone.model_ref) | copy-start | bytes 196612
  18.0 1.1 %copy-start.7 = (f32[2,8,128]{2,1,0:T(8,128)S(1)}, f32[2,8,128]{2,1,0:T(8,128)}, u32[]{:S(2)}) copy-start(f32[2,8,128]{2,1,0:T(8,128)} %constant.28.clone.turn_ref) | copy-start | bytes 24580
  18.0 9.3 %copy-start.3 = (f32[2,64,128]{2,1,0:T(8,128)S(1)}, f32[2,64,128]{2,1,0:T(8,128)}, u32[]{:S(2)}) copy-start(f32[2,64,128]{2,1,0:T(8,128)} %constant.23.clone.turn_ref) | copy-start | bytes 196612
  18.0 9.3 %copy-start.6 = (f32[32,128]{1,0:T(8,128)S(1)}, f32[32,128]{1,0:T(8,128)}, u32[]{:S(2)}) copy-start(f32[32,128]{1,0:T(8,128)} %constant.22.clone.window_ref) | copy-start | bytes 49156
  19.1 8.2 %copy-start = (bf16[2,256,256]{2,1,0:T(8,128)(2,1)S(1)}, bf16[2,256,256]{2,1,0:T(8,128)(2,1)}, u32[]{:S(2)}) copy-start(bf16[2,256,256]{2,1,0:T(8,128)(2,1)} %constant.25.clone.inner_ref) | copy-start | bytes 786436
  19.9 7.4 %copy-start.1 = (bf16[2,128,128]{2,1,0:T(8,128)(2,1)S(1)}, bf16[2,128,128]{2,1,0:T(8,128)(2,1)}, u32[]{:S(2)}) copy-start(bf16[2,128,128]{2,1,0:T(8,128)(2,1)} %constant.27.clone.partial_ref) | copy-start | bytes 196612
  20.0 7.3 %copy-start.2 = (bf16[2,128,128]{2,1,0:T(8,128)(2,1)S(1)}, bf16[2,128,128]{2,1,0:T(8,128)(2,1)}, u32[]{:S(2)}) copy-start(bf16[2,128,128]{2,1,0:T(8,128)(2,1)} %constant.26.clone.outer_ref) | copy-start | bytes 196612

commit v20 on v15

--- a/solution.py
+++ b/solution.py
@@ -14,7 +14,7 @@
 CONTRIB = 64
 FACET_ROWS = 8
 SUBGRID = FACET_ROWS * CONTRIB
-SEND_ORDER = (FACET_ROWS - 1, *range(FACET_ROWS - 1))
+SEND_ORDER = (FACET_ROWS - 2, *range(FACET_ROWS - 2), FACET_ROWS - 1)
 PLACE_ORDER = tuple(range(FACET_ROWS))
 LANES = 128
 HALF = LANES // 2
@@ -106,7 +106,7 @@
 
 def return_order(bands):
     order = [(b, member) for b in range(bands) for member in PLACE_ORDER]
-    return order[-1:] + order[:-1]
+    return order[-2:-1] + order[:-2] + order[-1:]
 
 
 def split(values):
@@ -350,19 +350,18 @@
 
 
 def late_kernel(
-    early_ref, offsets_ref, strips_ref, plain_ref, paired_ref, out_ref, real_ref, imag_ref,
-    *, plain, paired,
+    early_ref, offsets_ref, strips_ref, plain_ref, paired_ref, out_ref, pieces_ref, real_ref,
+    imag_ref, semaphore, *, plain, paired,
 ):
-    @pl.when(in_first_half())
-    def _():
-        out_ref[...] = early_ref[...]
-
     @pl.when(jnp.logical_not(in_first_half()))
     def _():
         predict(
             offsets_on_lanes(offsets_ref, strips_ref.shape[1], SEND_ORDER), (),
-            strips_ref, plain_ref, paired_ref, (real_ref, imag_ref), out_ref, plain, paired,
+            strips_ref, plain_ref, paired_ref, (real_ref, imag_ref), pieces_ref, plain, paired,
         )
+        copy = pltpu.make_async_copy(pieces_ref, out_ref, semaphore)
+        copy.start()
+        copy.wait()
 
 
 def prepare_kernel(offsets_ref, shift_ref, *refs, columns, share, blocks):
@@ -530,12 +529,15 @@
             ]
 
 
-def kernel_call(kernel, name, out_shape, spaces, scratch, *operands, flops=0):
+def kernel_call(
+    kernel, name, out_shape, spaces, scratch, *operands, flops=0, out_space=pltpu.VMEM, aliases={}
+):
     return pl.pallas_call(
         kernel,
         out_shape=out_shape,
         in_specs=[pl.BlockSpec(memory_space=space) for space in spaces],
-        out_specs=jax.tree.map(lambda _: pl.BlockSpec(memory_space=pltpu.VMEM), out_shape),
+        out_specs=jax.tree.map(lambda _: pl.BlockSpec(memory_space=out_space), out_shape),
+        input_output_aliases=aliases,
         scratch_shapes=scratch,
         compiler_params=pltpu.CompilerParams(vmem_limit_bytes=VMEM_LIMIT),
         cost_estimate=pl.CostEstimate(flops=flops, bytes_accessed=0, transcendentals=0)
@@ -585,8 +587,9 @@
     )
     pieces = kernel_call(
         functools.partial(late_kernel, plain=plain_places, paired=paired_places), "late",
-        jax.ShapeDtypeStruct((rows, LANES), BF16), [pltpu.VMEM] * 5, [wide(held)] * 2,
-        early, offsets, *large, flops=LATE_FLOPS,
+        jax.ShapeDtypeStruct((rows, LANES), BF16), [pltpu.HBM] + [pltpu.VMEM] * 4,
+        [pltpu.VMEM((rows, LANES), BF16)] + [wide(held)] * 2 + [pltpu.SemaphoreType.DMA],
+        early, offsets, *large, flops=LATE_FLOPS, out_space=pltpu.HBM, aliases={0: 0},
     )
     gathered = [packed]
     for step in range(1, groups):

time: 24.1 us -> 25.7 us (1.066)
  the two profiles are of different devices: /device:TPU:0 before, /device:TPU:25 now
where the time goes in v20:
time: 25.7 us; the launch traced here: 25.4 us
  blocking collectives  8.41 us (33%)
  starting transfers between devices  7.4 us (29%)
  Pallas kernels  7.15 us (28%)
  waiting for transfers between devices  2.22 us (9%)
    all_to_all x1, blocking collectives, local(): lax.all_to_all(returned, ('band', 'member'), split_axis=0, concat_axis=0,...  8.41 us
    pallas_call x5, Pallas kernels, kernel_call(): pl.pallas_call(kernel, out_shape=out_shape, in_specs=[pl.BlockSpec(memory...  7.15 us
    all_to_all x1, starting transfers between devices, local(): lax.all_to_all(pieces, 'member', split_axis=0, concat_axis=0, tiled=True,...  5.51 us
    all_to_all x1, waiting for transfers between devices, local(): lax.all_to_all(pieces, 'member', split_axis=0, concat_axis=0, tiled=True,...  2.22 us
    ppermute x1, starting transfers between devices, local(): gathered.append(lax.ppermute(packed, 'group', moves))  1.88 us
  transfers between devices with their start and end apart: 2, of which 1 were waited for; matrix products, arithmetic and copies ran while one was open for 0% of the time, Pallas kernels for 12%

profile of v20, /device:TPU:25, one launch (start us, length us, event | category | flops | bytes accessed | tf_op | source)
XLA Modules:
  0.0 25.4 jit_solution(11383211264478977559)
XLA Ops:
  0.0 0.0 copy-start.8
  0.0 0.0 copy-start.10
  0.0 0.0 copy-start.11
  0.0 1.5 %early.1 = (bf16[256,128]{1,0:T(8,128)(2,1)}, f32[8,512]{1,0:T(8,128)S(1)}) custom-call(s32[2,2,512]{2,1,0:T(2,128)} %bitcast.15, f32[2,2,512]{2,1,0:T(2,128)} %bitcast.16, f32[2,1,512]{2,1,0:T(1,128)} %bitcast.17, s32[2,1,512]{2,1,0:T(1,128)} %bitcast.18, s32[2,16]{1,0:T(2,128)} %offsets_ref.3, f32[2,8,4096]{2,1,0:T(8,128)} %bitcast.13, ...), custom_call_target="tpu_custom_call" | custom-call | flops 10000000000 | tf_op jit(solution)/shard_map/early/pallas_call | solution.py:535
  1.5 0.0 copy-start.9
  1.6 1.9 %collective-permute-start = (f32[8,512]{1,0:T(8,128)S(1)}, f32[8,512]{1,0:T(8,128)S(1)}, u32[]{:S(2)}, u32[]{:S(2)}) collective-permute-start(f32[8,512]{1,0:T(8,128)S(1)} %get-tuple-element.13.refs_0_), channel_id=1, source_target_pairs={{16,0},{0,16},{17,1},{1,17},{18,2},{2,18},{19,3},{3,19},{20,4},{4,... | collective-permute-start | bytes 49160 | tf_op jit(solution)/shard_map/ppermute | solution.py:597
  3.4 0.0 copy-done.8
  3.4 0.0 copy-done.10
  3.4 0.0 copy-done.11
  3.4 0.0 copy-done.9
  3.4 2.1 %late.1 = bf16[256,128]{1,0:T(8,128)(2,1)} custom-call(bf16[256,128]{1,0:T(8,128)(2,1)} %get-tuple-element.15.early_ref, s32[2,16]{1,0:T(2,128)S(1)} %copy-done.9, f32[2,8,4096]{2,1,0:T(8,128)S(1)} %bitcast.14, f32[160,128]{1,0:T(8,128)S(1)} %copy-done.11, bf16[1792,128]{1,0:T(8,128)(2,1)S(1)} %copy-done.10), custom_call_target="tpu_custom_call", output_to_operand_aliasing={{}: (0, {})} | custom-call | flops 10000000000 | tf_op jit(solution)/shard_map/late/pallas_call | solution.py:535
  5.5 0.0 copy-start.12
  5.6 5.5 %all-to-all-start = ((bf16[8,32,128]{2,1,0:T(8,128)(2,1)}), bf16[8,32,128]{2,1,0:T(8,128)(2,1)S(1)}, u32[]{:S(2)}, u32[]{:S(2)}) async-start(bf16[8,32,128]{2,1,0:T(8,128)(2,1)} %bitcast.5), calls=%async_computation | async-start | bytes 131072 | tf_op jit(solution)/shard_map/all_to_all | solution.py:598
  11.1 0.0 copy-start.4
  11.1 0.0 copy-start.5
  11.1 0.0 collective-permute-done.refs_1_
  11.1 0.0 copy-done.12
  11.1 0.0 copy-start.7
  11.1 0.0 copy-start.3
  11.1 0.0 copy-start.6
  11.1 1.1 %prepare.1 = (f32[256,128]{1,0:T(8,128)S(1)}, f32[256,128]{1,0:T(8,128)S(1)}, bf16[256,256]{1,0:T(8,128)(2,1)S(1)}, f32[128,128]{1,0:T(8,128)S(1)}, f32[128,128]{1,0:T(8,128)S(1)}, /*index=5*/s32[1,128]{1,0:T(1,128)S(1)}) custom-call(s32[2,16]{1,0:T(2,128)S(1)} %copy-done.9, bf16[2,64,256]{2,1,0:T(8,128)(2,1)S(1)} %copy-done.12, ...), custom_call_target="tpu_custom_call" | custom-call | flops 20000000000 | tf_op jit(solution)/shard_map/prepare/pallas_call | solution.py:535
  12.2 2.2 %all-to-all-done = bf16[8,32,128]{2,1,0:T(8,128)(2,1)S(1)} async-done(((bf16[8,32,128]{2,1,0:T(8,128)(2,1)}), bf16[8,32,128]{2,1,0:T(8,128)(2,1)S(1)}, u32[]{:S(2)}, u32[]{:S(2)}) %all-to-all-start) | async-done | bytes 65568 | tf_op jit(solution)/shard_map/all_to_all | solution.py:598
  14.4 0.0 copy-done.4
  14.4 0.0 copy-done.5
  14.4 0.0 copy-done.7
  14.4 0.0 copy-start
  14.4 0.8 %subgrid.1 = bf16[256,128]{1,0:T(8,128)(2,1)S(1)} custom-call(bf16[256,128]{1,0:T(8,128)(2,1)S(1)} %bitcast.11, f32[256,128]{1,0:T(8,128)S(1)} %get-tuple-element.16.value_ref, f32[256,128]{1,0:T(8,128)S(1)} %get-tuple-element.17.weight_ref, f32[2,8,128]{2,1,0:T(8,128)S(1)} %copy-done.7, bf16[2,128,128]{2,1,0:T(8,128)(2,1)S(1)} %copy-done.5, ...), custom_call_target="tpu_custom_call" | custom-call | tf_op jit(solution)/shard_map/subgrid/pallas_call | solution.py:535
  15.3 0.0 copy-start.1
  15.3 0.0 copy-start.2
  15.3 8.4 %all_to_all.22 = bf16[16,16,128]{2,1,0:T(8,128)(2,1)S(1)} all-to-all(bf16[16,16,128]{2,1,0:T(8,128)(2,1)S(1)} %bitcast.12), channel_id=1, replica_groups={{13,0,2,4,6,8,10,12,14,1,3,5,7,9,11,15},{29,16,18,20,22,24,26,28,30,17,..., dimensions={0} | all-to-all | bytes 131072 | tf_op jit(solution)/shard_map/all_to_all | solution.py:617
  23.7 0.0 copy-done.3
  23.7 0.0 copy-done.6
  23.7 0.0 copy-done
  23.7 0.0 copy-done.1
  23.7 0.0 copy-done.2
  23.7 1.6 %lines.1 = f32[4,2,4096]{2,1,0:T(2,128)} custom-call(s32[1,128]{1,0:T(1,128)S(1)} %get-tuple-element.14.places_ref, bf16[256,128]{1,0:T(8,128)(2,1)S(1)} %bitcast.10, f32[128,128]{1,0:T(8,128)S(1)} %get-tuple-element.18.straight_ref, f32[128,128]{1,0:T(8,128)S(1)} %get-tuple-element.19.crossed_ref, bf16[256,256]{1,0:T(8,128)(2,1)S(1)} %get-tuple-element.20.put_ref, ...), custom_call_target="tpu_custom_call" | custom-call | tf_op jit(solution)/shard_map/lines/pallas_call | solution.py:535
Async XLA Ops:
  0.0 3.4 %copy-start.8 = (f32[1,1,2,8,4096]{4,3,2,1,0:T(8,128)S(1)}, f32[1,1,2,8,4096]{4,3,2,1,0:T(8,128)}, u32[]{:S(2)}) copy-start(f32[1,1,2,8,4096]{4,3,2,1,0:T(8,128)} %param.17) | copy-start | bytes 786436
  0.0 3.4 %copy-start.10 = (bf16[1792,128]{1,0:T(8,128)(2,1)S(1)}, bf16[1792,128]{1,0:T(8,128)(2,1)}, u32[]{:S(2)}) copy-start(bf16[1792,128]{1,0:T(8,128)(2,1)} %constant.32.clone.paired_table.paired_ref) | copy-start | bytes 1376260
  0.0 3.4 %copy-start.11 = (f32[160,128]{1,0:T(8,128)S(1)}, f32[160,128]{1,0:T(8,128)}, u32[]{:S(2)}) copy-start(f32[160,128]{1,0:T(8,128)} %constant.31.clone.plain_table.plain_ref) | copy-start | bytes 245764
  1.5 1.9 %copy-start.9 = (s32[2,16]{1,0:T(2,128)S(1)}, s32[2,16]{1,0:T(2,128)}, u32[]{:S(2)}) copy-start(s32[2,16]{1,0:T(2,128)} %offsets_ref.3) | copy-start | bytes 388
  1.6 9.5 %collective-permute-start = (f32[8,512]{1,0:T(8,128)S(1)}, f32[8,512]{1,0:T(8,128)S(1)}, u32[]{:S(2)}, u32[]{:S(2)}) collective-permute-start(f32[8,512]{1,0:T(8,128)S(1)} %get-tuple-element.13.refs_0_), channel_id=1, source_target_pairs={{16,0},{0,16},{17,1},{1,17},{18,2},{2,18},{19,3},{3,19},{20,4},{4,... | collective-permute-start | bytes 49160 | tf_op jit(solution)/shard_map/ppermute | solution.py:597
  5.5 5.5 %copy-start.12 = (bf16[2,64,256]{2,1,0:T(8,128)(2,1)S(1)}, bf16[2,64,256]{2,1,0:T(8,128)(2,1)}, u32[]{:S(2)}) copy-start(bf16[2,64,256]{2,1,0:T(8,128)(2,1)} %constant.24.clone.shift_ref) | copy-start | bytes 196612
  5.6 8.8 %all-to-all-start = ((bf16[8,32,128]{2,1,0:T(8,128)(2,1)}), bf16[8,32,128]{2,1,0:T(8,128)(2,1)S(1)}, u32[]{:S(2)}, u32[]{:S(2)}) async-start(bf16[8,32,128]{2,1,0:T(8,128)(2,1)} %bitcast.5), calls=%async_computation | async-start | bytes 131072 | tf_op jit(solution)/shard_map/all_to_all | solution.py:598
  11.1 3.3 %copy-start.4 = (bf16[2,128,128]{2,1,0:T(8,128)(2,1)S(1)}, bf16[2,128,128]{2,1,0:T(8,128)(2,1)}, u32[]{:S(2)}) copy-start(bf16[2,128,128]{2,1,0:T(8,128)(2,1)} %constant.30.clone.back_ref) | copy-start | bytes 196612
  11.1 3.3 %copy-start.5 = (bf16[2,128,128]{2,1,0:T(8,128)(2,1)S(1)}, bf16[2,128,128]{2,1,0:T(8,128)(2,1)}, u32[]{:S(2)}) copy-start(bf16[2,128,128]{2,1,0:T(8,128)(2,1)} %constant.29.clone.model_ref) | copy-start | bytes 196612
  11.1 3.3 %copy-start.7 = (f32[2,8,128]{2,1,0:T(8,128)S(1)}, f32[2,8,128]{2,1,0:T(8,128)}, u32[]{:S(2)}) copy-start(f32[2,8,128]{2,1,0:T(8,128)} %constant.28.clone.turn_ref) | copy-start | bytes 24580
  11.1 12.6 %copy-start.3 = (f32[2,64,128]{2,1,0:T(8,128)S(1)}, f32[2,64,128]{2,1,0:T(8,128)}, u32[]{:S(2)}) copy-start(f32[2,64,128]{2,1,0:T(8,128)} %constant.23.clone.turn_ref) | copy-start | bytes 196612
  11.1 12.6 %copy-start.6 = (f32[32,128]{1,0:T(8,128)S(1)}, f32[32,128]{1,0:T(8,128)}, u32[]{:S(2)}) copy-start(f32[32,128]{1,0:T(8,128)} %constant.22.clone.window_ref) | copy-start | bytes 49156
  14.4 9.3 %copy-start = (bf16[2,256,256]{2,1,0:T(8,128)(2,1)S(1)}, bf16[2,256,256]{2,1,0:T(8,128)(2,1)}, u32[]{:S(2)}) copy-start(bf16[2,256,256]{2,1,0:T(8,128)(2,1)} %constant.25.clone.inner_ref) | copy-start | bytes 786436
  15.3 8.4 %copy-start.1 = (bf16[2,128,128]{2,1,0:T(8,128)(2,1)S(1)}, bf16[2,128,128]{2,1,0:T(8,128)(2,1)}, u32[]{:S(2)}) copy-start(bf16[2,128,128]{2,1,0:T(8,128)(2,1)} %constant.27.clone.partial_ref) | copy-start | bytes 196612
  15.3 8.4 %copy-start.2 = (bf16[2,128,128]{2,1,0:T(8,128)(2,1)S(1)}, bf16[2,128,128]{2,1,0:T(8,128)(2,1)}, u32[]{:S(2)}) copy-start(bf16[2,128,128]{2,1,0:T(8,128)(2,1)} %constant.26.clone.outer_ref) | copy-start | bytes 196612

commit v21 on v13

--- a/solution.py
+++ b/solution.py
@@ -106,7 +106,12 @@
 
 def return_order(bands):
     order = [(b, member) for b in range(bands) for member in PLACE_ORDER]
-    return order[-1:] + order[:-1]
+    last_band, last_member = order[-1]
+
+    def nearness(entry):
+        return -((entry[0] ^ last_band).bit_count() + ((entry[1] ^ last_member) >> 1).bit_count())
+
+    return order[-1:] + sorted(order[:-1], key=nearness)
 
 
 def split(values):

time: 24.1 us -> 24.1 us (level)
  no operation moved by 1% of the time
where the time goes in v21:
time: 24.1 us; the launch traced here: 23.8 us
  blocking collectives  7.66 us (32%)
  starting transfers between devices  7.47 us (31%)
  Pallas kernels  6.62 us (27%)
  waiting for transfers between devices  1.86 us (8%)
    all_to_all x1, blocking collectives, local(): lax.all_to_all(returned, ('band', 'member'), split_axis=0, concat_axis=0,...  7.66 us
    pallas_call x5, Pallas kernels, kernel_call(): pl.pallas_call(kernel, out_shape=out_shape, in_specs=[pl.BlockSpec(memory...  6.62 us
    all_to_all x1, starting transfers between devices, local(): lax.all_to_all(pieces, 'member', split_axis=0, concat_axis=0, tiled=True,...  5.05 us
    ppermute x1, starting transfers between devices, local(): gathered.append(lax.ppermute(packed, 'group', moves))  2.42 us
    all_to_all x1, waiting for transfers between devices, local(): lax.all_to_all(pieces, 'member', split_axis=0, concat_axis=0, tiled=True,...  1.85 us
  transfers between devices with their start and end apart: 2, of which 1 were waited for; matrix products, arithmetic and copies ran while one was open for 0% of the time, Pallas kernels for 6%

profile of v21, /device:TPU:0, one launch (start us, length us, event | category | flops | bytes accessed | tf_op | source)
XLA Modules:
  0.0 23.8 jit_solution(9251977009637484382)
XLA Ops:
  0.0 0.0 copy-start.8
  0.0 0.0 copy-start.9
  0.0 0.0 copy-start.10
  0.0 2.6 %early.1 = (bf16[256,128]{1,0:T(8,128)(2,1)S(1)}, f32[8,512]{1,0:T(8,128)S(1)}, s32[1,128]{1,0:T(1,128)S(1)}, s32[1,256]{1,0:T(1,128)S(1)}) custom-call(s32[2,16]{1,0:T(2,128)} %offsets.1, s32[2,2,512]{2,1,0:T(2,128)} %bitcast.15, f32[2,2,512]{2,1,0:T(2,128)} %bitcast.16, f32[2,1,512]{2,1,0:T(1,128)} %bitcast.17, s32[2,1,512]{2,1,0:T(1,128)} %bitcast.18, ...), custom_call_target="tpu_custom_call" | custom-call | flops 10000000000 | tf_op jit(solution)/shard_map/early/pallas_call | solution.py:533
  2.7 2.4 %collective-permute-start = (f32[8,512]{1,0:T(8,128)S(1)}, f32[8,512]{1,0:T(8,128)S(1)}, u32[]{:S(2)}, u32[]{:S(2)}) collective-permute-start(f32[8,512]{1,0:T(8,128)S(1)} %get-tuple-element.17.refs_0_), channel_id=1, source_target_pairs={{16,0},{0,16},{17,1},{1,17},{18,2},{2,18},{19,3},{3,19},{20,4},{4,... | collective-permute-start | bytes 49160 | tf_op jit(solution)/shard_map/ppermute | solution.py:599
  5.1 0.0 copy-done.8
  5.1 0.0 copy-done.9
  5.1 0.0 copy-done.10
  5.1 0.6 %late.1 = bf16[256,128]{1,0:T(8,128)(2,1)} custom-call(bf16[256,128]{1,0:T(8,128)(2,1)S(1)} %get-tuple-element.15.early_ref, s32[1,256]{1,0:T(1,128)S(1)} %get-tuple-element.16.spread_ref, f32[2,8,4096]{2,1,0:T(8,128)S(1)} %bitcast.14, f32[160,128]{1,0:T(8,128)S(1)} %copy-done.10, bf16[1792,128]{1,0:T(8,128)(2,1)S(1)} %copy-done.9), custom_call_target="tpu_custom_call" | custom-call | flops 10000000000 | tf_op jit(solution)/shard_map/late/pallas_call | solution.py:533
  5.7 0.0 copy-start.11
  5.7 5.0 %all-to-all-start = ((bf16[8,32,128]{2,1,0:T(8,128)(2,1)}), bf16[8,32,128]{2,1,0:T(8,128)(2,1)S(1)}, u32[]{:S(2)}, u32[]{:S(2)}) async-start(bf16[8,32,128]{2,1,0:T(8,128)(2,1)} %bitcast.5), calls=%async_computation | async-start | bytes 131072 | tf_op jit(solution)/shard_map/all_to_all | solution.py:600
  10.8 0.0 collective-permute-done.refs_1_
  10.8 0.0 copy-done.11
  10.8 0.0 copy-start.4
  10.8 0.0 copy-start.5
  10.8 0.0 copy-start.7
  10.8 0.0 copy-start.3
  10.8 0.0 copy-start.6
  10.9 0.8 %prepare.1 = (f32[256,128]{1,0:T(8,128)S(1)}, f32[256,128]{1,0:T(8,128)S(1)}, bf16[256,256]{1,0:T(8,128)(2,1)S(1)}, f32[128,128]{1,0:T(8,128)S(1)}, f32[128,128]{1,0:T(8,128)S(1)}) custom-call(s32[1,128]{1,0:T(1,128)S(1)} %get-tuple-element.14.places_ref, bf16[2,64,256]{2,1,0:T(8,128)(2,1)S(1)} %copy-done.11, f32[8,512]{1,0:T(8,128)S(1)} %get-tuple-element.17.refs_0_, ...), custom_call_target="tpu_custom_call" | custom-call | flops 20000000000 | tf_op jit(solution)/shard_map/prepare/pallas_call | solution.py:533
  11.7 1.9 %all-to-all-done = bf16[8,32,128]{2,1,0:T(8,128)(2,1)S(1)} async-done(((bf16[8,32,128]{2,1,0:T(8,128)(2,1)}), bf16[8,32,128]{2,1,0:T(8,128)(2,1)S(1)}, u32[]{:S(2)}, u32[]{:S(2)}) %all-to-all-start) | async-done | bytes 65568 | tf_op jit(solution)/shard_map/all_to_all | solution.py:600
  13.6 0.0 copy-done.4
  13.6 0.0 copy-done.5
  13.6 0.0 copy-done.7
  13.6 0.0 copy-start
  13.6 0.8 %subgrid.1 = bf16[256,128]{1,0:T(8,128)(2,1)S(1)} custom-call(bf16[256,128]{1,0:T(8,128)(2,1)S(1)} %bitcast.11, f32[256,128]{1,0:T(8,128)S(1)} %get-tuple-element.18.value_ref, f32[256,128]{1,0:T(8,128)S(1)} %get-tuple-element.19.weight_ref, f32[2,8,128]{2,1,0:T(8,128)S(1)} %copy-done.7, bf16[2,128,128]{2,1,0:T(8,128)(2,1)S(1)} %copy-done.5, ...), custom_call_target="tpu_custom_call" | custom-call | tf_op jit(solution)/shard_map/subgrid/pallas_call | solution.py:533
  14.4 0.0 copy-start.1
  14.5 0.0 copy-start.2
  14.5 7.7 %all_to_all.22 = bf16[16,16,128]{2,1,0:T(8,128)(2,1)S(1)} all-to-all(bf16[16,16,128]{2,1,0:T(8,128)(2,1)S(1)} %bitcast.12), channel_id=1, replica_groups={{15,0,2,4,6,8,10,1,3,12,14,5,7,9,11,13},{31,16,18,20,22,24,26,17,19,28,..., dimensions={0} | all-to-all | bytes 131072 | tf_op jit(solution)/shard_map/all_to_all | solution.py:618
  22.1 0.0 copy-done.3
  22.1 0.0 copy-done.6
  22.1 0.0 copy-done
  22.1 0.0 copy-done.1
  22.1 0.0 copy-done.2
  22.2 1.6 %lines.1 = f32[4,2,4096]{2,1,0:T(2,128)} custom-call(s32[1,128]{1,0:T(1,128)S(1)} %get-tuple-element.14.places_ref, bf16[256,128]{1,0:T(8,128)(2,1)S(1)} %bitcast.10, f32[128,128]{1,0:T(8,128)S(1)} %get-tuple-element.20.straight_ref, f32[128,128]{1,0:T(8,128)S(1)} %get-tuple-element.21.crossed_ref, bf16[256,256]{1,0:T(8,128)(2,1)S(1)} %get-tuple-element.22.put_ref, ...), custom_call_target="tpu_custom_call" | custom-call | tf_op jit(solution)/shard_map/lines/pallas_call | solution.py:533
Async XLA Ops:
  0.0 5.1 %copy-start.8 = (f32[1,1,2,8,4096]{4,3,2,1,0:T(8,128)S(1)}, f32[1,1,2,8,4096]{4,3,2,1,0:T(8,128)}, u32[]{:S(2)}) copy-start(f32[1,1,2,8,4096]{4,3,2,1,0:T(8,128)} %param.17) | copy-start | bytes 786436
  0.0 5.1 %copy-start.9 = (bf16[1792,128]{1,0:T(8,128)(2,1)S(1)}, bf16[1792,128]{1,0:T(8,128)(2,1)}, u32[]{:S(2)}) copy-start(bf16[1792,128]{1,0:T(8,128)(2,1)} %constant.32.clone.paired_table.paired_ref) | copy-start | bytes 1376260
  0.0 5.1 %copy-start.10 = (f32[160,128]{1,0:T(8,128)S(1)}, f32[160,128]{1,0:T(8,128)}, u32[]{:S(2)}) copy-start(f32[160,128]{1,0:T(8,128)} %constant.31.clone.plain_table.plain_ref) | copy-start | bytes 245764
  2.7 8.1 %collective-permute-start = (f32[8,512]{1,0:T(8,128)S(1)}, f32[8,512]{1,0:T(8,128)S(1)}, u32[]{:S(2)}, u32[]{:S(2)}) collective-permute-start(f32[8,512]{1,0:T(8,128)S(1)} %get-tuple-element.17.refs_0_), channel_id=1, source_target_pairs={{16,0},{0,16},{17,1},{1,17},{18,2},{2,18},{19,3},{3,19},{20,4},{4,... | collective-permute-start | bytes 49160 | tf_op jit(solution)/shard_map/ppermute | solution.py:599
  5.7 5.1 %copy-start.11 = (bf16[2,64,256]{2,1,0:T(8,128)(2,1)S(1)}, bf16[2,64,256]{2,1,0:T(8,128)(2,1)}, u32[]{:S(2)}) copy-start(bf16[2,64,256]{2,1,0:T(8,128)(2,1)} %constant.24.clone.shift_ref) | copy-start | bytes 196612
  5.7 7.8 %all-to-all-start = ((bf16[8,32,128]{2,1,0:T(8,128)(2,1)}), bf16[8,32,128]{2,1,0:T(8,128)(2,1)S(1)}, u32[]{:S(2)}, u32[]{:S(2)}) async-start(bf16[8,32,128]{2,1,0:T(8,128)(2,1)} %bitcast.5), calls=%async_computation | async-start | bytes 131072 | tf_op jit(solution)/shard_map/all_to_all | solution.py:600
  10.8 2.8 %copy-start.4 = (bf16[2,128,128]{2,1,0:T(8,128)(2,1)S(1)}, bf16[2,128,128]{2,1,0:T(8,128)(2,1)}, u32[]{:S(2)}) copy-start(bf16[2,128,128]{2,1,0:T(8,128)(2,1)} %constant.30.clone.back_ref) | copy-start | bytes 196612
  10.8 2.8 %copy-start.5 = (bf16[2,128,128]{2,1,0:T(8,128)(2,1)S(1)}, bf16[2,128,128]{2,1,0:T(8,128)(2,1)}, u32[]{:S(2)}) copy-start(bf16[2,128,128]{2,1,0:T(8,128)(2,1)} %constant.29.clone.model_ref) | copy-start | bytes 196612
  10.8 2.7 %copy-start.7 = (f32[2,8,128]{2,1,0:T(8,128)S(1)}, f32[2,8,128]{2,1,0:T(8,128)}, u32[]{:S(2)}) copy-start(f32[2,8,128]{2,1,0:T(8,128)} %constant.28.clone.turn_ref) | copy-start | bytes 24580
  10.8 11.3 %copy-start.3 = (f32[2,64,128]{2,1,0:T(8,128)S(1)}, f32[2,64,128]{2,1,0:T(8,128)}, u32[]{:S(2)}) copy-start(f32[2,64,128]{2,1,0:T(8,128)} %constant.23.clone.turn_ref) | copy-start | bytes 196612
  10.8 11.3 %copy-start.6 = (f32[32,128]{1,0:T(8,128)S(1)}, f32[32,128]{1,0:T(8,128)}, u32[]{:S(2)}) copy-start(f32[32,128]{1,0:T(8,128)} %constant.22.clone.window_ref) | copy-start | bytes 49156
  13.6 8.6 %copy-start = (bf16[2,256,256]{2,1,0:T(8,128)(2,1)S(1)}, bf16[2,256,256]{2,1,0:T(8,128)(2,1)}, u32[]{:S(2)}) copy-start(bf16[2,256,256]{2,1,0:T(8,128)(2,1)} %constant.25.clone.inner_ref) | copy-start | bytes 786436
  14.4 7.7 %copy-start.1 = (bf16[2,128,128]{2,1,0:T(8,128)(2,1)S(1)}, bf16[2,128,128]{2,1,0:T(8,128)(2,1)}, u32[]{:S(2)}) copy-start(bf16[2,128,128]{2,1,0:T(8,128)(2,1)} %constant.27.clone.partial_ref) | copy-start | bytes 196612
  14.5 7.7 %copy-start.2 = (bf16[2,128,128]{2,1,0:T(8,128)(2,1)S(1)}, bf16[2,128,128]{2,1,0:T(8,128)(2,1)}, u32[]{:S(2)}) copy-start(bf16[2,128,128]{2,1,0:T(8,128)(2,1)} %constant.26.clone.outer_ref) | copy-start | bytes 196612

commit v22 on v13

--- a/solution.py
+++ b/solution.py
@@ -90,11 +90,16 @@
                 piece=high_low(piece),
             )
         ),
-        window=window,
+        window=np.repeat(window, 2, axis=0),
         turn=turn,
         shift=shift,
         inner_plus=high_low(from_right(np.kron(pair, phases(short, short, CONTRIB, 1)))),
-        outer_plus=high_low(from_left(phases(outer, short, blocks, 1))),
+        outer_plus=high_low(
+            from_left(phases(outer, short, blocks, 1))
+            .reshape(2, blocks, 2 * CONTRIB)
+            .transpose(1, 0, 2)
+            .reshape(2 * blocks, 2 * CONTRIB)
+        ),
         partial=high_low(from_right(phases(short, short, CONTRIB, -1)).T * CONTRIB**-0.5),
         grid_turn=side_by_side(phases(np.arange(FACET_ROWS), short, SUBGRID, -1)).astype(
             np.float32
@@ -118,9 +123,9 @@
     return lax.dot_general(left, right, (dims, ((), ())), preferred_element_type=F32)
 
 
-def dot_split(values, right):
+def dot_split(values, right, dims=((1,), (0,))):
     rows = values.shape[0]
-    both = dot(jnp.concatenate(split(values), axis=0), right)
+    both = dot(jnp.concatenate(split(values), axis=0), right, dims)
     return both[:rows] + both[rows:]
 
 
@@ -471,9 +476,7 @@
     both = jnp.concatenate(
         [jnp.where(inside, residues, 0.0), jnp.where(inside, 0.0, residues)], axis=1
     )
-    put = put_ref[...]
-    high, low = split(both)
-    spectrum = dot(high, put, ((1,), (1,))) + dot(low, put, ((1,), (1,)))
+    spectrum = dot_split(both, put_ref[...], ((1,), (1,)))
     inner = times_table(
         jnp.concatenate(
             [
@@ -503,20 +506,13 @@
         ),
     )
     window = window_ref[...]
-    low_half = iota((groups, LANES), 1) < HALF
-    for part in range(2):
-        for pair in range(pairs):
-            lanes = slice(pair * LANES, (pair + 1) * LANES)
-            begin = part * blocks
-            even = lines[begin : begin + groups, lanes]
-            odd = lines[begin + groups : begin + blocks, lanes]
-            line_refs[2 * pair][pl.ds(part, groups, stride=2), :] = (
-                jnp.where(low_half, even, swap_halves(odd)) * window
-            )
-            if 2 * pair + 1 < columns:
-                line_refs[2 * pair + 1][pl.ds(part, groups, stride=2), :] = (
-                    jnp.where(low_half, swap_halves(even), odd) * window
-                )
+    low_half = iota((blocks, LANES), 1) < HALF
+    for pair in range(pairs):
+        lanes = slice(pair * LANES, (pair + 1) * LANES)
+        even, odd = lines[:blocks, lanes], lines[blocks:, lanes]
+        line_refs[2 * pair][...] = jnp.where(low_half, even, swap_halves(odd)) * window
+        if 2 * pair + 1 < columns:
+            line_refs[2 * pair + 1][...] = jnp.where(low_half, swap_halves(even), odd) * window
     for column in range(columns):
         for group in range(groups):
             out_ref[column, :, group * LANES : (group + 1) * LANES] = line_refs[column][

time: 24.1 us -> 24.1 us (level)
  no operation moved by 1% of the time
where the time goes in v22:
time: 24.1 us; the launch traced here: 23.8 us
  blocking collectives  7.66 us (32%)
  starting transfers between devices  7.47 us (31%)
  Pallas kernels  6.6 us (27%)
  waiting for transfers between devices  1.86 us (8%)
    all_to_all x1, blocking collectives, local(): lax.all_to_all(returned, ('band', 'member'), split_axis=0, concat_axis=0,...  7.66 us
    pallas_call x5, Pallas kernels, kernel_call(): pl.pallas_call(kernel, out_shape=out_shape, in_specs=[pl.BlockSpec(memory...  6.6 us
    all_to_all x1, starting transfers between devices, local(): lax.all_to_all(pieces, 'member', split_axis=0, concat_axis=0, tiled=True,...  5.05 us
    ppermute x1, starting transfers between devices, local(): gathered.append(lax.ppermute(packed, 'group', moves))  2.42 us
    all_to_all x1, waiting for transfers between devices, local(): lax.all_to_all(pieces, 'member', split_axis=0, concat_axis=0, tiled=True,...  1.85 us
  transfers between devices with their start and end apart: 2, of which 1 were waited for; matrix products, arithmetic and copies ran while one was open for 0% of the time, Pallas kernels for 6%

profile of v22, /device:TPU:0, one launch (start us, length us, event | category | flops | bytes accessed | tf_op | source)
XLA Modules:
  0.0 23.8 jit_solution(13149236324595633412)
XLA Ops:
  0.0 0.0 copy-start.8
  0.0 0.0 copy-start.9
  0.0 0.0 copy-start.10
  0.0 2.6 %early.1 = (bf16[256,128]{1,0:T(8,128)(2,1)S(1)}, f32[8,512]{1,0:T(8,128)S(1)}, s32[1,128]{1,0:T(1,128)S(1)}, s32[1,256]{1,0:T(1,128)S(1)}) custom-call(s32[2,16]{1,0:T(2,128)} %offsets.1, s32[2,2,512]{2,1,0:T(2,128)} %bitcast.15, f32[2,2,512]{2,1,0:T(2,128)} %bitcast.16, f32[2,1,512]{2,1,0:T(1,128)} %bitcast.17, s32[2,1,512]{2,1,0:T(1,128)} %bitcast.18, ...), custom_call_target="tpu_custom_call" | custom-call | flops 10000000000 | tf_op jit(solution)/shard_map/early/pallas_call | solution.py:524
  2.7 2.4 %collective-permute-start = (f32[8,512]{1,0:T(8,128)S(1)}, f32[8,512]{1,0:T(8,128)S(1)}, u32[]{:S(2)}, u32[]{:S(2)}) collective-permute-start(f32[8,512]{1,0:T(8,128)S(1)} %get-tuple-element.17.refs_0_), channel_id=1, source_target_pairs={{16,0},{0,16},{17,1},{1,17},{18,2},{2,18},{19,3},{3,19},{20,4},{4,... | collective-permute-start | bytes 49160 | tf_op jit(solution)/shard_map/ppermute | solution.py:590
  5.1 0.0 copy-done.8
  5.1 0.0 copy-done.9
  5.1 0.0 copy-done.10
  5.1 0.6 %late.1 = bf16[256,128]{1,0:T(8,128)(2,1)} custom-call(bf16[256,128]{1,0:T(8,128)(2,1)S(1)} %get-tuple-element.15.early_ref, s32[1,256]{1,0:T(1,128)S(1)} %get-tuple-element.16.spread_ref, f32[2,8,4096]{2,1,0:T(8,128)S(1)} %bitcast.14, f32[160,128]{1,0:T(8,128)S(1)} %copy-done.10, bf16[1792,128]{1,0:T(8,128)(2,1)S(1)} %copy-done.9), custom_call_target="tpu_custom_call" | custom-call | flops 10000000000 | tf_op jit(solution)/shard_map/late/pallas_call | solution.py:524
  5.7 0.0 copy-start.11
  5.7 5.0 %all-to-all-start = ((bf16[8,32,128]{2,1,0:T(8,128)(2,1)}), bf16[8,32,128]{2,1,0:T(8,128)(2,1)S(1)}, u32[]{:S(2)}, u32[]{:S(2)}) async-start(bf16[8,32,128]{2,1,0:T(8,128)(2,1)} %bitcast.5), calls=%async_computation | async-start | bytes 131072 | tf_op jit(solution)/shard_map/all_to_all | solution.py:591
  10.8 0.0 collective-permute-done.refs_1_
  10.8 0.0 copy-done.11
  10.8 0.0 copy-start.4
  10.8 0.0 copy-start.5
  10.8 0.0 copy-start.7
  10.8 0.0 copy-start.3
  10.8 0.0 copy-start.6
  10.9 0.8 %prepare.1 = (f32[256,128]{1,0:T(8,128)S(1)}, f32[256,128]{1,0:T(8,128)S(1)}, bf16[256,256]{1,0:T(8,128)(2,1)S(1)}, f32[128,128]{1,0:T(8,128)S(1)}, f32[128,128]{1,0:T(8,128)S(1)}) custom-call(s32[1,128]{1,0:T(1,128)S(1)} %get-tuple-element.14.places_ref, bf16[2,64,256]{2,1,0:T(8,128)(2,1)S(1)} %copy-done.11, f32[8,512]{1,0:T(8,128)S(1)} %get-tuple-element.17.refs_0_, ...), custom_call_target="tpu_custom_call" | custom-call | flops 20000000000 | tf_op jit(solution)/shard_map/prepare/pallas_call | solution.py:524
  11.7 1.9 %all-to-all-done = bf16[8,32,128]{2,1,0:T(8,128)(2,1)S(1)} async-done(((bf16[8,32,128]{2,1,0:T(8,128)(2,1)}), bf16[8,32,128]{2,1,0:T(8,128)(2,1)S(1)}, u32[]{:S(2)}, u32[]{:S(2)}) %all-to-all-start) | async-done | bytes 65568 | tf_op jit(solution)/shard_map/all_to_all | solution.py:591
  13.6 0.0 copy-done.4
  13.6 0.0 copy-done.5
  13.6 0.0 copy-done.7
  13.6 0.0 copy-start
  13.6 0.8 %subgrid.1 = bf16[256,128]{1,0:T(8,128)(2,1)S(1)} custom-call(bf16[256,128]{1,0:T(8,128)(2,1)S(1)} %bitcast.11, f32[256,128]{1,0:T(8,128)S(1)} %get-tuple-element.18.value_ref, f32[256,128]{1,0:T(8,128)S(1)} %get-tuple-element.19.weight_ref, f32[2,8,128]{2,1,0:T(8,128)S(1)} %copy-done.7, bf16[2,128,128]{2,1,0:T(8,128)(2,1)S(1)} %copy-done.5, ...), custom_call_target="tpu_custom_call" | custom-call | tf_op jit(solution)/shard_map/subgrid/pallas_call | solution.py:524
  14.4 0.0 copy-start.1
  14.5 0.0 copy-start.2
  14.5 7.7 %all_to_all.22 = bf16[16,16,128]{2,1,0:T(8,128)(2,1)S(1)} all-to-all(bf16[16,16,128]{2,1,0:T(8,128)(2,1)S(1)} %bitcast.12), channel_id=1, replica_groups={{15,0,2,4,6,8,10,12,14,1,3,5,7,9,11,13},{31,16,18,20,22,24,26,28,30,17,..., dimensions={0} | all-to-all | bytes 131072 | tf_op jit(solution)/shard_map/all_to_all | solution.py:609
  22.1 0.0 copy-done.3
  22.1 0.0 copy-done.6
  22.1 0.0 copy-done
  22.1 0.0 copy-done.1
  22.1 0.0 copy-done.2
  22.2 1.6 %lines.1 = f32[4,2,4096]{2,1,0:T(2,128)} custom-call(s32[1,128]{1,0:T(1,128)S(1)} %get-tuple-element.14.places_ref, bf16[256,128]{1,0:T(8,128)(2,1)S(1)} %bitcast.10, f32[128,128]{1,0:T(8,128)S(1)} %get-tuple-element.20.straight_ref, f32[128,128]{1,0:T(8,128)S(1)} %get-tuple-element.21.crossed_ref, bf16[256,256]{1,0:T(8,128)(2,1)S(1)} %get-tuple-element.22.put_ref, ...), custom_call_target="tpu_custom_call" | custom-call | tf_op jit(solution)/shard_map/lines/pallas_call | solution.py:524
Async XLA Ops:
  0.0 5.1 %copy-start.8 = (f32[1,1,2,8,4096]{4,3,2,1,0:T(8,128)S(1)}, f32[1,1,2,8,4096]{4,3,2,1,0:T(8,128)}, u32[]{:S(2)}) copy-start(f32[1,1,2,8,4096]{4,3,2,1,0:T(8,128)} %param.17) | copy-start | bytes 786436
  0.0 5.1 %copy-start.9 = (bf16[1792,128]{1,0:T(8,128)(2,1)S(1)}, bf16[1792,128]{1,0:T(8,128)(2,1)}, u32[]{:S(2)}) copy-start(bf16[1792,128]{1,0:T(8,128)(2,1)} %constant.32.clone.paired_table.paired_ref) | copy-start | bytes 1376260
  0.0 5.1 %copy-start.10 = (f32[160,128]{1,0:T(8,128)S(1)}, f32[160,128]{1,0:T(8,128)}, u32[]{:S(2)}) copy-start(f32[160,128]{1,0:T(8,128)} %constant.31.clone.plain_table.plain_ref) | copy-start | bytes 245764
  2.7 8.1 %collective-permute-start = (f32[8,512]{1,0:T(8,128)S(1)}, f32[8,512]{1,0:T(8,128)S(1)}, u32[]{:S(2)}, u32[]{:S(2)}) collective-permute-start(f32[8,512]{1,0:T(8,128)S(1)} %get-tuple-element.17.refs_0_), channel_id=1, source_target_pairs={{16,0},{0,16},{17,1},{1,17},{18,2},{2,18},{19,3},{3,19},{20,4},{4,... | collective-permute-start | bytes 49160 | tf_op jit(solution)/shard_map/ppermute | solution.py:590
  5.7 5.1 %copy-start.11 = (bf16[2,64,256]{2,1,0:T(8,128)(2,1)S(1)}, bf16[2,64,256]{2,1,0:T(8,128)(2,1)}, u32[]{:S(2)}) copy-start(bf16[2,64,256]{2,1,0:T(8,128)(2,1)} %constant.24.clone.shift_ref) | copy-start | bytes 196612
  5.7 7.8 %all-to-all-start = ((bf16[8,32,128]{2,1,0:T(8,128)(2,1)}), bf16[8,32,128]{2,1,0:T(8,128)(2,1)S(1)}, u32[]{:S(2)}, u32[]{:S(2)}) async-start(bf16[8,32,128]{2,1,0:T(8,128)(2,1)} %bitcast.5), calls=%async_computation | async-start | bytes 131072 | tf_op jit(solution)/shard_map/all_to_all | solution.py:591
  10.8 2.8 %copy-start.4 = (bf16[2,128,128]{2,1,0:T(8,128)(2,1)S(1)}, bf16[2,128,128]{2,1,0:T(8,128)(2,1)}, u32[]{:S(2)}) copy-start(bf16[2,128,128]{2,1,0:T(8,128)(2,1)} %constant.30.clone.back_ref) | copy-start | bytes 196612
  10.8 2.8 %copy-start.5 = (bf16[2,128,128]{2,1,0:T(8,128)(2,1)S(1)}, bf16[2,128,128]{2,1,0:T(8,128)(2,1)}, u32[]{:S(2)}) copy-start(bf16[2,128,128]{2,1,0:T(8,128)(2,1)} %constant.29.clone.model_ref) | copy-start | bytes 196612
  10.8 2.7 %copy-start.7 = (f32[2,8,128]{2,1,0:T(8,128)S(1)}, f32[2,8,128]{2,1,0:T(8,128)}, u32[]{:S(2)}) copy-start(f32[2,8,128]{2,1,0:T(8,128)} %constant.28.clone.turn_ref) | copy-start | bytes 24580
  10.8 11.3 %copy-start.3 = (f32[2,64,128]{2,1,0:T(8,128)S(1)}, f32[2,64,128]{2,1,0:T(8,128)}, u32[]{:S(2)}) copy-start(f32[2,64,128]{2,1,0:T(8,128)} %constant.23.clone.turn_ref) | copy-start | bytes 196612
  10.8 11.3 %copy-start.6 = (f32[64,128]{1,0:T(8,128)S(1)}, f32[64,128]{1,0:T(8,128)}, u32[]{:S(2)}) copy-start(f32[64,128]{1,0:T(8,128)} %constant.22.clone.window_ref) | copy-start | bytes 98308
  13.6 8.6 %copy-start = (bf16[2,256,256]{2,1,0:T(8,128)(2,1)S(1)}, bf16[2,256,256]{2,1,0:T(8,128)(2,1)}, u32[]{:S(2)}) copy-start(bf16[2,256,256]{2,1,0:T(8,128)(2,1)} %constant.25.clone.inner_ref) | copy-start | bytes 786436
  14.4 7.7 %copy-start.1 = (bf16[2,128,128]{2,1,0:T(8,128)(2,1)S(1)}, bf16[2,128,128]{2,1,0:T(8,128)(2,1)}, u32[]{:S(2)}) copy-start(bf16[2,128,128]{2,1,0:T(8,128)(2,1)} %constant.27.clone.partial_ref) | copy-start | bytes 196612
  14.5 7.7 %copy-start.2 = (bf16[2,128,128]{2,1,0:T(8,128)(2,1)S(1)}, bf16[2,128,128]{2,1,0:T(8,128)(2,1)}, u32[]{:S(2)}) copy-start(bf16[2,128,128]{2,1,0:T(8,128)(2,1)} %constant.26.clone.outer_ref) | copy-start | bytes 196612

commit v23 on v15

--- a/solution.py
+++ b/solution.py
@@ -90,11 +90,16 @@
                 piece=high_low(piece),
             )
         ),
-        window=window,
+        window=np.repeat(window, 2, axis=0),
         turn=turn,
         shift=shift,
         inner_plus=high_low(from_right(np.kron(pair, phases(short, short, CONTRIB, 1)))),
-        outer_plus=high_low(from_left(phases(outer, short, blocks, 1))),
+        outer_plus=high_low(
+            from_left(phases(outer, short, blocks, 1))
+            .reshape(2, blocks, 2 * CONTRIB)
+            .transpose(1, 0, 2)
+            .reshape(2 * blocks, 2 * CONTRIB)
+        ),
         partial=high_low(from_right(phases(short, short, CONTRIB, -1)).T * CONTRIB**-0.5),
         grid_turn=side_by_side(phases(np.arange(FACET_ROWS), short, SUBGRID, -1)).astype(
             np.float32
@@ -118,9 +123,9 @@
     return lax.dot_general(left, right, (dims, ((), ())), preferred_element_type=F32)
 
 
-def dot_split(values, right):
+def dot_split(values, right, dims=((1,), (0,))):
     rows = values.shape[0]
-    both = dot(jnp.concatenate(split(values), axis=0), right)
+    both = dot(jnp.concatenate(split(values), axis=0), right, dims)
     return both[:rows] + both[rows:]
 
 
@@ -477,9 +482,7 @@
     both = jnp.concatenate(
         [jnp.where(inside, residues, 0.0), jnp.where(inside, 0.0, residues)], axis=1
     )
-    put = put_ref[...]
-    high, low = split(both)
-    spectrum = dot(high, put, ((1,), (1,))) + dot(low, put, ((1,), (1,)))
+    spectrum = dot_split(both, put_ref[...], ((1,), (1,)))
     inner = times_table(
         jnp.concatenate(
             [
@@ -509,20 +512,13 @@
         ),
     )
     window = window_ref[...]
-    low_half = iota((groups, LANES), 1) < HALF
-    for part in range(2):
-        for pair in range(pairs):
-            lanes = slice(pair * LANES, (pair + 1) * LANES)
-            begin = part * blocks
-            even = lines[begin : begin + groups, lanes]
-            odd = lines[begin + groups : begin + blocks, lanes]
-            line_refs[2 * pair][pl.ds(part, groups, stride=2), :] = (
-                jnp.where(low_half, even, swap_halves(odd)) * window
-            )
-            if 2 * pair + 1 < columns:
-                line_refs[2 * pair + 1][pl.ds(part, groups, stride=2), :] = (
-                    jnp.where(low_half, swap_halves(even), odd) * window
-                )
+    low_half = iota((blocks, LANES), 1) < HALF
+    for pair in range(pairs):
+        lanes = slice(pair * LANES, (pair + 1) * LANES)
+        even, odd = lines[:blocks, lanes], lines[blocks:, lanes]
+        line_refs[2 * pair][...] = jnp.where(low_half, even, swap_halves(odd)) * window
+        if 2 * pair + 1 < columns:
+            line_refs[2 * pair + 1][...] = jnp.where(low_half, swap_halves(even), odd) * window
     for column in range(columns):
         for group in range(groups):
             out_ref[column, :, group * LANES : (group + 1) * LANES] = line_refs[column][
@@ -583,10 +579,11 @@
         landing(small + [offsets] + large) + [wide(held)] * 2 + [semaphores(4), semaphores(4)],
         *in_hbm(small + [offsets] + large), flops=EARLY_FLOPS,
     )
+    early, *later = lax.optimization_barrier((early, offsets, *large))
     pieces = kernel_call(
         functools.partial(late_kernel, plain=plain_places, paired=paired_places), "late",
         jax.ShapeDtypeStruct((rows, LANES), BF16), [pltpu.VMEM] * 5, [wide(held)] * 2,
-        early, offsets, *large, flops=LATE_FLOPS,
+        early, *later, flops=LATE_FLOPS,
     )
     gathered = [packed]
     for step in range(1, groups):

time: 24.1 us -> 24.1 us (level)
  no operation moved by 1% of the time
where the time goes in v23:
time: 24.1 us; the launch traced here: 23.8 us
  blocking collectives  7.7 us (32%)
  starting transfers between devices  7.41 us (31%)
  Pallas kernels  6.84 us (28%)
  waiting for transfers between devices  1.62 us (7%)
    all_to_all x1, blocking collectives, local(): lax.all_to_all(returned, ('band', 'member'), split_axis=0, concat_axis=0,...  7.7 us
    pallas_call x5, Pallas kernels, kernel_call(): pl.pallas_call(kernel, out_shape=out_shape, in_specs=[pl.BlockSpec(memory...  6.84 us
    all_to_all x1, starting transfers between devices, local(): lax.all_to_all(pieces, 'member', split_axis=0, concat_axis=0, tiled=True,...  5.09 us
    ppermute x1, starting transfers between devices, local(): gathered.append(lax.ppermute(packed, 'group', moves))  2.33 us
    all_to_all x1, waiting for transfers between devices, local(): lax.all_to_all(pieces, 'member', split_axis=0, concat_axis=0, tiled=True,...  1.62 us
  transfers between devices with their start and end apart: 2, of which 1 were waited for; matrix products, arithmetic and copies ran while one was open for 0% of the time, Pallas kernels for 7%

profile of v23, /device:TPU:0, one launch (start us, length us, event | category | flops | bytes accessed | tf_op | source)
XLA Modules:
  0.0 23.8 jit_solution(10020152744235205437)
XLA Ops:
  0.0 0.0 copy-start.8
  0.0 0.0 copy-start.10
  0.0 0.0 copy-start.11
  0.0 2.7 %early.1 = (bf16[256,128]{1,0:T(8,128)(2,1)S(1)}, f32[8,512]{1,0:T(8,128)S(1)}) custom-call(s32[2,2,512]{2,1,0:T(2,128)} %bitcast.15, f32[2,2,512]{2,1,0:T(2,128)} %bitcast.16, f32[2,1,512]{2,1,0:T(1,128)} %bitcast.17, s32[2,1,512]{2,1,0:T(1,128)} %bitcast.18, s32[2,16]{1,0:T(2,128)} %offsets_ref.2, f32[2,8,4096]{2,1,0:T(8,128)} %bitcast.13, ...), custom_call_target="tpu_custom_call" | custom-call | flops 10000000000 | tf_op jit(solution)/shard_map/early/pallas_call | solution.py:530
  2.7 0.0 copy-start.9
  2.7 2.3 %collective-permute-start = (f32[8,512]{1,0:T(8,128)S(1)}, f32[8,512]{1,0:T(8,128)S(1)}, u32[]{:S(2)}, u32[]{:S(2)}) collective-permute-start(f32[8,512]{1,0:T(8,128)S(1)} %get-tuple-element.18.refs_0_), channel_id=1, source_target_pairs={{16,0},{0,16},{17,1},{1,17},{18,2},{2,18},{19,3},{3,19},{20,4},{4,... | collective-permute-start | bytes 49160 | tf_op jit(solution)/shard_map/ppermute | solution.py:591
  5.0 0.0 copy-done.8
  5.0 0.0 copy-done.10
  5.0 0.0 copy-done.11
  5.0 0.0 copy-done.9
  5.0 0.7 %late.1 = bf16[256,128]{1,0:T(8,128)(2,1)} custom-call(bf16[256,128]{1,0:T(8,128)(2,1)S(1)} %get-tuple-element.21.early_ref, s32[2,16]{1,0:T(2,128)S(1)} %copy-done.9, f32[2,8,4096]{2,1,0:T(8,128)S(1)} %bitcast.14, f32[160,128]{1,0:T(8,128)S(1)} %copy-done.11, bf16[1792,128]{1,0:T(8,128)(2,1)S(1)} %copy-done.10), custom_call_target="tpu_custom_call" | custom-call | flops 10000000000 | tf_op jit(solution)/shard_map/late/pallas_call | solution.py:530
  5.7 0.0 copy-start.12
  5.7 5.1 %all-to-all-start = ((bf16[8,32,128]{2,1,0:T(8,128)(2,1)}), bf16[8,32,128]{2,1,0:T(8,128)(2,1)S(1)}, u32[]{:S(2)}, u32[]{:S(2)}) async-start(bf16[8,32,128]{2,1,0:T(8,128)(2,1)} %bitcast.5), calls=%async_computation | async-start | bytes 131072 | tf_op jit(solution)/shard_map/all_to_all | solution.py:592
  10.8 0.0 copy-start.4
  10.8 0.0 copy-start.5
  10.8 0.0 collective-permute-done.refs_1_
  10.8 0.0 copy-done.12
  10.8 0.0 copy-start.7
  10.8 0.0 copy-start.3
  10.8 0.0 copy-start.6
  10.8 1.0 %prepare.1 = (f32[256,128]{1,0:T(8,128)S(1)}, f32[256,128]{1,0:T(8,128)S(1)}, bf16[256,256]{1,0:T(8,128)(2,1)S(1)}, f32[128,128]{1,0:T(8,128)S(1)}, f32[128,128]{1,0:T(8,128)S(1)}, /*index=5*/s32[1,128]{1,0:T(1,128)S(1)}) custom-call(s32[2,16]{1,0:T(2,128)S(1)} %copy-done.9, bf16[2,64,256]{2,1,0:T(8,128)(2,1)S(1)} %copy-done.12, ...), custom_call_target="tpu_custom_call" | custom-call | flops 20000000000 | tf_op jit(solution)/shard_map/prepare/pallas_call | solution.py:530
  11.9 1.6 %all-to-all-done = bf16[8,32,128]{2,1,0:T(8,128)(2,1)S(1)} async-done(((bf16[8,32,128]{2,1,0:T(8,128)(2,1)}), bf16[8,32,128]{2,1,0:T(8,128)(2,1)S(1)}, u32[]{:S(2)}, u32[]{:S(2)}) %all-to-all-start) | async-done | bytes 65568 | tf_op jit(solution)/shard_map/all_to_all | solution.py:592
  13.5 0.0 copy-done.4
  13.5 0.0 copy-done.5
  13.5 0.0 copy-done.7
  13.5 0.0 copy-start
  13.5 0.8 %subgrid.1 = bf16[256,128]{1,0:T(8,128)(2,1)S(1)} custom-call(bf16[256,128]{1,0:T(8,128)(2,1)S(1)} %bitcast.11, f32[256,128]{1,0:T(8,128)S(1)} %get-tuple-element.26.value_ref, f32[256,128]{1,0:T(8,128)S(1)} %get-tuple-element.27.weight_ref, f32[2,8,128]{2,1,0:T(8,128)S(1)} %copy-done.7, bf16[2,128,128]{2,1,0:T(8,128)(2,1)S(1)} %copy-done.5, ...), custom_call_target="tpu_custom_call" | custom-call | tf_op jit(solution)/shard_map/subgrid/pallas_call | solution.py:530
  14.4 0.0 copy-start.1
  14.4 0.0 copy-start.2
  14.4 7.7 %all_to_all.22 = bf16[16,16,128]{2,1,0:T(8,128)(2,1)S(1)} all-to-all(bf16[16,16,128]{2,1,0:T(8,128)(2,1)S(1)} %bitcast.12), channel_id=1, replica_groups={{15,0,2,4,6,8,10,12,14,1,3,5,7,9,11,13},{31,16,18,20,22,24,26,28,30,17,..., dimensions={0} | all-to-all | bytes 131072 | tf_op jit(solution)/shard_map/all_to_all | solution.py:611
  22.1 0.0 copy-done.3
  22.1 0.0 copy-done.6
  22.1 0.0 copy-done
  22.1 0.0 copy-done.1
  22.1 0.0 copy-done.2
  22.1 1.6 %lines.1 = f32[4,2,4096]{2,1,0:T(2,128)} custom-call(s32[1,128]{1,0:T(1,128)S(1)} %get-tuple-element.19.places_ref, bf16[256,128]{1,0:T(8,128)(2,1)S(1)} %bitcast.10, f32[128,128]{1,0:T(8,128)S(1)} %get-tuple-element.28.straight_ref, f32[128,128]{1,0:T(8,128)S(1)} %get-tuple-element.29.crossed_ref, bf16[256,256]{1,0:T(8,128)(2,1)S(1)} %get-tuple-element.30.put_ref, ...), custom_call_target="tpu_custom_call" | custom-call | tf_op jit(solution)/shard_map/lines/pallas_call | solution.py:530
Async XLA Ops:
  0.0 5.0 %copy-start.8 = (f32[1,1,2,8,4096]{4,3,2,1,0:T(8,128)S(1)}, f32[1,1,2,8,4096]{4,3,2,1,0:T(8,128)}, u32[]{:S(2)}) copy-start(f32[1,1,2,8,4096]{4,3,2,1,0:T(8,128)} %param.17) | copy-start | bytes 786436
  0.0 5.0 %copy-start.10 = (bf16[1792,128]{1,0:T(8,128)(2,1)S(1)}, bf16[1792,128]{1,0:T(8,128)(2,1)}, u32[]{:S(2)}) copy-start(bf16[1792,128]{1,0:T(8,128)(2,1)} %constant.32.clone.paired_table.paired_ref) | copy-start | bytes 1376260
  0.0 5.0 %copy-start.11 = (f32[160,128]{1,0:T(8,128)S(1)}, f32[160,128]{1,0:T(8,128)}, u32[]{:S(2)}) copy-start(f32[160,128]{1,0:T(8,128)} %constant.31.clone.plain_table.plain_ref) | copy-start | bytes 245764
  2.7 2.3 %copy-start.9 = (s32[2,16]{1,0:T(2,128)S(1)}, s32[2,16]{1,0:T(2,128)}, u32[]{:S(2)}) copy-start(s32[2,16]{1,0:T(2,128)} %offsets_ref.2) | copy-start | bytes 388
  2.7 8.1 %collective-permute-start = (f32[8,512]{1,0:T(8,128)S(1)}, f32[8,512]{1,0:T(8,128)S(1)}, u32[]{:S(2)}, u32[]{:S(2)}) collective-permute-start(f32[8,512]{1,0:T(8,128)S(1)} %get-tuple-element.18.refs_0_), channel_id=1, source_target_pairs={{16,0},{0,16},{17,1},{1,17},{18,2},{2,18},{19,3},{3,19},{20,4},{4,... | collective-permute-start | bytes 49160 | tf_op jit(solution)/shard_map/ppermute | solution.py:591
  5.7 5.1 %copy-start.12 = (bf16[2,64,256]{2,1,0:T(8,128)(2,1)S(1)}, bf16[2,64,256]{2,1,0:T(8,128)(2,1)}, u32[]{:S(2)}) copy-start(bf16[2,64,256]{2,1,0:T(8,128)(2,1)} %constant.24.clone.shift_ref) | copy-start | bytes 196612
  5.7 7.8 %all-to-all-start = ((bf16[8,32,128]{2,1,0:T(8,128)(2,1)}), bf16[8,32,128]{2,1,0:T(8,128)(2,1)S(1)}, u32[]{:S(2)}, u32[]{:S(2)}) async-start(bf16[8,32,128]{2,1,0:T(8,128)(2,1)} %bitcast.5), calls=%async_computation | async-start | bytes 131072 | tf_op jit(solution)/shard_map/all_to_all | solution.py:592
  10.8 2.7 %copy-start.4 = (bf16[2,128,128]{2,1,0:T(8,128)(2,1)S(1)}, bf16[2,128,128]{2,1,0:T(8,128)(2,1)}, u32[]{:S(2)}) copy-start(bf16[2,128,128]{2,1,0:T(8,128)(2,1)} %constant.30.clone.back_ref) | copy-start | bytes 196612
  10.8 2.7 %copy-start.5 = (bf16[2,128,128]{2,1,0:T(8,128)(2,1)S(1)}, bf16[2,128,128]{2,1,0:T(8,128)(2,1)}, u32[]{:S(2)}) copy-start(bf16[2,128,128]{2,1,0:T(8,128)(2,1)} %constant.29.clone.model_ref) | copy-start | bytes 196612
  10.8 2.7 %copy-start.7 = (f32[2,8,128]{2,1,0:T(8,128)S(1)}, f32[2,8,128]{2,1,0:T(8,128)}, u32[]{:S(2)}) copy-start(f32[2,8,128]{2,1,0:T(8,128)} %constant.28.clone.turn_ref) | copy-start | bytes 24580
  10.8 11.3 %copy-start.3 = (f32[2,64,128]{2,1,0:T(8,128)S(1)}, f32[2,64,128]{2,1,0:T(8,128)}, u32[]{:S(2)}) copy-start(f32[2,64,128]{2,1,0:T(8,128)} %constant.23.clone.turn_ref) | copy-start | bytes 196612
  10.8 11.3 %copy-start.6 = (f32[64,128]{1,0:T(8,128)S(1)}, f32[64,128]{1,0:T(8,128)}, u32[]{:S(2)}) copy-start(f32[64,128]{1,0:T(8,128)} %constant.22.clone.window_ref) | copy-start | bytes 98308
  13.5 8.6 %copy-start = (bf16[2,256,256]{2,1,0:T(8,128)(2,1)S(1)}, bf16[2,256,256]{2,1,0:T(8,128)(2,1)}, u32[]{:S(2)}) copy-start(bf16[2,256,256]{2,1,0:T(8,128)(2,1)} %constant.25.clone.inner_ref) | copy-start | bytes 786436
  14.4 7.7 %copy-start.1 = (bf16[2,128,128]{2,1,0:T(8,128)(2,1)S(1)}, bf16[2,128,128]{2,1,0:T(8,128)(2,1)}, u32[]{:S(2)}) copy-start(bf16[2,128,128]{2,1,0:T(8,128)(2,1)} %constant.27.clone.partial_ref) | copy-start | bytes 196612
  14.4 7.7 %copy-start.2 = (bf16[2,128,128]{2,1,0:T(8,128)(2,1)S(1)}, bf16[2,128,128]{2,1,0:T(8,128)(2,1)}, u32[]{:S(2)}) copy-start(bf16[2,128,128]{2,1,0:T(8,128)(2,1)} %constant.26.clone.outer_ref) | copy-start | bytes 196612

commit v24 on v22

--- a/solution.py
+++ b/solution.py
@@ -111,7 +111,8 @@
 
 def return_order(bands):
     order = [(b, member) for b in range(bands) for member in PLACE_ORDER]
-    return order[-1:] + order[:-1]
+    lead = FACET_ROWS - 1
+    return order[lead : lead + 1] + order[:lead] + order[lead + 1 :]
 
 
 def split(values):

time: 24.1 us -> 24.8 us (1.029)
  blocking collectives: 7.66 us -> 8.37 us
    all_to_all x1, blocking collectives: 7.66 us -> 8.37 us  [local(): lax.all_to_all(returned, ('band', 'member'), split_axis=0, concat_axis=0,...]
where the time goes in v24:
time: 24.8 us; the launch traced here: 24.5 us
  blocking collectives  8.37 us (34%)
  starting transfers between devices  7.47 us (30%)
  Pallas kernels  6.6 us (27%)
  waiting for transfers between devices  1.86 us (8%)
    all_to_all x1, blocking collectives, local(): lax.all_to_all(returned, ('band', 'member'), split_axis=0, concat_axis=0,...  8.37 us
    pallas_call x5, Pallas kernels, kernel_call(): pl.pallas_call(kernel, out_shape=out_shape, in_specs=[pl.BlockSpec(memory...  6.6 us
    all_to_all x1, starting transfers between devices, local(): lax.all_to_all(pieces, 'member', split_axis=0, concat_axis=0, tiled=True,...  5.05 us
    ppermute x1, starting transfers between devices, local(): gathered.append(lax.ppermute(packed, 'group', moves))  2.42 us
    all_to_all x1, waiting for transfers between devices, local(): lax.all_to_all(pieces, 'member', split_axis=0, concat_axis=0, tiled=True,...  1.85 us
  transfers between devices with their start and end apart: 2, of which 1 were waited for; matrix products, arithmetic and copies ran while one was open for 0% of the time, Pallas kernels for 6%

profile of v24, /device:TPU:0, one launch (start us, length us, event | category | flops | bytes accessed | tf_op | source)
XLA Modules:
  0.0 24.5 jit_solution(3062185542655558050)
XLA Ops:
  0.0 0.0 copy-start.8
  0.0 0.0 copy-start.9
  0.0 0.0 copy-start.10
  0.0 2.6 %early.1 = (bf16[256,128]{1,0:T(8,128)(2,1)S(1)}, f32[8,512]{1,0:T(8,128)S(1)}, s32[1,128]{1,0:T(1,128)S(1)}, s32[1,256]{1,0:T(1,128)S(1)}) custom-call(s32[2,16]{1,0:T(2,128)} %offsets.1, s32[2,2,512]{2,1,0:T(2,128)} %bitcast.15, f32[2,2,512]{2,1,0:T(2,128)} %bitcast.16, f32[2,1,512]{2,1,0:T(1,128)} %bitcast.17, s32[2,1,512]{2,1,0:T(1,128)} %bitcast.18, ...), custom_call_target="tpu_custom_call" | custom-call | flops 10000000000 | tf_op jit(solution)/shard_map/early/pallas_call | solution.py:525
  2.7 2.4 %collective-permute-start = (f32[8,512]{1,0:T(8,128)S(1)}, f32[8,512]{1,0:T(8,128)S(1)}, u32[]{:S(2)}, u32[]{:S(2)}) collective-permute-start(f32[8,512]{1,0:T(8,128)S(1)} %get-tuple-element.17.refs_0_), channel_id=1, source_target_pairs={{16,0},{0,16},{17,1},{1,17},{18,2},{2,18},{19,3},{3,19},{20,4},{4,... | collective-permute-start | bytes 49160 | tf_op jit(solution)/shard_map/ppermute | solution.py:591
  5.1 0.0 copy-done.8
  5.1 0.0 copy-done.9
  5.1 0.0 copy-done.10
  5.1 0.6 %late.1 = bf16[256,128]{1,0:T(8,128)(2,1)} custom-call(bf16[256,128]{1,0:T(8,128)(2,1)S(1)} %get-tuple-element.15.early_ref, s32[1,256]{1,0:T(1,128)S(1)} %get-tuple-element.16.spread_ref, f32[2,8,4096]{2,1,0:T(8,128)S(1)} %bitcast.14, f32[160,128]{1,0:T(8,128)S(1)} %copy-done.10, bf16[1792,128]{1,0:T(8,128)(2,1)S(1)} %copy-done.9), custom_call_target="tpu_custom_call" | custom-call | flops 10000000000 | tf_op jit(solution)/shard_map/late/pallas_call | solution.py:525
  5.7 0.0 copy-start.11
  5.7 5.0 %all-to-all-start = ((bf16[8,32,128]{2,1,0:T(8,128)(2,1)}), bf16[8,32,128]{2,1,0:T(8,128)(2,1)S(1)}, u32[]{:S(2)}, u32[]{:S(2)}) async-start(bf16[8,32,128]{2,1,0:T(8,128)(2,1)} %bitcast.5), calls=%async_computation | async-start | bytes 131072 | tf_op jit(solution)/shard_map/all_to_all | solution.py:592
  10.8 0.0 collective-permute-done.refs_1_
  10.8 0.0 copy-done.11
  10.8 0.0 copy-start.4
  10.8 0.0 copy-start.5
  10.8 0.0 copy-start.7
  10.8 0.0 copy-start.3
  10.8 0.0 copy-start.6
  10.9 0.8 %prepare.1 = (f32[256,128]{1,0:T(8,128)S(1)}, f32[256,128]{1,0:T(8,128)S(1)}, bf16[256,256]{1,0:T(8,128)(2,1)S(1)}, f32[128,128]{1,0:T(8,128)S(1)}, f32[128,128]{1,0:T(8,128)S(1)}) custom-call(s32[1,128]{1,0:T(1,128)S(1)} %get-tuple-element.14.places_ref, bf16[2,64,256]{2,1,0:T(8,128)(2,1)S(1)} %copy-done.11, f32[8,512]{1,0:T(8,128)S(1)} %get-tuple-element.17.refs_0_, ...), custom_call_target="tpu_custom_call" | custom-call | flops 20000000000 | tf_op jit(solution)/shard_map/prepare/pallas_call | solution.py:525
  11.7 1.9 %all-to-all-done = bf16[8,32,128]{2,1,0:T(8,128)(2,1)S(1)} async-done(((bf16[8,32,128]{2,1,0:T(8,128)(2,1)}), bf16[8,32,128]{2,1,0:T(8,128)(2,1)S(1)}, u32[]{:S(2)}, u32[]{:S(2)}) %all-to-all-start) | async-done | bytes 65568 | tf_op jit(solution)/shard_map/all_to_all | solution.py:592
  13.6 0.0 copy-done.4
  13.6 0.0 copy-done.5
  13.6 0.0 copy-done.7
  13.6 0.0 copy-start
  13.6 0.8 %subgrid.1 = bf16[256,128]{1,0:T(8,128)(2,1)S(1)} custom-call(bf16[256,128]{1,0:T(8,128)(2,1)S(1)} %bitcast.11, f32[256,128]{1,0:T(8,128)S(1)} %get-tuple-element.18.value_ref, f32[256,128]{1,0:T(8,128)S(1)} %get-tuple-element.19.weight_ref, f32[2,8,128]{2,1,0:T(8,128)S(1)} %copy-done.7, bf16[2,128,128]{2,1,0:T(8,128)(2,1)S(1)} %copy-done.5, ...), custom_call_target="tpu_custom_call" | custom-call | tf_op jit(solution)/shard_map/subgrid/pallas_call | solution.py:525
  14.4 0.0 copy-start.1
  14.4 0.0 copy-start.2
  14.5 8.4 %all_to_all.22 = bf16[16,16,128]{2,1,0:T(8,128)(2,1)S(1)} all-to-all(bf16[16,16,128]{2,1,0:T(8,128)(2,1)S(1)} %bitcast.12), channel_id=1, replica_groups={{14,0,2,4,6,8,10,12,1,3,5,7,9,11,13,15},{30,16,18,20,22,24,26,28,17,19,..., dimensions={0} | all-to-all | bytes 131072 | tf_op jit(solution)/shard_map/all_to_all | solution.py:610
  22.8 0.0 copy-done.3
  22.8 0.0 copy-done.6
  22.8 0.0 copy-done
  22.8 0.0 copy-done.1
  22.9 0.0 copy-done.2
  22.9 1.6 %lines.1 = f32[4,2,4096]{2,1,0:T(2,128)} custom-call(s32[1,128]{1,0:T(1,128)S(1)} %get-tuple-element.14.places_ref, bf16[256,128]{1,0:T(8,128)(2,1)S(1)} %bitcast.10, f32[128,128]{1,0:T(8,128)S(1)} %get-tuple-element.20.straight_ref, f32[128,128]{1,0:T(8,128)S(1)} %get-tuple-element.21.crossed_ref, bf16[256,256]{1,0:T(8,128)(2,1)S(1)} %get-tuple-element.22.put_ref, ...), custom_call_target="tpu_custom_call" | custom-call | tf_op jit(solution)/shard_map/lines/pallas_call | solution.py:525
Async XLA Ops:
  0.0 5.1 %copy-start.8 = (f32[1,1,2,8,4096]{4,3,2,1,0:T(8,128)S(1)}, f32[1,1,2,8,4096]{4,3,2,1,0:T(8,128)}, u32[]{:S(2)}) copy-start(f32[1,1,2,8,4096]{4,3,2,1,0:T(8,128)} %param.17) | copy-start | bytes 786436
  0.0 5.1 %copy-start.9 = (bf16[1792,128]{1,0:T(8,128)(2,1)S(1)}, bf16[1792,128]{1,0:T(8,128)(2,1)}, u32[]{:S(2)}) copy-start(bf16[1792,128]{1,0:T(8,128)(2,1)} %constant.32.clone.paired_table.paired_ref) | copy-start | bytes 1376260
  0.0 5.1 %copy-start.10 = (f32[160,128]{1,0:T(8,128)S(1)}, f32[160,128]{1,0:T(8,128)}, u32[]{:S(2)}) copy-start(f32[160,128]{1,0:T(8,128)} %constant.31.clone.plain_table.plain_ref) | copy-start | bytes 245764
  2.7 8.1 %collective-permute-start = (f32[8,512]{1,0:T(8,128)S(1)}, f32[8,512]{1,0:T(8,128)S(1)}, u32[]{:S(2)}, u32[]{:S(2)}) collective-permute-start(f32[8,512]{1,0:T(8,128)S(1)} %get-tuple-element.17.refs_0_), channel_id=1, source_target_pairs={{16,0},{0,16},{17,1},{1,17},{18,2},{2,18},{19,3},{3,19},{20,4},{4,... | collective-permute-start | bytes 49160 | tf_op jit(solution)/shard_map/ppermute | solution.py:591
  5.7 5.1 %copy-start.11 = (bf16[2,64,256]{2,1,0:T(8,128)(2,1)S(1)}, bf16[2,64,256]{2,1,0:T(8,128)(2,1)}, u32[]{:S(2)}) copy-start(bf16[2,64,256]{2,1,0:T(8,128)(2,1)} %constant.24.clone.shift_ref) | copy-start | bytes 196612
  5.7 7.8 %all-to-all-start = ((bf16[8,32,128]{2,1,0:T(8,128)(2,1)}), bf16[8,32,128]{2,1,0:T(8,128)(2,1)S(1)}, u32[]{:S(2)}, u32[]{:S(2)}) async-start(bf16[8,32,128]{2,1,0:T(8,128)(2,1)} %bitcast.5), calls=%async_computation | async-start | bytes 131072 | tf_op jit(solution)/shard_map/all_to_all | solution.py:592
  10.8 2.8 %copy-start.4 = (bf16[2,128,128]{2,1,0:T(8,128)(2,1)S(1)}, bf16[2,128,128]{2,1,0:T(8,128)(2,1)}, u32[]{:S(2)}) copy-start(bf16[2,128,128]{2,1,0:T(8,128)(2,1)} %constant.30.clone.back_ref) | copy-start | bytes 196612
  10.8 2.8 %copy-start.5 = (bf16[2,128,128]{2,1,0:T(8,128)(2,1)S(1)}, bf16[2,128,128]{2,1,0:T(8,128)(2,1)}, u32[]{:S(2)}) copy-start(bf16[2,128,128]{2,1,0:T(8,128)(2,1)} %constant.29.clone.model_ref) | copy-start | bytes 196612
  10.8 2.7 %copy-start.7 = (f32[2,8,128]{2,1,0:T(8,128)S(1)}, f32[2,8,128]{2,1,0:T(8,128)}, u32[]{:S(2)}) copy-start(f32[2,8,128]{2,1,0:T(8,128)} %constant.28.clone.turn_ref) | copy-start | bytes 24580
  10.8 12.0 %copy-start.3 = (f32[2,64,128]{2,1,0:T(8,128)S(1)}, f32[2,64,128]{2,1,0:T(8,128)}, u32[]{:S(2)}) copy-start(f32[2,64,128]{2,1,0:T(8,128)} %constant.23.clone.turn_ref) | copy-start | bytes 196612
  10.8 12.0 %copy-start.6 = (f32[64,128]{1,0:T(8,128)S(1)}, f32[64,128]{1,0:T(8,128)}, u32[]{:S(2)}) copy-start(f32[64,128]{1,0:T(8,128)} %constant.22.clone.window_ref) | copy-start | bytes 98308
  13.6 9.3 %copy-start = (bf16[2,256,256]{2,1,0:T(8,128)(2,1)S(1)}, bf16[2,256,256]{2,1,0:T(8,128)(2,1)}, u32[]{:S(2)}) copy-start(bf16[2,256,256]{2,1,0:T(8,128)(2,1)} %constant.25.clone.inner_ref) | copy-start | bytes 786436
  14.4 8.4 %copy-start.1 = (bf16[2,128,128]{2,1,0:T(8,128)(2,1)S(1)}, bf16[2,128,128]{2,1,0:T(8,128)(2,1)}, u32[]{:S(2)}) copy-start(bf16[2,128,128]{2,1,0:T(8,128)(2,1)} %constant.27.clone.partial_ref) | copy-start | bytes 196612
  14.4 8.4 %copy-start.2 = (bf16[2,128,128]{2,1,0:T(8,128)(2,1)S(1)}, bf16[2,128,128]{2,1,0:T(8,128)(2,1)}, u32[]{:S(2)}) copy-start(bf16[2,128,128]{2,1,0:T(8,128)(2,1)} %constant.26.clone.outer_ref) | copy-start | bytes 196612

commit v25 on v22

--- a/solution.py
+++ b/solution.py
@@ -452,7 +452,7 @@
 
 def return_kernel(
     places_ref, pieces_ref, straight_ref, crossed_ref, put_ref, window_ref, turn_ref, partial_ref,
-    inner_ref, outer_ref, out_ref, *line_refs, bands,
+    inner_ref, outer_ref, out_ref, *, bands,
 ):
     columns, _, length = out_ref.shape
     blocks = length // CONTRIB
@@ -510,14 +510,16 @@
     for pair in range(pairs):
         lanes = slice(pair * LANES, (pair + 1) * LANES)
         even, odd = lines[:blocks, lanes], lines[blocks:, lanes]
-        line_refs[2 * pair][...] = jnp.where(low_half, even, swap_halves(odd)) * window
-        if 2 * pair + 1 < columns:
-            line_refs[2 * pair + 1][...] = jnp.where(low_half, swap_halves(even), odd) * window
-    for column in range(columns):
-        for group in range(groups):
-            out_ref[column, :, group * LANES : (group + 1) * LANES] = line_refs[column][
-                2 * group : 2 * group + 2, :
-            ]
+        both = (
+            jnp.where(low_half, even, swap_halves(odd)) * window,
+            jnp.where(low_half, swap_halves(even), odd) * window,
+        )
+        for column in range(2 * pair, min(2 * pair + 2, columns)):
+            line = both[column - 2 * pair]
+            for group in range(groups):
+                out_ref[column, :, group * LANES : (group + 1) * LANES] = line[
+                    2 * group : 2 * group + 2, :
+                ]
 
 
 def kernel_call(kernel, name, out_shape, spaces, scratch, *operands, flops=0):
@@ -615,7 +617,7 @@
     lines = kernel_call(
         functools.partial(return_kernel, bands=bands), "lines",
         jax.ShapeDtypeStruct((share, 2, length), F32), [pltpu.VMEM] * 10,
-        [wide(2 * length // LANES)] * share,
+        [],
         places, delivered, straight, crossed, put, made["window"], made["turn"],
         made["partial"], made["inner_plus"], made["outer_plus"],
     )

time: 24.1 us -> 24.1 us (level)
  no operation moved by 1% of the time
where the time goes in v25:
time: 24.1 us; the launch traced here: 23.8 us
  blocking collectives  7.66 us (32%)
  starting transfers between devices  7.47 us (31%)
  Pallas kernels  6.59 us (27%)
  waiting for transfers between devices  1.86 us (8%)
    all_to_all x1, blocking collectives, local(): lax.all_to_all(returned, ('band', 'member'), split_axis=0, concat_axis=0,...  7.66 us
    pallas_call x5, Pallas kernels, kernel_call(): pl.pallas_call(kernel, out_shape=out_shape, in_specs=[pl.BlockSpec(memory...  6.59 us
    all_to_all x1, starting transfers between devices, local(): lax.all_to_all(pieces, 'member', split_axis=0, concat_axis=0, tiled=True,...  5.05 us
    ppermute x1, starting transfers between devices, local(): gathered.append(lax.ppermute(packed, 'group', moves))  2.42 us
    all_to_all x1, waiting for transfers between devices, local(): lax.all_to_all(pieces, 'member', split_axis=0, concat_axis=0, tiled=True,...  1.85 us
  transfers between devices with their start and end apart: 2, of which 1 were waited for; matrix products, arithmetic and copies ran while one was open for 0% of the time, Pallas kernels for 6%

profile of v25, /device:TPU:0, one launch (start us, length us, event | category | flops | bytes accessed | tf_op | source)
XLA Modules:
  0.0 23.8 jit_solution(15013164472830196136)
XLA Ops:
  0.0 0.0 copy-start.8
  0.0 0.0 copy-start.9
  0.0 0.0 copy-start.10
  0.0 2.6 %early.1 = (bf16[256,128]{1,0:T(8,128)(2,1)S(1)}, f32[8,512]{1,0:T(8,128)S(1)}, s32[1,128]{1,0:T(1,128)S(1)}, s32[1,256]{1,0:T(1,128)S(1)}) custom-call(s32[2,16]{1,0:T(2,128)} %offsets.1, s32[2,2,512]{2,1,0:T(2,128)} %bitcast.15, f32[2,2,512]{2,1,0:T(2,128)} %bitcast.16, f32[2,1,512]{2,1,0:T(1,128)} %bitcast.17, s32[2,1,512]{2,1,0:T(1,128)} %bitcast.18, ...), custom_call_target="tpu_custom_call" | custom-call | flops 10000000000 | tf_op jit(solution)/shard_map/early/pallas_call | solution.py:526
  2.7 2.4 %collective-permute-start = (f32[8,512]{1,0:T(8,128)S(1)}, f32[8,512]{1,0:T(8,128)S(1)}, u32[]{:S(2)}, u32[]{:S(2)}) collective-permute-start(f32[8,512]{1,0:T(8,128)S(1)} %get-tuple-element.17.refs_0_), channel_id=1, source_target_pairs={{16,0},{0,16},{17,1},{1,17},{18,2},{2,18},{19,3},{3,19},{20,4},{4,... | collective-permute-start | bytes 49160 | tf_op jit(solution)/shard_map/ppermute | solution.py:592
  5.1 0.0 copy-done.8
  5.1 0.0 copy-done.9
  5.1 0.0 copy-done.10
  5.1 0.6 %late.1 = bf16[256,128]{1,0:T(8,128)(2,1)} custom-call(bf16[256,128]{1,0:T(8,128)(2,1)S(1)} %get-tuple-element.15.early_ref, s32[1,256]{1,0:T(1,128)S(1)} %get-tuple-element.16.spread_ref, f32[2,8,4096]{2,1,0:T(8,128)S(1)} %bitcast.14, f32[160,128]{1,0:T(8,128)S(1)} %copy-done.10, bf16[1792,128]{1,0:T(8,128)(2,1)S(1)} %copy-done.9), custom_call_target="tpu_custom_call" | custom-call | flops 10000000000 | tf_op jit(solution)/shard_map/late/pallas_call | solution.py:526
  5.7 0.0 copy-start.11
  5.7 5.0 %all-to-all-start = ((bf16[8,32,128]{2,1,0:T(8,128)(2,1)}), bf16[8,32,128]{2,1,0:T(8,128)(2,1)S(1)}, u32[]{:S(2)}, u32[]{:S(2)}) async-start(bf16[8,32,128]{2,1,0:T(8,128)(2,1)} %bitcast.5), calls=%async_computation | async-start | bytes 131072 | tf_op jit(solution)/shard_map/all_to_all | solution.py:593
  10.8 0.0 collective-permute-done.refs_1_
  10.8 0.0 copy-done.11
  10.8 0.0 copy-start.4
  10.8 0.0 copy-start.5
  10.8 0.0 copy-start.7
  10.8 0.0 copy-start.3
  10.8 0.0 copy-start.6
  10.9 0.8 %prepare.1 = (f32[256,128]{1,0:T(8,128)S(1)}, f32[256,128]{1,0:T(8,128)S(1)}, bf16[256,256]{1,0:T(8,128)(2,1)S(1)}, f32[128,128]{1,0:T(8,128)S(1)}, f32[128,128]{1,0:T(8,128)S(1)}) custom-call(s32[1,128]{1,0:T(1,128)S(1)} %get-tuple-element.14.places_ref, bf16[2,64,256]{2,1,0:T(8,128)(2,1)S(1)} %copy-done.11, f32[8,512]{1,0:T(8,128)S(1)} %get-tuple-element.17.refs_0_, ...), custom_call_target="tpu_custom_call" | custom-call | flops 20000000000 | tf_op jit(solution)/shard_map/prepare/pallas_call | solution.py:526
  11.7 1.9 %all-to-all-done = bf16[8,32,128]{2,1,0:T(8,128)(2,1)S(1)} async-done(((bf16[8,32,128]{2,1,0:T(8,128)(2,1)}), bf16[8,32,128]{2,1,0:T(8,128)(2,1)S(1)}, u32[]{:S(2)}, u32[]{:S(2)}) %all-to-all-start) | async-done | bytes 65568 | tf_op jit(solution)/shard_map/all_to_all | solution.py:593
  13.6 0.0 copy-done.4
  13.6 0.0 copy-done.5
  13.6 0.0 copy-done.7
  13.6 0.0 copy-start
  13.6 0.8 %subgrid.1 = bf16[256,128]{1,0:T(8,128)(2,1)S(1)} custom-call(bf16[256,128]{1,0:T(8,128)(2,1)S(1)} %bitcast.11, f32[256,128]{1,0:T(8,128)S(1)} %get-tuple-element.18.value_ref, f32[256,128]{1,0:T(8,128)S(1)} %get-tuple-element.19.weight_ref, f32[2,8,128]{2,1,0:T(8,128)S(1)} %copy-done.7, bf16[2,128,128]{2,1,0:T(8,128)(2,1)S(1)} %copy-done.5, ...), custom_call_target="tpu_custom_call" | custom-call | tf_op jit(solution)/shard_map/subgrid/pallas_call | solution.py:526
  14.4 0.0 copy-start.1
  14.5 0.0 copy-start.2
  14.5 7.7 %all_to_all.22 = bf16[16,16,128]{2,1,0:T(8,128)(2,1)S(1)} all-to-all(bf16[16,16,128]{2,1,0:T(8,128)(2,1)S(1)} %bitcast.12), channel_id=1, replica_groups={{15,0,2,4,6,8,10,12,14,1,3,5,7,9,11,13},{31,16,18,20,22,24,26,28,30,17,..., dimensions={0} | all-to-all | bytes 131072 | tf_op jit(solution)/shard_map/all_to_all | solution.py:611
  22.1 0.0 copy-done.3
  22.1 0.0 copy-done.6
  22.1 0.0 copy-done
  22.1 0.0 copy-done.1
  22.1 0.0 copy-done.2
  22.2 1.6 %lines.1 = f32[4,2,4096]{2,1,0:T(2,128)} custom-call(s32[1,128]{1,0:T(1,128)S(1)} %get-tuple-element.14.places_ref, bf16[256,128]{1,0:T(8,128)(2,1)S(1)} %bitcast.10, f32[128,128]{1,0:T(8,128)S(1)} %get-tuple-element.20.straight_ref, f32[128,128]{1,0:T(8,128)S(1)} %get-tuple-element.21.crossed_ref, bf16[256,256]{1,0:T(8,128)(2,1)S(1)} %get-tuple-element.22.put_ref, ...), custom_call_target="tpu_custom_call" | custom-call | tf_op jit(solution)/shard_map/lines/pallas_call | solution.py:526
Async XLA Ops:
  0.0 5.1 %copy-start.8 = (f32[1,1,2,8,4096]{4,3,2,1,0:T(8,128)S(1)}, f32[1,1,2,8,4096]{4,3,2,1,0:T(8,128)}, u32[]{:S(2)}) copy-start(f32[1,1,2,8,4096]{4,3,2,1,0:T(8,128)} %param.17) | copy-start | bytes 786436
  0.0 5.1 %copy-start.9 = (bf16[1792,128]{1,0:T(8,128)(2,1)S(1)}, bf16[1792,128]{1,0:T(8,128)(2,1)}, u32[]{:S(2)}) copy-start(bf16[1792,128]{1,0:T(8,128)(2,1)} %constant.32.clone.paired_table.paired_ref) | copy-start | bytes 1376260
  0.0 5.1 %copy-start.10 = (f32[160,128]{1,0:T(8,128)S(1)}, f32[160,128]{1,0:T(8,128)}, u32[]{:S(2)}) copy-start(f32[160,128]{1,0:T(8,128)} %constant.31.clone.plain_table.plain_ref) | copy-start | bytes 245764
  2.7 8.1 %collective-permute-start = (f32[8,512]{1,0:T(8,128)S(1)}, f32[8,512]{1,0:T(8,128)S(1)}, u32[]{:S(2)}, u32[]{:S(2)}) collective-permute-start(f32[8,512]{1,0:T(8,128)S(1)} %get-tuple-element.17.refs_0_), channel_id=1, source_target_pairs={{16,0},{0,16},{17,1},{1,17},{18,2},{2,18},{19,3},{3,19},{20,4},{4,... | collective-permute-start | bytes 49160 | tf_op jit(solution)/shard_map/ppermute | solution.py:592
  5.7 5.1 %copy-start.11 = (bf16[2,64,256]{2,1,0:T(8,128)(2,1)S(1)}, bf16[2,64,256]{2,1,0:T(8,128)(2,1)}, u32[]{:S(2)}) copy-start(bf16[2,64,256]{2,1,0:T(8,128)(2,1)} %constant.24.clone.shift_ref) | copy-start | bytes 196612
  5.7 7.8 %all-to-all-start = ((bf16[8,32,128]{2,1,0:T(8,128)(2,1)}), bf16[8,32,128]{2,1,0:T(8,128)(2,1)S(1)}, u32[]{:S(2)}, u32[]{:S(2)}) async-start(bf16[8,32,128]{2,1,0:T(8,128)(2,1)} %bitcast.5), calls=%async_computation | async-start | bytes 131072 | tf_op jit(solution)/shard_map/all_to_all | solution.py:593
  10.8 2.8 %copy-start.4 = (bf16[2,128,128]{2,1,0:T(8,128)(2,1)S(1)}, bf16[2,128,128]{2,1,0:T(8,128)(2,1)}, u32[]{:S(2)}) copy-start(bf16[2,128,128]{2,1,0:T(8,128)(2,1)} %constant.30.clone.back_ref) | copy-start | bytes 196612
  10.8 2.8 %copy-start.5 = (bf16[2,128,128]{2,1,0:T(8,128)(2,1)S(1)}, bf16[2,128,128]{2,1,0:T(8,128)(2,1)}, u32[]{:S(2)}) copy-start(bf16[2,128,128]{2,1,0:T(8,128)(2,1)} %constant.29.clone.model_ref) | copy-start | bytes 196612
  10.8 2.7 %copy-start.7 = (f32[2,8,128]{2,1,0:T(8,128)S(1)}, f32[2,8,128]{2,1,0:T(8,128)}, u32[]{:S(2)}) copy-start(f32[2,8,128]{2,1,0:T(8,128)} %constant.28.clone.turn_ref) | copy-start | bytes 24580
  10.8 11.3 %copy-start.3 = (f32[2,64,128]{2,1,0:T(8,128)S(1)}, f32[2,64,128]{2,1,0:T(8,128)}, u32[]{:S(2)}) copy-start(f32[2,64,128]{2,1,0:T(8,128)} %constant.23.clone.turn_ref) | copy-start | bytes 196612
  10.8 11.3 %copy-start.6 = (f32[64,128]{1,0:T(8,128)S(1)}, f32[64,128]{1,0:T(8,128)}, u32[]{:S(2)}) copy-start(f32[64,128]{1,0:T(8,128)} %constant.22.clone.window_ref) | copy-start | bytes 98308
  13.6 8.6 %copy-start = (bf16[2,256,256]{2,1,0:T(8,128)(2,1)S(1)}, bf16[2,256,256]{2,1,0:T(8,128)(2,1)}, u32[]{:S(2)}) copy-start(bf16[2,256,256]{2,1,0:T(8,128)(2,1)} %constant.25.clone.inner_ref) | copy-start | bytes 786436
  14.4 7.7 %copy-start.1 = (bf16[2,128,128]{2,1,0:T(8,128)(2,1)S(1)}, bf16[2,128,128]{2,1,0:T(8,128)(2,1)}, u32[]{:S(2)}) copy-start(bf16[2,128,128]{2,1,0:T(8,128)(2,1)} %constant.27.clone.partial_ref) | copy-start | bytes 196612
  14.5 7.7 %copy-start.2 = (bf16[2,128,128]{2,1,0:T(8,128)(2,1)S(1)}, bf16[2,128,128]{2,1,0:T(8,128)(2,1)}, u32[]{:S(2)}) copy-start(bf16[2,128,128]{2,1,0:T(8,128)(2,1)} %constant.26.clone.outer_ref) | copy-start | bytes 196612
